TPU v7x, 32 devices: a whole 2x2x4 slice. The times are simulated.
32 devices in a mesh: groups: 2 (over y), seq: 16 (over z, x, core).
Axes of the slice: x: 2, y: 2, z: 4, core: 2. Of those that a mesh axis runs over, the one named last changes fastest.
Arguments:
- queries: bfloat16 [4, 32, 64, 3072], P('groups', 'seq'), parts along dimension 0, may hold values from -10 to 10
- own_kv: bfloat16 [4, 32, 64, 1024], P('groups', 'seq'), parts along dimension 0, may hold values from -10 to 10
- past_kv: bfloat16 [64, 16, 1024], P(('groups', 'seq')), parts along dimension 0, may hold values from -8 to 8
- block_home: int32 [64], P('groups'), parts along dimension 0, may hold values from 0 to 31, as said below
- block_list: int32 [32, 16], P('groups'), parts along dimension 0, may hold values from 0 to 31, as said below
- list_len: int32 [32], P('groups'), parts along dimension 0, may hold values from 1 to 16, as said below
- final_weight: bfloat16 [3072, 64], P('seq'), may hold values from -0.4375 to 0.4375
- decoder_weight: bfloat16 [432, 512], P(None, 'seq'), may hold values from -0.3125 to 0.3125
Outputs:
- features: bfloat16 [4, 64, 128, 512], P('groups', 'seq'), parts along dimension 0
There are 2 independent parts, one for each index of `groups`. A program takes and returns all parts, laid end to end along the dimension named above; an argument that names none is the same for every part. Nothing has to cross between parts.
Inputs may be any that keep to these rules, and one draw needn't show every extreme that they name: Block i is stored at row block_home[i] of past_kv; every row holds one block. `block_list`: for each tile b the first list_len[b] entries name blocks stored by pairwise different devices (storage row // 2); later entries are not read. `list_len`: some tile lists 16 blocks.
All inputs are finite; a program needn't handle non-finite values.
Results may differ from a plain program's by a relative error of at most 0.0064.
Values may be sent and summed in bfloat16 or wider, within the bound.
No kernel may reach another device: no remote copies, remote signals or barrier semaphores. Data moves between devices by JAX's collectives and lax.ppermute only.
A program may use at most 64 MiB of HBM per device.

v0:
```python
import math

import jax
import jax.numpy as jnp
from jax import lax
from jax.sharding import PartitionSpec as P

HEADS = 24
KV_HEADS = 4
HEAD_DIM = 128


def extended(cells, sides, width):
    for axis, dim in sides:
        count = lax.axis_size(axis)
        ends = count - 1
        head = lax.slice_in_dim(cells, 0, width, axis=dim)
        tail = lax.slice_in_dim(cells, cells.shape[dim] - width, cells.shape[dim], axis=dim)
        cells = jnp.concatenate(
            [
                lax.ppermute(tail, axis, [(i, (i + 1) % count) for i in range(ends)]),
                cells,
                lax.ppermute(head, axis, [((i + 1) % count, i) for i in range(ends)]),
            ],
            axis=dim,
        )
    return cells


def pair_scores(query_block, key_rows):
    return lax.dot_general(
        query_block, key_rows, (((1,), (1,)), ((), ())), preferred_element_type=jnp.float32
    )


def local(queries, own_kv, past_kv, block_home, block_list, list_len, final_weight, decoder_weight):
    frames, patch_rows, patches, width_query = queries.shape
    tokens = frames * patch_rows * patches
    devices = lax.axis_size("seq")
    self_index = lax.axis_index("seq")
    key_width = own_kv.shape[3] // 2
    blocks_here = past_kv.shape[0]
    block_tokens = past_kv.shape[1]
    query_rows = queries.reshape(tokens, width_query)
    own_rows = own_kv.reshape(tokens, 2 * key_width)
    stored_at = block_home[block_list]
    entry_index = lax.broadcasted_iota(jnp.int32, block_list.shape, 1)
    listed = entry_index < list_len[:, None]
    own_homes = lax.dynamic_index_in_dim(stored_at, self_index, 0, keepdims=False)
    own_listed = lax.dynamic_index_in_dim(listed, self_index, 0, keepdims=False)
    owners = stored_at // blocks_here
    wanted = listed & (owners == self_index)
    local_index = jnp.sum(jnp.where(wanted, stored_at % blocks_here, 0), axis=1)
    selector = (
        jnp.any(wanted, axis=1)[:, None]
        & (local_index[:, None] == jnp.arange(blocks_here, dtype=jnp.int32)[None, :])
    ).astype(jnp.bfloat16)
    outgoing = jnp.einsum("rb,btc->rtc", selector, past_kv, preferred_element_type=jnp.bfloat16)
    arrived = lax.all_to_all(outgoing, "seq", split_axis=0, concat_axis=0, tiled=True)
    sources = jnp.arange(devices, dtype=jnp.int32)
    present = jnp.any(
        own_listed[:, None] & ((own_homes // blocks_here)[:, None] == sources[None, :]), axis=0
    )
    past_rows = arrived.reshape(devices * block_tokens, 2 * key_width)
    past_listed = jnp.repeat(present, block_tokens)
    group_size = HEADS // KV_HEADS
    pair_count = group_size // 2
    score_scale = 1.0 / math.sqrt(HEAD_DIM)
    query_blocks = query_rows.reshape(tokens, KV_HEADS, pair_count, 2, HEAD_DIM).transpose(
        1, 2, 3, 0, 4
    )
    query_blocks = query_blocks.reshape(KV_HEADS * pair_count, 2 * tokens, HEAD_DIM)

    def one_block(packed):
        query_block, block_index = packed
        head_index = block_index // pair_count
        keys_own = lax.dynamic_slice_in_dim(own_rows, head_index * HEAD_DIM, HEAD_DIM, 1)
        values_own = lax.dynamic_slice_in_dim(
            own_rows, key_width + head_index * HEAD_DIM, HEAD_DIM, 1
        )
        keys_past = lax.dynamic_slice_in_dim(past_rows, head_index * HEAD_DIM, HEAD_DIM, 1)
        values_past = lax.dynamic_slice_in_dim(
            past_rows, key_width + head_index * HEAD_DIM, HEAD_DIM, 1
        )
        scores_own = pair_scores(query_block, keys_own) * score_scale
        scores_past = jnp.where(
            past_listed[None, :], pair_scores(query_block, keys_past) * score_scale, -1e30
        )
        row_top = jnp.maximum(
            jnp.max(scores_own, axis=1, keepdims=True), jnp.max(scores_past, axis=1, keepdims=True)
        )
        exp_own = jnp.exp(scores_own - row_top)
        exp_past = jnp.where(past_listed[None, :], jnp.exp(scores_past - row_top), 0.0)
        denominator = jnp.sum(exp_own, axis=1, keepdims=True) + jnp.sum(
            exp_past, axis=1, keepdims=True
        )
        weights_own = (exp_own / denominator).astype(jnp.bfloat16)
        weights_past = (exp_past / denominator).astype(jnp.bfloat16)
        mixed = jnp.dot(weights_own, values_own, preferred_element_type=jnp.float32)
        return mixed + jnp.dot(weights_past, values_past, preferred_element_type=jnp.float32)

    outputs = lax.map(one_block, (query_blocks, jnp.arange(KV_HEADS * pair_count, dtype=jnp.int32)))
    attended = outputs.reshape(KV_HEADS, pair_count, 2, tokens, HEAD_DIM).transpose(3, 0, 1, 2, 4)
    attended = attended.reshape(tokens, width_query).astype(jnp.bfloat16)
    patch_values = final_weight.shape[1]
    predicted = jnp.dot(
        attended,
        lax.all_gather(final_weight, "seq", axis=0, tiled=True),
        preferred_element_type=jnp.float32,
    )
    predicted = predicted.astype(jnp.bfloat16)
    latent_width = patch_values // 4
    latent = predicted.reshape(frames, patch_rows, patches, 2, 2, latent_width).transpose(
        0, 1, 3, 2, 4, 5
    )
    latent = latent.reshape(frames, 2 * patch_rows, 2 * patches, latent_width)
    bordered = extended(latent, (("seq", 1),), 1)
    padded = jnp.pad(bordered, ((2, 0), (0, 0), (1, 1), (0, 0)))
    tall = 2 * patch_rows
    broad = 2 * patches
    tap_list = []
    for shift_t in range(3):
        for shift_y in range(3):
            for shift_x in range(3):
                tap_list.append(
                    padded[
                        shift_t : shift_t + frames,
                        shift_y : shift_y + tall,
                        shift_x : shift_x + broad,
                        :,
                    ]
                )
    columns = jnp.concatenate(tap_list, axis=3).reshape(frames * tall * broad, 27 * latent_width)
    features = jnp.dot(
        columns,
        lax.all_gather(decoder_weight, "seq", axis=1, tiled=True),
        preferred_element_type=jnp.float32,
    ).astype(jnp.bfloat16)
    return features.reshape(frames, tall, broad, features.shape[1])


def solution(mesh):
    return jax.shard_map(
        local,
        mesh=mesh,
        in_specs=(
            P("groups", "seq", None, None),
            P("groups", "seq", None, None),
            P(("groups", "seq"), None, None),
            P("groups"),
            P("groups", None),
            P("groups"),
            P("seq", None),
            P(None, "seq"),
        ),
        out_specs=P("groups", "seq", None, None),
        check_vma=False,
    )
```

profile of v0, /device:TPU:1, one launch (start us, length us, event | category | flops | bytes accessed | tf_op | source)
XLA Modules:
  0.0 185.7 jit_solution(17588288535597208281)
XLA Ops:
  0.9 1.9 %gather_fusion = s32[256]{0:T(256)S(1)} fusion(s32[32]{0:T(128)S(1)} %copy-done.1, s32[1024]{0:T(1024)S(1)} %pad_clamp_fusion), kind=kCustom, calls=%fused_computation | custom fusion | bytes 3072 | tf_op jit(solution)/shard_map/gather | solution.py:46
  3.5 1.1 copy.54
  4.6 7.3 %all-to-all-start = ((bf16[16,16,1024]{2,1,0:T(8,128)(2,1)}), bf16[16,16,1024]{2,1,0:T(8,128)(2,1)}, u32[]{:S(2)}, u32[]{:S(2)}) async-start(bf16[16,16,1024]{2,1,0:T(8,128)(2,1)} %copy.54), calls=%async_computation | async-start | bytes 1048576 | tf_op jit(solution)/shard_map/all_to_all | solution.py:59
  12.0 1.2 reshape_reshape.3
  13.9 24.9 %all-gather = bf16[16,192,64]{1,2,0:T(8,128)(2,1)S(1)} all-gather(bf16[1,192,64]{1,2,0:T(8,128)(2,1)S(1)} %bitcast.104), channel_id=1, replica_groups=mesh['groups'=2,'seq'=16] {'seq'}, dimensions={0}, use_global_device_ids=true | all-gather | bytes 417792 | tf_op jit(solution)/shard_map/all_gather | solution.py:108
  39.1 1.3 reshape.128
  40.6 97.7 %while.13 = (s32[]{:T(128)}, bf16[12,512,128]{2,1,0:T(8,128)(2,1)}, bf16[12,512,128]{2,1,0:T(8,128)(2,1)S(1)}, s32[12]{0:T(128)S(1)}, bf16[256,1024]{1,0:T(8,128...) while((s32[]{:T(128)}, bf16[12,512,128]{2,1,0:T(8,128)(2,1)}, ...), condition=%wide.region_8.9_spmd.clone, body=%wide.region_3.8_spmd.clone.sunk | while | flops 136510480 | bytes 4490867 | solution.py:102
  43.3 1.1 fusion.70
  44.4 1.1 fusion.69
  45.8 1.1 fusion.72
  46.9 1.9 fusion.73
  51.5 1.1 fusion.70
  52.5 1.1 fusion.69
  53.9 1.1 fusion.72
  55.0 1.9 %fusion.73 = bf16[12,512,128]{2,1,0:T(8,128)(2,1)} fusion(bf16[12,512,128]{2,1,0:T(8,128)(2,1)} %get-tuple-element.228, s32[]{:T(128)} %get-tuple-element.227, f32[512,128]{1,0:T(8,128)S(1)} %fusion.72, f32[512,256]{0,1:T(8,128)S(1)} %get-tuple-element.205, f32[512]{0:T(512)S(1)} %add.109, f32[512]{0:T(512)S(1)} %max.13, ...), kind=kOutput, calls=%fused_computation.7.clone.1 | convolution fusion | flops 34144256 | bytes 1118980 | tf_op jit(solution)/shard_map/while/body/eval_jaxpr/dot_general | solution.py:100
  59.6 1.1 fusion.70
  60.7 1.1 fusion.69
  62.0 1.1 fusion.72
  63.2 1.9 %fusion.73 = bf16[12,512,128]{2,1,0:T(8,128)(2,1)} fusion(bf16[12,512,128]{2,1,0:T(8,128)(2,1)} %get-tuple-element.228, s32[]{:T(128)} %get-tuple-element.227, f32[512,128]{1,0:T(8,128)S(1)} %fusion.72, f32[512,256]{0,1:T(8,128)S(1)} %get-tuple-element.205, f32[512]{0:T(512)S(1)} %add.109, f32[512]{0:T(512)S(1)} %max.13, ...), kind=kOutput, calls=%fused_computation.7.clone.1 | convolution fusion | flops 34144256 | bytes 1118980 | tf_op jit(solution)/shard_map/while/body/eval_jaxpr/dot_general | solution.py:100
  67.7 1.1 fusion.70
  68.8 1.1 fusion.69
  70.2 1.1 fusion.72
  71.3 1.9 %fusion.73 = bf16[12,512,128]{2,1,0:T(8,128)(2,1)} fusion(bf16[12,512,128]{2,1,0:T(8,128)(2,1)} %get-tuple-element.228, s32[]{:T(128)} %get-tuple-element.227, f32[512,128]{1,0:T(8,128)S(1)} %fusion.72, f32[512,256]{0,1:T(8,128)S(1)} %get-tuple-element.205, f32[512]{0:T(512)S(1)} %add.109, f32[512]{0:T(512)S(1)} %max.13, ...), kind=kOutput, calls=%fused_computation.7.clone.1 | convolution fusion | flops 34144256 | bytes 1118980 | tf_op jit(solution)/shard_map/while/body/eval_jaxpr/dot_general | solution.py:100
  75.9 1.1 fusion.70
  77.0 1.1 fusion.69
  78.3 1.1 fusion.72
  79.4 1.9 %fusion.73 = bf16[12,512,128]{2,1,0:T(8,128)(2,1)} fusion(bf16[12,512,128]{2,1,0:T(8,128)(2,1)} %get-tuple-element.228, s32[]{:T(128)} %get-tuple-element.227, f32[512,128]{1,0:T(8,128)S(1)} %fusion.72, f32[512,256]{0,1:T(8,128)S(1)} %get-tuple-element.205, f32[512]{0:T(512)S(1)} %add.109, f32[512]{0:T(512)S(1)} %max.13, ...), kind=kOutput, calls=%fused_computation.7.clone.1 | convolution fusion | flops 34144256 | bytes 1118980 | tf_op jit(solution)/shard_map/while/body/eval_jaxpr/dot_general | solution.py:100
  84.0 1.1 fusion.70
  85.1 1.1 fusion.69
  86.5 1.1 fusion.72
  87.6 1.9 fusion.73
  92.2 1.1 fusion.70
  93.2 1.1 fusion.69
  94.6 1.1 fusion.72
  95.7 1.9 %fusion.73 = bf16[12,512,128]{2,1,0:T(8,128)(2,1)} fusion(bf16[12,512,128]{2,1,0:T(8,128)(2,1)} %get-tuple-element.228, s32[]{:T(128)} %get-tuple-element.227, f32[512,128]{1,0:T(8,128)S(1)} %fusion.72, f32[512,256]{0,1:T(8,128)S(1)} %get-tuple-element.205, f32[512]{0:T(512)S(1)} %add.109, f32[512]{0:T(512)S(1)} %max.13, ...), kind=kOutput, calls=%fused_computation.7.clone.1 | convolution fusion | flops 34144256 | bytes 1118980 | tf_op jit(solution)/shard_map/while/body/eval_jaxpr/dot_general | solution.py:100
  100.3 1.1 fusion.70
  101.4 1.1 fusion.69
  102.7 1.1 fusion.72
  103.9 1.9 %fusion.73 = bf16[12,512,128]{2,1,0:T(8,128)(2,1)} fusion(bf16[12,512,128]{2,1,0:T(8,128)(2,1)} %get-tuple-element.228, s32[]{:T(128)} %get-tuple-element.227, f32[512,128]{1,0:T(8,128)S(1)} %fusion.72, f32[512,256]{0,1:T(8,128)S(1)} %get-tuple-element.205, f32[512]{0:T(512)S(1)} %add.109, f32[512]{0:T(512)S(1)} %max.13, ...), kind=kOutput, calls=%fused_computation.7.clone.1 | convolution fusion | flops 34144256 | bytes 1118980 | tf_op jit(solution)/shard_map/while/body/eval_jaxpr/dot_general | solution.py:100
  108.4 1.1 fusion.70
  109.5 1.1 fusion.69
  110.9 1.1 fusion.72
  112.0 1.9 %fusion.73 = bf16[12,512,128]{2,1,0:T(8,128)(2,1)} fusion(bf16[12,512,128]{2,1,0:T(8,128)(2,1)} %get-tuple-element.228, s32[]{:T(128)} %get-tuple-element.227, f32[512,128]{1,0:T(8,128)S(1)} %fusion.72, f32[512,256]{0,1:T(8,128)S(1)} %get-tuple-element.205, f32[512]{0:T(512)S(1)} %add.109, f32[512]{0:T(512)S(1)} %max.13, ...), kind=kOutput, calls=%fused_computation.7.clone.1 | convolution fusion | flops 34144256 | bytes 1118980 | tf_op jit(solution)/shard_map/while/body/eval_jaxpr/dot_general | solution.py:100
  116.6 1.1 fusion.70
  117.7 1.1 fusion.69
  119.0 1.1 fusion.72
  120.1 1.9 %fusion.73 = bf16[12,512,128]{2,1,0:T(8,128)(2,1)} fusion(bf16[12,512,128]{2,1,0:T(8,128)(2,1)} %get-tuple-element.228, s32[]{:T(128)} %get-tuple-element.227, f32[512,128]{1,0:T(8,128)S(1)} %fusion.72, f32[512,256]{0,1:T(8,128)S(1)} %get-tuple-element.205, f32[512]{0:T(512)S(1)} %add.109, f32[512]{0:T(512)S(1)} %max.13, ...), kind=kOutput, calls=%fused_computation.7.clone.1 | convolution fusion | flops 34144256 | bytes 1118980 | tf_op jit(solution)/shard_map/while/body/eval_jaxpr/dot_general | solution.py:100
  124.7 1.1 fusion.70
  125.8 1.1 fusion.69
  127.2 1.1 fusion.72
  128.3 1.9 %fusion.73 = bf16[12,512,128]{2,1,0:T(8,128)(2,1)} fusion(bf16[12,512,128]{2,1,0:T(8,128)(2,1)} %get-tuple-element.228, s32[]{:T(128)} %get-tuple-element.227, f32[512,128]{1,0:T(8,128)S(1)} %fusion.72, f32[512,256]{0,1:T(8,128)S(1)} %get-tuple-element.205, f32[512]{0:T(512)S(1)} %add.109, f32[512]{0:T(512)S(1)} %max.13, ...), kind=kOutput, calls=%fused_computation.7.clone.1 | convolution fusion | flops 34144256 | bytes 1118980 | tf_op jit(solution)/shard_map/while/body/eval_jaxpr/dot_general | solution.py:100
  132.9 1.1 fusion.70
  134.0 1.1 fusion.69
  135.3 1.1 fusion.72
  136.4 1.9 %fusion.73 = bf16[12,512,128]{2,1,0:T(8,128)(2,1)} fusion(bf16[12,512,128]{2,1,0:T(8,128)(2,1)} %get-tuple-element.228, s32[]{:T(128)} %get-tuple-element.227, f32[512,128]{1,0:T(8,128)S(1)} %fusion.72, f32[512,256]{0,1:T(8,128)S(1)} %get-tuple-element.205, f32[512]{0:T(512)S(1)} %add.109, f32[512]{0:T(512)S(1)} %max.13, ...), kind=kOutput, calls=%fused_computation.7.clone.1 | convolution fusion | flops 34144256 | bytes 1118980 | tf_op jit(solution)/shard_map/while/body/eval_jaxpr/dot_general | solution.py:100
  138.3 1.8 copy.55
  140.8 3.3 %collective-permute-start = (bf16[2,1,128,16]{3,2,1,0:T(8,128)(2,1)S(1)}, bf16[2,1,128,16]{3,2,1,0:T(8,128)(2,1)S(1)}, u32[]{:S(2)}, u32[]{:S(2)}) collective-permute-start(bf16[2,1,128,16]{3,2,1,0:T(8,128)(2,1)S(1)} %get-tuple-element.136), channel_id=1, source_target_pairs={{0,1},{1,2},{2,3},{3,4},{4,5},{5,6},{6,7},{7,8},{8,9},{9,10},{10,1... | collective-permute-start | bytes 24584 | tf_op jit(solution)/shard_map/ppermute | solution.py:21
  144.1 1.9 %collective-permute-start.1 = (bf16[2,1,128,16]{3,2,1,0:T(8,128)(2,1)S(1)}, bf16[2,1,128,16]{3,2,1,0:T(8,128)(2,1)S(1)}, u32[]{:S(2)}, u32[]{:S(2)}) collective-permute-start(bf16[2,1,128,16]{3,2,1,0:T(8,128)(2,1)S(1)} %get-tuple-element.137), channel_id=1, source_target_pairs={{1,0},{2,1},{3,2},{4,3},{5,4},{6,5},{7,6},{8,7},{9,8},{10,9},{11,1... | collective-permute-start | bytes 24584 | tf_op jit(solution)/shard_map/ppermute | solution.py:23
  146.0 22.6 %all_gather.7 = bf16[432,512]{0,1:T(8,128)(2,1)} all-gather(bf16[432,32]{0,1:T(8,128)(2,1)S(1)} %copy-done.5), channel_id=1, replica_groups=mesh['groups'=2,'seq'=16] {'seq'}, dimensions={1}, use_global_device_ids=true | all-gather | bytes 470016 | tf_op jit(solution)/shard_map/all_gather | solution.py:136
  171.3 0.9 copy.75
  172.1 0.9 copy.76
  173.0 0.9 copy.77
  176.4 6.2 %concatenate.70 = bf16[1024,432]{1,0:T(8,128)(2,1)} concatenate(bf16[1024,16]{1,0:T(8,128)(2,1)S(1)} %slice.74, bf16[1024,16]{1,0:T(8,128)(2,1)S(1)} %slice.74, bf16[1024,16]{1,0:T(8,128)(2,1)S(1)} %slice.74, bf16[1024,16]{1,0:T(8,128)(2,1)S(1)} %slice.74, bf16[1024,16]{1,0:T(8,128)(2,1)S(1)} %slice.74, bf16[1024,16]{1,0:T(8,128)(2,1)S(1)} %slice.74, ...), dimensions={1} | concatenate | bytes 1769472 | tf_op jit(solution)/shard_map/concatenate | solution.py:133
  182.6 3.1 %convolution_convert_fusion = bf16[1024,512]{1,0:T(8,128)(2,1)} fusion(bf16[1024,432]{1,0:T(8,128)(2,1)} %concatenate.70, bf16[432,512]{0,1:T(8,128)(2,1)} %all_gather.7), kind=kOutput, calls=%fused_computation.32 | convolution fusion | flops 453509120 | bytes 2375680 | tf_op jit(solution)/shard_map/dot_general | solution.py:134
  (129 shorter events, 20.3 us)
Async XLA Ops:
  0.0 3.1 %copy-start = (bf16[2,16,1024]{2,1,0:T(8,128)(2,1)S(1)}, bf16[2,16,1024]{2,1,0:T(8,128)(2,1)}, u32[]{:S(2)}) copy-start(bf16[2,16,1024]{2,1,0:T(8,128)(2,1)} %param.12) | copy-start | bytes 196612
  0.0 0.8 copy-start.1
  0.8 2.0 %copy-start.6 = (s32[16]{0:T(128)S(1)}, s32[16]{0:T(128)}, u32[]{:S(2)}) copy-start(s32[16]{0:T(128)} %param.15) | copy-start | bytes 196
  2.7 9.2 %copy-start.2 = (bf16[2,2,64,3072]{3,2,1,0:T(8,128)(2,1)S(1)}, bf16[2,2,64,3072]{3,2,1,0:T(8,128)(2,1)}, u32[]{:S(2)}) copy-start(bf16[2,2,64,3072]{3,2,1,0:T(8,128)(2,1)} %param.10) | copy-start | bytes 4718596
  4.6 36.0 %all-to-all-start = ((bf16[16,16,1024]{2,1,0:T(8,128)(2,1)}), bf16[16,16,1024]{2,1,0:T(8,128)(2,1)}, u32[]{:S(2)}, u32[]{:S(2)}) async-start(bf16[16,16,1024]{2,1,0:T(8,128)(2,1)} %copy.54), calls=%async_computation | async-start | bytes 1048576 | tf_op jit(solution)/shard_map/all_to_all | solution.py:59
  13.1 0.8 copy-start.4
  138.3 1.8 copy-start.3
  140.1 6.0 %copy-start.5 = (bf16[432,32]{0,1:T(8,128)(2,1)S(1)}, bf16[432,32]{0,1:T(8,128)(2,1)}, u32[]{:S(2)}) copy-start(bf16[432,32]{0,1:T(8,128)(2,1)} %param.17) | copy-start | bytes 82948
  140.8 28.0 %collective-permute-start = (bf16[2,1,128,16]{3,2,1,0:T(8,128)(2,1)S(1)}, bf16[2,1,128,16]{3,2,1,0:T(8,128)(2,1)S(1)}, u32[]{:S(2)}, u32[]{:S(2)}) collective-permute-start(bf16[2,1,128,16]{3,2,1,0:T(8,128)(2,1)S(1)} %get-tuple-element.136), channel_id=1, source_target_pairs={{0,1},{1,2},{2,3},{3,4},{4,5},{5,6},{6,7},{7,8},{8,9},{9,10},{10,1... | collective-permute-start | bytes 24584 | tf_op jit(solution)/shard_map/ppermute | solution.py:21
  144.1 24.8 %collective-permute-start.1 = (bf16[2,1,128,16]{3,2,1,0:T(8,128)(2,1)S(1)}, bf16[2,1,128,16]{3,2,1,0:T(8,128)(2,1)S(1)}, u32[]{:S(2)}, u32[]{:S(2)}) collective-permute-start(bf16[2,1,128,16]{3,2,1,0:T(8,128)(2,1)S(1)} %get-tuple-element.137), channel_id=1, source_target_pairs={{1,0},{2,1},{3,2},{4,3},{5,4},{6,5},{7,6},{8,7},{9,8},{10,9},{11,1... | collective-permute-start | bytes 24584 | tf_op jit(solution)/shard_map/ppermute | solution.py:23
where the time goes:
time: 189 us; the launch traced here: 186 us
  matrix products  65.9 us (35%)
  blocking collectives  47.5 us (25%)
  local copies, waits for them, and re-layouts  31.4 us (17%)
  loops' own time  24 us (13%)
  starting transfers between devices  12.5 us (7%)
  other arithmetic  4.05 us (2%)
    dot_general x24, matrix products, pair_scores(): lax.dot_general(query_block, key_rows, (((1,), (1,)), ((), ())), preferre...  26.2 us
    all_gather x1, blocking collectives, local(): lax.all_gather(final_weight, 'seq', axis=0, tiled=True)  24.9 us
    another operation x1, loops' own time, local(): lax.map(one_block, (query_blocks, jnp.arange(KV_HEADS * pair_count, dtype...  24 us
    all_gather x1, blocking collectives, local(): lax.all_gather(decoder_weight, 'seq', axis=1, tiled=True)  22.6 us
    dot_general x12, matrix products, one_block(): jnp.dot(weights_past, values_past, preferred_element_type=jnp.float32)  22.4 us
    dot_general x12, matrix products, one_block(): mixed = jnp.dot(weights_own, values_own, preferred_element_type=jnp.float32)  13.5 us
    all_to_all x1, starting transfers between devices, local(): lax.all_to_all(outgoing, 'seq', split_axis=0, concat_axis=0, tiled=True)  7.32 us
    slice x19, local copies, waits for them, and re-layouts, local(): padded[shift_t:shift_t + frames, shift_y:shift_y + tall, shift_x:shift_x...  7.27 us
  transfers between devices with their start and end apart: 3, of which 0 were waited for; matrix products, arithmetic and copies ran while one was open for 2% of the time, Pallas kernels for 0%

commit v1 on v0

v1 whole, which is shorter than its diff:
```python
import functools
import math

import jax
import jax.numpy as jnp
from jax import lax
from jax.experimental import pallas as pl
from jax.experimental.pallas import tpu as pltpu
from jax.sharding import PartitionSpec as P

HEADS = 24
KV_HEADS = 4
HEAD_DIM = 128
GROUP = HEADS // KV_HEADS
LOG2E = 1.4426950408889634
VMEM_LIMIT = 48 * 1024 * 1024


def attention_body(
    blocks_here, listed_max, table, home, blocks, lens, query, key_own, value_own, key_past,
    value_past, weight, out, keys, values, total
):
    step = pl.program_id(0)
    tokens = query.shape[0]
    block_tokens = key_past.shape[1]
    tile = table[0]
    count = lens[tile]

    @pl.when(step == 0)
    def _():
        values[:, HEAD_DIM:] = jnp.ones((values.shape[0], HEAD_DIM), jnp.bfloat16)
        total[...] = jnp.zeros_like(total)

    keys[:tokens] = key_own[...]
    values[:tokens, :HEAD_DIM] = value_own[...]

    def place(entry, carry):
        listed = entry < count
        stored = home[blocks[tile, jnp.where(listed, entry, 0)]]
        place_of = table[1 + ((stored // blocks_here) ^ tile)]
        slot = place_of * blocks_here + stored % blocks_here
        row = pl.multiple_of(tokens + entry * block_tokens, block_tokens)
        keys[pl.ds(row, block_tokens)] = key_past[slot]
        live = jnp.where(listed, 1.0, 0.0)
        values[pl.ds(row, block_tokens), :HEAD_DIM] = jnp.where(
            listed, value_past[slot], jnp.zeros((block_tokens, HEAD_DIM), jnp.bfloat16)
        )
        values[pl.ds(row, block_tokens), HEAD_DIM:] = jnp.full(
            (block_tokens, HEAD_DIM), live, jnp.float32
        ).astype(jnp.bfloat16)
        return carry

    lax.fori_loop(0, listed_max, place, 0, unroll=listed_max <= 16)

    scale = LOG2E / math.sqrt(HEAD_DIM)
    key_rows = keys[...]
    value_rows = values[...]
    part = total[...]
    for head in range(GROUP):
        score = lax.dot_general(
            query[:, head * HEAD_DIM : (head + 1) * HEAD_DIM],
            key_rows,
            (((1,), (1,)), ((), ())),
            preferred_element_type=jnp.float32,
        )
        top = jnp.max(score, axis=1, keepdims=True)
        weights = jnp.exp2((score - top) * scale).astype(jnp.bfloat16)
        mixed = jnp.dot(weights, value_rows, preferred_element_type=jnp.float32)
        attended = (mixed[:, :HEAD_DIM] / mixed[:, HEAD_DIM:]).astype(jnp.bfloat16)
        part += jnp.dot(
            attended,
            weight[head * HEAD_DIM : (head + 1) * HEAD_DIM],
            preferred_element_type=jnp.float32,
        )
    total[...] = part

    @pl.when(step == KV_HEADS - 1)
    def _():
        out[...] = part.astype(jnp.bfloat16)


def attention(tile, query_rows, own_rows, past, block_home, block_list, list_len, final_weight, blocks_here):
    tokens, width = query_rows.shape
    count, block_tokens, _ = past.shape
    listed_max = block_list.shape[1]
    rows = tokens + listed_max * block_tokens
    span = GROUP * HEAD_DIM
    columns = final_weight.shape[1]
    smem = pl.BlockSpec(memory_space=pltpu.SMEM)
    return pl.pallas_call(
        functools.partial(attention_body, blocks_here, listed_max),
        grid=(KV_HEADS,),
        in_specs=[
            smem,
            smem,
            smem,
            smem,
            pl.BlockSpec((tokens, span), lambda g: (0, g)),
            pl.BlockSpec((tokens, HEAD_DIM), lambda g: (0, g)),
            pl.BlockSpec((tokens, HEAD_DIM), lambda g: (0, KV_HEADS + g)),
            pl.BlockSpec((count, block_tokens, HEAD_DIM), lambda g: (0, 0, g)),
            pl.BlockSpec((count, block_tokens, HEAD_DIM), lambda g: (0, 0, KV_HEADS + g)),
            pl.BlockSpec((span, columns), lambda g: (g, 0)),
        ],
        out_specs=pl.BlockSpec((tokens, columns), lambda g: (0, 0)),
        out_shape=jax.ShapeDtypeStruct((tokens, columns), jnp.bfloat16),
        scratch_shapes=[
            pltpu.VMEM((rows, HEAD_DIM), jnp.bfloat16),
            pltpu.VMEM((rows, 2 * HEAD_DIM), jnp.bfloat16),
            pltpu.VMEM((tokens, columns), jnp.float32),
        ],
        compiler_params=pltpu.CompilerParams(vmem_limit_bytes=VMEM_LIMIT),
        cost_estimate=pl.CostEstimate(
            flops=6 * tokens * rows * width, bytes_accessed=4 * tokens * width, transcendentals=0
        ),
        name="attention",
    )(tile, block_home, block_list, list_len, query_rows, own_rows, own_rows, past, past, final_weight)


def decoder_body(lat, pred, above, below, kernel, out, wide, columns, panel):
    row = pl.program_id(0)
    frames, patch_rows, patches, _ = pred.shape
    broad = 2 * patches
    lanes = wide.shape[2]
    span = 3 * lanes

    @pl.when(row == 0)
    def _():
        wide[...] = jnp.zeros_like(wide)
        columns[...] = jnp.zeros_like(columns)
        panel[...] = jnp.zeros_like(panel)
        depth = (patch_rows + 2) * 4 * lat
        source = lax.broadcasted_iota(jnp.int32, (depth, lanes), 0)
        target = lax.broadcasted_iota(jnp.int32, (depth, lanes), 1)
        wanted = target == (source // (2 * lat) - 1) * lat + source % lat
        inside = (source >= 2 * lat) & (source < depth - 2 * lat)
        for frame in range(frames):
            cells = jnp.concatenate(
                [above[frame]] + [pred[frame, r] for r in range(patch_rows)] + [below[frame]], axis=1
            )
            for side in range(2):
                pick = wanted & inside & ((source // lat) % 2 == side)
                wide[frame, pl.ds(8 + side, patches, stride=2), :] = jnp.dot(
                    cells, pick.astype(jnp.float32).astype(jnp.bfloat16), preferred_element_type=jnp.float32
                )
        for frame in range(frames):
            for shift_t in range(3):
                source_frame = frame + shift_t - 2
                if source_frame < 0:
                    continue
                for shift_x in range(3):
                    columns[
                        frame * broad : (frame + 1) * broad,
                        shift_t * span + shift_x * lanes : shift_t * span + (shift_x + 1) * lanes,
                    ] = wide[source_frame, 7 + shift_x : 7 + shift_x + broad, :].astype(jnp.bfloat16)

    for shift_t in range(3):
        for shift_x in range(3):
            base = shift_t * span + shift_x * lanes

            @pl.when(row > 0)
            def _():
                before = pl.multiple_of(base + (row - 1) * lat, lat)
                panel[pl.ds(before, lat), :] = jnp.zeros((lat, panel.shape[1]), jnp.bfloat16)

            for shift_y in range(3):
                tap = ((3 * shift_t + shift_y) * 3 + shift_x) * lat
                start = pl.multiple_of(base + (row + shift_y) * lat, lat)
                panel[pl.ds(start, lat), :] = kernel[tap : tap + lat, :]
    features = jnp.dot(columns[...], panel[...], preferred_element_type=jnp.float32)
    out[...] = features.astype(jnp.bfloat16).reshape(out.shape)


def decoder(pred, above, below, kernel):
    frames, patch_rows, patches, values = pred.shape
    lat = values // 4
    lanes = 128
    tall, broad = 2 * patch_rows, 2 * patches
    channels = kernel.shape[1]
    depth = 9 * lanes
    assert (tall + 2) * lat <= lanes
    return pl.pallas_call(
        functools.partial(decoder_body, lat),
        grid=(tall,),
        in_specs=[
            pl.BlockSpec(pred.shape, lambda y: (0, 0, 0, 0)),
            pl.BlockSpec(above.shape, lambda y: (0, 0, 0)),
            pl.BlockSpec(below.shape, lambda y: (0, 0, 0)),
            pl.BlockSpec(kernel.shape, lambda y: (0, 0)),
        ],
        out_specs=pl.BlockSpec((frames, 1, broad, channels), lambda y: (0, y, 0, 0)),
        out_shape=jax.ShapeDtypeStruct((frames, tall, broad, channels), jnp.bfloat16),
        scratch_shapes=[
            pltpu.VMEM((frames, broad + 16, lanes), jnp.float32),
            pltpu.VMEM((frames * broad, depth), jnp.bfloat16),
            pltpu.VMEM((depth, channels), jnp.bfloat16),
        ],
        compiler_params=pltpu.CompilerParams(vmem_limit_bytes=VMEM_LIMIT),
        cost_estimate=pl.CostEstimate(
            flops=2 * frames * tall * broad * depth * channels,
            bytes_accessed=2 * frames * tall * broad * channels,
            transcendentals=0,
        ),
        name="decoder",
    )(pred, above, below, kernel)


def exchange(value, offset):
    count = lax.axis_size("seq")
    return lax.ppermute(value, "seq", [(i, i ^ offset) for i in range(count)])


def gather_relative(shard):
    count = lax.axis_size("seq")
    assert count & (count - 1) == 0
    bit = count // 2
    held = shard
    order = [0]
    while bit:
        held = jnp.concatenate([held, exchange(held, bit)], axis=0)
        order = order + [o ^ bit for o in order]
        bit //= 2
    return held, order


def local(queries, own_kv, past_kv, block_home, block_list, list_len, final_weight, decoder_weight):
    frames, patch_rows, patches, width = queries.shape
    tokens = frames * patch_rows * patches
    count = lax.axis_size("seq")
    blocks_here = past_kv.shape[0]
    tile = lax.axis_index("seq").astype(jnp.int32).reshape(1)
    held, order = gather_relative(past_kv)
    past = held
    places = jnp.array([order.index(k) for k in range(count)], jnp.int32)
    tile = jnp.concatenate([tile, places])
    fw = lax.all_gather(final_weight, "seq", axis=0, tiled=True)
    dw = lax.all_gather(decoder_weight, "seq", axis=1, tiled=True)
    predicted = attention(
        tile, queries.reshape(tokens, width), own_kv.reshape(tokens, own_kv.shape[3]), past,
        block_home, block_list, list_len, fw, blocks_here,
    )
    predicted = predicted.reshape(frames, patch_rows, patches, predicted.shape[1])
    above = lax.ppermute(predicted[:, -1], "seq", [(i, i + 1) for i in range(count - 1)])
    below = lax.ppermute(predicted[:, 0], "seq", [(i + 1, i) for i in range(count - 1)])
    return decoder(predicted, above, below, dw)


def solution(mesh):
    return jax.shard_map(
        local,
        mesh=mesh,
        in_specs=(
            P("groups", "seq", None, None),
            P("groups", "seq", None, None),
            P(("groups", "seq"), None, None),
            P("groups"),
            P("groups", None),
            P("groups"),
            P("seq", None),
            P(None, "seq"),
        ),
        out_specs=P("groups", "seq", None, None),
        check_vma=False,
    )
```

time: 189 us -> 82.4 us (0.44); the launches traced: 186 us -> 82.1 us
  matrix products: 65.9 us -> 0 us
  local copies, waits for them, and re-layouts: 31.4 us -> 0.71 us
  loops' own time: 24 us -> 0 us
  Pallas kernels: 0 us -> 15.3 us
  waiting for transfers between devices: 0.01 us -> 5.91 us
  other arithmetic: 4.05 us -> 1.85 us
    dot_general x51 -> x0, matrix products: 65.9 us -> none  [the longest x24 26.2 us: pair_scores(): lax.dot_general(query_block, key_rows, (((1,), (1,)), ((), ())), preferre...]
    another operation x1 -> x0, loops' own time: 24 us -> none  [local(): lax.map(one_block, (query_blocks, jnp.arange(KV_HEADS * pair_count, dtype...]
    pallas_call x0 -> x2, Pallas kernels: none -> 15.3 us  [the longest x1 11.8 us: attention(): pl.pallas_call(functools.partial(attention_body, blocks_here, listed_max)...]
    all_to_all x1 -> x0, starting transfers between devices: 7.32 us -> none  [local(): lax.all_to_all(outgoing, 'seq', split_axis=0, concat_axis=0, tiled=True)]
    slice x20 -> x0, local copies, waits for them, and re-layouts: 7.28 us -> none  [the longest x19 7.27 us: local(): padded[shift_t:shift_t + frames, shift_y:shift_y + tall, shift_x:shift_x...]
    dynamic_slice x12 -> x0, local copies, waits for them, and re-layouts: 6.99 us -> none  [local(): lax.map(one_block, (query_blocks, jnp.arange(KV_HEADS * pair_count, dtype...]
    concatenate x1, local copies, waits for them, and re-layouts: 6.18 us -> 0.04 us  [gather_relative(): held = jnp.concatenate([held, exchange(held, bit)], axis=0)]
    ppermute x2 -> x6, starting transfers between devices: 5.21 us -> 11.3 us  [the longest x4 7 us: exchange(): return lax.ppermute(value, 'seq', [(i, i ^ offset) for i in range(count)])]
  transfers between devices with their start and end apart: 3 -> 6, of which waited for: 0 -> 3; matrix products, arithmetic and copies ran while one was open for 2% -> 1% of each run, Pallas kernels for 0% -> 0%
where the time goes in v1:
time: 82.4 us; the launch traced here: 82.1 us
  blocking collectives  46.8 us (57%)
  Pallas kernels  15.3 us (19%)
  starting transfers between devices  11.3 us (14%)
  waiting for transfers between devices  5.91 us (7%)
  other arithmetic  1.85 us (2%)
    all_gather x1, blocking collectives, local(): fw = lax.all_gather(final_weight, 'seq', axis=0, tiled=True)  26.7 us
    all_gather x1, blocking collectives, local(): dw = lax.all_gather(decoder_weight, 'seq', axis=1, tiled=True)  20 us
    pallas_call x1, Pallas kernels, attention(): pl.pallas_call(functools.partial(attention_body, blocks_here, listed_max)...  11.8 us
    ppermute x4, starting transfers between devices, exchange(): return lax.ppermute(value, 'seq', [(i, i ^ offset) for i in range(count)])  7 us
    ppermute x4, waiting for transfers between devices, exchange(): return lax.ppermute(value, 'seq', [(i, i ^ offset) for i in range(count)])  5.9 us
    pallas_call x1, Pallas kernels, decoder(): pl.pallas_call(functools.partial(decoder_body, lat), grid=(tall,), in_spe...  3.47 us
    ppermute x1, starting transfers between devices, local(): lax.ppermute(predicted[:, 0], 'seq', [(i + 1, i) for i in range(count - 1)])  2.4 us
    ppermute x1, starting transfers between devices, local(): lax.ppermute(predicted[:, -1], 'seq', [(i, i + 1) for i in range(count -...  1.92 us
  transfers between devices with their start and end apart: 6, of which 3 were waited for; matrix products, arithmetic and copies ran while one was open for 1% of the time, Pallas kernels for 0%

profile of v1, /device:TPU:1, one launch (start us, length us, event | category | flops | bytes accessed | tf_op | source)
XLA Modules:
  0.0 82.1 jit_solution(12496326437364303984)
XLA Ops:
  0.0 0.0 copy-start.5
  0.0 3.1 %collective-permute-start = (bf16[2,16,1024]{2,1,0:T(8,128)(2,1)}, bf16[2,16,1024]{2,1,0:T(8,128)(2,1)S(1)}, u32[]{:S(2)}, u32[]{:S(2)}) collective-permute-start(bf16[2,16,1024]{2,1,0:T(8,128)(2,1)} %param.11), channel_id=1, source_target_pairs={{0,8},{1,9},{2,10},{3,11},{4,12},{5,13},{6,14},{7,15},{8,0},{9,1},... | collective-permute-start | bytes 196616 | tf_op jit(solution)/shard_map/ppermute | solution.py:210
  3.1 1.9 %collective-permute-done = bf16[2,16,1024]{2,1,0:T(8,128)(2,1)S(1)} collective-permute-done((bf16[2,16,1024]{2,1,0:T(8,128)(2,1)}, bf16[2,16,1024]{2,1,0:T(8,128)(2,1)S(1)}, u32[]{:S(2)}, u32[]{:S(2)}) %collective-permute-start) | collective-permute-done | bytes 65568 | tf_op jit(solution)/shard_map/ppermute | solution.py:210
  5.1 0.9 %pad_maximum_fusion.2 = bf16[4,16,1024]{2,1,0:T(8,128)(2,1)S(1)} fusion(bf16[2,16,1024]{2,1,0:T(8,128)(2,1)S(1)} %collective-permute-done, bf16[2,16,1024]{2,1,0:T(8,128)(2,1)} %param.11), kind=kLoop, calls=%fused_computation.2 | loop fusion | flops 65536 | bytes 262144 | tf_op jit(solution)/shard_map/concatenate | solution.py:220
  5.9 2.4 %collective-permute-start.1 = (bf16[4,16,1024]{2,1,0:T(8,128)(2,1)S(1)}, bf16[4,16,1024]{2,1,0:T(8,128)(2,1)S(1)}, u32[]{:S(2)}, u32[]{:S(2)}) collective-permute-start(bf16[4,16,1024]{2,1,0:T(8,128)(2,1)S(1)} %pad_maximum_fusion.2), channel_id=1, source_target_pairs={{0,4},{1,5},{2,6},{3,7},{4,0},{5,1},{6,2},{7,3},{8,12},{9,13},{10,... | collective-permute-start | bytes 393224 | tf_op jit(solution)/shard_map/ppermute | solution.py:210
  8.3 2.4 %collective-permute-done.1 = bf16[4,16,1024]{2,1,0:T(8,128)(2,1)S(1)} collective-permute-done((bf16[4,16,1024]{2,1,0:T(8,128)(2,1)S(1)}, bf16[4,16,1024]{2,1,0:T(8,128)(2,1)S(1)}, u32[]{:S(2)}, u32[]{:S(2)}) %collective-permute-start.1) | collective-permute-done | bytes 131104 | tf_op jit(solution)/shard_map/ppermute | solution.py:210
  10.6 0.9 %pad_maximum_fusion.1 = bf16[8,16,1024]{2,1,0:T(8,128)(2,1)S(1)} fusion(bf16[4,16,1024]{2,1,0:T(8,128)(2,1)S(1)} %collective-permute-done.1, bf16[2,16,1024]{2,1,0:T(8,128)(2,1)S(1)} %collective-permute-done, bf16[2,16,1024]{2,1,0:T(8,128)(2,1)} %param.11), kind=kLoop, calls=%fused_computation.1 | loop fusion | flops 262144 | bytes 524288 | tf_op jit(solution)/shard_map/concatenate | solution.py:220
  11.5 0.0 copy-start.7
  11.5 1.3 %collective-permute-start.2 = (bf16[8,16,1024]{2,1,0:T(8,128)(2,1)S(1)}, bf16[8,16,1024]{2,1,0:T(8,128)(2,1)S(1)}, u32[]{:S(2)}, u32[]{:S(2)}) collective-permute-start(bf16[8,16,1024]{2,1,0:T(8,128)(2,1)S(1)} %pad_maximum_fusion.1), channel_id=1, source_target_pairs={{0,2},{1,3},{2,0},{3,1},{4,6},{5,7},{6,4},{7,5},{8,10},{9,11},{10,... | collective-permute-start | bytes 786440 | tf_op jit(solution)/shard_map/ppermute | solution.py:210
  12.8 26.7 %all-gather = bf16[16,192,64]{1,2,0:T(8,128)(2,1)S(1)} all-gather(bf16[1,192,64]{1,2,0:T(8,128)(2,1)} %bitcast.20), channel_id=1, replica_groups=mesh['groups'=2,'seq'=16] {'seq'}, dimensions={0}, use_global_device_ids=true | all-gather | bytes 417792 | tf_op jit(solution)/shard_map/all_gather | solution.py:236
  39.5 0.4 copy.19
  39.9 0.0 copy-start
  39.9 0.0 copy-start.1
  39.9 0.0 copy-start.2
  40.0 0.0 copy-start.3
  40.0 0.0 copy-start.4
  40.0 0.0 collective-permute-done.2
  40.0 0.0 copy-done.5
  40.0 0.1 pad_maximum_fusion
  40.1 0.2 collective-permute-start.3
  40.3 0.0 copy-done.7
  40.3 0.1 pad_add_fusion.table
  40.4 1.6 %collective-permute-done.3 = bf16[16,16,1024]{2,1,0:T(8,128)(2,1)S(1)} collective-permute-done((bf16[16,16,1024]{2,1,0:T(8,128)(2,1)S(1)}, bf16[16,16,1024]{2,1,0:T(8,128)(2,1)S(1)}, u32[]{:S(2)}, u32[]{:S(2)}) %collective-permute-start.3) | collective-permute-done | bytes 524320 | tf_op jit(solution)/shard_map/ppermute | solution.py:210
  42.1 0.0 copy-done
  42.1 0.0 copy-done.1
  42.1 0.0 copy-done.2
  42.1 0.0 copy-done.3
  42.1 0.0 copy-done.4
  42.1 0.0 copy-start.6
  42.2 11.8 %attention.1 = bf16[256,64]{1,0:T(8,128)(2,1)S(1)} custom-call(s32[17]{0:T(128)S(1)} %pad_add_fusion.table, s32[32]{0:T(128)S(1)} %copy-done.3, s32[16,16]{1,0:T(8,128)S(1)} %copy-done.2, s32[16]{0:T(128)S(1)} %copy-done.4, bf16[256,3072]{1,0:T(8,128)(2,1)S(1)} %bitcast.17, bf16[256,1024]{1,0:T(8,128)(2,1)S(1)} %bitcast.18, bf16[256,1024]{1,0:T(8,128)(2,1)S(1)} %bitcast.19, ...), custom_call_target="tpu_custom_call" | custom-call | flops 2415919104 | bytes 3145728 | tf_op jit(solution)/shard_map/attention/pallas_call | solution.py:90
  54.0 1.9 %collective-permute-start.4 = (bf16[2,64,64]{2,1,0:T(8,128)(2,1)S(1)}, bf16[2,64,64]{2,1,0:T(8,128)(2,1)S(1)}, u32[]{:S(2)}, u32[]{:S(2)}) collective-permute-start(bf16[2,64,64]{2,1,0:T(8,128)(2,1)S(1)} %get-tuple-element.6), channel_id=1, source_target_pairs={{0,1},{1,2},{2,3},{3,4},{4,5},{5,6},{6,7},{7,8},{8,9},{9,10},{10,1... | collective-permute-start | bytes 49160 | tf_op jit(solution)/shard_map/ppermute | solution.py:243
  56.0 2.4 %collective-permute-start.5 = (bf16[2,64,64]{2,1,0:T(8,128)(2,1)S(1)}, bf16[2,64,64]{2,1,0:T(8,128)(2,1)S(1)}, u32[]{:S(2)}, u32[]{:S(2)}) collective-permute-start(bf16[2,64,64]{2,1,0:T(8,128)(2,1)S(1)} %get-tuple-element.5), channel_id=1, source_target_pairs={{1,0},{2,1},{3,2},{4,3},{5,4},{6,5},{7,6},{8,7},{9,8},{10,9},{11,1... | collective-permute-start | bytes 49160 | tf_op jit(solution)/shard_map/ppermute | solution.py:244
  58.4 0.0 copy-done.6
  58.4 20.0 %all_gather.7 = bf16[432,512]{0,1:T(8,128)(2,1)S(1)} all-gather(bf16[432,32]{0,1:T(8,128)(2,1)S(1)} %copy-done.6), channel_id=1, replica_groups=mesh['groups'=2,'seq'=16] {'seq'}, dimensions={1}, use_global_device_ids=true | all-gather | bytes 470016 | tf_op jit(solution)/shard_map/all_gather | solution.py:237
  78.4 0.2 copy.24.kernel
  78.6 0.0 collective-permute-done.4.above
  78.6 0.0 collective-permute-done.5.below
  78.6 3.5 %decoder.1 = bf16[2,4,128,512]{3,2,1,0:T(8,128)(2,1)} custom-call(bf16[2,2,64,64]{3,2,1,0:T(8,128)(2,1)S(1)} %bitcast.16, bf16[2,64,64]{2,1,0:T(8,128)(2,1)S(1)} %collective-permute-done.4.above, bf16[2,64,64]{2,1,0:T(8,128)(2,1)S(1)} %collective-permute-done.5.below, bf16[432,512]{1,0:T(8,128)(2,1)S(1)} %copy.24.kernel), custom_call_target="tpu_custom_call" | custom-call | flops 1207959552 | bytes 1048576 | tf_op jit(solution)/shard_map/decoder/pallas_call | solution.py:182
  (6 shorter events, 0.1 us)
Async XLA Ops:
  0.0 40.0 %copy-start.5 = (bf16[2,16,1024]{2,1,0:T(8,128)(2,1)S(1)}, bf16[2,16,1024]{2,1,0:T(8,128)(2,1)}, u32[]{:S(2)}) copy-start(bf16[2,16,1024]{2,1,0:T(8,128)(2,1)} %param.11) | copy-start | bytes 196612
  0.0 5.1 %collective-permute-start = (bf16[2,16,1024]{2,1,0:T(8,128)(2,1)}, bf16[2,16,1024]{2,1,0:T(8,128)(2,1)S(1)}, u32[]{:S(2)}, u32[]{:S(2)}) collective-permute-start(bf16[2,16,1024]{2,1,0:T(8,128)(2,1)} %param.11), channel_id=1, source_target_pairs={{0,8},{1,9},{2,10},{3,11},{4,12},{5,13},{6,14},{7,15},{8,0},{9,1},... | collective-permute-start | bytes 196616 | tf_op jit(solution)/shard_map/ppermute | solution.py:210
  5.9 4.7 %collective-permute-start.1 = (bf16[4,16,1024]{2,1,0:T(8,128)(2,1)S(1)}, bf16[4,16,1024]{2,1,0:T(8,128)(2,1)S(1)}, u32[]{:S(2)}, u32[]{:S(2)}) collective-permute-start(bf16[4,16,1024]{2,1,0:T(8,128)(2,1)S(1)} %pad_maximum_fusion.2), channel_id=1, source_target_pairs={{0,4},{1,5},{2,6},{3,7},{4,0},{5,1},{6,2},{7,3},{8,12},{9,13},{10,... | collective-permute-start | bytes 393224 | tf_op jit(solution)/shard_map/ppermute | solution.py:210
  11.5 28.8 %copy-start.7 = (s32[16]{0:T(128)S(1)}, s32[16]{0:T(128)}, u32[]{:S(2)}) copy-start(s32[16]{0:T(128)} %constant.6.clone) | copy-start | bytes 196
  11.5 28.5 %collective-permute-start.2 = (bf16[8,16,1024]{2,1,0:T(8,128)(2,1)S(1)}, bf16[8,16,1024]{2,1,0:T(8,128)(2,1)S(1)}, u32[]{:S(2)}, u32[]{:S(2)}) collective-permute-start(bf16[8,16,1024]{2,1,0:T(8,128)(2,1)S(1)} %pad_maximum_fusion.1), channel_id=1, source_target_pairs={{0,2},{1,3},{2,0},{3,1},{4,6},{5,7},{6,4},{7,5},{8,10},{9,11},{10,... | collective-permute-start | bytes 786440 | tf_op jit(solution)/shard_map/ppermute | solution.py:210
  39.9 2.2 %copy-start = (bf16[2,2,64,3072]{3,2,1,0:T(8,128)(2,1)S(1)}, bf16[2,2,64,3072]{3,2,1,0:T(8,128)(2,1)}, u32[]{:S(2)}) copy-start(bf16[2,2,64,3072]{3,2,1,0:T(8,128)(2,1)} %param.9) | copy-start | bytes 4718596
  39.9 2.2 %copy-start.1 = (bf16[2,2,64,1024]{3,2,1,0:T(8,128)(2,1)S(1)}, bf16[2,2,64,1024]{3,2,1,0:T(8,128)(2,1)}, u32[]{:S(2)}) copy-start(bf16[2,2,64,1024]{3,2,1,0:T(8,128)(2,1)} %param.10) | copy-start | bytes 1572868
  39.9 2.2 %copy-start.2 = (s32[16,16]{1,0:T(8,128)S(1)}, s32[16,16]{1,0:T(8,128)}, u32[]{:S(2)}) copy-start(s32[16,16]{1,0:T(8,128)} %blocks.1) | copy-start | bytes 3076
  40.0 2.2 %copy-start.3 = (s32[32]{0:T(128)S(1)}, s32[32]{0:T(128)}, u32[]{:S(2)}) copy-start(s32[32]{0:T(128)} %home.1) | copy-start | bytes 388
  40.0 2.2 %copy-start.4 = (s32[16]{0:T(128)S(1)}, s32[16]{0:T(128)}, u32[]{:S(2)}) copy-start(s32[16]{0:T(128)} %lens.1) | copy-start | bytes 196
  40.1 2.0 %collective-permute-start.3 = (bf16[16,16,1024]{2,1,0:T(8,128)(2,1)S(1)}, bf16[16,16,1024]{2,1,0:T(8,128)(2,1)S(1)}, u32[]{:S(2)}, u32[]{:S(2)}) collective-permute-start(bf16[16,16,1024]{2,1,0:T(8,128)(2,1)S(1)} %pad_maximum_fusion), channel_id=1, source_target_pairs={{0,1},{1,0},{2,3},{3,2},{4,5},{5,4},{6,7},{7,6},{8,9},{9,8},{10,11... | collective-permute-start | bytes 1572872 | tf_op jit(solution)/shard_map/ppermute | solution.py:210
  42.1 16.2 %copy-start.6 = (bf16[432,32]{0,1:T(8,128)(2,1)S(1)}, bf16[432,32]{0,1:T(8,128)(2,1)}, u32[]{:S(2)}) copy-start(bf16[432,32]{0,1:T(8,128)(2,1)} %param.16) | copy-start | bytes 82948
  54.0 24.6 %collective-permute-start.4 = (bf16[2,64,64]{2,1,0:T(8,128)(2,1)S(1)}, bf16[2,64,64]{2,1,0:T(8,128)(2,1)S(1)}, u32[]{:S(2)}, u32[]{:S(2)}) collective-permute-start(bf16[2,64,64]{2,1,0:T(8,128)(2,1)S(1)} %get-tuple-element.6), channel_id=1, source_target_pairs={{0,1},{1,2},{2,3},{3,4},{4,5},{5,6},{6,7},{7,8},{8,9},{9,10},{10,1... | collective-permute-start | bytes 49160 | tf_op jit(solution)/shard_map/ppermute | solution.py:243
  56.0 22.7 %collective-permute-start.5 = (bf16[2,64,64]{2,1,0:T(8,128)(2,1)S(1)}, bf16[2,64,64]{2,1,0:T(8,128)(2,1)S(1)}, u32[]{:S(2)}, u32[]{:S(2)}) collective-permute-start(bf16[2,64,64]{2,1,0:T(8,128)(2,1)S(1)} %get-tuple-element.5), channel_id=1, source_target_pairs={{1,0},{2,1},{3,2},{4,3},{5,4},{6,5},{7,6},{8,7},{9,8},{10,9},{11,1... | collective-permute-start | bytes 49160 | tf_op jit(solution)/shard_map/ppermute | solution.py:244

commit v2 on v0

v2 whole, which is shorter than its diff:
```python
import functools
import math

import jax
import jax.numpy as jnp
from jax import lax
from jax.experimental import pallas as pl
from jax.experimental.pallas import tpu as pltpu
from jax.sharding import PartitionSpec as P

HEADS = 24
KV_HEADS = 4
HEAD_DIM = 128
GROUP = HEADS // KV_HEADS
SCALE = math.log2(math.e) / math.sqrt(HEAD_DIM)
SAFE = 2.0**100
MIB = 1024 * 1024
WHOLE = pl.BlockSpec(memory_space=pltpu.VMEM)
SCALARS = pl.BlockSpec(memory_space=pltpu.SMEM)
BF16 = jnp.bfloat16
F32 = jnp.float32


def head_columns(index):
    return slice(index * HEAD_DIM, (index + 1) * HEAD_DIM)


def params(mib):
    return pltpu.CompilerParams(vmem_limit_bytes=mib * MIB)


def own_body(queries, own, packed, sums):
    tokens = queries.shape[0]

    def one(g, carry):
        def columns(index):
            return pl.ds(pl.multiple_of(index * HEAD_DIM, HEAD_DIM), HEAD_DIM)

        query = jnp.concatenate([queries[:, columns(g * GROUP + h)] for h in range(GROUP)], axis=0)
        value = jnp.concatenate(
            [own[:, columns(KV_HEADS + g)], jnp.ones((tokens, HEAD_DIM), BF16)], axis=1
        )
        score = lax.dot_general(
            query, own[:, columns(g)], (((1,), (1,)), ((), ())), preferred_element_type=F32
        )
        top = jnp.max(score, axis=1, keepdims=True)
        weights = jnp.exp2((score - top) * SCALE).astype(BF16)
        mixed = jnp.dot(weights, value, preferred_element_type=F32)
        total = mixed[:, HEAD_DIM:]
        sums[g] = mixed[:, :HEAD_DIM] / total
        level = top + jnp.log2(total) * (1.0 / SCALE)
        high = level.astype(BF16).astype(F32)
        middle = (level - high).astype(BF16).astype(F32)
        low = level - high - middle
        lane = lax.broadcasted_iota(jnp.int32, level.shape, 1)
        extra = jnp.where(lane == 0, high, jnp.where(lane == 1, middle, jnp.where(lane == 2, low, 0.0)))
        packed[g, :, :HEAD_DIM] = query
        packed[g, :, HEAD_DIM:] = extra.astype(BF16)
        return carry

    lax.fori_loop(0, KV_HEADS, one, 0)


def attend_own(query_rows, own_rows):
    tokens, width = query_rows.shape
    rows = GROUP * tokens
    return pl.pallas_call(
        own_body,
        in_specs=[WHOLE, WHOLE],
        out_specs=[WHOLE, WHOLE],
        out_shape=[
            jax.ShapeDtypeStruct((KV_HEADS, rows, 2 * HEAD_DIM), BF16),
            jax.ShapeDtypeStruct((KV_HEADS, rows, HEAD_DIM), F32),
        ],
        compiler_params=params(24),
        cost_estimate=pl.CostEstimate(
            flops=12 * tokens * tokens * width, bytes_accessed=10 * tokens * width, transcendentals=0
        ),
        name="attend_own",
    )(query_rows, own_rows)


def slots_body(blocks_here, table, home, blocks, lens, slots):
    tile = table[0]
    count = lens[tile]
    for entry in range(slots.shape[0]):
        listed = entry < count
        stored = home[blocks[tile, jnp.where(listed, entry, 0)]]
        place = table[1 + ((stored // blocks_here) ^ tile)]
        slots[entry] = jnp.where(listed, place * blocks_here + stored % blocks_here, -1)


def find_slots(table, block_home, block_list, list_len, blocks_here):
    return pl.pallas_call(
        functools.partial(slots_body, blocks_here),
        in_specs=[SCALARS] * 4,
        out_specs=SCALARS,
        out_shape=jax.ShapeDtypeStruct((block_list.shape[1],), jnp.int32),
        name="find_slots",
    )(table, block_home, block_list, list_len)


def past_body(slots, packed, past, sums, weight, out, keys, values, worst):
    entries = slots.shape[0]
    block_tokens = past.shape[1]
    tokens, columns = out.shape
    lane = lax.broadcasted_iota(jnp.int32, (block_tokens, HEAD_DIM), 1)
    minus = jnp.where(lane < 3, -1.0, 0.0)
    zero = jnp.zeros((block_tokens, HEAD_DIM), BF16)
    for entry in range(entries):
        listed = slots[entry] >= 0
        block = past[jnp.where(listed, slots[entry], slots[0])]
        live = jnp.where(listed, 1.0, 0.0)
        level = (minus * live).astype(BF16)
        counted = jnp.full((block_tokens, HEAD_DIM), live, F32).astype(BF16)
        rows = slice(entry * block_tokens, (entry + 1) * block_tokens)
        for g in range(KV_HEADS):
            keys[g, rows, :HEAD_DIM] = jnp.where(listed, block[:, head_columns(g)], zero)
            keys[g, rows, HEAD_DIM:] = level
            values[g, rows, :HEAD_DIM] = jnp.where(listed, block[:, head_columns(KV_HEADS + g)], zero)
            values[g, rows, HEAD_DIM:] = counted

    heads = GROUP if keys.shape[1] <= 512 else 1
    steps = KV_HEADS * GROUP // heads

    def over_steps(one, start):
        if heads == GROUP:
            for step in range(steps):
                start = one(step, start)
            return start
        return lax.fori_loop(0, steps, one, start)

    def place(step):
        if heads == GROUP:
            return step, slice(None), slice(step * GROUP * HEAD_DIM, (step + 1) * GROUP * HEAD_DIM)
        rows = pl.ds(pl.multiple_of((step % GROUP) * tokens, tokens), tokens)
        return step // GROUP, rows, pl.ds(pl.multiple_of(step * HEAD_DIM, HEAD_DIM), HEAD_DIM)

    def scores(g, rows):
        return SCALE * lax.dot_general(
            packed[g, rows], keys[g], (((1,), (1,)), ((), ())), preferred_element_type=F32
        )

    def projected(attended, weight_rows):
        panel = weight[weight_rows]
        part = jnp.zeros((tokens, columns), F32)
        for h in range(heads):
            part += jnp.dot(
                attended[h * tokens : (h + 1) * tokens], panel[head_columns(h)], preferred_element_type=F32
            )
        return part

    def quick(step, carry):
        total, largest = carry
        g, rows, weight_rows = place(step)
        weights = jnp.exp2(scores(g, rows)).astype(BF16)
        mixed = jnp.dot(weights, values[g], preferred_element_type=F32)
        below = mixed[:, HEAD_DIM:] + 1.0
        largest = jnp.maximum(largest, jnp.max(below.reshape((-1,) + largest.shape), axis=0))
        attended = ((mixed[:, :HEAD_DIM] + sums[g, rows]) / below).astype(BF16)
        return total + projected(attended, weight_rows), largest

    nothing = jnp.zeros((tokens, columns), F32)
    total, largest = over_steps(quick, (nothing, jnp.zeros(worst.shape, F32)))
    out[...] = total.astype(BF16)
    worst[...] = largest

    @pl.when(jnp.logical_not(jnp.max(worst[...]) < SAFE))
    def _():
        def careful(step, total):
            g, rows, weight_rows = place(step)
            score = scores(g, rows)
            top = jnp.maximum(jnp.max(score, axis=1, keepdims=True), 0.0)
            weights = jnp.exp2(score - top).astype(BF16)
            mixed = jnp.dot(weights, values[g], preferred_element_type=F32)
            share = jnp.exp2(-top)
            attended = (mixed[:, :HEAD_DIM] + share * sums[g, rows]) / (mixed[:, HEAD_DIM:] + share)
            return total + projected(attended.astype(BF16), weight_rows)

        out[...] = over_steps(careful, nothing).astype(BF16)


def attend_past(slots, packed, past, sums, weight):
    heads, rows, _ = packed.shape
    tokens = rows // GROUP
    keys = slots.shape[0] * past.shape[1]
    columns = weight.shape[1]
    return pl.pallas_call(
        past_body,
        in_specs=[SCALARS, WHOLE, WHOLE, WHOLE, WHOLE],
        out_specs=WHOLE,
        out_shape=jax.ShapeDtypeStruct((tokens, columns), BF16),
        scratch_shapes=[
            pltpu.VMEM((heads, keys, 2 * HEAD_DIM), BF16),
            pltpu.VMEM((heads, keys, 2 * HEAD_DIM), BF16),
            pltpu.VMEM((8, HEAD_DIM), F32),
        ],
        compiler_params=params(40 if keys > 256 else 24),
        cost_estimate=pl.CostEstimate(
            flops=8 * heads * rows * keys * HEAD_DIM, bytes_accessed=heads * rows * 1024, transcendentals=0
        ),
        name="attend_past",
    )(slots, packed, past, sums, weight)


def pack_body(final, decode, out):
    half = final.shape[0] // 2
    taps, width = decode.shape
    share = 128 // width
    tall = out.shape[0] - half
    out[:half] = jnp.concatenate([final[:half], final[half:]], axis=1)
    parts = []
    for part in range(share):
        rows = decode[part * tall : min((part + 1) * tall, taps)]
        missing = tall - rows.shape[0]
        if missing:
            rows = jnp.concatenate([rows, jnp.zeros((missing, width), BF16)], axis=0)
        parts.append(rows)
    out[half:] = jnp.concatenate(parts, axis=1)


def packed_rows(final, decode, lat):
    share = 128 // decode.shape[1]
    per_part = -(-(decode.shape[0] // lat) // share) * lat
    return final.shape[0] // 2 + per_part


def pack(final, decode, lat):
    return pl.pallas_call(
        pack_body,
        in_specs=[WHOLE, WHOLE],
        out_specs=WHOLE,
        out_shape=jax.ShapeDtypeStruct((packed_rows(final, decode, lat), 128), BF16),
        name="pack",
    )(final, decode)


def unpack_body(table, gathered, final, decode):
    count = gathered.shape[0]
    depth = final.shape[0] // count
    half = depth // 2
    width = decode.shape[1] // count
    share = 128 // width
    tall = gathered.shape[1] - half
    tile = table[0]
    for device in range(count):
        block = gathered[table[1 + (device ^ tile)], :half]
        final[device * depth : device * depth + half] = block[:, : final.shape[1]]
        final[device * depth + half : (device + 1) * depth] = block[:, final.shape[1] :]
    for column in range(count // share):
        blocks = [
            gathered[table[1 + ((column * share + k) ^ tile)], half:] for k in range(share)
        ]
        for part in range(share):
            rows = min((part + 1) * tall, decode.shape[0]) - part * tall
            decode[part * tall : part * tall + rows, column * 128 : (column + 1) * 128] = jnp.concatenate(
                [b[:rows, part * width : (part + 1) * width] for b in blocks], axis=1
            )


def unpack(table, gathered, final_shape, decode_shape):
    return pl.pallas_call(
        unpack_body,
        in_specs=[SCALARS, WHOLE],
        out_specs=[WHOLE, WHOLE],
        out_shape=[jax.ShapeDtypeStruct(final_shape, BF16), jax.ShapeDtypeStruct(decode_shape, BF16)],
        name="unpack",
    )(table, gathered)


def tap_rows(frames, cells, width):
    stacks = []
    for shift_t in range(3):
        rows = []
        for frame in range(frames):
            source = frame + shift_t - 2
            rows.append(cells[source] if source >= 0 else jnp.zeros((width, cells[0].shape[1]), BF16))
        stacks.append(jnp.concatenate(rows, axis=0))
    return stacks


def shifted(wide, frame, width, lat):
    chunks = []
    for chunk in range(wide.shape[1]):
        lane = lax.broadcasted_iota(jnp.int32, (width, 128), 1) + 128 * chunk
        shift = (lane // lat) % 3
        near = jnp.where(shift == 1, wide[frame, chunk, 8 : 8 + width], wide[frame, chunk, 9 : 9 + width])
        chunks.append(jnp.where(shift == 0, wide[frame, chunk, 7 : 7 + width], near).astype(BF16))
    return jnp.concatenate(chunks, axis=1)


def inner_body(lat, predicted, kernel, features, edges, wide, done, sems):
    frames, patch_rows, patches, values = predicted.shape
    tall, broad = 2 * patch_rows, 2 * patches
    span = 3 * lat
    chunks = wide.shape[1]
    lanes = 128 * chunks
    wide[:, :, 0:8] = jnp.zeros((frames, chunks, 8, 128), F32)
    wide[:, :, 8 + broad :] = jnp.zeros((frames, chunks, 8, 128), F32)
    source = lax.broadcasted_iota(jnp.int32, (values, lanes), 0)
    target = lax.broadcasted_iota(jnp.int32, (values, lanes), 1)
    for side in range(2):
        picks = []
        for r in range(patch_rows):
            upper = target // span - 2 * r
            wanted = (upper >= 0) & (upper < 2) & (source == upper * 2 * lat + side * lat + target % lat)
            picks.append(jnp.where(wanted, 1.0, 0.0).astype(BF16))
        for frame in range(frames):
            cells = jnp.zeros((patches, lanes), F32)
            for r in range(patch_rows):
                cells += jnp.dot(predicted[frame, r], picks[r], preferred_element_type=F32)
            for chunk in range(chunks):
                wide[frame, chunk, pl.ds(8 + side, patches, stride=2), :] = cells[:, 128 * chunk : 128 * (chunk + 1)]
    stacks = tap_rows(frames, [shifted(wide, f, broad, lat) for f in range(frames)], broad)
    copies = []
    for row in list(range(1, tall - 1)) + [0, tall - 1]:
        first, last = max(row - 1, 0), min(row + 1, tall - 1)
        total = jnp.zeros((frames * broad, kernel.shape[1]), F32)
        for shift_t in range(3):
            start = (3 * shift_t + first - (row - 1)) * span
            total += jnp.dot(
                stacks[shift_t][:, first * span : (last + 1) * span],
                kernel[start : start + (last + 1 - first) * span],
                preferred_element_type=F32,
            )
        if 0 < row < tall - 1:
            done[row - 1] = total.astype(BF16).reshape(done.shape[1:])
            copy = pltpu.make_async_copy(done.at[row - 1], features.at[:, row], sems.at[row - 1])
            copy.start()
            copies.append(copy)
        else:
            edges[0 if row == 0 else 1] = total
    for copy in copies:
        copy.wait()


def convolve_inner(predicted, kernel):
    frames, patch_rows, patches, values = predicted.shape
    lat = values // 4
    tall, broad = 2 * patch_rows, 2 * patches
    channels = kernel.shape[1]
    lanes = -(-tall * 3 * lat // 128) * 128
    return pl.pallas_call(
        functools.partial(inner_body, lat),
        in_specs=[WHOLE, WHOLE],
        out_specs=[pl.BlockSpec(memory_space=pl.ANY), WHOLE],
        out_shape=[
            jax.ShapeDtypeStruct((frames, tall, broad, channels), BF16),
            jax.ShapeDtypeStruct((2, frames * broad, channels), F32),
        ],
        scratch_shapes=[
            pltpu.VMEM((frames, lanes // 128, broad + 16, 128), F32),
            pltpu.VMEM((tall - 2, frames, broad, channels), BF16),
            pltpu.SemaphoreType.DMA((tall - 2,)),
        ],
        compiler_params=params(16),
        cost_estimate=pl.CostEstimate(
            flops=2 * frames * tall * broad * 27 * lat * channels,
            bytes_accessed=2 * frames * tall * broad * channels,
            transcendentals=0,
        ),
        name="convolve_inner",
    )(predicted, kernel)


def outer_body(lat, above, below, kernel, edges, given, features, wide, done, sems):
    frames, patches, values = above.shape
    broad = 2 * patches
    tall = features.shape[1]
    span = 3 * lat
    chunks = wide.shape[2]
    lanes = 128 * chunks
    source = lax.broadcasted_iota(jnp.int32, (values, lanes), 0)
    target = lax.broadcasted_iota(jnp.int32, (values, lanes), 1)
    lane = lax.broadcasted_iota(jnp.int32, (broad, lanes), 1)
    copies = []
    for edge, cells in enumerate((above, below)):
        wide[edge, :, :, 0:8] = jnp.zeros((frames, chunks, 8, 128), F32)
        wide[edge, :, :, 8 + broad :] = jnp.zeros((frames, chunks, 8, 128), F32)
        for side in range(2):
            wanted = (source == (1 - edge) * 2 * lat + side * lat + target % lat) & (target < 3 * span)
            pick = jnp.where(wanted, 1.0, 0.0).astype(BF16)
            for frame in range(frames):
                spread = jnp.dot(cells[frame], pick, preferred_element_type=F32)
                for chunk in range(chunks):
                    wide[edge, frame, chunk, pl.ds(8 + side, patches, stride=2), :] = spread[
                        :, 128 * chunk : 128 * (chunk + 1)
                    ]
        ready = [shifted(wide.at[edge], f, broad, lat) for f in range(frames)]
        rows = []
        for frame in range(frames):
            taps = jnp.zeros((broad, lanes), BF16)
            for shift_t in range(3):
                if frame + shift_t - 2 >= 0:
                    taps = jnp.where(lane // span == shift_t, ready[frame + shift_t - 2], taps)
            rows.append(taps)
        shift_y = 2 * edge
        panel = jnp.concatenate(
            [kernel[(3 * t + shift_y) * span : (3 * t + shift_y + 1) * span] for t in range(3)], axis=0
        )
        total = edges[edge] + jnp.dot(
            jnp.concatenate(rows, axis=0)[:, : 3 * span], panel, preferred_element_type=F32
        )
        done[edge] = total.astype(BF16).reshape(done.shape[1:])
        copy = pltpu.make_async_copy(done.at[edge], features.at[:, edge * (tall - 1)], sems.at[edge])
        copy.start()
        copies.append(copy)
    for copy in copies:
        copy.wait()


def convolve_outer(above, below, kernel, edges, features):
    frames, patches, values = above.shape
    lat = values // 4
    broad = 2 * patches
    channels = kernel.shape[1]
    lanes = -(-9 * lat // 128) * 128
    anywhere = pl.BlockSpec(memory_space=pl.ANY)
    return pl.pallas_call(
        functools.partial(outer_body, lat),
        in_specs=[WHOLE, WHOLE, WHOLE, WHOLE, anywhere],
        out_specs=anywhere,
        out_shape=jax.ShapeDtypeStruct(features.shape, BF16),
        input_output_aliases={4: 0},
        scratch_shapes=[
            pltpu.VMEM((2, frames, lanes // 128, broad + 16, 128), F32),
            pltpu.VMEM((2, frames, broad, channels), BF16),
            pltpu.SemaphoreType.DMA((2,)),
        ],
        compiler_params=params(16),
        name="convolve_outer",
    )(above, below, kernel, edges, features)


def exchange(value, offset):
    count = lax.axis_size("seq")
    return lax.ppermute(value, "seq", [(i, i ^ offset) for i in range(count)])


def places(order):
    return [order.index(k) for k in range(len(order))]


def gather_by_doubling(shard, bits):
    held, order = shard, [0]
    for bit in bits:
        held = jnp.concatenate([held, exchange(held, bit)], axis=0)
        order = order + [o ^ bit for o in order]
    return held, order


def local(queries, own_kv, past_kv, block_home, block_list, list_len, final_weight, decoder_weight):
    frames, patch_rows, patches, width = queries.shape
    tokens = frames * patch_rows * patches
    count = lax.axis_size("seq")
    assert count & (count - 1) == 0
    blocks_here = past_kv.shape[0]
    lat = final_weight.shape[1] // 4
    me = lax.axis_index("seq").astype(jnp.int32).reshape(1)
    bits = [1 << k for k in reversed(range(count.bit_length() - 1))]
    small = count == 16 and decoder_weight.shape[1] * 4 == 128 and final_weight.shape[0] % 32 == 0
    if small:
        far = [4, 8, 12]
        panels = pack(final_weight, decoder_weight, lat)[None]
        arrived = [exchange(past_kv, k) for k in far]
        panels = jnp.concatenate([panels, exchange(panels, 2)], axis=0)
        past = jnp.concatenate([past_kv] + arrived, axis=0)
        past = jnp.concatenate([past, exchange(past, 2)], axis=0)
        past = jnp.concatenate([past, exchange(past, 1)], axis=0)
        order = [0] + far
        order = order + [o ^ 2 for o in order]
        order = order + [o ^ 1 for o in order]
        panels = jnp.concatenate([panels] + [exchange(panels, k) for k in far], axis=0)
        panels = jnp.concatenate([panels, exchange(panels, 1)], axis=0)
        panel_order = [k ^ x for k in [0] + far for x in (0, 2)]
        panel_order = panel_order + [o ^ 1 for o in panel_order]
        panel_table = jnp.concatenate([me, jnp.array(places(panel_order), jnp.int32)])
        final, decode = unpack(
            panel_table,
            panels,
            (final_weight.shape[0] * count, final_weight.shape[1]),
            (decoder_weight.shape[0], decoder_weight.shape[1] * count),
        )
    else:
        past, order = gather_by_doubling(past_kv, bits)
        final = lax.all_gather(final_weight, "seq", axis=0, tiled=True)
        decode = lax.all_gather(decoder_weight, "seq", axis=1, tiled=True)
    table = jnp.concatenate([me, jnp.array(places(order), jnp.int32)])
    slots = find_slots(table, block_home, block_list, list_len, blocks_here)
    packed, sums = attend_own(queries.reshape(tokens, width), own_kv.reshape(tokens, own_kv.shape[3]))
    predicted = attend_past(slots, packed, past, sums, final)
    predicted = predicted.reshape(frames, patch_rows, patches, predicted.shape[1])
    above = lax.ppermute(predicted[:, -1], "seq", [(i, i + 1) for i in range(count - 1)])
    below = lax.ppermute(predicted[:, 0], "seq", [(i + 1, i) for i in range(count - 1)])
    features, edges = convolve_inner(predicted, decode)
    return convolve_outer(above, below, decode, edges, features)


def solution(mesh):
    return jax.shard_map(
        local,
        mesh=mesh,
        in_specs=(
            P("groups", "seq", None, None),
            P("groups", "seq", None, None),
            P(("groups", "seq"), None, None),
            P("groups"),
            P("groups", None),
            P("groups"),
            P("seq", None),
            P(None, "seq"),
        ),
        out_specs=P("groups", "seq", None, None),
        check_vma=False,
    )
```

time: 189 us -> 63.7 us (0.34)
  the two profiles are of different devices: /device:TPU:1 before, /device:TPU:12 now
where the time goes in v2:
time: 63.7 us; the launch traced here: 62.8 us
  local copies, waits for them, and re-layouts  23.5 us (37%)
  starting transfers between devices  17.1 us (27%)
  Pallas kernels  15.2 us (24%)
  waiting for transfers between devices  4.03 us (6%)
  other arithmetic  2.89 us (5%)
    unnamed x32, local copies, waits for them, and re-layouts  18.3 us
    ppermute x10, starting transfers between devices, exchange(): return lax.ppermute(value, 'seq', [(i, i ^ offset) for i in range(count)])  11.9 us
    pallas_call x1, Pallas kernels, attend_own(): pl.pallas_call(own_body, in_specs=[WHOLE, WHOLE], out_specs=[WHOLE, WHOLE...  3.67 us
    ppermute x1, starting transfers between devices, local(): lax.ppermute(predicted[:, 0], 'seq', [(i + 1, i) for i in range(count - 1)])  3.27 us
    pallas_call x1, Pallas kernels, attend_past(): pl.pallas_call(past_body, in_specs=[SCALARS, WHOLE, WHOLE, WHOLE, WHOLE],...  3.03 us
    ppermute x1, waiting for transfers between devices, local(): lax.ppermute(predicted[:, -1], 'seq', [(i, i + 1) for i in range(count -...  2.73 us
    pallas_call x1, Pallas kernels, unpack(): pl.pallas_call(unpack_body, in_specs=[SCALARS, WHOLE], out_specs=[WHOLE,...  2.57 us
    ppermute x1, starting transfers between devices, local(): lax.ppermute(predicted[:, -1], 'seq', [(i, i + 1) for i in range(count -...  1.92 us
  transfers between devices with their start and end apart: 12, of which 2 were waited for; matrix products, arithmetic and copies ran while one was open for 26% of the time, Pallas kernels for 17%

profile of v2, /device:TPU:12, one launch (start us, length us, event | category | flops | bytes accessed | tf_op | source)
XLA Modules:
  0.0 62.8 jit_solution(11358784492587858848)
XLA Ops:
  0.0 0.0 copy-start.10
  0.0 0.0 copy-start.9
  0.0 1.6 %collective-permute-start.2 = (bf16[2,16,1024]{2,1,0:T(8,128)(2,1)}, bf16[2,16,1024]{2,1,0:T(8,128)(2,1)S(1)}, u32[]{:S(2)}, u32[]{:S(2)}) collective-permute-start(bf16[2,16,1024]{2,1,0:T(8,128)(2,1)} %param.12), channel_id=1, source_target_pairs={{0,12},{1,13},{2,14},{3,15},{4,8},{5,9},{6,10},{7,11},{8,4},{9,5},... | collective-permute-start | bytes 196616 | tf_op jit(solution)/shard_map/ppermute | solution.py:437
  1.6 1.2 %collective-permute-start.1 = (bf16[2,16,1024]{2,1,0:T(8,128)(2,1)}, bf16[2,16,1024]{2,1,0:T(8,128)(2,1)S(1)}, u32[]{:S(2)}, u32[]{:S(2)}) collective-permute-start(bf16[2,16,1024]{2,1,0:T(8,128)(2,1)} %param.12), channel_id=1, source_target_pairs={{0,8},{1,9},{2,10},{3,11},{4,12},{5,13},{6,14},{7,15},{8,0},{9,1},... | collective-permute-start | bytes 196616 | tf_op jit(solution)/shard_map/ppermute | solution.py:437
  2.8 1.2 %collective-permute-start = (bf16[2,16,1024]{2,1,0:T(8,128)(2,1)}, bf16[2,16,1024]{2,1,0:T(8,128)(2,1)S(1)}, u32[]{:S(2)}, u32[]{:S(2)}) collective-permute-start(bf16[2,16,1024]{2,1,0:T(8,128)(2,1)} %param.12), channel_id=1, source_target_pairs={{0,4},{1,5},{2,6},{3,7},{4,0},{5,1},{6,2},{7,3},{8,12},{9,13},{10,... | collective-permute-start | bytes 196616 | tf_op jit(solution)/shard_map/ppermute | solution.py:437
  4.1 1.5 %copy.15.final = bf16[192,64]{1,0:T(8,128)(2,1)} copy(bf16[192,64]{0,1:T(8,128)(2,1)} %param.16) | data formatting | bytes 49152 | tf_op args[6]
  5.5 1.5 %copy.16.decode = bf16[432,32]{1,0:T(8,128)(2,1)} copy(bf16[432,32]{0,1:T(8,128)(2,1)} %param.17) | data formatting | bytes 55296 | tf_op args[7]
  7.1 1.6 %pack.1 = bf16[208,128]{1,0:T(8,128)(2,1)} custom-call(bf16[192,64]{1,0:T(8,128)(2,1)} %copy.15.final, bf16[432,32]{1,0:T(8,128)(2,1)} %copy.16.decode), custom_call_target="tpu_custom_call" | custom-call | tf_op jit(solution)/shard_map/pack/pallas_call | solution.py:229
  8.7 1.5 %collective-permute-start.5 = (bf16[1,208,128]{2,1,0:T(8,128)(2,1)}, bf16[1,208,128]{2,1,0:T(8,128)(2,1)S(1)}, u32[]{:S(2)}, u32[]{:S(2)}) collective-permute-start(bf16[1,208,128]{2,1,0:T(8,128)(2,1)} %bitcast.19), channel_id=1, source_target_pairs={{0,2},{1,3},{2,0},{3,1},{4,6},{5,7},{6,4},{7,5},{8,10},{9,11},{10,... | collective-permute-start | bytes 159752 | tf_op jit(solution)/shard_map/ppermute | solution.py:437
  10.2 1.5 %constant_dynamic-update-slice_fusion.15 = (bf16[8,208,128]{2,1,0:T(8,128)(2,1)}, bf16[16,208,128]{2,1,0:T(8,128)(2,1)}) fusion(bf16[208,128]{1,0:T(8,128)(2,1)} %pack.1), kind=kLoop, calls=%fused_computation.17 | loop fusion | bytes 159744
  11.7 1.5 %constant_dynamic-update-slice_fusion.4 = (bf16[16,16,1024]{2,1,0:T(8,128)(2,1)}, bf16[32,16,1024]{2,1,0:T(8,128)(2,1)S(1)}) fusion(bf16[2,16,1024]{2,1,0:T(8,128)(2,1)} %param.12), kind=kLoop, calls=%fused_computation.6 | loop fusion | bytes 196608
  13.2 0.0 collective-permute-done.5
  13.2 0.8 %pad_maximum_fusion.1 = bf16[2,208,128]{2,1,0:T(8,128)(2,1)S(1)} fusion(bf16[1,208,128]{2,1,0:T(8,128)(2,1)S(1)} %collective-permute-done.5, bf16[1,208,128]{2,1,0:T(8,128)(2,1)} %bitcast.20), kind=kLoop, calls=%fused_computation.1 | loop fusion | flops 53248 | bytes 212992 | tf_op jit(solution)/shard_map/concatenate | solution.py:466
  14.0 1.5 %collective-permute-start.8 = (bf16[2,208,128]{2,1,0:T(8,128)(2,1)S(1)}, bf16[2,208,128]{2,1,0:T(8,128)(2,1)S(1)}, u32[]{:S(2)}, u32[]{:S(2)}) collective-permute-start(bf16[2,208,128]{2,1,0:T(8,128)(2,1)S(1)} %pad_maximum_fusion.1), channel_id=1, source_target_pairs={{0,12},{1,13},{2,14},{3,15},{4,8},{5,9},{6,10},{7,11},{8,4},{9,5},... | collective-permute-start | bytes 319496 | tf_op jit(solution)/shard_map/ppermute | solution.py:437
  15.5 1.7 %collective-permute-start.7 = (bf16[2,208,128]{2,1,0:T(8,128)(2,1)S(1)}, bf16[2,208,128]{2,1,0:T(8,128)(2,1)S(1)}, u32[]{:S(2)}, u32[]{:S(2)}) collective-permute-start(bf16[2,208,128]{2,1,0:T(8,128)(2,1)S(1)} %pad_maximum_fusion.1), channel_id=1, source_target_pairs={{0,8},{1,9},{2,10},{3,11},{4,12},{5,13},{6,14},{7,15},{8,0},{9,1},... | collective-permute-start | bytes 319496 | tf_op jit(solution)/shard_map/ppermute | solution.py:437
  17.2 0.7 %constant_dynamic-update-slice_fusion.14 = (bf16[8,208,128]{2,1,0:T(8,128)(2,1)}, bf16[16,208,128]{2,1,0:T(8,128)(2,1)}) fusion(bf16[8,208,128]{2,1,0:T(8,128)(2,1)} %get-tuple-element.37, bf16[1,208,128]{2,1,0:T(8,128)(2,1)S(1)} %collective-permute-done.5, bf16[16,208,128]{2,1,0:T(8,128)(2,1)} %get-tuple-element.38), kind=kLoop, calls=%fused_computation.16 | loop fusion | bytes 159744
  17.9 0.0 collective-permute-done.2
  17.9 1.2 %collective-permute-start.6 = (bf16[2,208,128]{2,1,0:T(8,128)(2,1)S(1)}, bf16[2,208,128]{2,1,0:T(8,128)(2,1)S(1)}, u32[]{:S(2)}, u32[]{:S(2)}) collective-permute-start(bf16[2,208,128]{2,1,0:T(8,128)(2,1)S(1)} %pad_maximum_fusion.1), channel_id=1, source_target_pairs={{0,4},{1,5},{2,6},{3,7},{4,0},{5,1},{6,2},{7,3},{8,12},{9,13},{10,... | collective-permute-start | bytes 319496 | tf_op jit(solution)/shard_map/ppermute | solution.py:437
  19.1 0.0 collective-permute-done.1
  19.1 0.0 collective-permute-done
  19.1 0.9 %pad_maximum_fusion = bf16[8,16,1024]{2,1,0:T(8,128)(2,1)S(1)} fusion(bf16[2,16,1024]{2,1,0:T(8,128)(2,1)S(1)} %collective-permute-done.2, bf16[2,16,1024]{2,1,0:T(8,128)(2,1)S(1)} %collective-permute-done.1, bf16[2,16,1024]{2,1,0:T(8,128)(2,1)S(1)} %collective-permute-done, bf16[2,16,1024]{2,1,0:T(8,128)(2,1)} %param.12), kind=kLoop, calls=%fused_computation | loop fusion | flops 393216 | bytes 524288 | tf_op jit(solution)/shard_map/concatenate | solution.py:467
  20.0 1.4 %collective-permute-start.3 = (bf16[8,16,1024]{2,1,0:T(8,128)(2,1)S(1)}, bf16[8,16,1024]{2,1,0:T(8,128)(2,1)S(1)}, u32[]{:S(2)}, u32[]{:S(2)}) collective-permute-start(bf16[8,16,1024]{2,1,0:T(8,128)(2,1)S(1)} %pad_maximum_fusion), channel_id=1, source_target_pairs={{0,2},{1,3},{2,0},{3,1},{4,6},{5,7},{6,4},{7,5},{8,10},{9,11},{10,... | collective-permute-start | bytes 786440 | tf_op jit(solution)/shard_map/ppermute | solution.py:437
  21.4 0.6 %constant_dynamic-update-slice_fusion.3 = (bf16[16,16,1024]{2,1,0:T(8,128)(2,1)}, bf16[32,16,1024]{2,1,0:T(8,128)(2,1)S(1)}) fusion(bf16[16,16,1024]{2,1,0:T(8,128)(2,1)} %get-tuple-element.33, bf16[2,16,1024]{2,1,0:T(8,128)(2,1)S(1)} %collective-permute-done, bf16[32,16,1024]{2,1,0:T(8,128)(2,1)S(1)} %get-tuple-element.34), kind=kLoop, calls=%fused_computation.5 | loop fusion | bytes 196608
  22.1 0.6 %constant_dynamic-update-slice_fusion.2 = (bf16[16,16,1024]{2,1,0:T(8,128)(2,1)}, bf16[32,16,1024]{2,1,0:T(8,128)(2,1)S(1)}) fusion(bf16[16,16,1024]{2,1,0:T(8,128)(2,1)} %get-tuple-element.31, bf16[2,16,1024]{2,1,0:T(8,128)(2,1)S(1)} %collective-permute-done.1, bf16[32,16,1024]{2,1,0:T(8,128)(2,1)S(1)} %get-tuple-element.32), kind=kLoop, calls=%fused_computation.4 | loop fusion | bytes 196608
  22.7 0.6 %constant_dynamic-update-slice_fusion.1 = (bf16[16,16,1024]{2,1,0:T(8,128)(2,1)}, bf16[32,16,1024]{2,1,0:T(8,128)(2,1)S(1)}) fusion(bf16[16,16,1024]{2,1,0:T(8,128)(2,1)} %get-tuple-element.29, bf16[2,16,1024]{2,1,0:T(8,128)(2,1)S(1)} %collective-permute-done.2, bf16[32,16,1024]{2,1,0:T(8,128)(2,1)S(1)} %get-tuple-element.30), kind=kLoop, calls=%fused_computation.3 | loop fusion | bytes 196608
  23.3 1.3 %collective-permute-done.6 = bf16[2,208,128]{2,1,0:T(8,128)(2,1)S(1)} collective-permute-done((bf16[2,208,128]{2,1,0:T(8,128)(2,1)S(1)}, bf16[2,208,128]{2,1,0:T(8,128)(2,1)S(1)}, u32[]{:S(2)}, u32[]{:S(2)}) %collective-permute-start.6) | collective-permute-done | bytes 106528 | tf_op jit(solution)/shard_map/ppermute | solution.py:437
  24.6 0.7 %constant_dynamic-update-slice_fusion.13 = (bf16[8,208,128]{2,1,0:T(8,128)(2,1)}, bf16[16,208,128]{2,1,0:T(8,128)(2,1)}) fusion(bf16[8,208,128]{2,1,0:T(8,128)(2,1)} %get-tuple-element.35, bf16[2,208,128]{2,1,0:T(8,128)(2,1)S(1)} %collective-permute-done.6, bf16[16,208,128]{2,1,0:T(8,128)(2,1)} %get-tuple-element.36), kind=kLoop, calls=%fused_computation.15 | loop fusion | bytes 319488
  25.3 0.0 collective-permute-done.7
  25.3 0.7 %constant_dynamic-update-slice_fusion.12 = (bf16[8,208,128]{2,1,0:T(8,128)(2,1)}, bf16[16,208,128]{2,1,0:T(8,128)(2,1)}) fusion(bf16[8,208,128]{2,1,0:T(8,128)(2,1)} %get-tuple-element.23, bf16[2,208,128]{2,1,0:T(8,128)(2,1)S(1)} %collective-permute-done.7, bf16[16,208,128]{2,1,0:T(8,128)(2,1)} %get-tuple-element.24), kind=kLoop, calls=%fused_computation.14 | loop fusion | bytes 319488
  26.1 0.0 collective-permute-done.8
  26.1 0.7 %constant_dynamic-update-slice_fusion.11 = (bf16[8,208,128]{2,1,0:T(8,128)(2,1)}, bf16[16,208,128]{2,1,0:T(8,128)(2,1)}) fusion(bf16[8,208,128]{2,1,0:T(8,128)(2,1)} %get-tuple-element.21, bf16[2,208,128]{2,1,0:T(8,128)(2,1)S(1)} %collective-permute-done.8, bf16[16,208,128]{2,1,0:T(8,128)(2,1)} %get-tuple-element.22), kind=kLoop, calls=%fused_computation.13 | loop fusion | bytes 319488 | tf_op jit(solution)/shard_map/concatenate | solution.py:473
  26.8 0.0 collective-permute-start.9
  26.8 0.0 collective-permute-done.3
  26.8 0.8 %constant_dynamic-update-slice_fusion = (bf16[16,16,1024]{2,1,0:T(8,128)(2,1)}, bf16[32,16,1024]{2,1,0:T(8,128)(2,1)S(1)}) fusion(bf16[16,16,1024]{2,1,0:T(8,128)(2,1)} %get-tuple-element.27, bf16[8,16,1024]{2,1,0:T(8,128)(2,1)S(1)} %collective-permute-done.3, bf16[32,16,1024]{2,1,0:T(8,128)(2,1)S(1)} %get-tuple-element.28), kind=kLoop, calls=%fused_computation.2 | loop fusion | bytes 786432 | tf_op jit(solution)/shard_map/concatenate | solution.py:468
  27.5 0.0 copy-start.2
  27.5 0.5 collective-permute-start.4
  28.0 0.0 copy-done.10
  28.0 0.6 pad_add_fusion.table
  28.6 1.5 %find_slots.1.slots = s32[16]{0:T(128)} custom-call(s32[17]{0:T(128)} %pad_add_fusion.table, s32[32]{0:T(128)} %home.1, s32[16,16]{1,0:T(8,128)} %blocks.1, s32[16]{0:T(128)} %lens.1), custom_call_target="tpu_custom_call" | custom-call | tf_op jit(solution)/shard_map/find_slots/pallas_call | solution.py:94
  30.2 0.0 copy-done.9
  30.2 0.6 pad_add_fusion.1.table
  30.8 0.0 copy-done.2
  30.8 1.4 %copy-done.7 = bf16[2,2,64,3072]{3,2,1,0:T(8,128)(2,1)S(1)} copy-done((bf16[2,2,64,3072]{3,2,1,0:T(8,128)(2,1)S(1)}, bf16[2,2,64,3072]{3,2,1,0:T(8,128)(2,1)}, u32[]{:S(2)}) %copy-start.7) | copy-done | bytes 1572888
  32.2 1.0 %copy-done.8 = bf16[2,2,64,1024]{3,2,1,0:T(8,128)(2,1)S(1)} copy-done((bf16[2,2,64,1024]{3,2,1,0:T(8,128)(2,1)S(1)}, bf16[2,2,64,1024]{3,2,1,0:T(8,128)(2,1)}, u32[]{:S(2)}) %copy-start.8) | copy-done | bytes 524312
  33.2 3.7 %attend_own.1 = (bf16[4,1536,256]{2,1,0:T(8,128)(2,1)S(1)}, f32[4,1536,128]{2,1,0:T(8,128)S(1)}) custom-call(bf16[256,3072]{1,0:T(8,128)(2,1)S(1)} %bitcast.17, bf16[256,1024]{1,0:T(8,128)(2,1)S(1)} %bitcast.18), custom_call_target="tpu_custom_call" | custom-call | flops 2415919104 | bytes 7864320 | tf_op jit(solution)/shard_map/attend_own/pallas_call | solution.py:67
  36.9 0.0 copy-start
  36.9 1.6 %copy-done = f32[4,1536,128]{2,1,0:T(8,128)} copy-done((f32[4,1536,128]{2,1,0:T(8,128)}, f32[4,1536,128]{2,1,0:T(8,128)S(1)}, u32[]{:S(2)}) %copy-start) | copy-done | bytes 3145752
  38.5 0.0 collective-permute-done.9
  38.5 1.8 %constant_dynamic-update-slice_fusion.16.gathered = bf16[16,208,128]{2,1,0:T(8,128)(2,1)} fusion(bf16[16,208,128]{2,1,0:T(8,128)(2,1)} %get-tuple-element.20, bf16[8,208,128]{2,1,0:T(8,128)(2,1)} %collective-permute-done.9), kind=kLoop, calls=%fused_computation.18 | loop fusion | bytes 851968 | tf_op jit(solution)/shard_map/concatenate | solution.py:474
  40.3 2.6 %unpack.1 = (bf16[3072,64]{1,0:T(8,128)(2,1)}, bf16[432,512]{1,0:T(8,128)(2,1)}) custom-call(s32[17]{0:T(128)} %pad_add_fusion.1.table, bf16[16,208,128]{2,1,0:T(8,128)(2,1)} %constant_dynamic-update-slice_fusion.16.gathered), custom_call_target="tpu_custom_call" | custom-call | tf_op jit(solution)/shard_map/unpack/pallas_call | solution.py:262
  42.9 0.0 collective-permute-done.4
  42.9 1.9 %constant_dynamic-update-slice_fusion.5.past = bf16[32,16,1024]{2,1,0:T(8,128)(2,1)} fusion(bf16[32,16,1024]{2,1,0:T(8,128)(2,1)} %copy-done.2, bf16[16,16,1024]{2,1,0:T(8,128)(2,1)} %collective-permute-done.4), kind=kLoop, calls=%fused_computation.7 | loop fusion | bytes 1048576 | tf_op jit(solution)/shard_map/concatenate | solution.py:469
  44.8 0.0 copy-done.6
  44.8 1.9 %copy-done.1 = f32[4,1536,128]{2,1,0:T(8,128)S(1)} copy-done((f32[4,1536,128]{2,1,0:T(8,128)S(1)}, f32[4,1536,128]{2,1,0:T(8,128)}, u32[]{:S(2)}) %copy-start.1) | copy-done | bytes 3145752
  46.7 1.2 %copy-done.3 = bf16[32,16,1024]{2,1,0:T(8,128)(2,1)S(1)} copy-done((bf16[32,16,1024]{2,1,0:T(8,128)(2,1)S(1)}, bf16[32,16,1024]{2,1,0:T(8,128)(2,1)}, u32[]{:S(2)}) %copy-start.3) | copy-done | bytes 1048600
  47.9 1.1 %copy-done.4 = bf16[3072,64]{1,0:T(8,128)(2,1)S(1)} copy-done((bf16[3072,64]{1,0:T(8,128)(2,1)S(1)}, bf16[3072,64]{1,0:T(8,128)(2,1)}, u32[]{:S(2)}) %copy-start.4) | copy-done | bytes 393240
  49.0 3.0 %attend_past.1 = bf16[256,64]{1,0:T(8,128)(2,1)S(1)} custom-call(s32[16]{0:T(128)S(1)} %copy-done.6, bf16[4,1536,256]{2,1,0:T(8,128)(2,1)S(1)} %get-tuple-element.11.packed, bf16[32,16,1024]{2,1,0:T(8,128)(2,1)S(1)} %copy-done.3, f32[4,1536,128]{2,1,0:T(8,128)S(1)} %copy-done.1, bf16[3072,64]{1,0:T(8,128)(2,1)S(1)} %copy-done.4), custom_call_target="tpu_custom_call" | custom-call | flops 1610612736 | bytes 6291456 | tf_op jit(solution)/shard_map/attend_past/pallas_call | solution.py:188
  52.1 3.3 %collective-permute-start.11 = (bf16[2,64,64]{2,1,0:T(8,128)(2,1)S(1)}, bf16[2,64,64]{2,1,0:T(8,128)(2,1)S(1)}, u32[]{:S(2)}, u32[]{:S(2)}) collective-permute-start(bf16[2,64,64]{2,1,0:T(8,128)(2,1)S(1)} %get-tuple-element.25), channel_id=1, source_target_pairs={{1,0},{2,1},{3,2},{4,3},{5,4},{6,5},{7,6},{8,7},{9,8},{10,9},{11,1... | collective-permute-start | bytes 49160 | tf_op jit(solution)/shard_map/ppermute | solution.py:494
  55.3 1.9 %collective-permute-start.10 = (bf16[2,64,64]{2,1,0:T(8,128)(2,1)S(1)}, bf16[2,64,64]{2,1,0:T(8,128)(2,1)S(1)}, u32[]{:S(2)}, u32[]{:S(2)}) collective-permute-start(bf16[2,64,64]{2,1,0:T(8,128)(2,1)S(1)} %get-tuple-element.26), channel_id=1, source_target_pairs={{0,1},{1,2},{2,3},{3,4},{4,5},{5,6},{6,7},{7,8},{8,9},{9,10},{10,1... | collective-permute-start | bytes 49160 | tf_op jit(solution)/shard_map/ppermute | solution.py:493
  57.3 0.0 copy-done.5
  57.3 1.5 %convolve_inner.1 = (bf16[2,4,128,512]{3,2,1,0:T(8,128)(2,1)}, f32[2,256,512]{2,1,0:T(8,128)S(1)}) custom-call(bf16[2,2,64,64]{3,2,1,0:T(8,128)(2,1)S(1)} %bitcast.16, bf16[432,512]{1,0:T(8,128)(2,1)S(1)} %copy-done.5), custom_call_target="tpu_custom_call" | custom-call | flops 452984832 | bytes 1048576 | tf_op jit(solution)/shard_map/convolve_inner/pallas_call | solution.py:343
  58.7 0.0 collective-permute-done.11.below
  58.8 2.7 %collective-permute-done.10.above = bf16[2,64,64]{2,1,0:T(8,128)(2,1)S(1)} collective-permute-done((bf16[2,64,64]{2,1,0:T(8,128)(2,1)S(1)}, bf16[2,64,64]{2,1,0:T(8,128)(2,1)S(1)}, u32[]{:S(2)}, u32[]{:S(2)}) %collective-permute-start.10) | collective-permute-done | bytes 16416 | tf_op jit(solution)/shard_map/ppermute | solution.py:493
  61.5 1.3 %convolve_outer.1 = bf16[2,4,128,512]{3,2,1,0:T(8,128)(2,1)} custom-call(bf16[2,64,64]{2,1,0:T(8,128)(2,1)S(1)} %collective-permute-done.10.above, bf16[2,64,64]{2,1,0:T(8,128)(2,1)S(1)} %collective-permute-done.11.below, bf16[432,512]{1,0:T(8,128)(2,1)S(1)} %copy-done.5, ...), custom_call_target="tpu_custom_call", output_to_operand_aliasing={{}: (4, {})} | custom-call | tf_op jit(solution)/shard_map/convolve_outer/pallas_call | solution.py:419
  (8 shorter events, 0.0 us)
Async XLA Ops:
  0.0 28.0 %copy-start.10 = (s32[16]{0:T(128)S(1)}, s32[16]{0:T(128)}, u32[]{:S(2)}) copy-start(s32[16]{0:T(128)} %constant.9.clone) | copy-start | bytes 196
  0.0 30.2 %copy-start.9 = (s32[16]{0:T(128)S(1)}, s32[16]{0:T(128)}, u32[]{:S(2)}) copy-start(s32[16]{0:T(128)} %constant.8.clone) | copy-start | bytes 196
  0.0 17.9 %collective-permute-start.2 = (bf16[2,16,1024]{2,1,0:T(8,128)(2,1)}, bf16[2,16,1024]{2,1,0:T(8,128)(2,1)S(1)}, u32[]{:S(2)}, u32[]{:S(2)}) collective-permute-start(bf16[2,16,1024]{2,1,0:T(8,128)(2,1)} %param.12), channel_id=1, source_target_pairs={{0,12},{1,13},{2,14},{3,15},{4,8},{5,9},{6,10},{7,11},{8,4},{9,5},... | collective-permute-start | bytes 196616 | tf_op jit(solution)/shard_map/ppermute | solution.py:437
  1.6 17.5 %collective-permute-start.1 = (bf16[2,16,1024]{2,1,0:T(8,128)(2,1)}, bf16[2,16,1024]{2,1,0:T(8,128)(2,1)S(1)}, u32[]{:S(2)}, u32[]{:S(2)}) collective-permute-start(bf16[2,16,1024]{2,1,0:T(8,128)(2,1)} %param.12), channel_id=1, source_target_pairs={{0,8},{1,9},{2,10},{3,11},{4,12},{5,13},{6,14},{7,15},{8,0},{9,1},... | collective-permute-start | bytes 196616 | tf_op jit(solution)/shard_map/ppermute | solution.py:437
  2.8 16.3 %collective-permute-start = (bf16[2,16,1024]{2,1,0:T(8,128)(2,1)}, bf16[2,16,1024]{2,1,0:T(8,128)(2,1)S(1)}, u32[]{:S(2)}, u32[]{:S(2)}) collective-permute-start(bf16[2,16,1024]{2,1,0:T(8,128)(2,1)} %param.12), channel_id=1, source_target_pairs={{0,4},{1,5},{2,6},{3,7},{4,0},{5,1},{6,2},{7,3},{8,12},{9,13},{10,... | collective-permute-start | bytes 196616 | tf_op jit(solution)/shard_map/ppermute | solution.py:437
  8.7 4.5 %collective-permute-start.5 = (bf16[1,208,128]{2,1,0:T(8,128)(2,1)}, bf16[1,208,128]{2,1,0:T(8,128)(2,1)S(1)}, u32[]{:S(2)}, u32[]{:S(2)}) collective-permute-start(bf16[1,208,128]{2,1,0:T(8,128)(2,1)} %bitcast.19), channel_id=1, source_target_pairs={{0,2},{1,3},{2,0},{3,1},{4,6},{5,7},{6,4},{7,5},{8,10},{9,11},{10,... | collective-permute-start | bytes 159752 | tf_op jit(solution)/shard_map/ppermute | solution.py:437
  14.0 12.1 %collective-permute-start.8 = (bf16[2,208,128]{2,1,0:T(8,128)(2,1)S(1)}, bf16[2,208,128]{2,1,0:T(8,128)(2,1)S(1)}, u32[]{:S(2)}, u32[]{:S(2)}) collective-permute-start(bf16[2,208,128]{2,1,0:T(8,128)(2,1)S(1)} %pad_maximum_fusion.1), channel_id=1, source_target_pairs={{0,12},{1,13},{2,14},{3,15},{4,8},{5,9},{6,10},{7,11},{8,4},{9,5},... | collective-permute-start | bytes 319496 | tf_op jit(solution)/shard_map/ppermute | solution.py:437
  15.5 9.8 %collective-permute-start.7 = (bf16[2,208,128]{2,1,0:T(8,128)(2,1)S(1)}, bf16[2,208,128]{2,1,0:T(8,128)(2,1)S(1)}, u32[]{:S(2)}, u32[]{:S(2)}) collective-permute-start(bf16[2,208,128]{2,1,0:T(8,128)(2,1)S(1)} %pad_maximum_fusion.1), channel_id=1, source_target_pairs={{0,8},{1,9},{2,10},{3,11},{4,12},{5,13},{6,14},{7,15},{8,0},{9,1},... | collective-permute-start | bytes 319496 | tf_op jit(solution)/shard_map/ppermute | solution.py:437
  17.9 6.8 %collective-permute-start.6 = (bf16[2,208,128]{2,1,0:T(8,128)(2,1)S(1)}, bf16[2,208,128]{2,1,0:T(8,128)(2,1)S(1)}, u32[]{:S(2)}, u32[]{:S(2)}) collective-permute-start(bf16[2,208,128]{2,1,0:T(8,128)(2,1)S(1)} %pad_maximum_fusion.1), channel_id=1, source_target_pairs={{0,4},{1,5},{2,6},{3,7},{4,0},{5,1},{6,2},{7,3},{8,12},{9,13},{10,... | collective-permute-start | bytes 319496 | tf_op jit(solution)/shard_map/ppermute | solution.py:437
  20.0 6.8 %collective-permute-start.3 = (bf16[8,16,1024]{2,1,0:T(8,128)(2,1)S(1)}, bf16[8,16,1024]{2,1,0:T(8,128)(2,1)S(1)}, u32[]{:S(2)}, u32[]{:S(2)}) collective-permute-start(bf16[8,16,1024]{2,1,0:T(8,128)(2,1)S(1)} %pad_maximum_fusion), channel_id=1, source_target_pairs={{0,2},{1,3},{2,0},{3,1},{4,6},{5,7},{6,4},{7,5},{8,10},{9,11},{10,... | collective-permute-start | bytes 786440 | tf_op jit(solution)/shard_map/ppermute | solution.py:437
  26.8 11.8 %collective-permute-start.9 = (bf16[8,208,128]{2,1,0:T(8,128)(2,1)}, bf16[8,208,128]{2,1,0:T(8,128)(2,1)}, u32[]{:S(2)}, u32[]{:S(2)}) collective-permute-start(bf16[8,208,128]{2,1,0:T(8,128)(2,1)} %get-tuple-element.19), channel_id=1, source_target_pairs={{0,1},{1,0},{2,3},{3,2},{4,5},{5,4},{6,7},{7,6},{8,9},{9,8},{10,11... | collective-permute-start | bytes 1277960 | tf_op jit(solution)/shard_map/ppermute | solution.py:437
  27.5 3.2 %copy-start.2 = (bf16[32,16,1024]{2,1,0:T(8,128)(2,1)}, bf16[32,16,1024]{2,1,0:T(8,128)(2,1)S(1)}, u32[]{:S(2)}) copy-start(bf16[32,16,1024]{2,1,0:T(8,128)(2,1)S(1)} %get-tuple-element.18) | copy-start | bytes 3145732
  27.5 15.4 %collective-permute-start.4 = (bf16[16,16,1024]{2,1,0:T(8,128)(2,1)}, bf16[16,16,1024]{2,1,0:T(8,128)(2,1)}, u32[]{:S(2)}, u32[]{:S(2)}) collective-permute-start(bf16[16,16,1024]{2,1,0:T(8,128)(2,1)} %get-tuple-element.17), channel_id=1, source_target_pairs={{0,1},{1,0},{2,3},{3,2},{4,5},{5,4},{6,7},{7,6},{8,9},{9,8},{10,11... | collective-permute-start | bytes 1572872 | tf_op jit(solution)/shard_map/ppermute | solution.py:437
  30.8 1.4 %copy-start.7 = (bf16[2,2,64,3072]{3,2,1,0:T(8,128)(2,1)S(1)}, bf16[2,2,64,3072]{3,2,1,0:T(8,128)(2,1)}, u32[]{:S(2)}) copy-start(bf16[2,2,64,3072]{3,2,1,0:T(8,128)(2,1)} %param.10) | copy-start | bytes 4718596
  32.2 1.0 %copy-start.8 = (bf16[2,2,64,1024]{3,2,1,0:T(8,128)(2,1)S(1)}, bf16[2,2,64,1024]{3,2,1,0:T(8,128)(2,1)}, u32[]{:S(2)}) copy-start(bf16[2,2,64,1024]{3,2,1,0:T(8,128)(2,1)} %param.11) | copy-start | bytes 1572868
  33.2 11.6 %copy-start.6 = (s32[16]{0:T(128)S(1)}, s32[16]{0:T(128)}, u32[]{:S(2)}) copy-start(s32[16]{0:T(128)} %find_slots.1.slots) | copy-start | bytes 196
  36.9 1.6 %copy-start = (f32[4,1536,128]{2,1,0:T(8,128)}, f32[4,1536,128]{2,1,0:T(8,128)S(1)}, u32[]{:S(2)}) copy-start(f32[4,1536,128]{2,1,0:T(8,128)S(1)} %get-tuple-element.12.sums) | copy-start | bytes 9437188
  44.8 1.9 %copy-start.1 = (f32[4,1536,128]{2,1,0:T(8,128)S(1)}, f32[4,1536,128]{2,1,0:T(8,128)}, u32[]{:S(2)}) copy-start(f32[4,1536,128]{2,1,0:T(8,128)} %copy-done) | copy-start | bytes 9437188
  46.7 1.2 %copy-start.3 = (bf16[32,16,1024]{2,1,0:T(8,128)(2,1)S(1)}, bf16[32,16,1024]{2,1,0:T(8,128)(2,1)}, u32[]{:S(2)}) copy-start(bf16[32,16,1024]{2,1,0:T(8,128)(2,1)} %constant_dynamic-update-slice_fusion.5.past) | copy-start | bytes 3145732
  47.9 1.1 %copy-start.4 = (bf16[3072,64]{1,0:T(8,128)(2,1)S(1)}, bf16[3072,64]{1,0:T(8,128)(2,1)}, u32[]{:S(2)}) copy-start(bf16[3072,64]{1,0:T(8,128)(2,1)} %get-tuple-element.13.weight) | copy-start | bytes 1179652
  49.0 8.3 %copy-start.5 = (bf16[432,512]{1,0:T(8,128)(2,1)S(1)}, bf16[432,512]{1,0:T(8,128)(2,1)}, u32[]{:S(2)}) copy-start(bf16[432,512]{1,0:T(8,128)(2,1)} %get-tuple-element.14.kernel) | copy-start | bytes 1327108
  52.1 6.7 %collective-permute-start.11 = (bf16[2,64,64]{2,1,0:T(8,128)(2,1)S(1)}, bf16[2,64,64]{2,1,0:T(8,128)(2,1)S(1)}, u32[]{:S(2)}, u32[]{:S(2)}) collective-permute-start(bf16[2,64,64]{2,1,0:T(8,128)(2,1)S(1)} %get-tuple-element.25), channel_id=1, source_target_pairs={{1,0},{2,1},{3,2},{4,3},{5,4},{6,5},{7,6},{8,7},{9,8},{10,9},{11,1... | collective-permute-start | bytes 49160 | tf_op jit(solution)/shard_map/ppermute | solution.py:494
  55.3 6.1 %collective-permute-start.10 = (bf16[2,64,64]{2,1,0:T(8,128)(2,1)S(1)}, bf16[2,64,64]{2,1,0:T(8,128)(2,1)S(1)}, u32[]{:S(2)}, u32[]{:S(2)}) collective-permute-start(bf16[2,64,64]{2,1,0:T(8,128)(2,1)S(1)} %get-tuple-element.26), channel_id=1, source_target_pairs={{0,1},{1,2},{2,3},{3,4},{4,5},{5,6},{6,7},{7,8},{8,9},{9,10},{10,1... | collective-permute-start | bytes 49160 | tf_op jit(solution)/shard_map/ppermute | solution.py:493

commit v3 on v2

--- a/solution.py
+++ b/solution.py
@@ -29,8 +29,22 @@
     return pltpu.CompilerParams(vmem_limit_bytes=mib * MIB)
 
 
-def own_body(queries, own, packed, sums):
+def place_of(offset, turns):
+    return sum(((offset >> bit) & 1) << to for bit, to in turns)
+
+
+def own_body(turns, blocks_here, tile_ref, home, blocks, lens, queries, own, packed, sums, slots):
     tokens = queries.shape[0]
+    tile = tile_ref[0]
+    for place in range(slots.shape[0]):
+        slots[place] = -1
+
+    def find(entry, carry):
+        stored = home[blocks[tile, entry]]
+        slots[place_of((stored // blocks_here) ^ tile, turns)] = stored % blocks_here
+        return carry
+
+    lax.fori_loop(0, lens[tile], find, 0)
 
     def one(g, carry):
         def columns(index):
@@ -61,59 +75,43 @@
     lax.fori_loop(0, KV_HEADS, one, 0)
 
 
-def attend_own(query_rows, own_rows):
+def attend_own(tile, block_home, block_list, list_len, query_rows, own_rows, turns, blocks_here):
     tokens, width = query_rows.shape
     rows = GROUP * tokens
     return pl.pallas_call(
-        own_body,
-        in_specs=[WHOLE, WHOLE],
-        out_specs=[WHOLE, WHOLE],
+        functools.partial(own_body, turns, blocks_here),
+        in_specs=[SCALARS] * 4 + [WHOLE, WHOLE],
+        out_specs=[WHOLE, WHOLE, SCALARS],
         out_shape=[
             jax.ShapeDtypeStruct((KV_HEADS, rows, 2 * HEAD_DIM), BF16),
             jax.ShapeDtypeStruct((KV_HEADS, rows, HEAD_DIM), F32),
+            jax.ShapeDtypeStruct((1 << len(turns),), jnp.int32),
         ],
         compiler_params=params(24),
         cost_estimate=pl.CostEstimate(
             flops=12 * tokens * tokens * width, bytes_accessed=10 * tokens * width, transcendentals=0
         ),
         name="attend_own",
-    )(query_rows, own_rows)
-
-
-def slots_body(blocks_here, table, home, blocks, lens, slots):
-    tile = table[0]
-    count = lens[tile]
-    for entry in range(slots.shape[0]):
-        listed = entry < count
-        stored = home[blocks[tile, jnp.where(listed, entry, 0)]]
-        place = table[1 + ((stored // blocks_here) ^ tile)]
-        slots[entry] = jnp.where(listed, place * blocks_here + stored % blocks_here, -1)
-
-
-def find_slots(table, block_home, block_list, list_len, blocks_here):
-    return pl.pallas_call(
-        functools.partial(slots_body, blocks_here),
-        in_specs=[SCALARS] * 4,
-        out_specs=SCALARS,
-        out_shape=jax.ShapeDtypeStruct((block_list.shape[1],), jnp.int32),
-        name="find_slots",
-    )(table, block_home, block_list, list_len)
-
-
-def past_body(slots, packed, past, sums, weight, out, keys, values, worst):
-    entries = slots.shape[0]
-    block_tokens = past.shape[1]
-    tokens, columns = out.shape
+    )(tile, block_home, block_list, list_len, query_rows, own_rows)
+
+
+def past_body(sizes, slots, packed, sums, *refs):
+    gathered, (out, keys, values, worst) = refs[: len(sizes)], refs[len(sizes) :]
+    blocks_here = sum(ref.shape[0] for ref in gathered) // sum(sizes)
+    block_tokens = gathered[0].shape[1]
+    tokens = out.shape[0]
     lane = lax.broadcasted_iota(jnp.int32, (block_tokens, HEAD_DIM), 1)
     minus = jnp.where(lane < 3, -1.0, 0.0)
     zero = jnp.zeros((block_tokens, HEAD_DIM), BF16)
-    for entry in range(entries):
-        listed = slots[entry] >= 0
-        block = past[jnp.where(listed, slots[entry], slots[0])]
+    homes = [(ref, k) for ref, size in zip(gathered, sizes) for k in range(size)]
+    for place, (ref, k) in enumerate(homes):
+        slot = slots[place]
+        listed = slot >= 0
+        block = ref[k * blocks_here + jnp.maximum(slot, 0)]
         live = jnp.where(listed, 1.0, 0.0)
         level = (minus * live).astype(BF16)
         counted = jnp.full((block_tokens, HEAD_DIM), live, F32).astype(BF16)
-        rows = slice(entry * block_tokens, (entry + 1) * block_tokens)
+        rows = slice(place * block_tokens, (place + 1) * block_tokens)
         for g in range(KV_HEADS):
             keys[g, rows, :HEAD_DIM] = jnp.where(listed, block[:, head_columns(g)], zero)
             keys[g, rows, HEAD_DIM:] = level
@@ -132,64 +130,57 @@
 
     def place(step):
         if heads == GROUP:
-            return step, slice(None), slice(step * GROUP * HEAD_DIM, (step + 1) * GROUP * HEAD_DIM)
-        rows = pl.ds(pl.multiple_of((step % GROUP) * tokens, tokens), tokens)
-        return step // GROUP, rows, pl.ds(pl.multiple_of(step * HEAD_DIM, HEAD_DIM), HEAD_DIM)
+            return step, slice(None)
+        return step // GROUP, pl.ds(pl.multiple_of((step % GROUP) * tokens, tokens), tokens)
 
     def scores(g, rows):
         return SCALE * lax.dot_general(
             packed[g, rows], keys[g], (((1,), (1,)), ((), ())), preferred_element_type=F32
         )
 
-    def projected(attended, weight_rows):
-        panel = weight[weight_rows]
-        part = jnp.zeros((tokens, columns), F32)
+    def emit(step, attended):
+        attended = attended.astype(BF16)
         for h in range(heads):
-            part += jnp.dot(
-                attended[h * tokens : (h + 1) * tokens], panel[head_columns(h)], preferred_element_type=F32
-            )
-        return part
-
-    def quick(step, carry):
-        total, largest = carry
-        g, rows, weight_rows = place(step)
+            columns = (step * heads + h) * HEAD_DIM
+            if heads == 1:
+                columns = pl.multiple_of(columns, HEAD_DIM)
+            out[:, pl.ds(columns, HEAD_DIM)] = attended[h * tokens : (h + 1) * tokens]
+
+    def quick(step, largest):
+        g, rows = place(step)
         weights = jnp.exp2(scores(g, rows)).astype(BF16)
         mixed = jnp.dot(weights, values[g], preferred_element_type=F32)
         below = mixed[:, HEAD_DIM:] + 1.0
-        largest = jnp.maximum(largest, jnp.max(below.reshape((-1,) + largest.shape), axis=0))
-        attended = ((mixed[:, :HEAD_DIM] + sums[g, rows]) / below).astype(BF16)
-        return total + projected(attended, weight_rows), largest
-
-    nothing = jnp.zeros((tokens, columns), F32)
-    total, largest = over_steps(quick, (nothing, jnp.zeros(worst.shape, F32)))
-    out[...] = total.astype(BF16)
-    worst[...] = largest
+        emit(step, (mixed[:, :HEAD_DIM] + sums[g, rows]) / below)
+        return jnp.maximum(largest, jnp.max(below.reshape((-1,) + largest.shape), axis=0))
+
+    worst[...] = over_steps(quick, jnp.zeros(worst.shape, F32))
 
     @pl.when(jnp.logical_not(jnp.max(worst[...]) < SAFE))
     def _():
-        def careful(step, total):
-            g, rows, weight_rows = place(step)
+        def careful(step, carry):
+            g, rows = place(step)
             score = scores(g, rows)
             top = jnp.maximum(jnp.max(score, axis=1, keepdims=True), 0.0)
             weights = jnp.exp2(score - top).astype(BF16)
             mixed = jnp.dot(weights, values[g], preferred_element_type=F32)
             share = jnp.exp2(-top)
-            attended = (mixed[:, :HEAD_DIM] + share * sums[g, rows]) / (mixed[:, HEAD_DIM:] + share)
-            return total + projected(attended.astype(BF16), weight_rows)
-
-        out[...] = over_steps(careful, nothing).astype(BF16)
-
-
-def attend_past(slots, packed, past, sums, weight):
+            emit(step, (mixed[:, :HEAD_DIM] + share * sums[g, rows]) / (mixed[:, HEAD_DIM:] + share))
+            return carry
+
+        over_steps(careful, 0)
+
+
+def attend_past(slots, packed, sums, gathered, blocks_here):
     heads, rows, _ = packed.shape
     tokens = rows // GROUP
-    keys = slots.shape[0] * past.shape[1]
-    columns = weight.shape[1]
-    return pl.pallas_call(
-        past_body,
-        in_specs=[SCALARS, WHOLE, WHOLE, WHOLE, WHOLE],
+    sizes = [array.shape[0] // blocks_here for array in gathered]
+    keys = sum(sizes) * gathered[0].shape[1]
+    return pl.pallas_call(
+        functools.partial(past_body, sizes),
+        in_specs=[SCALARS] + [WHOLE] * (2 + len(gathered)),
         out_specs=WHOLE,
-        out_shape=jax.ShapeDtypeStruct((tokens, columns), BF16),
+        out_shape=jax.ShapeDtypeStruct((tokens, HEADS * HEAD_DIM), BF16),
         scratch_shapes=[
             pltpu.VMEM((heads, keys, 2 * HEAD_DIM), BF16),
             pltpu.VMEM((heads, keys, 2 * HEAD_DIM), BF16),
@@ -200,72 +191,107 @@
             flops=8 * heads * rows * keys * HEAD_DIM, bytes_accessed=heads * rows * 1024, transcendentals=0
         ),
         name="attend_past",
-    )(slots, packed, past, sums, weight)
+    )(slots, packed, sums, *gathered)
+
+
+def join_body(*refs):
+    *parts, out = refs
+    row = 0
+    for part in parts:
+        out[row : row + part.shape[0]] = part[...]
+        row += part.shape[0]
+
+
+def join(parts, name):
+    rows = sum(part.shape[0] for part in parts)
+    return pl.pallas_call(
+        join_body,
+        in_specs=[WHOLE] * len(parts),
+        out_specs=WHOLE,
+        out_shape=jax.ShapeDtypeStruct((rows,) + parts[0].shape[1:], BF16),
+        name=name,
+    )(*parts)
 
 
 def pack_body(final, decode, out):
-    half = final.shape[0] // 2
-    taps, width = decode.shape
-    share = 128 // width
-    tall = out.shape[0] - half
-    out[:half] = jnp.concatenate([final[:half], final[half:]], axis=1)
-    parts = []
-    for part in range(share):
-        rows = decode[part * tall : min((part + 1) * tall, taps)]
-        missing = tall - rows.shape[0]
-        if missing:
-            rows = jnp.concatenate([rows, jnp.zeros((missing, width), BF16)], axis=0)
-        parts.append(rows)
-    out[half:] = jnp.concatenate(parts, axis=1)
-
-
-def packed_rows(final, decode, lat):
-    share = 128 // decode.shape[1]
-    per_part = -(-(decode.shape[0] // lat) // share) * lat
-    return final.shape[0] // 2 + per_part
-
-
-def pack(final, decode, lat):
+    half, depth = final.shape[0] // 2, final.shape[1]
+    taps = decode.shape[1]
+    blank = out.shape[2] - 2 * depth - taps
+    out[0] = jnp.concatenate(
+        [final[:half], final[half:], decode[...], jnp.zeros((half, blank), BF16)], axis=1
+    )
+
+
+def pack(final, decode):
+    lanes = -(-(2 * final.shape[1] + decode.shape[1]) // 128) * 128
     return pl.pallas_call(
         pack_body,
         in_specs=[WHOLE, WHOLE],
         out_specs=WHOLE,
-        out_shape=jax.ShapeDtypeStruct((packed_rows(final, decode, lat), 128), BF16),
+        out_shape=jax.ShapeDtypeStruct((1, decode.shape[0], lanes), BF16),
         name="pack",
     )(final, decode)
 
 
-def unpack_body(table, gathered, final, decode):
-    count = gathered.shape[0]
-    depth = final.shape[0] // count
-    half = depth // 2
-    width = decode.shape[1] // count
-    share = 128 // width
-    tall = gathered.shape[1] - half
-    tile = table[0]
-    for device in range(count):
-        block = gathered[table[1 + (device ^ tile)], :half]
-        final[device * depth : device * depth + half] = block[:, : final.shape[1]]
-        final[device * depth + half : (device + 1) * depth] = block[:, final.shape[1] :]
-    for column in range(count // share):
-        blocks = [
-            gathered[table[1 + ((column * share + k) ^ tile)], half:] for k in range(share)
-        ]
-        for part in range(share):
-            rows = min((part + 1) * tall, decode.shape[0]) - part * tall
-            decode[part * tall : part * tall + rows, column * 128 : (column + 1) * 128] = jnp.concatenate(
-                [b[:rows, part * width : (part + 1) * width] for b in blocks], axis=1
-            )
-
-
-def unpack(table, gathered, final_shape, decode_shape):
-    return pl.pallas_call(
-        unpack_body,
-        in_specs=[SCALARS, WHOLE],
-        out_specs=[WHOLE, WHOLE],
-        out_shape=[jax.ShapeDtypeStruct(final_shape, BF16), jax.ShapeDtypeStruct(decode_shape, BF16)],
+def project_body(depth, order, tile_ref, attended, *refs):
+    *panels, out, staged, whole = refs
+    place = 0
+    half = staged.shape[1]
+    for panel in panels:
+        for k in range(panel.shape[0]):
+            staged[tile_ref[0] ^ order[place]] = panel[k, :, : staged.shape[2]]
+            place += 1
+    for device in range(len(order)):
+        for part in range(2):
+            whole[part * half : (part + 1) * half, device * depth : (device + 1) * depth] = staged[
+                device, :, part * depth : (part + 1) * depth
+            ]
+    out[...] = lax.dot_general(
+        attended[...], whole[...], (((1,), (1,)), ((), ())), preferred_element_type=F32
+    ).astype(BF16)
+
+
+def project(tile, attended, panels, order, depth, columns):
+    tokens, width = attended.shape
+    lanes = -(-2 * depth // 128) * 128
+    return pl.pallas_call(
+        functools.partial(project_body, depth, order),
+        in_specs=[SCALARS] + [WHOLE] * (1 + len(panels)),
+        out_specs=WHOLE,
+        out_shape=jax.ShapeDtypeStruct((tokens, columns), BF16),
+        scratch_shapes=[
+            pltpu.VMEM((len(order), columns // 2, lanes), BF16),
+            pltpu.VMEM((columns, width), BF16),
+        ],
+        compiler_params=params(16),
+        name="project",
+    )(tile, attended, *panels)
+
+
+def unpack_body(depth, order, tile_ref, *refs):
+    *panels, out, staged = refs
+    place = 0
+    width = staged.shape[1]
+    taps = out.shape[0]
+    for panel in panels:
+        for k in range(panel.shape[0]):
+            staged[tile_ref[0] ^ order[place]] = panel[k]
+            place += 1
+    whole = jnp.concatenate([staged[d, :, 2 * depth : 2 * depth + taps] for d in range(len(order))], axis=0)
+    out[...] = whole.T
+
+
+def unpack(tile, panels, order, depth, taps):
+    width, lanes = panels[0].shape[1:]
+    return pl.pallas_call(
+        functools.partial(unpack_body, depth, order),
+        in_specs=[SCALARS] + [WHOLE] * len(panels),
+        out_specs=WHOLE,
+        out_shape=jax.ShapeDtypeStruct((taps, width * len(order)), BF16),
+        scratch_shapes=[pltpu.VMEM((len(order), width, lanes), BF16)],
+        compiler_params=params(16),
         name="unpack",
-    )(table, gathered)
+    )(tile, *panels)
 
 
 def tap_rows(frames, cells, width):
@@ -437,59 +463,49 @@
     return lax.ppermute(value, "seq", [(i, i ^ offset) for i in range(count)])
 
 
-def places(order):
-    return [order.index(k) for k in range(len(order))]
-
-
-def gather_by_doubling(shard, bits):
-    held, order = shard, [0]
-    for bit in bits:
-        held = jnp.concatenate([held, exchange(held, bit)], axis=0)
-        order = order + [o ^ bit for o in order]
-    return held, order
-
-
 def local(queries, own_kv, past_kv, block_home, block_list, list_len, final_weight, decoder_weight):
     frames, patch_rows, patches, width = queries.shape
     tokens = frames * patch_rows * patches
     count = lax.axis_size("seq")
     assert count & (count - 1) == 0
+    bits = count.bit_length() - 1
     blocks_here = past_kv.shape[0]
-    lat = final_weight.shape[1] // 4
-    me = lax.axis_index("seq").astype(jnp.int32).reshape(1)
-    bits = [1 << k for k in reversed(range(count.bit_length() - 1))]
-    small = count == 16 and decoder_weight.shape[1] * 4 == 128 and final_weight.shape[0] % 32 == 0
-    if small:
+    depth, columns = final_weight.shape
+    taps, panel_width = decoder_weight.shape
+    tile = lax.axis_index("seq").astype(jnp.int32).reshape(1)
+    query_rows = queries.reshape(tokens, width)
+    own_rows = own_kv.reshape(tokens, own_kv.shape[3])
+    if count == 16 and panel_width == columns // 2:
         far = [4, 8, 12]
-        panels = pack(final_weight, decoder_weight, lat)[None]
-        arrived = [exchange(past_kv, k) for k in far]
-        panels = jnp.concatenate([panels, exchange(panels, 2)], axis=0)
-        past = jnp.concatenate([past_kv] + arrived, axis=0)
-        past = jnp.concatenate([past, exchange(past, 2)], axis=0)
-        past = jnp.concatenate([past, exchange(past, 1)], axis=0)
-        order = [0] + far
-        order = order + [o ^ 2 for o in order]
-        order = order + [o ^ 1 for o in order]
-        panels = jnp.concatenate([panels] + [exchange(panels, k) for k in far], axis=0)
-        panels = jnp.concatenate([panels, exchange(panels, 1)], axis=0)
-        panel_order = [k ^ x for k in [0] + far for x in (0, 2)]
-        panel_order = panel_order + [o ^ 1 for o in panel_order]
-        panel_table = jnp.concatenate([me, jnp.array(places(panel_order), jnp.int32)])
-        final, decode = unpack(
-            panel_table,
-            panels,
-            (final_weight.shape[0] * count, final_weight.shape[1]),
-            (decoder_weight.shape[0], decoder_weight.shape[1] * count),
-        )
+        turns = [(2, 0), (3, 1), (1, 2), (0, 3)]
+        steps = [exchange(past_kv, k) for k in far]
+        panel = pack(final_weight.T, decoder_weight.T)
+        pair = join([panel, exchange(panel, 2)], "join_panels")
+        packed, sums, slots = attend_own(
+            tile, block_home, block_list, list_len, query_rows, own_rows, turns, blocks_here
+        )
+        line = join([past_kv] + steps, "join_past")
+        across = exchange(line, 2)
+        gathered = [line, across, exchange(line, 1), exchange(across, 1)]
+        panels = [pair] + [exchange(pair, k) for k in far]
+        panels = panels + [exchange(p, 1) for p in panels]
+        order = [k ^ x ^ c for c in (0, 1) for k in [0] + far for x in (0, 2)]
+        attended = attend_past(slots, packed, sums, gathered, blocks_here)
+        predicted = project(tile, attended, panels, order, depth, columns)
+        decode = unpack(tile, panels, order, depth, taps)
     else:
-        past, order = gather_by_doubling(past_kv, bits)
+        turns = [(bit, bits - 1 - bit) for bit in range(bits)]
+        held = past_kv
+        for bit in reversed(range(bits)):
+            held = jnp.concatenate([held, exchange(held, 1 << bit)], axis=0)
+        packed, sums, slots = attend_own(
+            tile, block_home, block_list, list_len, query_rows, own_rows, turns, blocks_here
+        )
+        attended = attend_past(slots, packed, sums, [held], blocks_here)
         final = lax.all_gather(final_weight, "seq", axis=0, tiled=True)
         decode = lax.all_gather(decoder_weight, "seq", axis=1, tiled=True)
-    table = jnp.concatenate([me, jnp.array(places(order), jnp.int32)])
-    slots = find_slots(table, block_home, block_list, list_len, blocks_here)
-    packed, sums = attend_own(queries.reshape(tokens, width), own_kv.reshape(tokens, own_kv.shape[3]))
-    predicted = attend_past(slots, packed, past, sums, final)
-    predicted = predicted.reshape(frames, patch_rows, patches, predicted.shape[1])
+        predicted = jnp.dot(attended, final, preferred_element_type=F32).astype(BF16)
+    predicted = predicted.reshape(frames, patch_rows, patches, columns)
     above = lax.ppermute(predicted[:, -1], "seq", [(i, i + 1) for i in range(count - 1)])
     below = lax.ppermute(predicted[:, 0], "seq", [(i + 1, i) for i in range(count - 1)])
     features, edges = convolve_inner(predicted, decode)

time: 63.7 us -> 59 us (0.926)
  the two profiles are of different devices: /device:TPU:12 before, /device:TPU:1 now
where the time goes in v3:
time: 59 us; the launch traced here: 58 us
  starting transfers between devices  25.3 us (43%)
  Pallas kernels  15.8 us (27%)
  waiting for transfers between devices  11.1 us (19%)
  local copies, waits for them, and re-layouts  5.71 us (10%)
    ppermute x14, starting transfers between devices, exchange(): return lax.ppermute(value, 'seq', [(i, i ^ offset) for i in range(count)])  20.4 us
    ppermute x14, waiting for transfers between devices, exchange(): return lax.ppermute(value, 'seq', [(i, i ^ offset) for i in range(count)])  9.23 us
    unnamed x22, local copies, waits for them, and re-layouts  5.7 us
    pallas_call x1, Pallas kernels, attend_own(): pl.pallas_call(functools.partial(own_body, turns, blocks_here), in_specs=...  4.57 us
    pallas_call x2, Pallas kernels, join(): pl.pallas_call(join_body, in_specs=[WHOLE] * len(parts), out_specs=WHOLE,...  3.16 us
    ppermute x1, starting transfers between devices, local(): lax.ppermute(predicted[:, -1], 'seq', [(i, i + 1) for i in range(count -...  2.94 us
    pallas_call x1, Pallas kernels, attend_past(): pl.pallas_call(functools.partial(past_body, sizes), in_specs=[SCALARS] +...  2.88 us
    ppermute x1, starting transfers between devices, local(): lax.ppermute(predicted[:, 0], 'seq', [(i + 1, i) for i in range(count - 1)])  1.92 us
  transfers between devices with their start and end apart: 16, of which 4 were waited for; matrix products, arithmetic and copies ran while one was open for 0% of the time, Pallas kernels for 16%

profile of v3, /device:TPU:1, one launch (start us, length us, event | category | flops | bytes accessed | tf_op | source)
XLA Modules:
  0.0 58.0 jit_solution(9655324786265498764)
XLA Ops:
  0.0 2.1 %collective-permute-start = (bf16[2,16,1024]{2,1,0:T(8,128)(2,1)}, bf16[2,16,1024]{2,1,0:T(8,128)(2,1)S(1)}, u32[]{:S(2)}, u32[]{:S(2)}) collective-permute-start(bf16[2,16,1024]{2,1,0:T(8,128)(2,1)} %refs_0_.1), channel_id=1, source_target_pairs={{0,4},{1,5},{2,6},{3,7},{4,0},{5,1},{6,2},{7,3},{8,12},{9,13},{10,... | collective-permute-start | bytes 196616 | tf_op jit(solution)/shard_map/ppermute | solution.py:463
  2.1 2.3 %collective-permute-start.1 = (bf16[2,16,1024]{2,1,0:T(8,128)(2,1)}, bf16[2,16,1024]{2,1,0:T(8,128)(2,1)S(1)}, u32[]{:S(2)}, u32[]{:S(2)}) collective-permute-start(bf16[2,16,1024]{2,1,0:T(8,128)(2,1)} %refs_0_.1), channel_id=1, source_target_pairs={{0,8},{1,9},{2,10},{3,11},{4,12},{5,13},{6,14},{7,15},{8,0},{9,1},... | collective-permute-start | bytes 196616 | tf_op jit(solution)/shard_map/ppermute | solution.py:463
  4.4 0.0 collective-permute-start.2
  4.4 0.0 collective-permute-done.refs_1_
  4.4 0.0 copy-start.7
  4.4 2.6 %collective-permute-done.1.refs_2_ = bf16[2,16,1024]{2,1,0:T(8,128)(2,1)S(1)} collective-permute-done((bf16[2,16,1024]{2,1,0:T(8,128)(2,1)}, bf16[2,16,1024]{2,1,0:T(8,128)(2,1)S(1)}, u32[]{:S(2)}, u32[]{:S(2)}) %collective-permute-start.1) | collective-permute-done | bytes 65568 | tf_op jit(solution)/shard_map/ppermute | solution.py:463
  7.0 0.0 copy-start.8
  7.0 2.7 %collective-permute-done.2.refs_3_ = bf16[2,16,1024]{2,1,0:T(8,128)(2,1)S(1)} collective-permute-done((bf16[2,16,1024]{2,1,0:T(8,128)(2,1)}, bf16[2,16,1024]{2,1,0:T(8,128)(2,1)S(1)}, u32[]{:S(2)}, u32[]{:S(2)}) %collective-permute-start.2) | collective-permute-done | bytes 65568 | tf_op jit(solution)/shard_map/ppermute | solution.py:463
  9.7 0.0 copy-done.7
  9.7 0.0 copy-done.8
  9.7 0.0 copy-start.9
  9.7 0.6 %copy-done.9 = bf16[2,16,1024]{2,1,0:T(8,128)(2,1)} copy-done((bf16[2,16,1024]{2,1,0:T(8,128)(2,1)}, bf16[2,16,1024]{2,1,0:T(8,128)(2,1)S(1)}, u32[]{:S(2)}) %copy-start.9) | copy-done | bytes 65560
  10.3 1.7 %join_past.1.refs_0_ = bf16[8,16,1024]{2,1,0:T(8,128)(2,1)} custom-call(bf16[2,16,1024]{2,1,0:T(8,128)(2,1)} %refs_0_.1, bf16[2,16,1024]{2,1,0:T(8,128)(2,1)} %copy-done.7, bf16[2,16,1024]{2,1,0:T(8,128)(2,1)} %copy-done.8, bf16[2,16,1024]{2,1,0:T(8,128)(2,1)} %copy-done.9), custom_call_target="tpu_custom_call" | custom-call | tf_op jit(solution)/shard_map/join_past/pallas_call | solution.py:207
  11.9 1.2 %collective-permute-start.3 = (bf16[8,16,1024]{2,1,0:T(8,128)(2,1)}, bf16[8,16,1024]{2,1,0:T(8,128)(2,1)S(1)}, u32[]{:S(2)}, u32[]{:S(2)}) collective-permute-start(bf16[8,16,1024]{2,1,0:T(8,128)(2,1)} %join_past.1.refs_0_), channel_id=1, source_target_pairs={{0,2},{1,3},{2,0},{3,1},{4,6},{5,7},{6,4},{7,5},{8,10},{9,11},{10,... | collective-permute-start | bytes 786440 | tf_op jit(solution)/shard_map/ppermute | solution.py:463
  13.2 1.5 %pack.1.refs_0_ = bf16[1,32,896]{2,1,0:T(8,128)(2,1)} custom-call(bf16[64,192]{1,0:T(8,128)(2,1)} %bitcast.18, bf16[32,432]{1,0:T(8,128)(2,1)} %bitcast.19), custom_call_target="tpu_custom_call" | custom-call | tf_op jit(solution)/shard_map/pack/pallas_call | solution.py:227
  14.6 0.3 collective-permute-start.6
  14.9 4.0 %collective-permute-done.6.refs_1_ = bf16[1,32,896]{2,1,0:T(8,128)(2,1)S(1)} collective-permute-done((bf16[1,32,896]{2,1,0:T(8,128)(2,1)}, bf16[1,32,896]{2,1,0:T(8,128)(2,1)S(1)}, u32[]{:S(2)}, u32[]{:S(2)}) %collective-permute-start.6) | collective-permute-done | bytes 57376 | tf_op jit(solution)/shard_map/ppermute | solution.py:463
  18.9 0.0 copy-start.10
  18.9 0.6 %copy-done.10 = bf16[1,32,896]{2,1,0:T(8,128)(2,1)} copy-done((bf16[1,32,896]{2,1,0:T(8,128)(2,1)}, bf16[1,32,896]{2,1,0:T(8,128)(2,1)S(1)}, u32[]{:S(2)}) %copy-start.10) | copy-done | bytes 57368
  19.5 1.5 %join_panels.1.refs_0_ = bf16[2,32,896]{2,1,0:T(8,128)(2,1)} custom-call(bf16[1,32,896]{2,1,0:T(8,128)(2,1)} %pack.1.refs_0_, bf16[1,32,896]{2,1,0:T(8,128)(2,1)} %copy-done.10), custom_call_target="tpu_custom_call" | custom-call | tf_op jit(solution)/shard_map/join_panels/pallas_call | solution.py:207
  21.0 1.2 %collective-permute-start.7 = (bf16[2,32,896]{2,1,0:T(8,128)(2,1)}, bf16[2,32,896]{2,1,0:T(8,128)(2,1)S(1)}, u32[]{:S(2)}, u32[]{:S(2)}) collective-permute-start(bf16[2,32,896]{2,1,0:T(8,128)(2,1)} %join_panels.1.refs_0_), channel_id=1, source_target_pairs={{0,4},{1,5},{2,6},{3,7},{4,0},{5,1},{6,2},{7,3},{8,12},{9,13},{10,... | collective-permute-start | bytes 344072 | tf_op jit(solution)/shard_map/ppermute | solution.py:463
  22.2 1.0 %collective-permute-start.8 = (bf16[2,32,896]{2,1,0:T(8,128)(2,1)}, bf16[2,32,896]{2,1,0:T(8,128)(2,1)S(1)}, u32[]{:S(2)}, u32[]{:S(2)}) collective-permute-start(bf16[2,32,896]{2,1,0:T(8,128)(2,1)} %join_panels.1.refs_0_), channel_id=1, source_target_pairs={{0,8},{1,9},{2,10},{3,11},{4,12},{5,13},{6,14},{7,15},{8,0},{9,1},... | collective-permute-start | bytes 344072 | tf_op jit(solution)/shard_map/ppermute | solution.py:463
  23.2 1.4 %collective-permute-start.9 = (bf16[2,32,896]{2,1,0:T(8,128)(2,1)}, bf16[2,32,896]{2,1,0:T(8,128)(2,1)S(1)}, u32[]{:S(2)}, u32[]{:S(2)}) collective-permute-start(bf16[2,32,896]{2,1,0:T(8,128)(2,1)} %join_panels.1.refs_0_), channel_id=1, source_target_pairs={{0,12},{1,13},{2,14},{3,15},{4,8},{5,9},{6,10},{7,11},{8,4},{9,5},... | collective-permute-start | bytes 344072 | tf_op jit(solution)/shard_map/ppermute | solution.py:463
  24.5 4.1 %collective-permute-start.10 = (bf16[2,32,896]{2,1,0:T(8,128)(2,1)}, bf16[2,32,896]{2,1,0:T(8,128)(2,1)S(1)}, u32[]{:S(2)}, u32[]{:S(2)}) collective-permute-start(bf16[2,32,896]{2,1,0:T(8,128)(2,1)} %join_panels.1.refs_0_), channel_id=1, source_target_pairs={{0,1},{1,0},{2,3},{3,2},{4,5},{5,4},{6,7},{7,6},{8,9},{9,8},{10,11... | collective-permute-start | bytes 344072 | tf_op jit(solution)/shard_map/ppermute | solution.py:463
  28.6 0.0 collective-permute-done.7.refs_1_
  28.6 2.5 %collective-permute-start.4 = (bf16[8,16,1024]{2,1,0:T(8,128)(2,1)}, bf16[8,16,1024]{2,1,0:T(8,128)(2,1)S(1)}, u32[]{:S(2)}, u32[]{:S(2)}) collective-permute-start(bf16[8,16,1024]{2,1,0:T(8,128)(2,1)} %join_past.1.refs_0_), channel_id=1, source_target_pairs={{0,1},{1,0},{2,3},{3,2},{4,5},{5,4},{6,7},{7,6},{8,9},{9,8},{10,11... | collective-permute-start | bytes 786440 | tf_op jit(solution)/shard_map/ppermute | solution.py:463
  31.1 0.0 collective-permute-done.3.refs_1_
  31.1 0.0 collective-permute-start.5
  31.1 0.0 collective-permute-done.8.refs_2_
  31.1 3.9 %collective-permute-start.11 = (bf16[2,32,896]{2,1,0:T(8,128)(2,1)S(1)}, bf16[2,32,896]{2,1,0:T(8,128)(2,1)S(1)}, u32[]{:S(2)}, u32[]{:S(2)}) collective-permute-start(bf16[2,32,896]{2,1,0:T(8,128)(2,1)S(1)} %collective-permute-done.7.refs_1_), channel_id=1, source_target_pairs={{0,1},{1,0},{2,3},{3,2},{4,5},{5,4},{6,7},{7,6},{8,9},{9,8},{10,11... | collective-permute-start | bytes 344072 | tf_op jit(solution)/shard_map/ppermute | solution.py:463
  35.0 0.0 collective-permute-done.9.refs_3_
  35.0 0.0 collective-permute-start.12
  35.0 0.0 collective-permute-done.10.refs_4_
  35.0 0.5 collective-permute-start.13
  35.5 0.0 copy-start.2
  35.5 1.4 %copy-done.2 = bf16[2,2,64,3072]{3,2,1,0:T(8,128)(2,1)S(1)} copy-done((bf16[2,2,64,3072]{3,2,1,0:T(8,128)(2,1)S(1)}, bf16[2,2,64,3072]{3,2,1,0:T(8,128)(2,1)}, u32[]{:S(2)}) %copy-start.2) | copy-done | bytes 1572888
  36.9 0.0 copy-start.3
  36.9 1.0 %copy-done.3 = bf16[2,2,64,1024]{3,2,1,0:T(8,128)(2,1)S(1)} copy-done((bf16[2,2,64,1024]{3,2,1,0:T(8,128)(2,1)S(1)}, bf16[2,2,64,1024]{3,2,1,0:T(8,128)(2,1)}, u32[]{:S(2)}) %copy-start.3) | copy-done | bytes 524312
  38.0 0.0 copy-start.4
  38.0 0.7 %copy-done.4 = s32[16,16]{1,0:T(8,128)S(1)} copy-done((s32[16,16]{1,0:T(8,128)S(1)}, s32[16,16]{1,0:T(8,128)}, u32[]{:S(2)}) %copy-start.4) | copy-done | bytes 1048
  38.7 0.0 copy-start.5
  38.7 0.7 %copy-done.5 = s32[32]{0:T(128)S(1)} copy-done((s32[32]{0:T(128)S(1)}, s32[32]{0:T(128)}, u32[]{:S(2)}) %copy-start.5) | copy-done | bytes 152
  39.3 0.0 copy-start.6
  39.3 0.7 %copy-done.6 = s32[16]{0:T(128)S(1)} copy-done((s32[16]{0:T(128)S(1)}, s32[16]{0:T(128)}, u32[]{:S(2)}) %copy-start.6) | copy-done | bytes 88
  40.0 0.0 copy-start.1
  40.0 0.0 copy-start
  40.0 4.6 %attend_own.1 = (bf16[4,1536,256]{2,1,0:T(8,128)(2,1)S(1)}, f32[4,1536,128]{2,1,0:T(8,128)S(1)}, s32[16]{0:T(128)S(1)}) custom-call(s32[1]{0:T(128)} %bitcast.tile_ref, s32[32]{0:T(128)S(1)} %copy-done.5, s32[16,16]{1,0:T(8,128)S(1)} %copy-done.4, s32[16]{0:T(128)S(1)} %copy-done.6, bf16[256,3072]{1,0:T(8,128)(2,1)S(1)} %bitcast.16, ...), custom_call_target="tpu_custom_call" | custom-call | flops 2415919104 | bytes 7864320 | tf_op jit(solution)/shard_map/attend_own/pallas_call | solution.py:81
  44.6 0.0 collective-permute-done.11.refs_5_
  44.6 0.0 collective-permute-done.12.refs_6_
  44.6 0.0 collective-permute-done.13.refs_7_
  44.6 0.0 copy-done.1
  44.6 0.3 unpack.1.kernel
  44.9 0.0 collective-permute-done.4.refs_2_
  44.9 0.0 collective-permute-done.5.refs_3_
  44.9 0.0 copy-done
  44.9 2.9 %attend_past.1.attended = bf16[256,3072]{1,0:T(8,128)(2,1)S(1)} custom-call(s32[16]{0:T(128)S(1)} %get-tuple-element.10.slots, bf16[4,1536,256]{2,1,0:T(8,128)(2,1)S(1)} %get-tuple-element.11.packed, f32[4,1536,128]{2,1,0:T(8,128)S(1)} %get-tuple-element.12.sums, bf16[8,16,1024]{2,1,0:T(8,128)(2,1)S(1)} %copy-done, ...), custom_call_target="tpu_custom_call" | custom-call | flops 1610612736 | bytes 6291456 | tf_op jit(solution)/shard_map/attend_past/pallas_call | solution.py:179
  47.8 0.7 %project.1 = bf16[256,64]{1,0:T(8,128)(2,1)S(1)} custom-call(s32[1]{0:T(128)} %bitcast.tile_ref, bf16[256,3072]{1,0:T(8,128)(2,1)S(1)} %attend_past.1.attended, bf16[2,32,896]{2,1,0:T(8,128)(2,1)S(1)} %copy-done.1, bf16[2,32,896]{2,1,0:T(8,128)(2,1)S(1)} %collective-permute-done.7.refs_1_, bf16[2,32,896]{2,1,0:T(8,128)(2,1)S(1)} %collective-permute-done.8.refs_2_, ...), custom_call_target="tpu_custom_call" | custom-call | tf_op jit(solution)/shard_map/project/pallas_call | solution.py:257
  48.5 2.9 %collective-permute-start.14 = (bf16[2,64,64]{2,1,0:T(8,128)(2,1)S(1)}, bf16[2,64,64]{2,1,0:T(8,128)(2,1)S(1)}, u32[]{:S(2)}, u32[]{:S(2)}) collective-permute-start(bf16[2,64,64]{2,1,0:T(8,128)(2,1)S(1)} %get-tuple-element.16), channel_id=1, source_target_pairs={{0,1},{1,2},{2,3},{3,4},{4,5},{5,6},{6,7},{7,8},{8,9},{9,10},{10,1... | collective-permute-start | bytes 49160 | tf_op jit(solution)/shard_map/ppermute | solution.py:509
  51.5 1.9 %collective-permute-start.15 = (bf16[2,64,64]{2,1,0:T(8,128)(2,1)S(1)}, bf16[2,64,64]{2,1,0:T(8,128)(2,1)S(1)}, u32[]{:S(2)}, u32[]{:S(2)}) collective-permute-start(bf16[2,64,64]{2,1,0:T(8,128)(2,1)S(1)} %get-tuple-element.15), channel_id=1, source_target_pairs={{1,0},{2,1},{3,2},{4,3},{5,4},{6,5},{7,6},{8,7},{9,8},{10,9},{11,1... | collective-permute-start | bytes 49160 | tf_op jit(solution)/shard_map/ppermute | solution.py:510
  53.4 1.4 %convolve_inner.1 = (bf16[2,4,128,512]{3,2,1,0:T(8,128)(2,1)}, f32[2,256,512]{2,1,0:T(8,128)S(1)}) custom-call(bf16[2,2,64,64]{3,2,1,0:T(8,128)(2,1)S(1)} %bitcast.15, bf16[432,512]{1,0:T(8,128)(2,1)S(1)} %unpack.1.kernel), custom_call_target="tpu_custom_call" | custom-call | flops 452984832 | bytes 1048576 | tf_op jit(solution)/shard_map/convolve_inner/pallas_call | solution.py:369
  54.9 0.0 collective-permute-done.14.above
  54.9 1.8 %collective-permute-done.15.below = bf16[2,64,64]{2,1,0:T(8,128)(2,1)S(1)} collective-permute-done((bf16[2,64,64]{2,1,0:T(8,128)(2,1)S(1)}, bf16[2,64,64]{2,1,0:T(8,128)(2,1)S(1)}, u32[]{:S(2)}, u32[]{:S(2)}) %collective-permute-start.15) | collective-permute-done | bytes 16416 | tf_op jit(solution)/shard_map/ppermute | solution.py:510
  56.7 1.3 %convolve_outer.1 = bf16[2,4,128,512]{3,2,1,0:T(8,128)(2,1)} custom-call(bf16[2,64,64]{2,1,0:T(8,128)(2,1)S(1)} %collective-permute-done.14.above, bf16[2,64,64]{2,1,0:T(8,128)(2,1)S(1)} %collective-permute-done.15.below, bf16[432,512]{1,0:T(8,128)(2,1)S(1)} %unpack.1.kernel, ...), custom_call_target="tpu_custom_call", output_to_operand_aliasing={{}: (4, {})} | custom-call | tf_op jit(solution)/shard_map/convolve_outer/pallas_call | solution.py:445
  (1 shorter events, 0.0 us)
Async XLA Ops:
  0.0 4.4 %collective-permute-start = (bf16[2,16,1024]{2,1,0:T(8,128)(2,1)}, bf16[2,16,1024]{2,1,0:T(8,128)(2,1)S(1)}, u32[]{:S(2)}, u32[]{:S(2)}) collective-permute-start(bf16[2,16,1024]{2,1,0:T(8,128)(2,1)} %refs_0_.1), channel_id=1, source_target_pairs={{0,4},{1,5},{2,6},{3,7},{4,0},{5,1},{6,2},{7,3},{8,12},{9,13},{10,... | collective-permute-start | bytes 196616 | tf_op jit(solution)/shard_map/ppermute | solution.py:463
  2.1 4.9 %collective-permute-start.1 = (bf16[2,16,1024]{2,1,0:T(8,128)(2,1)}, bf16[2,16,1024]{2,1,0:T(8,128)(2,1)S(1)}, u32[]{:S(2)}, u32[]{:S(2)}) collective-permute-start(bf16[2,16,1024]{2,1,0:T(8,128)(2,1)} %refs_0_.1), channel_id=1, source_target_pairs={{0,8},{1,9},{2,10},{3,11},{4,12},{5,13},{6,14},{7,15},{8,0},{9,1},... | collective-permute-start | bytes 196616 | tf_op jit(solution)/shard_map/ppermute | solution.py:463
  4.4 5.2 %collective-permute-start.2 = (bf16[2,16,1024]{2,1,0:T(8,128)(2,1)}, bf16[2,16,1024]{2,1,0:T(8,128)(2,1)S(1)}, u32[]{:S(2)}, u32[]{:S(2)}) collective-permute-start(bf16[2,16,1024]{2,1,0:T(8,128)(2,1)} %refs_0_.1), channel_id=1, source_target_pairs={{0,12},{1,13},{2,14},{3,15},{4,8},{5,9},{6,10},{7,11},{8,4},{9,5},... | collective-permute-start | bytes 196616 | tf_op jit(solution)/shard_map/ppermute | solution.py:463
  4.4 5.2 %copy-start.7 = (bf16[2,16,1024]{2,1,0:T(8,128)(2,1)}, bf16[2,16,1024]{2,1,0:T(8,128)(2,1)S(1)}, u32[]{:S(2)}) copy-start(bf16[2,16,1024]{2,1,0:T(8,128)(2,1)S(1)} %collective-permute-done.refs_1_) | copy-start | bytes 196612
  7.0 2.7 %copy-start.8 = (bf16[2,16,1024]{2,1,0:T(8,128)(2,1)}, bf16[2,16,1024]{2,1,0:T(8,128)(2,1)S(1)}, u32[]{:S(2)}) copy-start(bf16[2,16,1024]{2,1,0:T(8,128)(2,1)S(1)} %collective-permute-done.1.refs_2_) | copy-start | bytes 196612
  9.7 0.6 %copy-start.9 = (bf16[2,16,1024]{2,1,0:T(8,128)(2,1)}, bf16[2,16,1024]{2,1,0:T(8,128)(2,1)S(1)}, u32[]{:S(2)}) copy-start(bf16[2,16,1024]{2,1,0:T(8,128)(2,1)S(1)} %collective-permute-done.2.refs_3_) | copy-start | bytes 196612
  11.9 19.1 %collective-permute-start.3 = (bf16[8,16,1024]{2,1,0:T(8,128)(2,1)}, bf16[8,16,1024]{2,1,0:T(8,128)(2,1)S(1)}, u32[]{:S(2)}, u32[]{:S(2)}) collective-permute-start(bf16[8,16,1024]{2,1,0:T(8,128)(2,1)} %join_past.1.refs_0_), channel_id=1, source_target_pairs={{0,2},{1,3},{2,0},{3,1},{4,6},{5,7},{6,4},{7,5},{8,10},{9,11},{10,... | collective-permute-start | bytes 786440 | tf_op jit(solution)/shard_map/ppermute | solution.py:463
  14.6 4.2 %collective-permute-start.6 = (bf16[1,32,896]{2,1,0:T(8,128)(2,1)}, bf16[1,32,896]{2,1,0:T(8,128)(2,1)S(1)}, u32[]{:S(2)}, u32[]{:S(2)}) collective-permute-start(bf16[1,32,896]{2,1,0:T(8,128)(2,1)} %pack.1.refs_0_), channel_id=1, source_target_pairs={{0,2},{1,3},{2,0},{3,1},{4,6},{5,7},{6,4},{7,5},{8,10},{9,11},{10,... | collective-permute-start | bytes 172040 | tf_op jit(solution)/shard_map/ppermute | solution.py:463
  18.9 0.6 %copy-start.10 = (bf16[1,32,896]{2,1,0:T(8,128)(2,1)}, bf16[1,32,896]{2,1,0:T(8,128)(2,1)S(1)}, u32[]{:S(2)}) copy-start(bf16[1,32,896]{2,1,0:T(8,128)(2,1)S(1)} %collective-permute-done.6.refs_1_) | copy-start | bytes 172036
  21.0 7.6 %collective-permute-start.7 = (bf16[2,32,896]{2,1,0:T(8,128)(2,1)}, bf16[2,32,896]{2,1,0:T(8,128)(2,1)S(1)}, u32[]{:S(2)}, u32[]{:S(2)}) collective-permute-start(bf16[2,32,896]{2,1,0:T(8,128)(2,1)} %join_panels.1.refs_0_), channel_id=1, source_target_pairs={{0,4},{1,5},{2,6},{3,7},{4,0},{5,1},{6,2},{7,3},{8,12},{9,13},{10,... | collective-permute-start | bytes 344072 | tf_op jit(solution)/shard_map/ppermute | solution.py:463
  22.2 8.9 %collective-permute-start.8 = (bf16[2,32,896]{2,1,0:T(8,128)(2,1)}, bf16[2,32,896]{2,1,0:T(8,128)(2,1)S(1)}, u32[]{:S(2)}, u32[]{:S(2)}) collective-permute-start(bf16[2,32,896]{2,1,0:T(8,128)(2,1)} %join_panels.1.refs_0_), channel_id=1, source_target_pairs={{0,8},{1,9},{2,10},{3,11},{4,12},{5,13},{6,14},{7,15},{8,0},{9,1},... | collective-permute-start | bytes 344072 | tf_op jit(solution)/shard_map/ppermute | solution.py:463
  23.2 11.8 %collective-permute-start.9 = (bf16[2,32,896]{2,1,0:T(8,128)(2,1)}, bf16[2,32,896]{2,1,0:T(8,128)(2,1)S(1)}, u32[]{:S(2)}, u32[]{:S(2)}) collective-permute-start(bf16[2,32,896]{2,1,0:T(8,128)(2,1)} %join_panels.1.refs_0_), channel_id=1, source_target_pairs={{0,12},{1,13},{2,14},{3,15},{4,8},{5,9},{6,10},{7,11},{8,4},{9,5},... | collective-permute-start | bytes 344072 | tf_op jit(solution)/shard_map/ppermute | solution.py:463
  24.5 10.5 %collective-permute-start.10 = (bf16[2,32,896]{2,1,0:T(8,128)(2,1)}, bf16[2,32,896]{2,1,0:T(8,128)(2,1)S(1)}, u32[]{:S(2)}, u32[]{:S(2)}) collective-permute-start(bf16[2,32,896]{2,1,0:T(8,128)(2,1)} %join_panels.1.refs_0_), channel_id=1, source_target_pairs={{0,1},{1,0},{2,3},{3,2},{4,5},{5,4},{6,7},{7,6},{8,9},{9,8},{10,11... | collective-permute-start | bytes 344072 | tf_op jit(solution)/shard_map/ppermute | solution.py:463
  28.6 16.3 %collective-permute-start.4 = (bf16[8,16,1024]{2,1,0:T(8,128)(2,1)}, bf16[8,16,1024]{2,1,0:T(8,128)(2,1)S(1)}, u32[]{:S(2)}, u32[]{:S(2)}) collective-permute-start(bf16[8,16,1024]{2,1,0:T(8,128)(2,1)} %join_past.1.refs_0_), channel_id=1, source_target_pairs={{0,1},{1,0},{2,3},{3,2},{4,5},{5,4},{6,7},{7,6},{8,9},{9,8},{10,11... | collective-permute-start | bytes 786440 | tf_op jit(solution)/shard_map/ppermute | solution.py:463
  31.1 13.8 %collective-permute-start.5 = (bf16[8,16,1024]{2,1,0:T(8,128)(2,1)S(1)}, bf16[8,16,1024]{2,1,0:T(8,128)(2,1)S(1)}, u32[]{:S(2)}, u32[]{:S(2)}) collective-permute-start(bf16[8,16,1024]{2,1,0:T(8,128)(2,1)S(1)} %collective-permute-done.3.refs_1_), channel_id=1, source_target_pairs={{0,1},{1,0},{2,3},{3,2},{4,5},{5,4},{6,7},{7,6},{8,9},{9,8},{10,11... | collective-permute-start | bytes 786440 | tf_op jit(solution)/shard_map/ppermute | solution.py:463
  31.1 13.5 %collective-permute-start.11 = (bf16[2,32,896]{2,1,0:T(8,128)(2,1)S(1)}, bf16[2,32,896]{2,1,0:T(8,128)(2,1)S(1)}, u32[]{:S(2)}, u32[]{:S(2)}) collective-permute-start(bf16[2,32,896]{2,1,0:T(8,128)(2,1)S(1)} %collective-permute-done.7.refs_1_), channel_id=1, source_target_pairs={{0,1},{1,0},{2,3},{3,2},{4,5},{5,4},{6,7},{7,6},{8,9},{9,8},{10,11... | collective-permute-start | bytes 344072 | tf_op jit(solution)/shard_map/ppermute | solution.py:463
  35.0 9.6 %collective-permute-start.12 = (bf16[2,32,896]{2,1,0:T(8,128)(2,1)S(1)}, bf16[2,32,896]{2,1,0:T(8,128)(2,1)S(1)}, u32[]{:S(2)}, u32[]{:S(2)}) collective-permute-start(bf16[2,32,896]{2,1,0:T(8,128)(2,1)S(1)} %collective-permute-done.8.refs_2_), channel_id=1, source_target_pairs={{0,1},{1,0},{2,3},{3,2},{4,5},{5,4},{6,7},{7,6},{8,9},{9,8},{10,11... | collective-permute-start | bytes 344072 | tf_op jit(solution)/shard_map/ppermute | solution.py:463
  35.0 9.6 %collective-permute-start.13 = (bf16[2,32,896]{2,1,0:T(8,128)(2,1)S(1)}, bf16[2,32,896]{2,1,0:T(8,128)(2,1)S(1)}, u32[]{:S(2)}, u32[]{:S(2)}) collective-permute-start(bf16[2,32,896]{2,1,0:T(8,128)(2,1)S(1)} %collective-permute-done.9.refs_3_), channel_id=1, source_target_pairs={{0,1},{1,0},{2,3},{3,2},{4,5},{5,4},{6,7},{7,6},{8,9},{9,8},{10,11... | collective-permute-start | bytes 344072 | tf_op jit(solution)/shard_map/ppermute | solution.py:463
  35.5 1.4 %copy-start.2 = (bf16[2,2,64,3072]{3,2,1,0:T(8,128)(2,1)S(1)}, bf16[2,2,64,3072]{3,2,1,0:T(8,128)(2,1)}, u32[]{:S(2)}) copy-start(bf16[2,2,64,3072]{3,2,1,0:T(8,128)(2,1)} %param.8) | copy-start | bytes 4718596
  36.9 1.0 %copy-start.3 = (bf16[2,2,64,1024]{3,2,1,0:T(8,128)(2,1)S(1)}, bf16[2,2,64,1024]{3,2,1,0:T(8,128)(2,1)}, u32[]{:S(2)}) copy-start(bf16[2,2,64,1024]{3,2,1,0:T(8,128)(2,1)} %param.9) | copy-start | bytes 1572868
  38.0 0.7 %copy-start.4 = (s32[16,16]{1,0:T(8,128)S(1)}, s32[16,16]{1,0:T(8,128)}, u32[]{:S(2)}) copy-start(s32[16,16]{1,0:T(8,128)} %blocks.1) | copy-start | bytes 3076
  38.7 0.7 %copy-start.5 = (s32[32]{0:T(128)S(1)}, s32[32]{0:T(128)}, u32[]{:S(2)}) copy-start(s32[32]{0:T(128)} %home.1) | copy-start | bytes 388
  39.3 0.7 %copy-start.6 = (s32[16]{0:T(128)S(1)}, s32[16]{0:T(128)}, u32[]{:S(2)}) copy-start(s32[16]{0:T(128)} %lens.1) | copy-start | bytes 196
  40.0 4.6 %copy-start.1 = (bf16[2,32,896]{2,1,0:T(8,128)(2,1)S(1)}, bf16[2,32,896]{2,1,0:T(8,128)(2,1)}, u32[]{:S(2)}) copy-start(bf16[2,32,896]{2,1,0:T(8,128)(2,1)} %join_panels.1.refs_0_) | copy-start | bytes 344068
  40.0 4.9 %copy-start = (bf16[8,16,1024]{2,1,0:T(8,128)(2,1)S(1)}, bf16[8,16,1024]{2,1,0:T(8,128)(2,1)}, u32[]{:S(2)}) copy-start(bf16[8,16,1024]{2,1,0:T(8,128)(2,1)} %join_past.1.refs_0_) | copy-start | bytes 786436
  48.5 6.3 %collective-permute-start.14 = (bf16[2,64,64]{2,1,0:T(8,128)(2,1)S(1)}, bf16[2,64,64]{2,1,0:T(8,128)(2,1)S(1)}, u32[]{:S(2)}, u32[]{:S(2)}) collective-permute-start(bf16[2,64,64]{2,1,0:T(8,128)(2,1)S(1)} %get-tuple-element.16), channel_id=1, source_target_pairs={{0,1},{1,2},{2,3},{3,4},{4,5},{5,6},{6,7},{7,8},{8,9},{9,10},{10,1... | collective-permute-start | bytes 49160 | tf_op jit(solution)/shard_map/ppermute | solution.py:509
  51.5 5.2 %collective-permute-start.15 = (bf16[2,64,64]{2,1,0:T(8,128)(2,1)S(1)}, bf16[2,64,64]{2,1,0:T(8,128)(2,1)S(1)}, u32[]{:S(2)}, u32[]{:S(2)}) collective-permute-start(bf16[2,64,64]{2,1,0:T(8,128)(2,1)S(1)} %get-tuple-element.15), channel_id=1, source_target_pairs={{1,0},{2,1},{3,2},{4,3},{5,4},{6,5},{7,6},{8,7},{9,8},{10,9},{11,1... | collective-permute-start | bytes 49160 | tf_op jit(solution)/shard_map/ppermute | solution.py:510

commit v4 on v3

--- a/solution.py
+++ b/solution.py
@@ -16,6 +16,7 @@
 SAFE = 2.0**100
 MIB = 1024 * 1024
 WHOLE = pl.BlockSpec(memory_space=pltpu.VMEM)
+ANYWHERE = pl.BlockSpec(memory_space=pl.ANY)
 SCALARS = pl.BlockSpec(memory_space=pltpu.SMEM)
 BF16 = jnp.bfloat16
 F32 = jnp.float32
@@ -33,9 +34,19 @@
     return sum(((offset >> bit) & 1) << to for bit, to in turns)
 
 
-def own_body(turns, blocks_here, tile_ref, home, blocks, lens, queries, own, packed, sums, slots):
+def own_body(
+    turns, blocks_here, tile_ref, home, blocks, lens, queries_from, own_from, packed, sums, slots,
+    queries, own, sems
+):
     tokens = queries.shape[0]
     tile = tile_ref[0]
+    span = GROUP * HEAD_DIM
+    copies = [pltpu.make_async_copy(own_from, own, sems.at[KV_HEADS])]
+    for g in range(KV_HEADS):
+        part = pl.ds(g * span, span)
+        copies.append(pltpu.make_async_copy(queries_from.at[:, part], queries.at[:, part], sems.at[g]))
+    for copy in copies:
+        copy.start()
     for place in range(slots.shape[0]):
         slots[place] = -1
 
@@ -46,16 +57,15 @@
 
     lax.fori_loop(0, lens[tile], find, 0)
 
-    def one(g, carry):
-        def columns(index):
-            return pl.ds(pl.multiple_of(index * HEAD_DIM, HEAD_DIM), HEAD_DIM)
-
-        query = jnp.concatenate([queries[:, columns(g * GROUP + h)] for h in range(GROUP)], axis=0)
+    copies[0].wait()
+    for g in range(KV_HEADS):
+        copies[1 + g].wait()
+        query = jnp.concatenate([queries[:, head_columns(g * GROUP + h)] for h in range(GROUP)], axis=0)
         value = jnp.concatenate(
-            [own[:, columns(KV_HEADS + g)], jnp.ones((tokens, HEAD_DIM), BF16)], axis=1
+            [own[:, head_columns(KV_HEADS + g)], jnp.ones((tokens, HEAD_DIM), BF16)], axis=1
         )
         score = lax.dot_general(
-            query, own[:, columns(g)], (((1,), (1,)), ((), ())), preferred_element_type=F32
+            query, own[:, head_columns(g)], (((1,), (1,)), ((), ())), preferred_element_type=F32
         )
         top = jnp.max(score, axis=1, keepdims=True)
         weights = jnp.exp2((score - top) * SCALE).astype(BF16)
@@ -70,9 +80,6 @@
         extra = jnp.where(lane == 0, high, jnp.where(lane == 1, middle, jnp.where(lane == 2, low, 0.0)))
         packed[g, :, :HEAD_DIM] = query
         packed[g, :, HEAD_DIM:] = extra.astype(BF16)
-        return carry
-
-    lax.fori_loop(0, KV_HEADS, one, 0)
 
 
 def attend_own(tile, block_home, block_list, list_len, query_rows, own_rows, turns, blocks_here):
@@ -80,12 +87,17 @@
     rows = GROUP * tokens
     return pl.pallas_call(
         functools.partial(own_body, turns, blocks_here),
-        in_specs=[SCALARS] * 4 + [WHOLE, WHOLE],
+        in_specs=[SCALARS] * 4 + [ANYWHERE] * 2,
         out_specs=[WHOLE, WHOLE, SCALARS],
         out_shape=[
             jax.ShapeDtypeStruct((KV_HEADS, rows, 2 * HEAD_DIM), BF16),
             jax.ShapeDtypeStruct((KV_HEADS, rows, HEAD_DIM), F32),
             jax.ShapeDtypeStruct((1 << len(turns),), jnp.int32),
+        ],
+        scratch_shapes=[
+            pltpu.VMEM(query_rows.shape, BF16),
+            pltpu.VMEM(own_rows.shape, BF16),
+            pltpu.SemaphoreType.DMA((KV_HEADS + 1,)),
         ],
         compiler_params=params(24),
         cost_estimate=pl.CostEstimate(
@@ -209,14 +221,14 @@
         in_specs=[WHOLE] * len(parts),
         out_specs=WHOLE,
         out_shape=jax.ShapeDtypeStruct((rows,) + parts[0].shape[1:], BF16),
+        compiler_params=params(4),
         name=name,
     )(*parts)
 
 
 def pack_body(final, decode, out):
-    half, depth = final.shape[0] // 2, final.shape[1]
-    taps = decode.shape[1]
-    blank = out.shape[2] - 2 * depth - taps
+    half = final.shape[0] // 2
+    blank = out.shape[2] - 2 * final.shape[1] - decode.shape[1]
     out[0] = jnp.concatenate(
         [final[:half], final[half:], decode[...], jnp.zeros((half, blank), BF16)], axis=1
     )
@@ -229,12 +241,15 @@
         in_specs=[WHOLE, WHOLE],
         out_specs=WHOLE,
         out_shape=jax.ShapeDtypeStruct((1, decode.shape[0], lanes), BF16),
+        compiler_params=params(4),
+        cost_estimate=pl.CostEstimate(flops=5 * 10**9, bytes_accessed=0, transcendentals=0),
         name="pack",
     )(final, decode)
 
 
-def project_body(depth, order, tile_ref, attended, *refs):
-    *panels, out, staged, whole = refs
+def project_body(order, shape, depth, tile_ref, attended, *refs):
+    *panels, out, to_pair, to_next, staged, whole = refs
+    frames, patch_rows, patches = shape
     place = 0
     half = staged.shape[1]
     for panel in panels:
@@ -246,45 +261,53 @@
             whole[part * half : (part + 1) * half, device * depth : (device + 1) * depth] = staged[
                 device, :, part * depth : (part + 1) * depth
             ]
-    out[...] = lax.dot_general(
+    predicted = lax.dot_general(
         attended[...], whole[...], (((1,), (1,)), ((), ())), preferred_element_type=F32
     ).astype(BF16)
-
-
-def project(tile, attended, panels, order, depth, columns):
+    out[...] = predicted
+    even = tile_ref[0] % 2 == 0
+    for frame in range(frames):
+        rows = predicted[frame * patch_rows * patches : (frame + 1) * patch_rows * patches]
+        first, last = rows[:patches], rows[(patch_rows - 1) * patches :]
+        to_pair[frame] = jnp.where(even, last, first)
+        to_next[frame] = jnp.where(even, first, last)
+
+
+def project(tile, attended, panels, order, shape):
     tokens, width = attended.shape
-    lanes = -(-2 * depth // 128) * 128
-    return pl.pallas_call(
-        functools.partial(project_body, depth, order),
+    half = panels[0].shape[1]
+    depth = width // len(order)
+    border = jax.ShapeDtypeStruct((shape[0], shape[2], 2 * half), BF16)
+    return pl.pallas_call(
+        functools.partial(project_body, order, shape, depth),
         in_specs=[SCALARS] + [WHOLE] * (1 + len(panels)),
-        out_specs=WHOLE,
-        out_shape=jax.ShapeDtypeStruct((tokens, columns), BF16),
+        out_specs=[WHOLE] * 3,
+        out_shape=[jax.ShapeDtypeStruct((tokens, 2 * half), BF16), border, border],
         scratch_shapes=[
-            pltpu.VMEM((len(order), columns // 2, lanes), BF16),
-            pltpu.VMEM((columns, width), BF16),
+            pltpu.VMEM((len(order), half, -(-2 * depth // 128) * 128), BF16),
+            pltpu.VMEM((2 * half, width), BF16),
         ],
         compiler_params=params(16),
         name="project",
     )(tile, attended, *panels)
 
 
-def unpack_body(depth, order, tile_ref, *refs):
+def unpack_body(order, skip, tile_ref, *refs):
     *panels, out, staged = refs
+    taps = out.shape[0]
     place = 0
-    width = staged.shape[1]
-    taps = out.shape[0]
     for panel in panels:
         for k in range(panel.shape[0]):
             staged[tile_ref[0] ^ order[place]] = panel[k]
             place += 1
-    whole = jnp.concatenate([staged[d, :, 2 * depth : 2 * depth + taps] for d in range(len(order))], axis=0)
-    out[...] = whole.T
-
-
-def unpack(tile, panels, order, depth, taps):
+    whole = [staged[device, :, skip : skip + taps] for device in range(len(order))]
+    out[...] = jnp.concatenate(whole, axis=0).T
+
+
+def unpack(tile, panels, order, skip, taps):
     width, lanes = panels[0].shape[1:]
     return pl.pallas_call(
-        functools.partial(unpack_body, depth, order),
+        functools.partial(unpack_body, order, skip),
         in_specs=[SCALARS] + [WHOLE] * len(panels),
         out_specs=WHOLE,
         out_shape=jax.ShapeDtypeStruct((taps, width * len(order)), BF16),
@@ -369,7 +392,7 @@
     return pl.pallas_call(
         functools.partial(inner_body, lat),
         in_specs=[WHOLE, WHOLE],
-        out_specs=[pl.BlockSpec(memory_space=pl.ANY), WHOLE],
+        out_specs=[ANYWHERE, WHOLE],
         out_shape=[
             jax.ShapeDtypeStruct((frames, tall, broad, channels), BF16),
             jax.ShapeDtypeStruct((2, frames * broad, channels), F32),
@@ -389,8 +412,9 @@
     )(predicted, kernel)
 
 
-def outer_body(lat, above, below, kernel, edges, given, features, wide, done, sems):
-    frames, patches, values = above.shape
+def outer_body(lat, tile_ref, from_pair, from_next, kernel, edges, given, features, wide, done, sems):
+    frames, patches, values = from_pair.shape
+    even = tile_ref[0] % 2 == 0
     broad = 2 * patches
     tall = features.shape[1]
     span = 3 * lat
@@ -400,7 +424,10 @@
     target = lax.broadcasted_iota(jnp.int32, (values, lanes), 1)
     lane = lax.broadcasted_iota(jnp.int32, (broad, lanes), 1)
     copies = []
-    for edge, cells in enumerate((above, below)):
+    for edge in range(2):
+        cells = [
+            jnp.where(even == (edge == 0), from_next[frame], from_pair[frame]) for frame in range(frames)
+        ]
         wide[edge, :, :, 0:8] = jnp.zeros((frames, chunks, 8, 128), F32)
         wide[edge, :, :, 8 + broad :] = jnp.zeros((frames, chunks, 8, 128), F32)
         for side in range(2):
@@ -435,19 +462,18 @@
         copy.wait()
 
 
-def convolve_outer(above, below, kernel, edges, features):
-    frames, patches, values = above.shape
+def convolve_outer(tile, from_pair, from_next, kernel, edges, features):
+    frames, patches, values = from_pair.shape
     lat = values // 4
     broad = 2 * patches
     channels = kernel.shape[1]
     lanes = -(-9 * lat // 128) * 128
-    anywhere = pl.BlockSpec(memory_space=pl.ANY)
     return pl.pallas_call(
         functools.partial(outer_body, lat),
-        in_specs=[WHOLE, WHOLE, WHOLE, WHOLE, anywhere],
-        out_specs=anywhere,
+        in_specs=[SCALARS] + [WHOLE] * 4 + [ANYWHERE],
+        out_specs=ANYWHERE,
         out_shape=jax.ShapeDtypeStruct(features.shape, BF16),
-        input_output_aliases={4: 0},
+        input_output_aliases={5: 0},
         scratch_shapes=[
             pltpu.VMEM((2, frames, lanes // 128, broad + 16, 128), F32),
             pltpu.VMEM((2, frames, broad, channels), BF16),
@@ -455,7 +481,7 @@
         ],
         compiler_params=params(16),
         name="convolve_outer",
-    )(above, below, kernel, edges, features)
+    )(tile, from_pair, from_next, kernel, edges, features)
 
 
 def exchange(value, offset):
@@ -470,29 +496,37 @@
     assert count & (count - 1) == 0
     bits = count.bit_length() - 1
     blocks_here = past_kv.shape[0]
-    depth, columns = final_weight.shape
-    taps, panel_width = decoder_weight.shape
+    columns = final_weight.shape[1]
     tile = lax.axis_index("seq").astype(jnp.int32).reshape(1)
     query_rows = queries.reshape(tokens, width)
     own_rows = own_kv.reshape(tokens, own_kv.shape[3])
-    if count == 16 and panel_width == columns // 2:
+    shape = (frames, patch_rows, patches)
+    if count == 16 and columns == 2 * decoder_weight.shape[1]:
         far = [4, 8, 12]
         turns = [(2, 0), (3, 1), (1, 2), (0, 3)]
-        steps = [exchange(past_kv, k) for k in far]
+        line = [exchange(past_kv, k) for k in far]
         panel = pack(final_weight.T, decoder_weight.T)
-        pair = join([panel, exchange(panel, 2)], "join_panels")
+        panel_across = exchange(panel, 2)
         packed, sums, slots = attend_own(
             tile, block_home, block_list, list_len, query_rows, own_rows, turns, blocks_here
         )
-        line = join([past_kv] + steps, "join_past")
+        *line, panel_across, slots = lax.optimization_barrier((*line, panel_across, slots))
+        line = join([past_kv] + line, "join_line")
         across = exchange(line, 2)
-        gathered = [line, across, exchange(line, 1), exchange(across, 1)]
-        panels = [pair] + [exchange(pair, k) for k in far]
-        panels = panels + [exchange(p, 1) for p in panels]
-        order = [k ^ x ^ c for c in (0, 1) for k in [0] + far for x in (0, 2)]
+        beside = exchange(line, 1)
+        panels = join([panel, panel_across], "join_pair")
+        order = [k ^ x for k in [0] + far for x in (0, 2)]
+        order = order + [k ^ 1 for k in order]
+        panels_far = [exchange(panels, far[0])]
+        panels, across, beside = lax.optimization_barrier((panels, across, beside))
+        panels_far = panels_far + [exchange(panels, k) for k in far[1:]]
+        gathered = [line, across, beside, exchange(across, 1)]
         attended = attend_past(slots, packed, sums, gathered, blocks_here)
-        predicted = project(tile, attended, panels, order, depth, columns)
-        decode = unpack(tile, panels, order, depth, taps)
+        *panels_far, attended = lax.optimization_barrier((*panels_far, attended))
+        panels = join([panels] + panels_far, "join_panels")
+        panels = [panels, exchange(panels, 1)]
+        predicted, to_pair, to_next = project(tile, attended, panels, order, shape)
+        decode = unpack(tile, panels, order, 2 * final_weight.shape[0], decoder_weight.shape[0])
     else:
         turns = [(bit, bits - 1 - bit) for bit in range(bits)]
         held = past_kv
@@ -505,11 +539,16 @@
         final = lax.all_gather(final_weight, "seq", axis=0, tiled=True)
         decode = lax.all_gather(decoder_weight, "seq", axis=1, tiled=True)
         predicted = jnp.dot(attended, final, preferred_element_type=F32).astype(BF16)
-    predicted = predicted.reshape(frames, patch_rows, patches, columns)
-    above = lax.ppermute(predicted[:, -1], "seq", [(i, i + 1) for i in range(count - 1)])
-    below = lax.ppermute(predicted[:, 0], "seq", [(i + 1, i) for i in range(count - 1)])
+        rows = predicted.reshape(shape + (columns,))
+        even = tile[0] % 2 == 0
+        to_pair = jnp.where(even, rows[:, -1], rows[:, 0])
+        to_next = jnp.where(even, rows[:, 0], rows[:, -1])
+    predicted = predicted.reshape(shape + (columns,))
+    from_pair = exchange(to_pair, 1)
+    swaps = [(i, i + 1) for i in range(1, count - 1, 2)] + [(i + 1, i) for i in range(1, count - 1, 2)]
+    from_next = lax.ppermute(to_next, "seq", swaps)
     features, edges = convolve_inner(predicted, decode)
-    return convolve_outer(above, below, decode, edges, features)
+    return convolve_outer(tile, from_pair, from_next, decode, edges, features)
 
 
 def solution(mesh):

time: 59 us -> 44.9 us (0.76)
  the two profiles are of different devices: /device:TPU:1 before, /device:TPU:15 now
where the time goes in v4:
time: 44.9 us; the launch traced here: 44.6 us
  starting transfers between devices  15.2 us (34%)
  waiting for transfers between devices  15 us (33%)
  Pallas kernels  11.6 us (26%)
  local copies, waits for them, and re-layouts  2.69 us (6%)
    ppermute x12, waiting for transfers between devices, exchange(): return lax.ppermute(value, 'seq', [(i, i ^ offset) for i in range(count)])  13.6 us
    ppermute x12, starting transfers between devices, exchange(): return lax.ppermute(value, 'seq', [(i, i ^ offset) for i in range(count)])  12.2 us
    pallas_call x1, Pallas kernels, attend_own(): pl.pallas_call(functools.partial(own_body, turns, blocks_here), in_specs=...  4.87 us
    ppermute x1, starting transfers between devices, local(): from_next = lax.ppermute(to_next, 'seq', swaps)  3.03 us
    pallas_call x1, Pallas kernels, attend_past(): pl.pallas_call(functools.partial(past_body, sizes), in_specs=[SCALARS] +...  2.89 us
    unnamed x16, local copies, waits for them, and re-layouts  2.69 us
    pallas_call x1, Pallas kernels, convolve_inner(): pl.pallas_call(functools.partial(inner_body, lat), in_specs=[WHOLE, WHOLE...  1.45 us
    ppermute x1, waiting for transfers between devices, local(): from_next = lax.ppermute(to_next, 'seq', swaps)  1.35 us
  transfers between devices with their start and end apart: 13, of which 5 were waited for; matrix products, arithmetic and copies ran while one was open for 0% of the time, Pallas kernels for 21%

profile of v4, /device:TPU:15, one launch (start us, length us, event | category | flops | bytes accessed | tf_op | source)
XLA Modules:
  0.0 44.6 jit_solution(1627030160637411537)
XLA Ops:
  0.0 0.2 collective-permute-start
  0.2 2.3 %collective-permute-start.1 = (bf16[2,16,1024]{2,1,0:T(8,128)(2,1)}, bf16[2,16,1024]{2,1,0:T(8,128)(2,1)S(1)}, u32[]{:S(2)}, u32[]{:S(2)}) collective-permute-start(bf16[2,16,1024]{2,1,0:T(8,128)(2,1)} %refs_0_.1), channel_id=1, source_target_pairs={{0,8},{1,9},{2,10},{3,11},{4,12},{5,13},{6,14},{7,15},{8,0},{9,1},... | collective-permute-start | bytes 196616 | tf_op jit(solution)/shard_map/ppermute | solution.py:489
  2.5 0.2 collective-permute-start.2
  2.7 0.0 copy-start.3
  2.7 0.8 %copy-done.3 = bf16[192,64]{0,1:T(8,128)(2,1)S(1)} copy-done((bf16[192,64]{0,1:T(8,128)(2,1)S(1)}, bf16[192,64]{0,1:T(8,128)(2,1)}, u32[]{:S(2)}) %copy-start.3) | copy-done | bytes 24600
  3.4 0.0 copy-start.4
  3.4 0.8 %copy-done.4 = bf16[432,32]{0,1:T(8,128)(2,1)S(1)} copy-done((bf16[432,32]{0,1:T(8,128)(2,1)S(1)}, bf16[432,32]{0,1:T(8,128)(2,1)}, u32[]{:S(2)}) %copy-start.4) | copy-done | bytes 27672
  4.2 0.0 copy-start.1
  4.2 0.0 copy-start.2
  4.2 0.0 copy-start.5
  4.2 0.0 copy-start.6
  4.2 0.0 copy-start.7
  4.2 0.1 pack.1.refs_0_
  4.3 0.3 collective-permute-start.3
  4.5 1.0 %copy-done.1 = bf16[2,2,64,3072]{3,2,1,0:T(8,128)(2,1)S(1)} copy-done((bf16[2,2,64,3072]{3,2,1,0:T(8,128)(2,1)S(1)}, bf16[2,2,64,3072]{3,2,1,0:T(8,128)(2,1)}, u32[]{:S(2)}) %copy-start.1) | copy-done | bytes 1572888
  5.6 0.1 copy-done.2
  5.7 0.0 copy-done.5
  5.7 0.0 copy-done.6
  5.7 0.0 copy-done.7
  5.7 0.0 copy-start
  5.7 4.9 %attend_own.1 = (bf16[4,1536,256]{2,1,0:T(8,128)(2,1)S(1)}, f32[4,1536,128]{2,1,0:T(8,128)S(1)}, s32[16]{0:T(128)S(1)}) custom-call(s32[1]{0:T(128)} %bitcast.tile_ref, s32[32]{0:T(128)S(1)} %copy-done.6, s32[16,16]{1,0:T(8,128)S(1)} %copy-done.5, s32[16]{0:T(128)S(1)} %copy-done.7, bf16[256,3072]{1,0:T(8,128)(2,1)S(1)} %bitcast.6, bf16[256,1024]{1,0:T(8,128)(2,1)S(1)} %bitcast.7), custom_call_target="tpu_custom_call" | custom-call | flops 2415919104 | bytes 7864320 | tf_op jit(solution)/shard_map/attend_own/pallas_call | solution.py:88
  10.6 0.0 collective-permute-done.3.refs_1_
  10.6 0.0 collective-permute-done.refs_1_
  10.6 0.0 collective-permute-done.1.refs_2_
  10.6 0.0 collective-permute-done.2.refs_3_
  10.6 0.0 copy-done
  10.7 0.3 collective-permute-start.5
  11.0 1.8 %collective-permute-start.6 = (bf16[8,16,1024]{2,1,0:T(8,128)(2,1)S(1)}, bf16[8,16,1024]{2,1,0:T(8,128)(2,1)S(1)}, u32[]{:S(2)}, u32[]{:S(2)}) collective-permute-start(bf16[8,16,1024]{2,1,0:T(8,128)(2,1)S(1)} %join_line.1.refs_0_), channel_id=1, source_target_pairs={{0,1},{1,0},{2,3},{3,2},{4,5},{5,4},{6,7},{7,6},{8,9},{9,8},{10,11... | collective-permute-start | bytes 786440 | tf_op jit(solution)/shard_map/ppermute | solution.py:489
  12.8 4.4 %collective-permute-done.5.refs_1_ = bf16[8,16,1024]{2,1,0:T(8,128)(2,1)S(1)} collective-permute-done((bf16[8,16,1024]{2,1,0:T(8,128)(2,1)S(1)}, bf16[8,16,1024]{2,1,0:T(8,128)(2,1)S(1)}, u32[]{:S(2)}, u32[]{:S(2)}) %collective-permute-start.5) | collective-permute-done | bytes 262176 | tf_op jit(solution)/shard_map/ppermute | solution.py:489
  17.2 0.0 collective-permute-done.6.refs_2_
  17.2 2.2 %collective-permute-start.9 = (bf16[8,16,1024]{2,1,0:T(8,128)(2,1)S(1)}, bf16[8,16,1024]{2,1,0:T(8,128)(2,1)S(1)}, u32[]{:S(2)}, u32[]{:S(2)}) collective-permute-start(bf16[8,16,1024]{2,1,0:T(8,128)(2,1)S(1)} %collective-permute-done.5.refs_1_), channel_id=1, source_target_pairs={{0,1},{1,0},{2,3},{3,2},{4,5},{5,4},{6,7},{7,6},{8,9},{9,8},{10,11... | collective-permute-start | bytes 786440 | tf_op jit(solution)/shard_map/ppermute | solution.py:489
  19.4 0.9 %collective-permute-start.4 = (bf16[2,32,896]{2,1,0:T(8,128)(2,1)S(1)}, bf16[2,32,896]{2,1,0:T(8,128)(2,1)S(1)}, u32[]{:S(2)}, u32[]{:S(2)}) collective-permute-start(bf16[2,32,896]{2,1,0:T(8,128)(2,1)S(1)} %join_pair.1.refs_0_), channel_id=1, source_target_pairs={{0,4},{1,5},{2,6},{3,7},{4,0},{5,1},{6,2},{7,3},{8,12},{9,13},{10,... | collective-permute-start | bytes 344072 | tf_op jit(solution)/shard_map/ppermute | solution.py:489
  20.4 2.3 %collective-permute-start.7 = (bf16[2,32,896]{2,1,0:T(8,128)(2,1)S(1)}, bf16[2,32,896]{2,1,0:T(8,128)(2,1)S(1)}, u32[]{:S(2)}, u32[]{:S(2)}) collective-permute-start(bf16[2,32,896]{2,1,0:T(8,128)(2,1)S(1)} %join_pair.1.refs_0_), channel_id=1, source_target_pairs={{0,8},{1,9},{2,10},{3,11},{4,12},{5,13},{6,14},{7,15},{8,0},{9,1},... | collective-permute-start | bytes 344072 | tf_op jit(solution)/shard_map/ppermute | solution.py:489
  22.7 0.3 collective-permute-start.8
  23.0 0.0 collective-permute-done.9.refs_3_
  23.0 2.9 %attend_past.1.attended = bf16[256,3072]{1,0:T(8,128)(2,1)S(1)} custom-call(s32[16]{0:T(128)S(1)} %get-tuple-element.31.slots, bf16[4,1536,256]{2,1,0:T(8,128)(2,1)S(1)} %get-tuple-element.32.packed, f32[4,1536,128]{2,1,0:T(8,128)S(1)} %get-tuple-element.33.sums, bf16[8,16,1024]{2,1,0:T(8,128)(2,1)S(1)} %join_line.1.refs_0_, ...), custom_call_target="tpu_custom_call" | custom-call | flops 1610612736 | bytes 6291456 | tf_op jit(solution)/shard_map/attend_past/pallas_call | solution.py:191
  25.9 0.0 collective-permute-done.4.refs_1_
  25.9 4.1 %collective-permute-done.7.refs_2_ = bf16[2,32,896]{2,1,0:T(8,128)(2,1)S(1)} collective-permute-done((bf16[2,32,896]{2,1,0:T(8,128)(2,1)S(1)}, bf16[2,32,896]{2,1,0:T(8,128)(2,1)S(1)}, u32[]{:S(2)}, u32[]{:S(2)}) %collective-permute-start.7) | collective-permute-done | bytes 114720 | tf_op jit(solution)/shard_map/ppermute | solution.py:489
  30.0 3.7 %collective-permute-done.8.refs_3_ = bf16[2,32,896]{2,1,0:T(8,128)(2,1)S(1)} collective-permute-done((bf16[2,32,896]{2,1,0:T(8,128)(2,1)S(1)}, bf16[2,32,896]{2,1,0:T(8,128)(2,1)S(1)}, u32[]{:S(2)}, u32[]{:S(2)}) %collective-permute-start.8) | collective-permute-done | bytes 114720 | tf_op jit(solution)/shard_map/ppermute | solution.py:489
  33.8 0.8 %collective-permute-start.10 = (bf16[8,32,896]{2,1,0:T(8,128)(2,1)S(1)}, bf16[8,32,896]{2,1,0:T(8,128)(2,1)S(1)}, u32[]{:S(2)}, u32[]{:S(2)}) collective-permute-start(bf16[8,32,896]{2,1,0:T(8,128)(2,1)S(1)} %join_panels.1.refs_0_), channel_id=1, source_target_pairs={{0,1},{1,0},{2,3},{3,2},{4,5},{5,4},{6,7},{7,6},{8,9},{9,8},{10,11... | collective-permute-start | bytes 1376264 | tf_op jit(solution)/shard_map/ppermute | solution.py:489
  34.6 1.4 %collective-permute-done.10.refs_1_ = bf16[8,32,896]{2,1,0:T(8,128)(2,1)S(1)} collective-permute-done((bf16[8,32,896]{2,1,0:T(8,128)(2,1)S(1)}, bf16[8,32,896]{2,1,0:T(8,128)(2,1)S(1)}, u32[]{:S(2)}, u32[]{:S(2)}) %collective-permute-start.10) | collective-permute-done | bytes 458784 | tf_op jit(solution)/shard_map/ppermute | solution.py:489
  36.1 0.7 %project.1 = (bf16[256,64]{1,0:T(8,128)(2,1)S(1)}, bf16[2,64,64]{2,1,0:T(8,128)(2,1)S(1)}, bf16[2,64,64]{2,1,0:T(8,128)(2,1)S(1)}) custom-call(s32[1]{0:T(128)} %bitcast.tile_ref, bf16[256,3072]{1,0:T(8,128)(2,1)S(1)} %attend_past.1.attended, bf16[8,32,896]{2,1,0:T(8,128)(2,1)S(1)} %join_panels.1.refs_0_, bf16[8,32,896]{2,1,0:T(8,128)(2,1)S(1)} %collective-permute-done.10.refs_1_), custom_call_target="tpu_custom_call" | custom-call | tf_op jit(solution)/shard_map/project/pallas_call | solution.py:281
  36.8 0.4 collective-permute-start.11
  37.2 3.0 %collective-permute-start.12 = (bf16[2,64,64]{2,1,0:T(8,128)(2,1)S(1)}, bf16[2,64,64]{2,1,0:T(8,128)(2,1)S(1)}, u32[]{:S(2)}, u32[]{:S(2)}) collective-permute-start(bf16[2,64,64]{2,1,0:T(8,128)(2,1)S(1)} %get-tuple-element.41), channel_id=1, source_target_pairs={{1,2},{3,4},{5,6},{7,8},{9,10},{11,12},{13,14},{2,1},{4,3},{6,5},{... | collective-permute-start | bytes 49160 | tf_op jit(solution)/shard_map/ppermute | solution.py:549
  40.2 0.3 unpack.1.kernel
  40.5 1.5 %convolve_inner.1 = (bf16[2,4,128,512]{3,2,1,0:T(8,128)(2,1)}, f32[2,256,512]{2,1,0:T(8,128)S(1)}) custom-call(bf16[2,2,64,64]{3,2,1,0:T(8,128)(2,1)S(1)} %bitcast.8, bf16[432,512]{1,0:T(8,128)(2,1)S(1)} %unpack.1.kernel), custom_call_target="tpu_custom_call" | custom-call | flops 452984832 | bytes 1048576 | tf_op jit(solution)/shard_map/convolve_inner/pallas_call | solution.py:392
  42.0 0.0 collective-permute-done.11.from_pair
  42.0 1.3 %collective-permute-done.12.from_next = bf16[2,64,64]{2,1,0:T(8,128)(2,1)S(1)} collective-permute-done((bf16[2,64,64]{2,1,0:T(8,128)(2,1)S(1)}, bf16[2,64,64]{2,1,0:T(8,128)(2,1)S(1)}, u32[]{:S(2)}, u32[]{:S(2)}) %collective-permute-start.12) | collective-permute-done | bytes 16416 | tf_op jit(solution)/shard_map/ppermute | solution.py:549
  43.3 1.3 %convolve_outer.1 = bf16[2,4,128,512]{3,2,1,0:T(8,128)(2,1)} custom-call(s32[1]{0:T(128)} %bitcast.tile_ref, bf16[2,64,64]{2,1,0:T(8,128)(2,1)S(1)} %collective-permute-done.11.from_pair, bf16[2,64,64]{2,1,0:T(8,128)(2,1)S(1)} %collective-permute-done.12.from_next, bf16[432,512]{1,0:T(8,128)(2,1)S(1)} %unpack.1.kernel, ...), custom_call_target="tpu_custom_call", output_to_operand_aliasing={{}: (5, {})} | custom-call | tf_op jit(solution)/shard_map/convolve_outer/pallas_call | solution.py:471
  (3 shorter events, 0.1 us)
Async XLA Ops:
  0.0 10.6 %collective-permute-start = (bf16[2,16,1024]{2,1,0:T(8,128)(2,1)}, bf16[2,16,1024]{2,1,0:T(8,128)(2,1)S(1)}, u32[]{:S(2)}, u32[]{:S(2)}) collective-permute-start(bf16[2,16,1024]{2,1,0:T(8,128)(2,1)} %refs_0_.1), channel_id=1, source_target_pairs={{0,4},{1,5},{2,6},{3,7},{4,0},{5,1},{6,2},{7,3},{8,12},{9,13},{10,... | collective-permute-start | bytes 196616 | tf_op jit(solution)/shard_map/ppermute | solution.py:489
  0.2 10.4 %collective-permute-start.1 = (bf16[2,16,1024]{2,1,0:T(8,128)(2,1)}, bf16[2,16,1024]{2,1,0:T(8,128)(2,1)S(1)}, u32[]{:S(2)}, u32[]{:S(2)}) collective-permute-start(bf16[2,16,1024]{2,1,0:T(8,128)(2,1)} %refs_0_.1), channel_id=1, source_target_pairs={{0,8},{1,9},{2,10},{3,11},{4,12},{5,13},{6,14},{7,15},{8,0},{9,1},... | collective-permute-start | bytes 196616 | tf_op jit(solution)/shard_map/ppermute | solution.py:489
  2.5 8.1 %collective-permute-start.2 = (bf16[2,16,1024]{2,1,0:T(8,128)(2,1)}, bf16[2,16,1024]{2,1,0:T(8,128)(2,1)S(1)}, u32[]{:S(2)}, u32[]{:S(2)}) collective-permute-start(bf16[2,16,1024]{2,1,0:T(8,128)(2,1)} %refs_0_.1), channel_id=1, source_target_pairs={{0,12},{1,13},{2,14},{3,15},{4,8},{5,9},{6,10},{7,11},{8,4},{9,5},... | collective-permute-start | bytes 196616 | tf_op jit(solution)/shard_map/ppermute | solution.py:489
  2.7 0.8 %copy-start.3 = (bf16[192,64]{0,1:T(8,128)(2,1)S(1)}, bf16[192,64]{0,1:T(8,128)(2,1)}, u32[]{:S(2)}) copy-start(bf16[192,64]{0,1:T(8,128)(2,1)} %param.14) | copy-start | bytes 73732
  3.4 0.8 %copy-start.4 = (bf16[432,32]{0,1:T(8,128)(2,1)S(1)}, bf16[432,32]{0,1:T(8,128)(2,1)}, u32[]{:S(2)}) copy-start(bf16[432,32]{0,1:T(8,128)(2,1)} %param.15) | copy-start | bytes 82948
  4.2 1.4 %copy-start.1 = (bf16[2,2,64,3072]{3,2,1,0:T(8,128)(2,1)S(1)}, bf16[2,2,64,3072]{3,2,1,0:T(8,128)(2,1)}, u32[]{:S(2)}) copy-start(bf16[2,2,64,3072]{3,2,1,0:T(8,128)(2,1)} %param.8) | copy-start | bytes 4718596
  4.2 1.5 %copy-start.2 = (bf16[2,2,64,1024]{3,2,1,0:T(8,128)(2,1)S(1)}, bf16[2,2,64,1024]{3,2,1,0:T(8,128)(2,1)}, u32[]{:S(2)}) copy-start(bf16[2,2,64,1024]{3,2,1,0:T(8,128)(2,1)} %param.9) | copy-start | bytes 1572868
  4.2 1.5 %copy-start.5 = (s32[16,16]{1,0:T(8,128)S(1)}, s32[16,16]{1,0:T(8,128)}, u32[]{:S(2)}) copy-start(s32[16,16]{1,0:T(8,128)} %blocks.1) | copy-start | bytes 3076
  4.2 1.5 %copy-start.6 = (s32[32]{0:T(128)S(1)}, s32[32]{0:T(128)}, u32[]{:S(2)}) copy-start(s32[32]{0:T(128)} %home.1) | copy-start | bytes 388
  4.2 1.5 %copy-start.7 = (s32[16]{0:T(128)S(1)}, s32[16]{0:T(128)}, u32[]{:S(2)}) copy-start(s32[16]{0:T(128)} %lens.1) | copy-start | bytes 196
  4.3 6.3 %collective-permute-start.3 = (bf16[1,32,896]{2,1,0:T(8,128)(2,1)S(1)}, bf16[1,32,896]{2,1,0:T(8,128)(2,1)S(1)}, u32[]{:S(2)}, u32[]{:S(2)}) collective-permute-start(bf16[1,32,896]{2,1,0:T(8,128)(2,1)S(1)} %pack.1.refs_0_), channel_id=1, source_target_pairs={{0,2},{1,3},{2,0},{3,1},{4,6},{5,7},{6,4},{7,5},{8,10},{9,11},{10,... | collective-permute-start | bytes 172040 | tf_op jit(solution)/shard_map/ppermute | solution.py:489
  5.7 4.9 %copy-start = (bf16[2,16,1024]{2,1,0:T(8,128)(2,1)S(1)}, bf16[2,16,1024]{2,1,0:T(8,128)(2,1)}, u32[]{:S(2)}) copy-start(bf16[2,16,1024]{2,1,0:T(8,128)(2,1)} %refs_0_.1) | copy-start | bytes 196612
  10.7 6.5 %collective-permute-start.5 = (bf16[8,16,1024]{2,1,0:T(8,128)(2,1)S(1)}, bf16[8,16,1024]{2,1,0:T(8,128)(2,1)S(1)}, u32[]{:S(2)}, u32[]{:S(2)}) collective-permute-start(bf16[8,16,1024]{2,1,0:T(8,128)(2,1)S(1)} %join_line.1.refs_0_), channel_id=1, source_target_pairs={{0,2},{1,3},{2,0},{3,1},{4,6},{5,7},{6,4},{7,5},{8,10},{9,11},{10,... | collective-permute-start | bytes 786440 | tf_op jit(solution)/shard_map/ppermute | solution.py:489
  11.0 6.2 %collective-permute-start.6 = (bf16[8,16,1024]{2,1,0:T(8,128)(2,1)S(1)}, bf16[8,16,1024]{2,1,0:T(8,128)(2,1)S(1)}, u32[]{:S(2)}, u32[]{:S(2)}) collective-permute-start(bf16[8,16,1024]{2,1,0:T(8,128)(2,1)S(1)} %join_line.1.refs_0_), channel_id=1, source_target_pairs={{0,1},{1,0},{2,3},{3,2},{4,5},{5,4},{6,7},{7,6},{8,9},{9,8},{10,11... | collective-permute-start | bytes 786440 | tf_op jit(solution)/shard_map/ppermute | solution.py:489
  17.2 5.8 %collective-permute-start.9 = (bf16[8,16,1024]{2,1,0:T(8,128)(2,1)S(1)}, bf16[8,16,1024]{2,1,0:T(8,128)(2,1)S(1)}, u32[]{:S(2)}, u32[]{:S(2)}) collective-permute-start(bf16[8,16,1024]{2,1,0:T(8,128)(2,1)S(1)} %collective-permute-done.5.refs_1_), channel_id=1, source_target_pairs={{0,1},{1,0},{2,3},{3,2},{4,5},{5,4},{6,7},{7,6},{8,9},{9,8},{10,11... | collective-permute-start | bytes 786440 | tf_op jit(solution)/shard_map/ppermute | solution.py:489
  19.4 6.5 %collective-permute-start.4 = (bf16[2,32,896]{2,1,0:T(8,128)(2,1)S(1)}, bf16[2,32,896]{2,1,0:T(8,128)(2,1)S(1)}, u32[]{:S(2)}, u32[]{:S(2)}) collective-permute-start(bf16[2,32,896]{2,1,0:T(8,128)(2,1)S(1)} %join_pair.1.refs_0_), channel_id=1, source_target_pairs={{0,4},{1,5},{2,6},{3,7},{4,0},{5,1},{6,2},{7,3},{8,12},{9,13},{10,... | collective-permute-start | bytes 344072 | tf_op jit(solution)/shard_map/ppermute | solution.py:489
  20.4 9.7 %collective-permute-start.7 = (bf16[2,32,896]{2,1,0:T(8,128)(2,1)S(1)}, bf16[2,32,896]{2,1,0:T(8,128)(2,1)S(1)}, u32[]{:S(2)}, u32[]{:S(2)}) collective-permute-start(bf16[2,32,896]{2,1,0:T(8,128)(2,1)S(1)} %join_pair.1.refs_0_), channel_id=1, source_target_pairs={{0,8},{1,9},{2,10},{3,11},{4,12},{5,13},{6,14},{7,15},{8,0},{9,1},... | collective-permute-start | bytes 344072 | tf_op jit(solution)/shard_map/ppermute | solution.py:489
  22.7 11.0 %collective-permute-start.8 = (bf16[2,32,896]{2,1,0:T(8,128)(2,1)S(1)}, bf16[2,32,896]{2,1,0:T(8,128)(2,1)S(1)}, u32[]{:S(2)}, u32[]{:S(2)}) collective-permute-start(bf16[2,32,896]{2,1,0:T(8,128)(2,1)S(1)} %join_pair.1.refs_0_), channel_id=1, source_target_pairs={{0,12},{1,13},{2,14},{3,15},{4,8},{5,9},{6,10},{7,11},{8,4},{9,5},... | collective-permute-start | bytes 344072 | tf_op jit(solution)/shard_map/ppermute | solution.py:489
  33.8 2.3 %collective-permute-start.10 = (bf16[8,32,896]{2,1,0:T(8,128)(2,1)S(1)}, bf16[8,32,896]{2,1,0:T(8,128)(2,1)S(1)}, u32[]{:S(2)}, u32[]{:S(2)}) collective-permute-start(bf16[8,32,896]{2,1,0:T(8,128)(2,1)S(1)} %join_panels.1.refs_0_), channel_id=1, source_target_pairs={{0,1},{1,0},{2,3},{3,2},{4,5},{5,4},{6,7},{7,6},{8,9},{9,8},{10,11... | collective-permute-start | bytes 1376264 | tf_op jit(solution)/shard_map/ppermute | solution.py:489
  36.8 5.2 %collective-permute-start.11 = (bf16[2,64,64]{2,1,0:T(8,128)(2,1)S(1)}, bf16[2,64,64]{2,1,0:T(8,128)(2,1)S(1)}, u32[]{:S(2)}, u32[]{:S(2)}) collective-permute-start(bf16[2,64,64]{2,1,0:T(8,128)(2,1)S(1)} %get-tuple-element.40), channel_id=1, source_target_pairs={{0,1},{1,0},{2,3},{3,2},{4,5},{5,4},{6,7},{7,6},{8,9},{9,8},{10,11... | collective-permute-start | bytes 49160 | tf_op jit(solution)/shard_map/ppermute | solution.py:489
  37.2 6.1 %collective-permute-start.12 = (bf16[2,64,64]{2,1,0:T(8,128)(2,1)S(1)}, bf16[2,64,64]{2,1,0:T(8,128)(2,1)S(1)}, u32[]{:S(2)}, u32[]{:S(2)}) collective-permute-start(bf16[2,64,64]{2,1,0:T(8,128)(2,1)S(1)} %get-tuple-element.41), channel_id=1, source_target_pairs={{1,2},{3,4},{5,6},{7,8},{9,10},{11,12},{13,14},{2,1},{4,3},{6,5},{... | collective-permute-start | bytes 49160 | tf_op jit(solution)/shard_map/ppermute | solution.py:549

commit v5 on v4

--- a/solution.py
+++ b/solution.py
@@ -34,19 +34,9 @@
     return sum(((offset >> bit) & 1) << to for bit, to in turns)
 
 
-def own_body(
-    turns, blocks_here, tile_ref, home, blocks, lens, queries_from, own_from, packed, sums, slots,
-    queries, own, sems
-):
+def own_body(turns, blocks_here, groups, tile_ref, home, blocks, lens, queries, own, packed, sums, slots):
     tokens = queries.shape[0]
     tile = tile_ref[0]
-    span = GROUP * HEAD_DIM
-    copies = [pltpu.make_async_copy(own_from, own, sems.at[KV_HEADS])]
-    for g in range(KV_HEADS):
-        part = pl.ds(g * span, span)
-        copies.append(pltpu.make_async_copy(queries_from.at[:, part], queries.at[:, part], sems.at[g]))
-    for copy in copies:
-        copy.start()
     for place in range(slots.shape[0]):
         slots[place] = -1
 
@@ -55,11 +45,9 @@
         slots[place_of((stored // blocks_here) ^ tile, turns)] = stored % blocks_here
         return carry
 
-    lax.fori_loop(0, lens[tile], find, 0)
-
-    copies[0].wait()
-    for g in range(KV_HEADS):
-        copies[1 + g].wait()
+    if groups[-1] == KV_HEADS - 1:
+        lax.fori_loop(0, lens[tile], find, 0)
+    for index, g in enumerate(groups):
         query = jnp.concatenate([queries[:, head_columns(g * GROUP + h)] for h in range(GROUP)], axis=0)
         value = jnp.concatenate(
             [own[:, head_columns(KV_HEADS + g)], jnp.ones((tokens, HEAD_DIM), BF16)], axis=1
@@ -71,44 +59,41 @@
         weights = jnp.exp2((score - top) * SCALE).astype(BF16)
         mixed = jnp.dot(weights, value, preferred_element_type=F32)
         total = mixed[:, HEAD_DIM:]
-        sums[g] = mixed[:, :HEAD_DIM] / total
+        sums[index] = mixed[:, :HEAD_DIM] / total
         level = top + jnp.log2(total) * (1.0 / SCALE)
         high = level.astype(BF16).astype(F32)
         middle = (level - high).astype(BF16).astype(F32)
         low = level - high - middle
         lane = lax.broadcasted_iota(jnp.int32, level.shape, 1)
         extra = jnp.where(lane == 0, high, jnp.where(lane == 1, middle, jnp.where(lane == 2, low, 0.0)))
-        packed[g, :, :HEAD_DIM] = query
-        packed[g, :, HEAD_DIM:] = extra.astype(BF16)
-
-
-def attend_own(tile, block_home, block_list, list_len, query_rows, own_rows, turns, blocks_here):
+        packed[index, :, :HEAD_DIM] = query
+        packed[index, :, HEAD_DIM:] = extra.astype(BF16)
+
+
+def attend_own(groups, tile, block_home, block_list, list_len, query_rows, own_rows, turns, blocks_here):
     tokens, width = query_rows.shape
     rows = GROUP * tokens
     return pl.pallas_call(
-        functools.partial(own_body, turns, blocks_here),
-        in_specs=[SCALARS] * 4 + [ANYWHERE] * 2,
+        functools.partial(own_body, turns, blocks_here, groups),
+        in_specs=[SCALARS] * 4 + [WHOLE] * 2,
         out_specs=[WHOLE, WHOLE, SCALARS],
         out_shape=[
-            jax.ShapeDtypeStruct((KV_HEADS, rows, 2 * HEAD_DIM), BF16),
-            jax.ShapeDtypeStruct((KV_HEADS, rows, HEAD_DIM), F32),
+            jax.ShapeDtypeStruct((len(groups), rows, 2 * HEAD_DIM), BF16),
+            jax.ShapeDtypeStruct((len(groups), rows, HEAD_DIM), F32),
             jax.ShapeDtypeStruct((1 << len(turns),), jnp.int32),
         ],
-        scratch_shapes=[
-            pltpu.VMEM(query_rows.shape, BF16),
-            pltpu.VMEM(own_rows.shape, BF16),
-            pltpu.SemaphoreType.DMA((KV_HEADS + 1,)),
-        ],
-        compiler_params=params(24),
+        compiler_params=params(20),
         cost_estimate=pl.CostEstimate(
-            flops=12 * tokens * tokens * width, bytes_accessed=10 * tokens * width, transcendentals=0
+            flops=3 * len(groups) * tokens * tokens * width, bytes_accessed=0, transcendentals=0
         ),
         name="attend_own",
     )(tile, block_home, block_list, list_len, query_rows, own_rows)
 
 
-def past_body(sizes, slots, packed, sums, *refs):
+def past_body(sizes, split, slots, *refs):
+    packed, sums, refs = refs[:split], refs[split : 2 * split], refs[2 * split :]
     gathered, (out, keys, values, worst) = refs[: len(sizes)], refs[len(sizes) :]
+    groups = KV_HEADS // split
     blocks_here = sum(ref.shape[0] for ref in gathered) // sum(sizes)
     block_tokens = gathered[0].shape[1]
     tokens = out.shape[0]
@@ -145,9 +130,14 @@
             return step, slice(None)
         return step // GROUP, pl.ds(pl.multiple_of((step % GROUP) * tokens, tokens), tokens)
 
+    def own_part(arrays, g, rows):
+        if split == 1:
+            return arrays[0][g, rows]
+        return arrays[g // groups][g % groups, rows]
+
     def scores(g, rows):
         return SCALE * lax.dot_general(
-            packed[g, rows], keys[g], (((1,), (1,)), ((), ())), preferred_element_type=F32
+            own_part(packed, g, rows), keys[g], (((1,), (1,)), ((), ())), preferred_element_type=F32
         )
 
     def emit(step, attended):
@@ -163,7 +153,7 @@
         weights = jnp.exp2(scores(g, rows)).astype(BF16)
         mixed = jnp.dot(weights, values[g], preferred_element_type=F32)
         below = mixed[:, HEAD_DIM:] + 1.0
-        emit(step, (mixed[:, :HEAD_DIM] + sums[g, rows]) / below)
+        emit(step, (mixed[:, :HEAD_DIM] + own_part(sums, g, rows)) / below)
         return jnp.maximum(largest, jnp.max(below.reshape((-1,) + largest.shape), axis=0))
 
     worst[...] = over_steps(quick, jnp.zeros(worst.shape, F32))
@@ -177,20 +167,22 @@
             weights = jnp.exp2(score - top).astype(BF16)
             mixed = jnp.dot(weights, values[g], preferred_element_type=F32)
             share = jnp.exp2(-top)
-            emit(step, (mixed[:, :HEAD_DIM] + share * sums[g, rows]) / (mixed[:, HEAD_DIM:] + share))
+            joined = mixed[:, :HEAD_DIM] + share * own_part(sums, g, rows)
+            emit(step, joined / (mixed[:, HEAD_DIM:] + share))
             return carry
 
         over_steps(careful, 0)
 
 
 def attend_past(slots, packed, sums, gathered, blocks_here):
-    heads, rows, _ = packed.shape
+    heads = KV_HEADS
+    rows = packed[0].shape[1]
     tokens = rows // GROUP
     sizes = [array.shape[0] // blocks_here for array in gathered]
     keys = sum(sizes) * gathered[0].shape[1]
     return pl.pallas_call(
-        functools.partial(past_body, sizes),
-        in_specs=[SCALARS] + [WHOLE] * (2 + len(gathered)),
+        functools.partial(past_body, sizes, len(packed)),
+        in_specs=[SCALARS] + [WHOLE] * (2 * len(packed) + len(gathered)),
         out_specs=WHOLE,
         out_shape=jax.ShapeDtypeStruct((tokens, HEADS * HEAD_DIM), BF16),
         scratch_shapes=[
@@ -203,7 +195,7 @@
             flops=8 * heads * rows * keys * HEAD_DIM, bytes_accessed=heads * rows * 1024, transcendentals=0
         ),
         name="attend_past",
-    )(slots, packed, sums, *gathered)
+    )(slots, *packed, *sums, *gathered)
 
 
 def join_body(*refs):
@@ -226,25 +218,25 @@
     )(*parts)
 
 
-def pack_body(final, decode, out):
+def pack_body(final, decode, final_across, decode_across, out):
     half = final.shape[0] // 2
     blank = out.shape[2] - 2 * final.shape[1] - decode.shape[1]
-    out[0] = jnp.concatenate(
-        [final[:half], final[half:], decode[...], jnp.zeros((half, blank), BF16)], axis=1
-    )
-
-
-def pack(final, decode):
+    for k, (left, right) in enumerate(((final, decode), (final_across, decode_across))):
+        out[k] = jnp.concatenate(
+            [left[:half], left[half:], right[...], jnp.zeros((half, blank), BF16)], axis=1
+        )
+
+
+def pack(final, decode, final_across, decode_across):
     lanes = -(-(2 * final.shape[1] + decode.shape[1]) // 128) * 128
     return pl.pallas_call(
         pack_body,
-        in_specs=[WHOLE, WHOLE],
+        in_specs=[WHOLE] * 4,
         out_specs=WHOLE,
-        out_shape=jax.ShapeDtypeStruct((1, decode.shape[0], lanes), BF16),
+        out_shape=jax.ShapeDtypeStruct((2, decode.shape[0], lanes), BF16),
         compiler_params=params(4),
-        cost_estimate=pl.CostEstimate(flops=5 * 10**9, bytes_accessed=0, transcendentals=0),
         name="pack",
-    )(final, decode)
+    )(final, decode, final_across, decode_across)
 
 
 def project_body(order, shape, depth, tile_ref, attended, *refs):
@@ -338,7 +330,39 @@
     return jnp.concatenate(chunks, axis=1)
 
 
-def inner_body(lat, predicted, kernel, features, edges, wide, done, sems):
+def spread_body(lat, patch_rows, inner, outer):
+    span = 3 * lat
+    for side in range(2):
+        source = lax.broadcasted_iota(jnp.int32, inner.shape[2:], 0)
+        target = lax.broadcasted_iota(jnp.int32, inner.shape[2:], 1)
+        for r in range(patch_rows):
+            upper = target // span - 2 * r
+            wanted = (upper >= 0) & (upper < 2) & (source == upper * 2 * lat + side * lat + target % lat)
+            inner[side, r] = jnp.where(wanted, 1.0, 0.0).astype(BF16)
+        source = lax.broadcasted_iota(jnp.int32, outer.shape[2:], 0)
+        target = lax.broadcasted_iota(jnp.int32, outer.shape[2:], 1)
+        for edge in range(2):
+            wanted = source == (1 - edge) * 2 * lat + side * lat + target % lat
+            wanted = wanted & (target < 3 * span)
+            outer[edge, side] = jnp.where(wanted, 1.0, 0.0).astype(BF16)
+
+
+def spreads(lat, patch_rows):
+    tall = 2 * patch_rows
+    return pl.pallas_call(
+        functools.partial(spread_body, lat, patch_rows),
+        out_specs=[WHOLE, WHOLE],
+        out_shape=[
+            jax.ShapeDtypeStruct((2, patch_rows, 4 * lat, -(-tall * 3 * lat // 128) * 128), BF16),
+            jax.ShapeDtypeStruct((2, 2, 4 * lat, -(-9 * lat // 128) * 128), BF16),
+        ],
+        compiler_params=params(4),
+        cost_estimate=pl.CostEstimate(flops=5 * 10**9, bytes_accessed=0, transcendentals=0),
+        name="spreads",
+    )()
+
+
+def inner_body(lat, predicted, picks, kernel, features, edges, wide, done, sems):
     frames, patch_rows, patches, values = predicted.shape
     tall, broad = 2 * patch_rows, 2 * patches
     span = 3 * lat
@@ -346,18 +370,11 @@
     lanes = 128 * chunks
     wide[:, :, 0:8] = jnp.zeros((frames, chunks, 8, 128), F32)
     wide[:, :, 8 + broad :] = jnp.zeros((frames, chunks, 8, 128), F32)
-    source = lax.broadcasted_iota(jnp.int32, (values, lanes), 0)
-    target = lax.broadcasted_iota(jnp.int32, (values, lanes), 1)
     for side in range(2):
-        picks = []
-        for r in range(patch_rows):
-            upper = target // span - 2 * r
-            wanted = (upper >= 0) & (upper < 2) & (source == upper * 2 * lat + side * lat + target % lat)
-            picks.append(jnp.where(wanted, 1.0, 0.0).astype(BF16))
         for frame in range(frames):
             cells = jnp.zeros((patches, lanes), F32)
             for r in range(patch_rows):
-                cells += jnp.dot(predicted[frame, r], picks[r], preferred_element_type=F32)
+                cells += jnp.dot(predicted[frame, r], picks[side, r], preferred_element_type=F32)
             for chunk in range(chunks):
                 wide[frame, chunk, pl.ds(8 + side, patches, stride=2), :] = cells[:, 128 * chunk : 128 * (chunk + 1)]
     stacks = tap_rows(frames, [shifted(wide, f, broad, lat) for f in range(frames)], broad)
@@ -383,7 +400,7 @@
         copy.wait()
 
 
-def convolve_inner(predicted, kernel):
+def convolve_inner(predicted, picks, kernel):
     frames, patch_rows, patches, values = predicted.shape
     lat = values // 4
     tall, broad = 2 * patch_rows, 2 * patches
@@ -391,7 +408,7 @@
     lanes = -(-tall * 3 * lat // 128) * 128
     return pl.pallas_call(
         functools.partial(inner_body, lat),
-        in_specs=[WHOLE, WHOLE],
+        in_specs=[WHOLE] * 3,
         out_specs=[ANYWHERE, WHOLE],
         out_shape=[
             jax.ShapeDtypeStruct((frames, tall, broad, channels), BF16),
@@ -409,10 +426,10 @@
             transcendentals=0,
         ),
         name="convolve_inner",
-    )(predicted, kernel)
-
-
-def outer_body(lat, tile_ref, from_pair, from_next, kernel, edges, given, features, wide, done, sems):
+    )(predicted, picks, kernel)
+
+
+def outer_body(lat, tile_ref, from_pair, from_next, picks, kernel, edges, given, features, wide, done, sems):
     frames, patches, values = from_pair.shape
     even = tile_ref[0] % 2 == 0
     broad = 2 * patches
@@ -420,8 +437,6 @@
     span = 3 * lat
     chunks = wide.shape[2]
     lanes = 128 * chunks
-    source = lax.broadcasted_iota(jnp.int32, (values, lanes), 0)
-    target = lax.broadcasted_iota(jnp.int32, (values, lanes), 1)
     lane = lax.broadcasted_iota(jnp.int32, (broad, lanes), 1)
     copies = []
     for edge in range(2):
@@ -431,10 +446,8 @@
         wide[edge, :, :, 0:8] = jnp.zeros((frames, chunks, 8, 128), F32)
         wide[edge, :, :, 8 + broad :] = jnp.zeros((frames, chunks, 8, 128), F32)
         for side in range(2):
-            wanted = (source == (1 - edge) * 2 * lat + side * lat + target % lat) & (target < 3 * span)
-            pick = jnp.where(wanted, 1.0, 0.0).astype(BF16)
             for frame in range(frames):
-                spread = jnp.dot(cells[frame], pick, preferred_element_type=F32)
+                spread = jnp.dot(cells[frame], picks[edge, side], preferred_element_type=F32)
                 for chunk in range(chunks):
                     wide[edge, frame, chunk, pl.ds(8 + side, patches, stride=2), :] = spread[
                         :, 128 * chunk : 128 * (chunk + 1)
@@ -462,7 +475,7 @@
         copy.wait()
 
 
-def convolve_outer(tile, from_pair, from_next, kernel, edges, features):
+def convolve_outer(tile, from_pair, from_next, picks, kernel, edges, features):
     frames, patches, values = from_pair.shape
     lat = values // 4
     broad = 2 * patches
@@ -470,10 +483,10 @@
     lanes = -(-9 * lat // 128) * 128
     return pl.pallas_call(
         functools.partial(outer_body, lat),
-        in_specs=[SCALARS] + [WHOLE] * 4 + [ANYWHERE],
+        in_specs=[SCALARS] + [WHOLE] * 5 + [ANYWHERE],
         out_specs=ANYWHERE,
         out_shape=jax.ShapeDtypeStruct(features.shape, BF16),
-        input_output_aliases={5: 0},
+        input_output_aliases={6: 0},
         scratch_shapes=[
             pltpu.VMEM((2, frames, lanes // 128, broad + 16, 128), F32),
             pltpu.VMEM((2, frames, broad, channels), BF16),
@@ -481,7 +494,7 @@
         ],
         compiler_params=params(16),
         name="convolve_outer",
-    )(tile, from_pair, from_next, kernel, edges, features)
+    )(tile, from_pair, from_next, picks, kernel, edges, features)
 
 
 def exchange(value, offset):
@@ -501,30 +514,40 @@
     query_rows = queries.reshape(tokens, width)
     own_rows = own_kv.reshape(tokens, own_kv.shape[3])
     shape = (frames, patch_rows, patches)
+    inner_picks, outer_picks = spreads(columns // 4, patch_rows)
+    half = KV_HEADS // 2
+    lists = (tile, block_home, block_list, list_len)
     if count == 16 and columns == 2 * decoder_weight.shape[1]:
         far = [4, 8, 12]
         turns = [(2, 0), (3, 1), (1, 2), (0, 3)]
         line = [exchange(past_kv, k) for k in far]
-        panel = pack(final_weight.T, decoder_weight.T)
-        panel_across = exchange(panel, 2)
-        packed, sums, slots = attend_own(
-            tile, block_home, block_list, list_len, query_rows, own_rows, turns, blocks_here
-        )
-        *line, panel_across, slots = lax.optimization_barrier((*line, panel_across, slots))
-        line = join([past_kv] + line, "join_line")
-        across = exchange(line, 2)
-        beside = exchange(line, 1)
-        panels = join([panel, panel_across], "join_pair")
-        order = [k ^ x for k in [0] + far for x in (0, 2)]
+        final, decode = final_weight.T, decoder_weight.T
+        final_across, decode_across = exchange(final, 2), exchange(decode, 2)
+        own_rows, inner_picks, outer_picks = lax.optimization_barrier((own_rows, inner_picks, outer_picks))
+        packed, sums, _ = attend_own(range(half), *lists, query_rows, own_rows, turns, blocks_here)
+        *line, final_across, decode_across, packed = lax.optimization_barrier(
+            (*line, final_across, decode_across, packed)
+        )
+        near = join([past_kv] + line, "join_near")
+        across = exchange(near, 2)
+        beside = exchange(near, 1)
+        panels = pack(final, decode, final_across, decode_across)
+        panels_far, panels_near = exchange(panels, 8), exchange(panels, 4)
+        own_rows, near = lax.optimization_barrier((own_rows, near))
+        others = attend_own(range(half, KV_HEADS), *lists, query_rows, own_rows, turns, blocks_here)
+        packed, sums, slots = [packed, others[0]], [sums, others[1]], others[2]
+        across, beside, panels_far, panels_near, slots = lax.optimization_barrier(
+            (across, beside, panels_far, panels_near, slots)
+        )
+        gathered = [near, across, beside, exchange(across, 1)]
+        panels_last = exchange(panels_far, 4)
+        panels = join([panels, panels_far, panels_near], "join_panels")
+        panels_beside = exchange(panels, 1)
+        attended = attend_past(slots, packed, sums, gathered, blocks_here)
+        panels_last, panels_beside, attended = lax.optimization_barrier((panels_last, panels_beside, attended))
+        panels = [panels, panels_last, panels_beside, exchange(panels_last, 1)]
+        order = [k ^ x for k in (0, 8, 4, 12) for x in (0, 2)]
         order = order + [k ^ 1 for k in order]
-        panels_far = [exchange(panels, far[0])]
-        panels, across, beside = lax.optimization_barrier((panels, across, beside))
-        panels_far = panels_far + [exchange(panels, k) for k in far[1:]]
-        gathered = [line, across, beside, exchange(across, 1)]
-        attended = attend_past(slots, packed, sums, gathered, blocks_here)
-        *panels_far, attended = lax.optimization_barrier((*panels_far, attended))
-        panels = join([panels] + panels_far, "join_panels")
-        panels = [panels, exchange(panels, 1)]
         predicted, to_pair, to_next = project(tile, attended, panels, order, shape)
         decode = unpack(tile, panels, order, 2 * final_weight.shape[0], decoder_weight.shape[0])
     else:
@@ -533,9 +556,9 @@
         for bit in reversed(range(bits)):
             held = jnp.concatenate([held, exchange(held, 1 << bit)], axis=0)
         packed, sums, slots = attend_own(
-            tile, block_home, block_list, list_len, query_rows, own_rows, turns, blocks_here
-        )
-        attended = attend_past(slots, packed, sums, [held], blocks_here)
+            range(KV_HEADS), *lists, query_rows, own_rows, turns, blocks_here
+        )
+        attended = attend_past(slots, [packed], [sums], [held], blocks_here)
         final = lax.all_gather(final_weight, "seq", axis=0, tiled=True)
         decode = lax.all_gather(decoder_weight, "seq", axis=1, tiled=True)
         predicted = jnp.dot(attended, final, preferred_element_type=F32).astype(BF16)
@@ -544,11 +567,11 @@
         to_pair = jnp.where(even, rows[:, -1], rows[:, 0])
         to_next = jnp.where(even, rows[:, 0], rows[:, -1])
     predicted = predicted.reshape(shape + (columns,))
-    from_pair = exchange(to_pair, 1)
     swaps = [(i, i + 1) for i in range(1, count - 1, 2)] + [(i + 1, i) for i in range(1, count - 1, 2)]
     from_next = lax.ppermute(to_next, "seq", swaps)
-    features, edges = convolve_inner(predicted, decode)
-    return convolve_outer(tile, from_pair, from_next, decode, edges, features)
+    from_pair = exchange(to_pair, 1)
+    features, edges = convolve_inner(predicted, inner_picks, decode)
+    return convolve_outer(tile, from_pair, from_next, outer_picks, decode, edges, features)
 
 
 def solution(mesh):

time: 44.9 us -> 37.5 us (0.84)
  the two profiles are of different devices: /device:TPU:15 before, /device:TPU:1 now
where the time goes in v5:
time: 37.5 us; the launch traced here: 37.3 us
  starting transfers between devices  17.2 us (46%)
  Pallas kernels  11.4 us (30%)
  waiting for transfers between devices  7.38 us (20%)
  local copies, waits for them, and re-layouts  1.15 us (3%)
    ppermute x14, starting transfers between devices, exchange(): return lax.ppermute(value, 'seq', [(i, i ^ offset) for i in range(count)])  15.2 us
    ppermute x14, waiting for transfers between devices, exchange(): return lax.ppermute(value, 'seq', [(i, i ^ offset) for i in range(count)])  5.93 us
    pallas_call x2, Pallas kernels, attend_own(): pl.pallas_call(functools.partial(own_body, turns, blocks_here, groups), i...  4.65 us
    pallas_call x1, Pallas kernels, attend_past(): pl.pallas_call(functools.partial(past_body, sizes, len(packed)), in_specs...  2.89 us
    ppermute x1, starting transfers between devices, local(): from_next = lax.ppermute(to_next, 'seq', swaps)  2.05 us
    ppermute x1, waiting for transfers between devices, local(): from_next = lax.ppermute(to_next, 'seq', swaps)  1.45 us
    pallas_call x1, Pallas kernels, convolve_inner(): pl.pallas_call(functools.partial(inner_body, lat), in_specs=[WHOLE] * 3,...  1.43 us
    pallas_call x1, Pallas kernels, convolve_outer(): pl.pallas_call(functools.partial(outer_body, lat), in_specs=[SCALARS] + [...  1.33 us
  transfers between devices with their start and end apart: 15, of which 6 were waited for; matrix products, arithmetic and copies ran while one was open for 0% of the time, Pallas kernels for 25%

profile of v5, /device:TPU:1, one launch (start us, length us, event | category | flops | bytes accessed | tf_op | source)
XLA Modules:
  0.0 37.3 jit_solution(314009722333081177)
XLA Ops:
  0.0 2.1 %collective-permute-start = (bf16[2,16,1024]{2,1,0:T(8,128)(2,1)}, bf16[2,16,1024]{2,1,0:T(8,128)(2,1)S(1)}, u32[]{:S(2)}, u32[]{:S(2)}) collective-permute-start(bf16[2,16,1024]{2,1,0:T(8,128)(2,1)} %refs_0_.1), channel_id=1, source_target_pairs={{0,4},{1,5},{2,6},{3,7},{4,0},{5,1},{6,2},{7,3},{8,12},{9,13},{10,... | collective-permute-start | bytes 196616 | tf_op jit(solution)/shard_map/ppermute | solution.py:502
  2.1 2.3 %collective-permute-start.1 = (bf16[2,16,1024]{2,1,0:T(8,128)(2,1)}, bf16[2,16,1024]{2,1,0:T(8,128)(2,1)S(1)}, u32[]{:S(2)}, u32[]{:S(2)}) collective-permute-start(bf16[2,16,1024]{2,1,0:T(8,128)(2,1)} %refs_0_.1), channel_id=1, source_target_pairs={{0,8},{1,9},{2,10},{3,11},{4,12},{5,13},{6,14},{7,15},{8,0},{9,1},... | collective-permute-start | bytes 196616 | tf_op jit(solution)/shard_map/ppermute | solution.py:502
  4.4 0.0 collective-permute-start.2
  4.4 1.2 %collective-permute-start.3 = (bf16[64,192]{1,0:T(8,128)(2,1)}, bf16[64,192]{1,0:T(8,128)(2,1)S(1)}, u32[]{:S(2)}, u32[]{:S(2)}) collective-permute-start(bf16[64,192]{1,0:T(8,128)(2,1)} %bitcast.6), channel_id=1, source_target_pairs={{0,2},{1,3},{2,0},{3,1},{4,6},{5,7},{6,4},{7,5},{8,10},{9,11},{10,... | collective-permute-start | bytes 73736 | tf_op jit(solution)/shard_map/ppermute | solution.py:502
  5.7 0.0 copy-start.3
  5.7 0.0 copy-start.4
  5.7 0.0 copy-start.5
  5.7 0.0 copy-start.6
  5.7 0.0 copy-start.7
  5.7 0.3 collective-permute-start.4
  6.0 1.0 %copy-done.3 = bf16[2,2,64,3072]{3,2,1,0:T(8,128)(2,1)S(1)} copy-done((bf16[2,2,64,3072]{3,2,1,0:T(8,128)(2,1)S(1)}, bf16[2,2,64,3072]{3,2,1,0:T(8,128)(2,1)}, u32[]{:S(2)}) %copy-start.3) | copy-done | bytes 1572888
  7.1 0.1 copy-done.4
  7.2 0.0 copy-done.5
  7.2 0.0 copy-done.6
  7.2 0.0 copy-done.7
  7.2 0.0 copy-start
  7.2 0.0 copy-start.1
  7.2 0.0 copy-start.2
  7.2 2.3 %attend_own.2 = (bf16[2,1536,256]{2,1,0:T(8,128)(2,1)S(1)}, f32[2,1536,128]{2,1,0:T(8,128)S(1)}, s32[16]{0:T(128)}) custom-call(s32[1]{0:T(128)} %bitcast.tile_ref, s32[32]{0:T(128)S(1)} %copy-done.6, s32[16,16]{1,0:T(8,128)S(1)} %copy-done.5, s32[16]{0:T(128)S(1)} %copy-done.7, bf16[256,3072]{1,0:T(8,128)(2,1)S(1)} %bitcast.10, bf16[256,1024]{1,0:T(8,128)(2,1)S(1)} %bitcast.12), custom_call_target="tpu_custom_call" | custom-call | flops 1207959552 | tf_op jit(solution)/shard_map/attend_own/pallas_call | solution.py:76
  9.5 0.0 collective-permute-done.3.final_across
  9.5 0.0 collective-permute-done.4.decode_across
  9.5 0.0 collective-permute-done.refs_1_
  9.5 0.0 collective-permute-done.1.refs_2_
  9.5 0.1 collective-permute-done.2.refs_3_
  9.7 0.0 copy-done
  9.7 1.3 %collective-permute-start.5 = (bf16[8,16,1024]{2,1,0:T(8,128)(2,1)S(1)}, bf16[8,16,1024]{2,1,0:T(8,128)(2,1)S(1)}, u32[]{:S(2)}, u32[]{:S(2)}) collective-permute-start(bf16[8,16,1024]{2,1,0:T(8,128)(2,1)S(1)} %join_near.1.refs_4_), channel_id=1, source_target_pairs={{0,2},{1,3},{2,0},{3,1},{4,6},{5,7},{6,4},{7,5},{8,10},{9,11},{10,... | collective-permute-start | bytes 786440 | tf_op jit(solution)/shard_map/ppermute | solution.py:502
  11.0 2.6 %collective-permute-start.6 = (bf16[8,16,1024]{2,1,0:T(8,128)(2,1)S(1)}, bf16[8,16,1024]{2,1,0:T(8,128)(2,1)S(1)}, u32[]{:S(2)}, u32[]{:S(2)}) collective-permute-start(bf16[8,16,1024]{2,1,0:T(8,128)(2,1)S(1)} %join_near.1.refs_4_), channel_id=1, source_target_pairs={{0,1},{1,0},{2,3},{3,2},{4,5},{5,4},{6,7},{7,6},{8,9},{9,8},{10,11... | collective-permute-start | bytes 786440 | tf_op jit(solution)/shard_map/ppermute | solution.py:502
  13.6 0.0 copy-done.1
  13.6 0.0 copy-done.2
  13.6 0.1 pack.1.refs_0_
  13.6 1.3 %collective-permute-start.7 = (bf16[2,32,896]{2,1,0:T(8,128)(2,1)S(1)}, bf16[2,32,896]{2,1,0:T(8,128)(2,1)S(1)}, u32[]{:S(2)}, u32[]{:S(2)}) collective-permute-start(bf16[2,32,896]{2,1,0:T(8,128)(2,1)S(1)} %pack.1.refs_0_), channel_id=1, source_target_pairs={{0,8},{1,9},{2,10},{3,11},{4,12},{5,13},{6,14},{7,15},{8,0},{9,1},... | collective-permute-start | bytes 344072 | tf_op jit(solution)/shard_map/ppermute | solution.py:502
  15.0 1.0 %collective-permute-start.8 = (bf16[2,32,896]{2,1,0:T(8,128)(2,1)S(1)}, bf16[2,32,896]{2,1,0:T(8,128)(2,1)S(1)}, u32[]{:S(2)}, u32[]{:S(2)}) collective-permute-start(bf16[2,32,896]{2,1,0:T(8,128)(2,1)S(1)} %pack.1.refs_0_), channel_id=1, source_target_pairs={{0,4},{1,5},{2,6},{3,7},{4,0},{5,1},{6,2},{7,3},{8,12},{9,13},{10,... | collective-permute-start | bytes 344072 | tf_op jit(solution)/shard_map/ppermute | solution.py:502
  16.0 2.4 %attend_own.3 = (bf16[2,1536,256]{2,1,0:T(8,128)(2,1)S(1)}, f32[2,1536,128]{2,1,0:T(8,128)S(1)}, s32[16]{0:T(128)S(1)}) custom-call(s32[1]{0:T(128)} %bitcast.tile_ref, s32[32]{0:T(128)S(1)} %copy-done.6, s32[16,16]{1,0:T(8,128)S(1)} %copy-done.5, s32[16]{0:T(128)S(1)} %copy-done.7, bf16[256,3072]{1,0:T(8,128)(2,1)S(1)} %bitcast.11, ...), custom_call_target="tpu_custom_call" | custom-call | flops 1207959552 | tf_op jit(solution)/shard_map/attend_own/pallas_call | solution.py:76
  18.4 3.5 %collective-permute-done.7.refs_1_ = bf16[2,32,896]{2,1,0:T(8,128)(2,1)S(1)} collective-permute-done((bf16[2,32,896]{2,1,0:T(8,128)(2,1)S(1)}, bf16[2,32,896]{2,1,0:T(8,128)(2,1)S(1)}, u32[]{:S(2)}, u32[]{:S(2)}) %collective-permute-start.7) | collective-permute-done | bytes 114720 | tf_op jit(solution)/shard_map/ppermute | solution.py:502
  21.9 0.0 collective-permute-done.8.refs_2_
  21.9 0.0 collective-permute-done.5.refs_5_
  21.9 0.0 collective-permute-done.6.refs_6_
  21.9 1.1 %collective-permute-start.11 = (bf16[8,16,1024]{2,1,0:T(8,128)(2,1)S(1)}, bf16[8,16,1024]{2,1,0:T(8,128)(2,1)S(1)}, u32[]{:S(2)}, u32[]{:S(2)}) collective-permute-start(bf16[8,16,1024]{2,1,0:T(8,128)(2,1)S(1)} %collective-permute-done.5.refs_5_), channel_id=1, source_target_pairs={{0,1},{1,0},{2,3},{3,2},{4,5},{5,4},{6,7},{7,6},{8,9},{9,8},{10,11... | collective-permute-start | bytes 786440 | tf_op jit(solution)/shard_map/ppermute | solution.py:502
  23.0 0.1 collective-permute-start.10
  23.1 0.1 collective-permute-start.9
  23.2 0.9 %collective-permute-done.11.refs_7_ = bf16[8,16,1024]{2,1,0:T(8,128)(2,1)S(1)} collective-permute-done((bf16[8,16,1024]{2,1,0:T(8,128)(2,1)S(1)}, bf16[8,16,1024]{2,1,0:T(8,128)(2,1)S(1)}, u32[]{:S(2)}, u32[]{:S(2)}) %collective-permute-start.11) | collective-permute-done | bytes 262176 | tf_op jit(solution)/shard_map/ppermute | solution.py:502
  24.1 2.9 %attend_past.1.attended = bf16[256,3072]{1,0:T(8,128)(2,1)S(1)} custom-call(s32[16]{0:T(128)S(1)} %get-tuple-element.49.slots, bf16[2,1536,256]{2,1,0:T(8,128)(2,1)S(1)} %get-tuple-element.50.refs_0_, bf16[2,1536,256]{2,1,0:T(8,128)(2,1)S(1)} %get-tuple-element.51.refs_1_, f32[2,1536,128]{2,1,0:T(8,128)S(1)} %get-tuple-element.52.refs_2_, ...), custom_call_target="tpu_custom_call" | custom-call | flops 1610612736 | bytes 6291456 | tf_op jit(solution)/shard_map/attend_past/pallas_call | solution.py:183
  27.0 0.4 %collective-permute-done.9.refs_1_ = bf16[2,32,896]{2,1,0:T(8,128)(2,1)S(1)} collective-permute-done((bf16[2,32,896]{2,1,0:T(8,128)(2,1)S(1)}, bf16[2,32,896]{2,1,0:T(8,128)(2,1)S(1)}, u32[]{:S(2)}, u32[]{:S(2)}) %collective-permute-start.9) | collective-permute-done | bytes 114720 | tf_op jit(solution)/shard_map/ppermute | solution.py:502
  27.4 0.0 collective-permute-done.10.refs_2_
  27.4 1.3 %collective-permute-start.12 = (bf16[2,32,896]{2,1,0:T(8,128)(2,1)S(1)}, bf16[2,32,896]{2,1,0:T(8,128)(2,1)S(1)}, u32[]{:S(2)}, u32[]{:S(2)}) collective-permute-start(bf16[2,32,896]{2,1,0:T(8,128)(2,1)S(1)} %collective-permute-done.9.refs_1_), channel_id=1, source_target_pairs={{0,1},{1,0},{2,3},{3,2},{4,5},{5,4},{6,7},{7,6},{8,9},{9,8},{10,11... | collective-permute-start | bytes 344072 | tf_op jit(solution)/shard_map/ppermute | solution.py:502
  28.7 1.0 %collective-permute-done.12.refs_3_ = bf16[2,32,896]{2,1,0:T(8,128)(2,1)S(1)} collective-permute-done((bf16[2,32,896]{2,1,0:T(8,128)(2,1)S(1)}, bf16[2,32,896]{2,1,0:T(8,128)(2,1)S(1)}, u32[]{:S(2)}, u32[]{:S(2)}) %collective-permute-start.12) | collective-permute-done | bytes 114720 | tf_op jit(solution)/shard_map/ppermute | solution.py:502
  29.7 0.7 %project.1 = (bf16[256,64]{1,0:T(8,128)(2,1)S(1)}, bf16[2,64,64]{2,1,0:T(8,128)(2,1)S(1)}, bf16[2,64,64]{2,1,0:T(8,128)(2,1)S(1)}) custom-call(s32[1]{0:T(128)} %bitcast.tile_ref, bf16[256,3072]{1,0:T(8,128)(2,1)S(1)} %attend_past.1.attended, bf16[6,32,896]{2,1,0:T(8,128)(2,1)S(1)} %join_panels.1.refs_0_, ...), custom_call_target="tpu_custom_call" | custom-call | tf_op jit(solution)/shard_map/project/pallas_call | solution.py:273
  30.4 0.4 %collective-permute-start.13 = (bf16[2,64,64]{2,1,0:T(8,128)(2,1)S(1)}, bf16[2,64,64]{2,1,0:T(8,128)(2,1)S(1)}, u32[]{:S(2)}, u32[]{:S(2)}) collective-permute-start(bf16[2,64,64]{2,1,0:T(8,128)(2,1)S(1)} %get-tuple-element.60), channel_id=1, source_target_pairs={{0,1},{1,0},{2,3},{3,2},{4,5},{5,4},{6,7},{7,6},{8,9},{9,8},{10,11... | collective-permute-start | bytes 49160 | tf_op jit(solution)/shard_map/ppermute | solution.py:502
  30.8 2.0 %collective-permute-start.14 = (bf16[2,64,64]{2,1,0:T(8,128)(2,1)S(1)}, bf16[2,64,64]{2,1,0:T(8,128)(2,1)S(1)}, u32[]{:S(2)}, u32[]{:S(2)}) collective-permute-start(bf16[2,64,64]{2,1,0:T(8,128)(2,1)S(1)} %get-tuple-element.61), channel_id=1, source_target_pairs={{1,2},{3,4},{5,6},{7,8},{9,10},{11,12},{13,14},{2,1},{4,3},{6,5},{... | collective-permute-start | bytes 49160 | tf_op jit(solution)/shard_map/ppermute | solution.py:571
  32.8 0.3 unpack.1.kernel
  33.1 1.4 %convolve_inner.1 = (bf16[2,4,128,512]{3,2,1,0:T(8,128)(2,1)}, f32[2,256,512]{2,1,0:T(8,128)S(1)}) custom-call(bf16[2,2,64,64]{3,2,1,0:T(8,128)(2,1)S(1)} %bitcast.14, bf16[2,2,64,256]{3,2,1,0:T(8,128)(2,1)S(1)} %get-tuple-element.64.picks, bf16[432,512]{1,0:T(8,128)(2,1)S(1)} %unpack.1.kernel), custom_call_target="tpu_custom_call" | custom-call | flops 452984832 | bytes 1048576 | tf_op jit(solution)/shard_map/convolve_inner/pallas_call | solution.py:409
  34.6 0.0 collective-permute-done.13.from_pair
  34.6 1.4 %collective-permute-done.14.from_next = bf16[2,64,64]{2,1,0:T(8,128)(2,1)S(1)} collective-permute-done((bf16[2,64,64]{2,1,0:T(8,128)(2,1)S(1)}, bf16[2,64,64]{2,1,0:T(8,128)(2,1)S(1)}, u32[]{:S(2)}, u32[]{:S(2)}) %collective-permute-start.14) | collective-permute-done | bytes 16416 | tf_op jit(solution)/shard_map/ppermute | solution.py:571
  36.0 1.3 %convolve_outer.1 = bf16[2,4,128,512]{3,2,1,0:T(8,128)(2,1)} custom-call(s32[1]{0:T(128)} %bitcast.tile_ref, bf16[2,64,64]{2,1,0:T(8,128)(2,1)S(1)} %collective-permute-done.13.from_pair, bf16[2,64,64]{2,1,0:T(8,128)(2,1)S(1)} %collective-permute-done.14.from_next, ...), custom_call_target="tpu_custom_call", output_to_operand_aliasing={{}: (6, {})} | custom-call | tf_op jit(solution)/shard_map/convolve_outer/pallas_call | solution.py:484
  (3 shorter events, 0.1 us)
Async XLA Ops:
  0.0 9.5 %collective-permute-start = (bf16[2,16,1024]{2,1,0:T(8,128)(2,1)}, bf16[2,16,1024]{2,1,0:T(8,128)(2,1)S(1)}, u32[]{:S(2)}, u32[]{:S(2)}) collective-permute-start(bf16[2,16,1024]{2,1,0:T(8,128)(2,1)} %refs_0_.1), channel_id=1, source_target_pairs={{0,4},{1,5},{2,6},{3,7},{4,0},{5,1},{6,2},{7,3},{8,12},{9,13},{10,... | collective-permute-start | bytes 196616 | tf_op jit(solution)/shard_map/ppermute | solution.py:502
  2.1 7.4 %collective-permute-start.1 = (bf16[2,16,1024]{2,1,0:T(8,128)(2,1)}, bf16[2,16,1024]{2,1,0:T(8,128)(2,1)S(1)}, u32[]{:S(2)}, u32[]{:S(2)}) collective-permute-start(bf16[2,16,1024]{2,1,0:T(8,128)(2,1)} %refs_0_.1), channel_id=1, source_target_pairs={{0,8},{1,9},{2,10},{3,11},{4,12},{5,13},{6,14},{7,15},{8,0},{9,1},... | collective-permute-start | bytes 196616 | tf_op jit(solution)/shard_map/ppermute | solution.py:502
  4.4 5.2 %collective-permute-start.2 = (bf16[2,16,1024]{2,1,0:T(8,128)(2,1)}, bf16[2,16,1024]{2,1,0:T(8,128)(2,1)S(1)}, u32[]{:S(2)}, u32[]{:S(2)}) collective-permute-start(bf16[2,16,1024]{2,1,0:T(8,128)(2,1)} %refs_0_.1), channel_id=1, source_target_pairs={{0,12},{1,13},{2,14},{3,15},{4,8},{5,9},{6,10},{7,11},{8,4},{9,5},... | collective-permute-start | bytes 196616 | tf_op jit(solution)/shard_map/ppermute | solution.py:502
  4.4 5.0 %collective-permute-start.3 = (bf16[64,192]{1,0:T(8,128)(2,1)}, bf16[64,192]{1,0:T(8,128)(2,1)S(1)}, u32[]{:S(2)}, u32[]{:S(2)}) collective-permute-start(bf16[64,192]{1,0:T(8,128)(2,1)} %bitcast.6), channel_id=1, source_target_pairs={{0,2},{1,3},{2,0},{3,1},{4,6},{5,7},{6,4},{7,5},{8,10},{9,11},{10,... | collective-permute-start | bytes 73736 | tf_op jit(solution)/shard_map/ppermute | solution.py:502
  5.7 1.4 %copy-start.3 = (bf16[2,2,64,3072]{3,2,1,0:T(8,128)(2,1)S(1)}, bf16[2,2,64,3072]{3,2,1,0:T(8,128)(2,1)}, u32[]{:S(2)}) copy-start(bf16[2,2,64,3072]{3,2,1,0:T(8,128)(2,1)} %param.8) | copy-start | bytes 4718596
  5.7 1.5 %copy-start.4 = (bf16[2,2,64,1024]{3,2,1,0:T(8,128)(2,1)S(1)}, bf16[2,2,64,1024]{3,2,1,0:T(8,128)(2,1)}, u32[]{:S(2)}) copy-start(bf16[2,2,64,1024]{3,2,1,0:T(8,128)(2,1)} %param.9) | copy-start | bytes 1572868
  5.7 1.5 %copy-start.5 = (s32[16,16]{1,0:T(8,128)S(1)}, s32[16,16]{1,0:T(8,128)}, u32[]{:S(2)}) copy-start(s32[16,16]{1,0:T(8,128)} %blocks.3) | copy-start | bytes 3076
  5.7 1.5 %copy-start.6 = (s32[32]{0:T(128)S(1)}, s32[32]{0:T(128)}, u32[]{:S(2)}) copy-start(s32[32]{0:T(128)} %home.3) | copy-start | bytes 388
  5.7 1.5 %copy-start.7 = (s32[16]{0:T(128)S(1)}, s32[16]{0:T(128)}, u32[]{:S(2)}) copy-start(s32[16]{0:T(128)} %lens.3) | copy-start | bytes 196
  5.7 3.8 %collective-permute-start.4 = (bf16[32,432]{1,0:T(8,128)(2,1)}, bf16[32,432]{1,0:T(8,128)(2,1)S(1)}, u32[]{:S(2)}, u32[]{:S(2)}) collective-permute-start(bf16[32,432]{1,0:T(8,128)(2,1)} %bitcast.8), channel_id=1, source_target_pairs={{0,2},{1,3},{2,0},{3,1},{4,6},{5,7},{6,4},{7,5},{8,10},{9,11},{10,... | collective-permute-start | bytes 82952 | tf_op jit(solution)/shard_map/ppermute | solution.py:502
  7.2 2.5 %copy-start = (bf16[2,16,1024]{2,1,0:T(8,128)(2,1)S(1)}, bf16[2,16,1024]{2,1,0:T(8,128)(2,1)}, u32[]{:S(2)}) copy-start(bf16[2,16,1024]{2,1,0:T(8,128)(2,1)} %refs_0_.1) | copy-start | bytes 196612
  7.2 6.4 %copy-start.1 = (bf16[192,64]{0,1:T(8,128)(2,1)S(1)}, bf16[192,64]{0,1:T(8,128)(2,1)}, u32[]{:S(2)}) copy-start(bf16[192,64]{0,1:T(8,128)(2,1)} %param.14) | copy-start | bytes 73732
  7.2 6.4 %copy-start.2 = (bf16[432,32]{0,1:T(8,128)(2,1)S(1)}, bf16[432,32]{0,1:T(8,128)(2,1)}, u32[]{:S(2)}) copy-start(bf16[432,32]{0,1:T(8,128)(2,1)} %param.15) | copy-start | bytes 82948
  9.7 12.2 %collective-permute-start.5 = (bf16[8,16,1024]{2,1,0:T(8,128)(2,1)S(1)}, bf16[8,16,1024]{2,1,0:T(8,128)(2,1)S(1)}, u32[]{:S(2)}, u32[]{:S(2)}) collective-permute-start(bf16[8,16,1024]{2,1,0:T(8,128)(2,1)S(1)} %join_near.1.refs_4_), channel_id=1, source_target_pairs={{0,2},{1,3},{2,0},{3,1},{4,6},{5,7},{6,4},{7,5},{8,10},{9,11},{10,... | collective-permute-start | bytes 786440 | tf_op jit(solution)/shard_map/ppermute | solution.py:502
  11.0 10.9 %collective-permute-start.6 = (bf16[8,16,1024]{2,1,0:T(8,128)(2,1)S(1)}, bf16[8,16,1024]{2,1,0:T(8,128)(2,1)S(1)}, u32[]{:S(2)}, u32[]{:S(2)}) collective-permute-start(bf16[8,16,1024]{2,1,0:T(8,128)(2,1)S(1)} %join_near.1.refs_4_), channel_id=1, source_target_pairs={{0,1},{1,0},{2,3},{3,2},{4,5},{5,4},{6,7},{7,6},{8,9},{9,8},{10,11... | collective-permute-start | bytes 786440 | tf_op jit(solution)/shard_map/ppermute | solution.py:502
  13.6 8.2 %collective-permute-start.7 = (bf16[2,32,896]{2,1,0:T(8,128)(2,1)S(1)}, bf16[2,32,896]{2,1,0:T(8,128)(2,1)S(1)}, u32[]{:S(2)}, u32[]{:S(2)}) collective-permute-start(bf16[2,32,896]{2,1,0:T(8,128)(2,1)S(1)} %pack.1.refs_0_), channel_id=1, source_target_pairs={{0,8},{1,9},{2,10},{3,11},{4,12},{5,13},{6,14},{7,15},{8,0},{9,1},... | collective-permute-start | bytes 344072 | tf_op jit(solution)/shard_map/ppermute | solution.py:502
  15.0 6.9 %collective-permute-start.8 = (bf16[2,32,896]{2,1,0:T(8,128)(2,1)S(1)}, bf16[2,32,896]{2,1,0:T(8,128)(2,1)S(1)}, u32[]{:S(2)}, u32[]{:S(2)}) collective-permute-start(bf16[2,32,896]{2,1,0:T(8,128)(2,1)S(1)} %pack.1.refs_0_), channel_id=1, source_target_pairs={{0,4},{1,5},{2,6},{3,7},{4,0},{5,1},{6,2},{7,3},{8,12},{9,13},{10,... | collective-permute-start | bytes 344072 | tf_op jit(solution)/shard_map/ppermute | solution.py:502
  21.9 2.2 %collective-permute-start.11 = (bf16[8,16,1024]{2,1,0:T(8,128)(2,1)S(1)}, bf16[8,16,1024]{2,1,0:T(8,128)(2,1)S(1)}, u32[]{:S(2)}, u32[]{:S(2)}) collective-permute-start(bf16[8,16,1024]{2,1,0:T(8,128)(2,1)S(1)} %collective-permute-done.5.refs_5_), channel_id=1, source_target_pairs={{0,1},{1,0},{2,3},{3,2},{4,5},{5,4},{6,7},{7,6},{8,9},{9,8},{10,11... | collective-permute-start | bytes 786440 | tf_op jit(solution)/shard_map/ppermute | solution.py:502
  23.0 4.4 %collective-permute-start.10 = (bf16[6,32,896]{2,1,0:T(8,128)(2,1)S(1)}, bf16[6,32,896]{2,1,0:T(8,128)(2,1)S(1)}, u32[]{:S(2)}, u32[]{:S(2)}) collective-permute-start(bf16[6,32,896]{2,1,0:T(8,128)(2,1)S(1)} %join_panels.1.refs_0_), channel_id=1, source_target_pairs={{0,1},{1,0},{2,3},{3,2},{4,5},{5,4},{6,7},{7,6},{8,9},{9,8},{10,11... | collective-permute-start | bytes 1032200 | tf_op jit(solution)/shard_map/ppermute | solution.py:502
  23.1 4.4 %collective-permute-start.9 = (bf16[2,32,896]{2,1,0:T(8,128)(2,1)S(1)}, bf16[2,32,896]{2,1,0:T(8,128)(2,1)S(1)}, u32[]{:S(2)}, u32[]{:S(2)}) collective-permute-start(bf16[2,32,896]{2,1,0:T(8,128)(2,1)S(1)} %collective-permute-done.7.refs_1_), channel_id=1, source_target_pairs={{0,4},{1,5},{2,6},{3,7},{4,0},{5,1},{6,2},{7,3},{8,12},{9,13},{10,... | collective-permute-start | bytes 344072 | tf_op jit(solution)/shard_map/ppermute | solution.py:502
  27.4 2.2 %collective-permute-start.12 = (bf16[2,32,896]{2,1,0:T(8,128)(2,1)S(1)}, bf16[2,32,896]{2,1,0:T(8,128)(2,1)S(1)}, u32[]{:S(2)}, u32[]{:S(2)}) collective-permute-start(bf16[2,32,896]{2,1,0:T(8,128)(2,1)S(1)} %collective-permute-done.9.refs_1_), channel_id=1, source_target_pairs={{0,1},{1,0},{2,3},{3,2},{4,5},{5,4},{6,7},{7,6},{8,9},{9,8},{10,11... | collective-permute-start | bytes 344072 | tf_op jit(solution)/shard_map/ppermute | solution.py:502
  30.4 4.2 %collective-permute-start.13 = (bf16[2,64,64]{2,1,0:T(8,128)(2,1)S(1)}, bf16[2,64,64]{2,1,0:T(8,128)(2,1)S(1)}, u32[]{:S(2)}, u32[]{:S(2)}) collective-permute-start(bf16[2,64,64]{2,1,0:T(8,128)(2,1)S(1)} %get-tuple-element.60), channel_id=1, source_target_pairs={{0,1},{1,0},{2,3},{3,2},{4,5},{5,4},{6,7},{7,6},{8,9},{9,8},{10,11... | collective-permute-start | bytes 49160 | tf_op jit(solution)/shard_map/ppermute | solution.py:502
  30.8 5.2 %collective-permute-start.14 = (bf16[2,64,64]{2,1,0:T(8,128)(2,1)S(1)}, bf16[2,64,64]{2,1,0:T(8,128)(2,1)S(1)}, u32[]{:S(2)}, u32[]{:S(2)}) collective-permute-start(bf16[2,64,64]{2,1,0:T(8,128)(2,1)S(1)} %get-tuple-element.61), channel_id=1, source_target_pairs={{1,2},{3,4},{5,6},{7,8},{9,10},{11,12},{13,14},{2,1},{4,3},{6,5},{... | collective-permute-start | bytes 49160 | tf_op jit(solution)/shard_map/ppermute | solution.py:571

commit v6 on v5

--- a/solution.py
+++ b/solution.py
@@ -239,49 +239,75 @@
     )(final, decode, final_across, decode_across)
 
 
-def project_body(order, shape, depth, tile_ref, attended, *refs):
-    *panels, out, to_pair, to_next, staged, whole = refs
+def project_pairs(offsets, depth, tile, attended, ours, theirs):
+    even = tile % 2 == 0
+    total = jnp.zeros((attended.shape[0], 2 * ours[0].shape[1]), F32)
+    ours = [(ref, k) for ref in ours for k in range(ref.shape[0])]
+    theirs = [(ref, k) for ref in theirs for k in range(ref.shape[0])]
+    for offset, (our, i), (their, j) in zip(offsets, ours, theirs):
+        left, right = our[i], their[j]
+        left, right = jnp.where(even, left, right), jnp.where(even, right, left)
+        rows = [
+            jnp.concatenate([panel[:, part * depth : (part + 1) * depth] for panel in (left, right)], axis=1)
+            for part in range(2)
+        ]
+        start = pl.multiple_of(((tile ^ offset) // 2) * (2 * depth), 128)
+        total += lax.dot_general(
+            attended[:, pl.ds(start, 2 * depth)],
+            jnp.concatenate(rows, axis=0),
+            (((1,), (1,)), ((), ())),
+            preferred_element_type=F32,
+        )
+    return total
+
+
+def project_body(offsets, depth, tile_ref, attended, ours, theirs, out):
+    out[...] = project_pairs(offsets, depth, tile_ref[0], attended, [ours], [theirs])
+
+
+def project(tile, attended, ours, theirs, offsets, depth):
+    return pl.pallas_call(
+        functools.partial(project_body, offsets, depth),
+        in_specs=[SCALARS] + [WHOLE] * 3,
+        out_specs=WHOLE,
+        out_shape=jax.ShapeDtypeStruct((attended.shape[0], 2 * ours.shape[1]), F32),
+        compiler_params=params(16),
+        name="project",
+    )(tile, attended, ours, theirs)
+
+
+def finish_body(offsets, depth, shape, tile_ref, attended, ours, theirs, part, out, to_pair, to_next):
     frames, patch_rows, patches = shape
-    place = 0
-    half = staged.shape[1]
-    for panel in panels:
-        for k in range(panel.shape[0]):
-            staged[tile_ref[0] ^ order[place]] = panel[k, :, : staged.shape[2]]
-            place += 1
-    for device in range(len(order)):
-        for part in range(2):
-            whole[part * half : (part + 1) * half, device * depth : (device + 1) * depth] = staged[
-                device, :, part * depth : (part + 1) * depth
-            ]
-    predicted = lax.dot_general(
-        attended[...], whole[...], (((1,), (1,)), ((), ())), preferred_element_type=F32
-    ).astype(BF16)
+    tile = tile_ref[0]
+    predicted = part[...] + project_pairs(offsets, depth, tile, attended, [ours], [theirs])
+    predicted = predicted.astype(BF16)
     out[...] = predicted
-    even = tile_ref[0] % 2 == 0
+    even = tile % 2 == 0
+    values = predicted.shape[1] // 2
+    folds = 128 // values
+    count = patches // folds
+
+    def folded(rows):
+        return jnp.concatenate([rows[k * count : (k + 1) * count] for k in range(folds)], axis=1)
+
     for frame in range(frames):
         rows = predicted[frame * patch_rows * patches : (frame + 1) * patch_rows * patches]
-        first, last = rows[:patches], rows[(patch_rows - 1) * patches :]
+        first, last = folded(rows[:patches, :values]), folded(rows[(patch_rows - 1) * patches :, values:])
         to_pair[frame] = jnp.where(even, last, first)
         to_next[frame] = jnp.where(even, first, last)
 
 
-def project(tile, attended, panels, order, shape):
-    tokens, width = attended.shape
-    half = panels[0].shape[1]
-    depth = width // len(order)
-    border = jax.ShapeDtypeStruct((shape[0], shape[2], 2 * half), BF16)
-    return pl.pallas_call(
-        functools.partial(project_body, order, shape, depth),
-        in_specs=[SCALARS] + [WHOLE] * (1 + len(panels)),
+def finish(tile, attended, ours, theirs, part, offsets, depth, shape):
+    tokens, columns = part.shape
+    border = jax.ShapeDtypeStruct((shape[0], shape[2] * (columns // 2) // 128, 128), BF16)
+    return pl.pallas_call(
+        functools.partial(finish_body, offsets, depth, shape),
+        in_specs=[SCALARS] + [WHOLE] * 4,
         out_specs=[WHOLE] * 3,
-        out_shape=[jax.ShapeDtypeStruct((tokens, 2 * half), BF16), border, border],
-        scratch_shapes=[
-            pltpu.VMEM((len(order), half, -(-2 * depth // 128) * 128), BF16),
-            pltpu.VMEM((2 * half, width), BF16),
-        ],
+        out_shape=[jax.ShapeDtypeStruct((tokens, columns), BF16), border, border],
         compiler_params=params(16),
-        name="project",
-    )(tile, attended, *panels)
+        name="finish",
+    )(tile, attended, ours, theirs, part)
 
 
 def unpack_body(order, skip, tile_ref, *refs):
@@ -339,12 +365,10 @@
             upper = target // span - 2 * r
             wanted = (upper >= 0) & (upper < 2) & (source == upper * 2 * lat + side * lat + target % lat)
             inner[side, r] = jnp.where(wanted, 1.0, 0.0).astype(BF16)
-        source = lax.broadcasted_iota(jnp.int32, outer.shape[2:], 0)
-        target = lax.broadcasted_iota(jnp.int32, outer.shape[2:], 1)
-        for edge in range(2):
-            wanted = source == (1 - edge) * 2 * lat + side * lat + target % lat
-            wanted = wanted & (target < 3 * span)
-            outer[edge, side] = jnp.where(wanted, 1.0, 0.0).astype(BF16)
+        source = lax.broadcasted_iota(jnp.int32, outer.shape[1:], 0)
+        target = lax.broadcasted_iota(jnp.int32, outer.shape[1:], 1)
+        wanted = (source == side * lat + target % lat) & (target < 3 * span)
+        outer[side] = jnp.where(wanted, 1.0, 0.0).astype(BF16)
 
 
 def spreads(lat, patch_rows):
@@ -354,7 +378,7 @@
         out_specs=[WHOLE, WHOLE],
         out_shape=[
             jax.ShapeDtypeStruct((2, patch_rows, 4 * lat, -(-tall * 3 * lat // 128) * 128), BF16),
-            jax.ShapeDtypeStruct((2, 2, 4 * lat, -(-9 * lat // 128) * 128), BF16),
+            jax.ShapeDtypeStruct((2, 2 * lat, -(-9 * lat // 128) * 128), BF16),
         ],
         compiler_params=params(4),
         cost_estimate=pl.CostEstimate(flops=5 * 10**9, bytes_accessed=0, transcendentals=0),
@@ -430,7 +454,9 @@
 
 
 def outer_body(lat, tile_ref, from_pair, from_next, picks, kernel, edges, given, features, wide, done, sems):
-    frames, patches, values = from_pair.shape
+    frames, values = from_pair.shape[0], picks.shape[1]
+    folds = 128 // values
+    patches = from_pair.shape[1] * folds
     even = tile_ref[0] % 2 == 0
     broad = 2 * patches
     tall = features.shape[1]
@@ -440,14 +466,16 @@
     lane = lax.broadcasted_iota(jnp.int32, (broad, lanes), 1)
     copies = []
     for edge in range(2):
-        cells = [
-            jnp.where(even == (edge == 0), from_next[frame], from_pair[frame]) for frame in range(frames)
-        ]
+        cells = []
+        for frame in range(frames):
+            rows = jnp.where(even == (edge == 0), from_next[frame], from_pair[frame])
+            parts = [rows[:, k * values : (k + 1) * values] for k in range(folds)]
+            cells.append(jnp.concatenate(parts, axis=0))
         wide[edge, :, :, 0:8] = jnp.zeros((frames, chunks, 8, 128), F32)
         wide[edge, :, :, 8 + broad :] = jnp.zeros((frames, chunks, 8, 128), F32)
         for side in range(2):
             for frame in range(frames):
-                spread = jnp.dot(cells[frame], picks[edge, side], preferred_element_type=F32)
+                spread = jnp.dot(cells[frame], picks[side], preferred_element_type=F32)
                 for chunk in range(chunks):
                     wide[edge, frame, chunk, pl.ds(8 + side, patches, stride=2), :] = spread[
                         :, 128 * chunk : 128 * (chunk + 1)
@@ -476,9 +504,8 @@
 
 
 def convolve_outer(tile, from_pair, from_next, picks, kernel, edges, features):
-    frames, patches, values = from_pair.shape
-    lat = values // 4
-    broad = 2 * patches
+    frames, tall, broad, _ = features.shape
+    lat = picks.shape[1] // 2
     channels = kernel.shape[1]
     lanes = -(-9 * lat // 128) * 128
     return pl.pallas_call(
@@ -521,25 +548,24 @@
         far = [4, 8, 12]
         turns = [(2, 0), (3, 1), (1, 2), (0, 3)]
         line = [exchange(past_kv, k) for k in far]
-        final, decode = final_weight.T, decoder_weight.T
+        final, decode, own_rows, inner_picks, outer_picks = lax.optimization_barrier(
+            (final_weight.T, decoder_weight.T, own_rows, inner_picks, outer_picks)
+        )
         final_across, decode_across = exchange(final, 2), exchange(decode, 2)
-        own_rows, inner_picks, outer_picks = lax.optimization_barrier((own_rows, inner_picks, outer_picks))
         packed, sums, _ = attend_own(range(half), *lists, query_rows, own_rows, turns, blocks_here)
         *line, final_across, decode_across, packed = lax.optimization_barrier(
             (*line, final_across, decode_across, packed)
         )
         near = join([past_kv] + line, "join_near")
         across = exchange(near, 2)
-        beside = exchange(near, 1)
         panels = pack(final, decode, final_across, decode_across)
         panels_far, panels_near = exchange(panels, 8), exchange(panels, 4)
         own_rows, near = lax.optimization_barrier((own_rows, near))
         others = attend_own(range(half, KV_HEADS), *lists, query_rows, own_rows, turns, blocks_here)
         packed, sums, slots = [packed, others[0]], [sums, others[1]], others[2]
-        across, beside, panels_far, panels_near, slots = lax.optimization_barrier(
-            (across, beside, panels_far, panels_near, slots)
-        )
-        gathered = [near, across, beside, exchange(across, 1)]
+        across, panels_far, panels_near, slots = lax.optimization_barrier((across, panels_far, panels_near, slots))
+        gathered = join([near, across], "join_chip")
+        gathered = [gathered, exchange(gathered, 1)]
         panels_last = exchange(panels_far, 4)
         panels = join([panels, panels_far, panels_near], "join_panels")
         panels_beside = exchange(panels, 1)
@@ -548,7 +574,11 @@
         panels = [panels, panels_last, panels_beside, exchange(panels_last, 1)]
         order = [k ^ x for k in (0, 8, 4, 12) for x in (0, 2)]
         order = order + [k ^ 1 for k in order]
-        predicted, to_pair, to_next = project(tile, attended, panels, order, shape)
+        depth = final_weight.shape[0]
+        part = project(tile, attended, panels[0], panels[2], order[:6], depth)
+        predicted, to_pair, to_next = finish(
+            tile, attended, panels[1], panels[3], part, order[6:8], depth, shape
+        )
         decode = unpack(tile, panels, order, 2 * final_weight.shape[0], decoder_weight.shape[0])
     else:
         turns = [(bit, bits - 1 - bit) for bit in range(bits)]
@@ -563,9 +593,16 @@
         decode = lax.all_gather(decoder_weight, "seq", axis=1, tiled=True)
         predicted = jnp.dot(attended, final, preferred_element_type=F32).astype(BF16)
         rows = predicted.reshape(shape + (columns,))
+        values = columns // 2
+        folds = 128 // values
+
+        def folded(cells):
+            parts = cells.reshape(frames, folds, patches // folds, values)
+            return parts.transpose(0, 2, 1, 3).reshape(frames, patches // folds, 128)
+
+        first, last = folded(rows[:, 0, :, :values]), folded(rows[:, -1, :, values:])
         even = tile[0] % 2 == 0
-        to_pair = jnp.where(even, rows[:, -1], rows[:, 0])
-        to_next = jnp.where(even, rows[:, 0], rows[:, -1])
+        to_pair, to_next = jnp.where(even, last, first), jnp.where(even, first, last)
     predicted = predicted.reshape(shape + (columns,))
     swaps = [(i, i + 1) for i in range(1, count - 1, 2)] + [(i + 1, i) for i in range(1, count - 1, 2)]
     from_next = lax.ppermute(to_next, "seq", swaps)

time: 37.5 us -> 35.2 us (0.939)
  waiting for transfers between devices: 7.38 us -> 5.75 us
  local copies, waits for them, and re-layouts: 1.15 us -> 0.03 us
  Pallas kernels: 11.4 us -> 11.8 us
    ppermute x14 -> x13, waiting for transfers between devices: 5.93 us -> 4.8 us  [exchange(): return lax.ppermute(value, 'seq', [(i, i ^ offset) for i in range(count)])]
    unnamed x16, local copies, waits for them, and re-layouts: 1.15 us -> 0.03 us
    ppermute x1, waiting for transfers between devices: 1.45 us -> 0.95 us  [local(): from_next = lax.ppermute(to_next, 'seq', swaps)]
    pallas_call x1 -> x2, Pallas kernels: 0.69 us -> 0.94 us  [the longest x1 0.54 us: project(): pl.pallas_call(functools.partial(project_body, offsets, depth), in_specs=...]
    ppermute x14 -> x13, starting transfers between devices: 15.2 us -> 15 us  [exchange(): return lax.ppermute(value, 'seq', [(i, i ^ offset) for i in range(count)])]
  transfers between devices with their start and end apart: 15 -> 14, of which waited for: 6 -> 7; matrix products, arithmetic and copies ran while one was open for 0% -> 0% of each run, Pallas kernels for 25% -> 28%
where the time goes in v6:
time: 35.2 us; the launch traced here: 35.1 us
  starting transfers between devices  17.3 us (49%)
  Pallas kernels  11.8 us (34%)
  waiting for transfers between devices  5.75 us (16%)
    ppermute x13, starting transfers between devices, exchange(): return lax.ppermute(value, 'seq', [(i, i ^ offset) for i in range(count)])  15 us
    ppermute x13, waiting for transfers between devices, exchange(): return lax.ppermute(value, 'seq', [(i, i ^ offset) for i in range(count)])  4.8 us
    pallas_call x2, Pallas kernels, attend_own(): pl.pallas_call(functools.partial(own_body, turns, blocks_here, groups), i...  4.7 us
    pallas_call x1, Pallas kernels, attend_past(): pl.pallas_call(functools.partial(past_body, sizes, len(packed)), in_specs...  2.89 us
    ppermute x1, starting transfers between devices, local(): from_next = lax.ppermute(to_next, 'seq', swaps)  2.28 us
    pallas_call x1, Pallas kernels, convolve_inner(): pl.pallas_call(functools.partial(inner_body, lat), in_specs=[WHOLE] * 3,...  1.44 us
    pallas_call x1, Pallas kernels, convolve_outer(): pl.pallas_call(functools.partial(outer_body, lat), in_specs=[SCALARS] + [...  1.38 us
    ppermute x1, waiting for transfers between devices, local(): from_next = lax.ppermute(to_next, 'seq', swaps)  0.95 us
  transfers between devices with their start and end apart: 14, of which 7 were waited for; matrix products, arithmetic and copies ran while one was open for 0% of the time, Pallas kernels for 28%

profile of v6, /device:TPU:1, one launch (start us, length us, event | category | flops | bytes accessed | tf_op | source)
XLA Modules:
  0.0 35.1 jit_solution(9141866077798149416)
XLA Ops:
  0.0 0.0 copy-start.1
  0.0 0.0 copy-start.2
  0.0 0.0 copy-start.4
  0.0 0.0 copy-start.3
  0.0 0.0 copy-start.6
  0.0 0.0 copy-start.5
  0.0 0.0 copy-start.7
  0.0 2.2 %collective-permute-start = (bf16[2,16,1024]{2,1,0:T(8,128)(2,1)}, bf16[2,16,1024]{2,1,0:T(8,128)(2,1)S(1)}, u32[]{:S(2)}, u32[]{:S(2)}) collective-permute-start(bf16[2,16,1024]{2,1,0:T(8,128)(2,1)} %refs_0_.1), channel_id=1, source_target_pairs={{0,4},{1,5},{2,6},{3,7},{4,0},{5,1},{6,2},{7,3},{8,12},{9,13},{10,... | collective-permute-start | bytes 196616 | tf_op jit(solution)/shard_map/ppermute | solution.py:529
  2.2 2.3 %collective-permute-start.1 = (bf16[2,16,1024]{2,1,0:T(8,128)(2,1)}, bf16[2,16,1024]{2,1,0:T(8,128)(2,1)S(1)}, u32[]{:S(2)}, u32[]{:S(2)}) collective-permute-start(bf16[2,16,1024]{2,1,0:T(8,128)(2,1)} %refs_0_.1), channel_id=1, source_target_pairs={{0,8},{1,9},{2,10},{3,11},{4,12},{5,13},{6,14},{7,15},{8,0},{9,1},... | collective-permute-start | bytes 196616 | tf_op jit(solution)/shard_map/ppermute | solution.py:529
  4.6 0.0 collective-permute-start.2
  4.6 0.0 copy-done.1
  4.6 1.3 %collective-permute-start.3 = (bf16[64,192]{1,0:T(8,128)(2,1)S(1)}, bf16[64,192]{1,0:T(8,128)(2,1)S(1)}, u32[]{:S(2)}, u32[]{:S(2)}) collective-permute-start(bf16[64,192]{1,0:T(8,128)(2,1)S(1)} %bitcast.6), channel_id=1, source_target_pairs={{0,2},{1,3},{2,0},{3,1},{4,6},{5,7},{6,4},{7,5},{8,10},{9,11},{10,... | collective-permute-start | bytes 73736 | tf_op jit(solution)/shard_map/ppermute | solution.py:529
  5.9 0.0 copy-done.2
  5.9 0.3 collective-permute-start.4
  6.1 0.0 copy-done.4
  6.1 0.0 copy-done.3
  6.2 0.0 copy-done.6
  6.2 0.0 copy-done.5
  6.2 0.0 copy-done.7
  6.2 0.0 copy-start
  6.2 2.3 %attend_own.2 = (bf16[2,1536,256]{2,1,0:T(8,128)(2,1)S(1)}, f32[2,1536,128]{2,1,0:T(8,128)S(1)}, s32[16]{0:T(128)}) custom-call(s32[1]{0:T(128)} %bitcast.tile_ref, s32[32]{0:T(128)S(1)} %copy-done.6, s32[16,16]{1,0:T(8,128)S(1)} %copy-done.5, s32[16]{0:T(128)S(1)} %copy-done.7, bf16[256,3072]{1,0:T(8,128)(2,1)S(1)} %bitcast.10, bf16[256,1024]{1,0:T(8,128)(2,1)S(1)} %bitcast.12), custom_call_target="tpu_custom_call" | custom-call | flops 1207959552 | tf_op jit(solution)/shard_map/attend_own/pallas_call | solution.py:76
  8.5 0.0 collective-permute-done.3.final_across
  8.5 0.5 %collective-permute-done.4.decode_across = bf16[32,432]{1,0:T(8,128)(2,1)S(1)} collective-permute-done((bf16[32,432]{1,0:T(8,128)(2,1)S(1)}, bf16[32,432]{1,0:T(8,128)(2,1)S(1)}, u32[]{:S(2)}, u32[]{:S(2)}) %collective-permute-start.4) | collective-permute-done | bytes 27680 | tf_op jit(solution)/shard_map/ppermute | solution.py:529
  9.0 0.0 collective-permute-done.refs_1_
  9.0 0.0 collective-permute-done.1.refs_2_
  9.0 0.8 %collective-permute-done.2.refs_3_ = bf16[2,16,1024]{2,1,0:T(8,128)(2,1)S(1)} collective-permute-done((bf16[2,16,1024]{2,1,0:T(8,128)(2,1)}, bf16[2,16,1024]{2,1,0:T(8,128)(2,1)S(1)}, u32[]{:S(2)}, u32[]{:S(2)}) %collective-permute-start.2) | collective-permute-done | bytes 65568 | tf_op jit(solution)/shard_map/ppermute | solution.py:529
  9.8 0.0 copy-done
  9.8 1.3 %collective-permute-start.5 = (bf16[8,16,1024]{2,1,0:T(8,128)(2,1)S(1)}, bf16[8,16,1024]{2,1,0:T(8,128)(2,1)S(1)}, u32[]{:S(2)}, u32[]{:S(2)}) collective-permute-start(bf16[8,16,1024]{2,1,0:T(8,128)(2,1)S(1)} %join_near.1.refs_0_), channel_id=1, source_target_pairs={{0,2},{1,3},{2,0},{3,1},{4,6},{5,7},{6,4},{7,5},{8,10},{9,11},{10,... | collective-permute-start | bytes 786440 | tf_op jit(solution)/shard_map/ppermute | solution.py:529
  11.1 0.1 pack.1.refs_0_
  11.2 1.9 %collective-permute-start.6 = (bf16[2,32,896]{2,1,0:T(8,128)(2,1)S(1)}, bf16[2,32,896]{2,1,0:T(8,128)(2,1)S(1)}, u32[]{:S(2)}, u32[]{:S(2)}) collective-permute-start(bf16[2,32,896]{2,1,0:T(8,128)(2,1)S(1)} %pack.1.refs_0_), channel_id=1, source_target_pairs={{0,8},{1,9},{2,10},{3,11},{4,12},{5,13},{6,14},{7,15},{8,0},{9,1},... | collective-permute-start | bytes 344072 | tf_op jit(solution)/shard_map/ppermute | solution.py:529
  13.0 0.5 %collective-permute-start.7 = (bf16[2,32,896]{2,1,0:T(8,128)(2,1)S(1)}, bf16[2,32,896]{2,1,0:T(8,128)(2,1)S(1)}, u32[]{:S(2)}, u32[]{:S(2)}) collective-permute-start(bf16[2,32,896]{2,1,0:T(8,128)(2,1)S(1)} %pack.1.refs_0_), channel_id=1, source_target_pairs={{0,4},{1,5},{2,6},{3,7},{4,0},{5,1},{6,2},{7,3},{8,12},{9,13},{10,... | collective-permute-start | bytes 344072 | tf_op jit(solution)/shard_map/ppermute | solution.py:529
  13.5 2.4 %attend_own.3 = (bf16[2,1536,256]{2,1,0:T(8,128)(2,1)S(1)}, f32[2,1536,128]{2,1,0:T(8,128)S(1)}, s32[16]{0:T(128)S(1)}) custom-call(s32[1]{0:T(128)} %bitcast.tile_ref, s32[32]{0:T(128)S(1)} %copy-done.6, s32[16,16]{1,0:T(8,128)S(1)} %copy-done.5, s32[16]{0:T(128)S(1)} %copy-done.7, bf16[256,3072]{1,0:T(8,128)(2,1)S(1)} %bitcast.11, ...), custom_call_target="tpu_custom_call" | custom-call | flops 1207959552 | tf_op jit(solution)/shard_map/attend_own/pallas_call | solution.py:76
  15.9 1.1 %collective-permute-done.6.refs_1_ = bf16[2,32,896]{2,1,0:T(8,128)(2,1)S(1)} collective-permute-done((bf16[2,32,896]{2,1,0:T(8,128)(2,1)S(1)}, bf16[2,32,896]{2,1,0:T(8,128)(2,1)S(1)}, u32[]{:S(2)}, u32[]{:S(2)}) %collective-permute-start.6) | collective-permute-done | bytes 114720 | tf_op jit(solution)/shard_map/ppermute | solution.py:529
  17.1 0.6 %collective-permute-done.7.refs_2_ = bf16[2,32,896]{2,1,0:T(8,128)(2,1)S(1)} collective-permute-done((bf16[2,32,896]{2,1,0:T(8,128)(2,1)S(1)}, bf16[2,32,896]{2,1,0:T(8,128)(2,1)S(1)}, u32[]{:S(2)}, u32[]{:S(2)}) %collective-permute-start.7) | collective-permute-done | bytes 114720 | tf_op jit(solution)/shard_map/ppermute | solution.py:529
  17.7 0.0 collective-permute-done.5.refs_1_
  17.7 3.5 %collective-permute-start.10 = (bf16[16,16,1024]{2,1,0:T(8,128)(2,1)S(1)}, bf16[16,16,1024]{2,1,0:T(8,128)(2,1)S(1)}, u32[]{:S(2)}, u32[]{:S(2)}) collective-permute-start(bf16[16,16,1024]{2,1,0:T(8,128)(2,1)S(1)} %join_chip.1.refs_4_), channel_id=1, source_target_pairs={{0,1},{1,0},{2,3},{3,2},{4,5},{5,4},{6,7},{7,6},{8,9},{9,8},{10,11... | collective-permute-start | bytes 1572872 | tf_op jit(solution)/shard_map/ppermute | solution.py:529
  21.2 0.1 collective-permute-start.9
  21.3 0.1 collective-permute-start.8
  21.4 1.3 %collective-permute-done.10.refs_5_ = bf16[16,16,1024]{2,1,0:T(8,128)(2,1)S(1)} collective-permute-done((bf16[16,16,1024]{2,1,0:T(8,128)(2,1)S(1)}, bf16[16,16,1024]{2,1,0:T(8,128)(2,1)S(1)}, u32[]{:S(2)}, u32[]{:S(2)}) %collective-permute-start.10) | collective-permute-done | bytes 524320 | tf_op jit(solution)/shard_map/ppermute | solution.py:529
  22.7 2.9 %attend_past.1.attended = bf16[256,3072]{1,0:T(8,128)(2,1)S(1)} custom-call(s32[16]{0:T(128)S(1)} %get-tuple-element.52.slots, bf16[2,1536,256]{2,1,0:T(8,128)(2,1)S(1)} %get-tuple-element.53.refs_0_, bf16[2,1536,256]{2,1,0:T(8,128)(2,1)S(1)} %get-tuple-element.54.refs_1_, f32[2,1536,128]{2,1,0:T(8,128)S(1)} %get-tuple-element.55.refs_2_, ...), custom_call_target="tpu_custom_call" | custom-call | flops 1610612736 | bytes 6291456 | tf_op jit(solution)/shard_map/attend_past/pallas_call | solution.py:183
  25.6 0.0 collective-permute-done.8.ours.refs_1_
  25.7 0.0 collective-permute-done.9.theirs.refs_2_
  25.7 1.3 %collective-permute-start.11 = (bf16[2,32,896]{2,1,0:T(8,128)(2,1)S(1)}, bf16[2,32,896]{2,1,0:T(8,128)(2,1)S(1)}, u32[]{:S(2)}, u32[]{:S(2)}) collective-permute-start(bf16[2,32,896]{2,1,0:T(8,128)(2,1)S(1)} %collective-permute-done.8.ours.refs_1_), channel_id=1, source_target_pairs={{0,1},{1,0},{2,3},{3,2},{4,5},{5,4},{6,7},{7,6},{8,9},{9,8},{10,11... | collective-permute-start | bytes 344072 | tf_op jit(solution)/shard_map/ppermute | solution.py:529
  26.9 0.5 %project.1.part = f32[256,64]{1,0:T(8,128)S(1)} custom-call(s32[1]{0:T(128)} %bitcast.tile_ref, bf16[256,3072]{1,0:T(8,128)(2,1)S(1)} %attend_past.1.attended, bf16[6,32,896]{2,1,0:T(8,128)(2,1)S(1)} %join_panels.1.ours.refs_0_, bf16[6,32,896]{2,1,0:T(8,128)(2,1)S(1)} %collective-permute-done.9.theirs.refs_2_), custom_call_target="tpu_custom_call" | custom-call | tf_op jit(solution)/shard_map/project/pallas_call | solution.py:269
  27.5 0.4 %collective-permute-done.11.theirs.refs_3_ = bf16[2,32,896]{2,1,0:T(8,128)(2,1)S(1)} collective-permute-done((bf16[2,32,896]{2,1,0:T(8,128)(2,1)S(1)}, bf16[2,32,896]{2,1,0:T(8,128)(2,1)S(1)}, u32[]{:S(2)}, u32[]{:S(2)}) %collective-permute-start.11) | collective-permute-done | bytes 114720 | tf_op jit(solution)/shard_map/ppermute | solution.py:529
  27.9 0.4 %finish.1 = (bf16[256,64]{1,0:T(8,128)(2,1)S(1)}, bf16[2,16,128]{2,1,0:T(8,128)(2,1)S(1)}, bf16[2,16,128]{2,1,0:T(8,128)(2,1)S(1)}) custom-call(s32[1]{0:T(128)} %bitcast.tile_ref, bf16[256,3072]{1,0:T(8,128)(2,1)S(1)} %attend_past.1.attended, bf16[2,32,896]{2,1,0:T(8,128)(2,1)S(1)} %collective-permute-done.8.ours.refs_1_, ...), custom_call_target="tpu_custom_call" | custom-call | tf_op jit(solution)/shard_map/finish/pallas_call | solution.py:303
  28.3 0.4 %collective-permute-start.12 = (bf16[2,16,128]{2,1,0:T(8,128)(2,1)S(1)}, bf16[2,16,128]{2,1,0:T(8,128)(2,1)S(1)}, u32[]{:S(2)}, u32[]{:S(2)}) collective-permute-start(bf16[2,16,128]{2,1,0:T(8,128)(2,1)S(1)} %get-tuple-element.62), channel_id=1, source_target_pairs={{0,1},{1,0},{2,3},{3,2},{4,5},{5,4},{6,7},{7,6},{8,9},{9,8},{10,11... | collective-permute-start | bytes 24584 | tf_op jit(solution)/shard_map/ppermute | solution.py:529
  28.7 2.3 %collective-permute-start.13 = (bf16[2,16,128]{2,1,0:T(8,128)(2,1)S(1)}, bf16[2,16,128]{2,1,0:T(8,128)(2,1)S(1)}, u32[]{:S(2)}, u32[]{:S(2)}) collective-permute-start(bf16[2,16,128]{2,1,0:T(8,128)(2,1)S(1)} %get-tuple-element.63), channel_id=1, source_target_pairs={{1,2},{3,4},{5,6},{7,8},{9,10},{11,12},{13,14},{2,1},{4,3},{6,5},{... | collective-permute-start | bytes 24584 | tf_op jit(solution)/shard_map/ppermute | solution.py:608
  31.0 0.3 unpack.1.kernel
  31.3 1.4 %convolve_inner.1 = (bf16[2,4,128,512]{3,2,1,0:T(8,128)(2,1)}, f32[2,256,512]{2,1,0:T(8,128)S(1)}) custom-call(bf16[2,2,64,64]{3,2,1,0:T(8,128)(2,1)S(1)} %bitcast.14, bf16[2,2,64,256]{3,2,1,0:T(8,128)(2,1)S(1)} %get-tuple-element.66.picks, bf16[432,512]{1,0:T(8,128)(2,1)S(1)} %unpack.1.kernel), custom_call_target="tpu_custom_call" | custom-call | flops 452984832 | bytes 1048576 | tf_op jit(solution)/shard_map/convolve_inner/pallas_call | solution.py:433
  32.7 0.0 collective-permute-done.12.from_pair
  32.7 0.9 %collective-permute-done.13.from_next = bf16[2,16,128]{2,1,0:T(8,128)(2,1)S(1)} collective-permute-done((bf16[2,16,128]{2,1,0:T(8,128)(2,1)S(1)}, bf16[2,16,128]{2,1,0:T(8,128)(2,1)S(1)}, u32[]{:S(2)}, u32[]{:S(2)}) %collective-permute-start.13) | collective-permute-done | bytes 8224 | tf_op jit(solution)/shard_map/ppermute | solution.py:608
  33.7 1.4 %convolve_outer.1 = bf16[2,4,128,512]{3,2,1,0:T(8,128)(2,1)} custom-call(s32[1]{0:T(128)} %bitcast.tile_ref, bf16[2,16,128]{2,1,0:T(8,128)(2,1)S(1)} %collective-permute-done.12.from_pair, bf16[2,16,128]{2,1,0:T(8,128)(2,1)S(1)} %collective-permute-done.13.from_next, ...), custom_call_target="tpu_custom_call", output_to_operand_aliasing={{}: (6, {})} | custom-call | tf_op jit(solution)/shard_map/convolve_outer/pallas_call | solution.py:511
  (4 shorter events, 0.1 us)
Async XLA Ops:
  0.0 4.6 %copy-start.1 = (bf16[192,64]{0,1:T(8,128)(2,1)S(1)}, bf16[192,64]{0,1:T(8,128)(2,1)}, u32[]{:S(2)}) copy-start(bf16[192,64]{0,1:T(8,128)(2,1)} %param.14) | copy-start | bytes 73732
  0.0 5.9 %copy-start.2 = (bf16[432,32]{0,1:T(8,128)(2,1)S(1)}, bf16[432,32]{0,1:T(8,128)(2,1)}, u32[]{:S(2)}) copy-start(bf16[432,32]{0,1:T(8,128)(2,1)} %param.15) | copy-start | bytes 82948
  0.0 6.1 %copy-start.4 = (bf16[2,2,64,1024]{3,2,1,0:T(8,128)(2,1)S(1)}, bf16[2,2,64,1024]{3,2,1,0:T(8,128)(2,1)}, u32[]{:S(2)}) copy-start(bf16[2,2,64,1024]{3,2,1,0:T(8,128)(2,1)} %param.9) | copy-start | bytes 1572868
  0.0 6.1 %copy-start.3 = (bf16[2,2,64,3072]{3,2,1,0:T(8,128)(2,1)S(1)}, bf16[2,2,64,3072]{3,2,1,0:T(8,128)(2,1)}, u32[]{:S(2)}) copy-start(bf16[2,2,64,3072]{3,2,1,0:T(8,128)(2,1)} %param.8) | copy-start | bytes 4718596
  0.0 6.1 %copy-start.6 = (s32[32]{0:T(128)S(1)}, s32[32]{0:T(128)}, u32[]{:S(2)}) copy-start(s32[32]{0:T(128)} %home.3) | copy-start | bytes 388
  0.0 6.1 %copy-start.5 = (s32[16,16]{1,0:T(8,128)S(1)}, s32[16,16]{1,0:T(8,128)}, u32[]{:S(2)}) copy-start(s32[16,16]{1,0:T(8,128)} %blocks.3) | copy-start | bytes 3076
  0.0 6.1 %copy-start.7 = (s32[16]{0:T(128)S(1)}, s32[16]{0:T(128)}, u32[]{:S(2)}) copy-start(s32[16]{0:T(128)} %lens.3) | copy-start | bytes 196
  0.0 8.9 %collective-permute-start = (bf16[2,16,1024]{2,1,0:T(8,128)(2,1)}, bf16[2,16,1024]{2,1,0:T(8,128)(2,1)S(1)}, u32[]{:S(2)}, u32[]{:S(2)}) collective-permute-start(bf16[2,16,1024]{2,1,0:T(8,128)(2,1)} %refs_0_.1), channel_id=1, source_target_pairs={{0,4},{1,5},{2,6},{3,7},{4,0},{5,1},{6,2},{7,3},{8,12},{9,13},{10,... | collective-permute-start | bytes 196616 | tf_op jit(solution)/shard_map/ppermute | solution.py:529
  2.2 6.7 %collective-permute-start.1 = (bf16[2,16,1024]{2,1,0:T(8,128)(2,1)}, bf16[2,16,1024]{2,1,0:T(8,128)(2,1)S(1)}, u32[]{:S(2)}, u32[]{:S(2)}) collective-permute-start(bf16[2,16,1024]{2,1,0:T(8,128)(2,1)} %refs_0_.1), channel_id=1, source_target_pairs={{0,8},{1,9},{2,10},{3,11},{4,12},{5,13},{6,14},{7,15},{8,0},{9,1},... | collective-permute-start | bytes 196616 | tf_op jit(solution)/shard_map/ppermute | solution.py:529
  4.6 5.2 %collective-permute-start.2 = (bf16[2,16,1024]{2,1,0:T(8,128)(2,1)}, bf16[2,16,1024]{2,1,0:T(8,128)(2,1)S(1)}, u32[]{:S(2)}, u32[]{:S(2)}) collective-permute-start(bf16[2,16,1024]{2,1,0:T(8,128)(2,1)} %refs_0_.1), channel_id=1, source_target_pairs={{0,12},{1,13},{2,14},{3,15},{4,8},{5,9},{6,10},{7,11},{8,4},{9,5},... | collective-permute-start | bytes 196616 | tf_op jit(solution)/shard_map/ppermute | solution.py:529
  4.6 3.8 %collective-permute-start.3 = (bf16[64,192]{1,0:T(8,128)(2,1)S(1)}, bf16[64,192]{1,0:T(8,128)(2,1)S(1)}, u32[]{:S(2)}, u32[]{:S(2)}) collective-permute-start(bf16[64,192]{1,0:T(8,128)(2,1)S(1)} %bitcast.6), channel_id=1, source_target_pairs={{0,2},{1,3},{2,0},{3,1},{4,6},{5,7},{6,4},{7,5},{8,10},{9,11},{10,... | collective-permute-start | bytes 73736 | tf_op jit(solution)/shard_map/ppermute | solution.py:529
  5.9 3.1 %collective-permute-start.4 = (bf16[32,432]{1,0:T(8,128)(2,1)S(1)}, bf16[32,432]{1,0:T(8,128)(2,1)S(1)}, u32[]{:S(2)}, u32[]{:S(2)}) collective-permute-start(bf16[32,432]{1,0:T(8,128)(2,1)S(1)} %bitcast.8), channel_id=1, source_target_pairs={{0,2},{1,3},{2,0},{3,1},{4,6},{5,7},{6,4},{7,5},{8,10},{9,11},{10,... | collective-permute-start | bytes 82952 | tf_op jit(solution)/shard_map/ppermute | solution.py:529
  6.2 3.6 %copy-start = (bf16[2,16,1024]{2,1,0:T(8,128)(2,1)S(1)}, bf16[2,16,1024]{2,1,0:T(8,128)(2,1)}, u32[]{:S(2)}) copy-start(bf16[2,16,1024]{2,1,0:T(8,128)(2,1)} %refs_0_.1) | copy-start | bytes 196612
  9.8 7.9 %collective-permute-start.5 = (bf16[8,16,1024]{2,1,0:T(8,128)(2,1)S(1)}, bf16[8,16,1024]{2,1,0:T(8,128)(2,1)S(1)}, u32[]{:S(2)}, u32[]{:S(2)}) collective-permute-start(bf16[8,16,1024]{2,1,0:T(8,128)(2,1)S(1)} %join_near.1.refs_0_), channel_id=1, source_target_pairs={{0,2},{1,3},{2,0},{3,1},{4,6},{5,7},{6,4},{7,5},{8,10},{9,11},{10,... | collective-permute-start | bytes 786440 | tf_op jit(solution)/shard_map/ppermute | solution.py:529
  11.2 5.9 %collective-permute-start.6 = (bf16[2,32,896]{2,1,0:T(8,128)(2,1)S(1)}, bf16[2,32,896]{2,1,0:T(8,128)(2,1)S(1)}, u32[]{:S(2)}, u32[]{:S(2)}) collective-permute-start(bf16[2,32,896]{2,1,0:T(8,128)(2,1)S(1)} %pack.1.refs_0_), channel_id=1, source_target_pairs={{0,8},{1,9},{2,10},{3,11},{4,12},{5,13},{6,14},{7,15},{8,0},{9,1},... | collective-permute-start | bytes 344072 | tf_op jit(solution)/shard_map/ppermute | solution.py:529
  13.0 4.6 %collective-permute-start.7 = (bf16[2,32,896]{2,1,0:T(8,128)(2,1)S(1)}, bf16[2,32,896]{2,1,0:T(8,128)(2,1)S(1)}, u32[]{:S(2)}, u32[]{:S(2)}) collective-permute-start(bf16[2,32,896]{2,1,0:T(8,128)(2,1)S(1)} %pack.1.refs_0_), channel_id=1, source_target_pairs={{0,4},{1,5},{2,6},{3,7},{4,0},{5,1},{6,2},{7,3},{8,12},{9,13},{10,... | collective-permute-start | bytes 344072 | tf_op jit(solution)/shard_map/ppermute | solution.py:529
  17.7 5.0 %collective-permute-start.10 = (bf16[16,16,1024]{2,1,0:T(8,128)(2,1)S(1)}, bf16[16,16,1024]{2,1,0:T(8,128)(2,1)S(1)}, u32[]{:S(2)}, u32[]{:S(2)}) collective-permute-start(bf16[16,16,1024]{2,1,0:T(8,128)(2,1)S(1)} %join_chip.1.refs_4_), channel_id=1, source_target_pairs={{0,1},{1,0},{2,3},{3,2},{4,5},{5,4},{6,7},{7,6},{8,9},{9,8},{10,11... | collective-permute-start | bytes 1572872 | tf_op jit(solution)/shard_map/ppermute | solution.py:529
  21.2 4.4 %collective-permute-start.9 = (bf16[6,32,896]{2,1,0:T(8,128)(2,1)S(1)}, bf16[6,32,896]{2,1,0:T(8,128)(2,1)S(1)}, u32[]{:S(2)}, u32[]{:S(2)}) collective-permute-start(bf16[6,32,896]{2,1,0:T(8,128)(2,1)S(1)} %join_panels.1.ours.refs_0_), channel_id=1, source_target_pairs={{0,1},{1,0},{2,3},{3,2},{4,5},{5,4},{6,7},{7,6},{8,9},{9,8},{10,11... | collective-permute-start | bytes 1032200 | tf_op jit(solution)/shard_map/ppermute | solution.py:529
  21.3 4.3 %collective-permute-start.8 = (bf16[2,32,896]{2,1,0:T(8,128)(2,1)S(1)}, bf16[2,32,896]{2,1,0:T(8,128)(2,1)S(1)}, u32[]{:S(2)}, u32[]{:S(2)}) collective-permute-start(bf16[2,32,896]{2,1,0:T(8,128)(2,1)S(1)} %collective-permute-done.6.refs_1_), channel_id=1, source_target_pairs={{0,4},{1,5},{2,6},{3,7},{4,0},{5,1},{6,2},{7,3},{8,12},{9,13},{10,... | collective-permute-start | bytes 344072 | tf_op jit(solution)/shard_map/ppermute | solution.py:529
  25.7 2.2 %collective-permute-start.11 = (bf16[2,32,896]{2,1,0:T(8,128)(2,1)S(1)}, bf16[2,32,896]{2,1,0:T(8,128)(2,1)S(1)}, u32[]{:S(2)}, u32[]{:S(2)}) collective-permute-start(bf16[2,32,896]{2,1,0:T(8,128)(2,1)S(1)} %collective-permute-done.8.ours.refs_1_), channel_id=1, source_target_pairs={{0,1},{1,0},{2,3},{3,2},{4,5},{5,4},{6,7},{7,6},{8,9},{9,8},{10,11... | collective-permute-start | bytes 344072 | tf_op jit(solution)/shard_map/ppermute | solution.py:529
  28.3 4.4 %collective-permute-start.12 = (bf16[2,16,128]{2,1,0:T(8,128)(2,1)S(1)}, bf16[2,16,128]{2,1,0:T(8,128)(2,1)S(1)}, u32[]{:S(2)}, u32[]{:S(2)}) collective-permute-start(bf16[2,16,128]{2,1,0:T(8,128)(2,1)S(1)} %get-tuple-element.62), channel_id=1, source_target_pairs={{0,1},{1,0},{2,3},{3,2},{4,5},{5,4},{6,7},{7,6},{8,9},{9,8},{10,11... | collective-permute-start | bytes 24584 | tf_op jit(solution)/shard_map/ppermute | solution.py:529
  28.7 5.0 %collective-permute-start.13 = (bf16[2,16,128]{2,1,0:T(8,128)(2,1)S(1)}, bf16[2,16,128]{2,1,0:T(8,128)(2,1)S(1)}, u32[]{:S(2)}, u32[]{:S(2)}) collective-permute-start(bf16[2,16,128]{2,1,0:T(8,128)(2,1)S(1)} %get-tuple-element.63), channel_id=1, source_target_pairs={{1,2},{3,4},{5,6},{7,8},{9,10},{11,12},{13,14},{2,1},{4,3},{6,5},{... | collective-permute-start | bytes 24584 | tf_op jit(solution)/shard_map/ppermute | solution.py:608

commit v7 on v6

--- a/solution.py
+++ b/solution.py
@@ -15,6 +15,7 @@
 SCALE = math.log2(math.e) / math.sqrt(HEAD_DIM)
 SAFE = 2.0**100
 MIB = 1024 * 1024
+PART = 16
 WHOLE = pl.BlockSpec(memory_space=pltpu.VMEM)
 ANYWHERE = pl.BlockSpec(memory_space=pl.ANY)
 SCALARS = pl.BlockSpec(memory_space=pltpu.SMEM)
@@ -148,15 +149,24 @@
                 columns = pl.multiple_of(columns, HEAD_DIM)
             out[:, pl.ds(columns, HEAD_DIM)] = attended[h * tokens : (h + 1) * tokens]
 
-    def quick(step, largest):
+    def quick(step, score, largest):
         g, rows = place(step)
-        weights = jnp.exp2(scores(g, rows)).astype(BF16)
+        weights = jnp.exp2(score).astype(BF16)
         mixed = jnp.dot(weights, values[g], preferred_element_type=F32)
         below = mixed[:, HEAD_DIM:] + 1.0
         emit(step, (mixed[:, :HEAD_DIM] + own_part(sums, g, rows)) / below)
         return jnp.maximum(largest, jnp.max(below.reshape((-1,) + largest.shape), axis=0))
 
-    worst[...] = over_steps(quick, jnp.zeros(worst.shape, F32))
+    largest = jnp.zeros(worst.shape, F32)
+    if heads == GROUP:
+        score = scores(*place(0))
+        for step in range(steps):
+            ahead = scores(*place(step + 1)) if step + 1 < steps else None
+            largest = quick(step, score, largest)
+            score = ahead
+    else:
+        largest = over_steps(lambda step, seen: quick(step, scores(*place(step)), seen), largest)
+    worst[...] = largest
 
     @pl.when(jnp.logical_not(jnp.max(worst[...]) < SAFE))
     def _():
@@ -192,7 +202,7 @@
         ],
         compiler_params=params(40 if keys > 256 else 24),
         cost_estimate=pl.CostEstimate(
-            flops=8 * heads * rows * keys * HEAD_DIM, bytes_accessed=heads * rows * 1024, transcendentals=0
+            flops=10**10, bytes_accessed=0, transcendentals=0
         ),
         name="attend_past",
     )(slots, *packed, *sums, *gathered)
@@ -218,30 +228,32 @@
     )(*parts)
 
 
+def parts_of(panel):
+    return [panel[row : row + PART] for row in range(0, panel.shape[0], PART)]
+
+
 def pack_body(final, decode, final_across, decode_across, out):
-    half = final.shape[0] // 2
-    blank = out.shape[2] - 2 * final.shape[1] - decode.shape[1]
     for k, (left, right) in enumerate(((final, decode), (final_across, decode_across))):
-        out[k] = jnp.concatenate(
-            [left[:half], left[half:], right[...], jnp.zeros((half, blank), BF16)], axis=1
-        )
+        parts = parts_of(left) + parts_of(right)
+        blank = out.shape[2] - sum(part.shape[1] for part in parts)
+        out[k] = jnp.concatenate(parts + [jnp.zeros((PART, blank), BF16)], axis=1)
 
 
 def pack(final, decode, final_across, decode_across):
-    lanes = -(-(2 * final.shape[1] + decode.shape[1]) // 128) * 128
+    lanes = (final.size + decode.size) // PART
     return pl.pallas_call(
         pack_body,
         in_specs=[WHOLE] * 4,
         out_specs=WHOLE,
-        out_shape=jax.ShapeDtypeStruct((2, decode.shape[0], lanes), BF16),
+        out_shape=jax.ShapeDtypeStruct((2, PART, -(-lanes // 128) * 128), BF16),
         compiler_params=params(4),
         name="pack",
     )(final, decode, final_across, decode_across)
 
 
-def project_pairs(offsets, depth, tile, attended, ours, theirs):
+def project_pairs(offsets, depth, columns, tile, attended, ours, theirs):
     even = tile % 2 == 0
-    total = jnp.zeros((attended.shape[0], 2 * ours[0].shape[1]), F32)
+    total = jnp.zeros((attended.shape[0], columns), F32)
     ours = [(ref, k) for ref in ours for k in range(ref.shape[0])]
     theirs = [(ref, k) for ref in theirs for k in range(ref.shape[0])]
     for offset, (our, i), (their, j) in zip(offsets, ours, theirs):
@@ -249,7 +261,7 @@
         left, right = jnp.where(even, left, right), jnp.where(even, right, left)
         rows = [
             jnp.concatenate([panel[:, part * depth : (part + 1) * depth] for panel in (left, right)], axis=1)
-            for part in range(2)
+            for part in range(columns // PART)
         ]
         start = pl.multiple_of(((tile ^ offset) // 2) * (2 * depth), 128)
         total += lax.dot_general(
@@ -262,15 +274,15 @@
 
 
 def project_body(offsets, depth, tile_ref, attended, ours, theirs, out):
-    out[...] = project_pairs(offsets, depth, tile_ref[0], attended, [ours], [theirs])
-
-
-def project(tile, attended, ours, theirs, offsets, depth):
+    out[...] = project_pairs(offsets, depth, out.shape[1], tile_ref[0], attended, [ours], [theirs])
+
+
+def project(tile, attended, ours, theirs, offsets, depth, columns):
     return pl.pallas_call(
         functools.partial(project_body, offsets, depth),
         in_specs=[SCALARS] + [WHOLE] * 3,
         out_specs=WHOLE,
-        out_shape=jax.ShapeDtypeStruct((attended.shape[0], 2 * ours.shape[1]), F32),
+        out_shape=jax.ShapeDtypeStruct((attended.shape[0], columns), F32),
         compiler_params=params(16),
         name="project",
     )(tile, attended, ours, theirs)
@@ -279,7 +291,7 @@
 def finish_body(offsets, depth, shape, tile_ref, attended, ours, theirs, part, out, to_pair, to_next):
     frames, patch_rows, patches = shape
     tile = tile_ref[0]
-    predicted = part[...] + project_pairs(offsets, depth, tile, attended, [ours], [theirs])
+    predicted = part[...] + project_pairs(offsets, depth, part.shape[1], tile, attended, [ours], [theirs])
     predicted = predicted.astype(BF16)
     out[...] = predicted
     even = tile % 2 == 0
@@ -318,18 +330,22 @@
         for k in range(panel.shape[0]):
             staged[tile_ref[0] ^ order[place]] = panel[k]
             place += 1
-    whole = [staged[device, :, skip : skip + taps] for device in range(len(order))]
+    width = out.shape[1] // len(order)
+    whole = [
+        staged[device, :, skip + part * taps : skip + (part + 1) * taps]
+        for device in range(len(order))
+        for part in range(width // PART)
+    ]
     out[...] = jnp.concatenate(whole, axis=0).T
 
 
-def unpack(tile, panels, order, skip, taps):
-    width, lanes = panels[0].shape[1:]
+def unpack(tile, panels, order, skip, taps, width):
     return pl.pallas_call(
         functools.partial(unpack_body, order, skip),
         in_specs=[SCALARS] + [WHOLE] * len(panels),
         out_specs=WHOLE,
         out_shape=jax.ShapeDtypeStruct((taps, width * len(order)), BF16),
-        scratch_shapes=[pltpu.VMEM((len(order), width, lanes), BF16)],
+        scratch_shapes=[pltpu.VMEM((len(order),) + panels[0].shape[1:], BF16)],
         compiler_params=params(16),
         name="unpack",
     )(tile, *panels)
@@ -544,10 +560,10 @@
     inner_picks, outer_picks = spreads(columns // 4, patch_rows)
     half = KV_HEADS // 2
     lists = (tile, block_home, block_list, list_len)
-    if count == 16 and columns == 2 * decoder_weight.shape[1]:
+    if count == 16 and columns % PART == 0 and decoder_weight.shape[1] % PART == 0:
         far = [4, 8, 12]
         turns = [(2, 0), (3, 1), (1, 2), (0, 3)]
-        line = [exchange(past_kv, k) for k in far]
+        line = [exchange(past_kv, k) for k in reversed(far)][::-1]
         final, decode, own_rows, inner_picks, outer_picks = lax.optimization_barrier(
             (final_weight.T, decoder_weight.T, own_rows, inner_picks, outer_picks)
         )
@@ -575,11 +591,11 @@
         order = [k ^ x for k in (0, 8, 4, 12) for x in (0, 2)]
         order = order + [k ^ 1 for k in order]
         depth = final_weight.shape[0]
-        part = project(tile, attended, panels[0], panels[2], order[:6], depth)
+        part = project(tile, attended, panels[0], panels[2], order[:6], depth, columns)
         predicted, to_pair, to_next = finish(
             tile, attended, panels[1], panels[3], part, order[6:8], depth, shape
         )
-        decode = unpack(tile, panels, order, 2 * final_weight.shape[0], decoder_weight.shape[0])
+        decode = unpack(tile, panels, order, final_weight.size // PART, *decoder_weight.shape)
     else:
         turns = [(bit, bits - 1 - bit) for bit in range(bits)]
         held = past_kv

time: 35.2 us -> 34.9 us (level)
  transfers between devices with their start and end apart: 14 -> 14, of which waited for: 7 -> 8; matrix products, arithmetic and copies ran while one was open for 0% -> 0% of each run, Pallas kernels for 28% -> 29%
where the time goes in v7:
time: 34.9 us; the launch traced here: 34.7 us
  starting transfers between devices  17 us (49%)
  Pallas kernels  11.7 us (34%)
  waiting for transfers between devices  5.8 us (17%)
    ppermute x13, starting transfers between devices, exchange(): return lax.ppermute(value, 'seq', [(i, i ^ offset) for i in range(count)])  14.9 us
    pallas_call x2, Pallas kernels, attend_own(): pl.pallas_call(functools.partial(own_body, turns, blocks_here, groups), i...  4.78 us
    ppermute x13, waiting for transfers between devices, exchange(): return lax.ppermute(value, 'seq', [(i, i ^ offset) for i in range(count)])  4.75 us
    pallas_call x1, Pallas kernels, attend_past(): pl.pallas_call(functools.partial(past_body, sizes, len(packed)), in_specs...  2.67 us
    ppermute x1, starting transfers between devices, local(): from_next = lax.ppermute(to_next, 'seq', swaps)  2.1 us
    pallas_call x1, Pallas kernels, convolve_inner(): pl.pallas_call(functools.partial(inner_body, lat), in_specs=[WHOLE] * 3,...  1.44 us
    pallas_call x1, Pallas kernels, convolve_outer(): pl.pallas_call(functools.partial(outer_body, lat), in_specs=[SCALARS] + [...  1.38 us
    ppermute x1, waiting for transfers between devices, local(): from_next = lax.ppermute(to_next, 'seq', swaps)  1.06 us
  transfers between devices with their start and end apart: 14, of which 8 were waited for; matrix products, arithmetic and copies ran while one was open for 0% of the time, Pallas kernels for 29%

profile of v7, /device:TPU:1, one launch (start us, length us, event | category | flops | bytes accessed | tf_op | source)
XLA Modules:
  0.0 34.7 jit_solution(2011060345283875819)
XLA Ops:
  0.0 0.0 copy-start.1
  0.0 0.0 copy-start.2
  0.0 0.0 copy-start.4
  0.0 0.0 copy-start.3
  0.0 0.0 copy-start.6
  0.0 0.0 copy-start.5
  0.0 0.0 copy-start.7
  0.0 2.2 %collective-permute-start = (bf16[2,16,1024]{2,1,0:T(8,128)(2,1)}, bf16[2,16,1024]{2,1,0:T(8,128)(2,1)S(1)}, u32[]{:S(2)}, u32[]{:S(2)}) collective-permute-start(bf16[2,16,1024]{2,1,0:T(8,128)(2,1)} %refs_0_.1), channel_id=1, source_target_pairs={{0,4},{1,5},{2,6},{3,7},{4,0},{5,1},{6,2},{7,3},{8,12},{9,13},{10,... | collective-permute-start | bytes 196616 | tf_op jit(solution)/shard_map/ppermute | solution.py:545
  2.2 2.3 %collective-permute-start.1 = (bf16[2,16,1024]{2,1,0:T(8,128)(2,1)}, bf16[2,16,1024]{2,1,0:T(8,128)(2,1)S(1)}, u32[]{:S(2)}, u32[]{:S(2)}) collective-permute-start(bf16[2,16,1024]{2,1,0:T(8,128)(2,1)} %refs_0_.1), channel_id=1, source_target_pairs={{0,8},{1,9},{2,10},{3,11},{4,12},{5,13},{6,14},{7,15},{8,0},{9,1},... | collective-permute-start | bytes 196616 | tf_op jit(solution)/shard_map/ppermute | solution.py:545
  4.6 0.0 collective-permute-start.2
  4.6 0.0 copy-done.1
  4.6 1.3 %collective-permute-start.3 = (bf16[64,192]{1,0:T(8,128)(2,1)S(1)}, bf16[64,192]{1,0:T(8,128)(2,1)S(1)}, u32[]{:S(2)}, u32[]{:S(2)}) collective-permute-start(bf16[64,192]{1,0:T(8,128)(2,1)S(1)} %bitcast.6), channel_id=1, source_target_pairs={{0,2},{1,3},{2,0},{3,1},{4,6},{5,7},{6,4},{7,5},{8,10},{9,11},{10,... | collective-permute-start | bytes 73736 | tf_op jit(solution)/shard_map/ppermute | solution.py:545
  5.9 0.0 copy-done.2
  5.9 0.3 collective-permute-start.4
  6.1 0.0 copy-done.4
  6.1 0.0 copy-done.3
  6.2 0.0 copy-done.6
  6.2 0.0 copy-done.5
  6.2 0.0 copy-done.7
  6.2 0.0 copy-start
  6.2 2.3 %attend_own.2 = (bf16[2,1536,256]{2,1,0:T(8,128)(2,1)S(1)}, f32[2,1536,128]{2,1,0:T(8,128)S(1)}, s32[16]{0:T(128)}) custom-call(s32[1]{0:T(128)} %bitcast.tile_ref, s32[32]{0:T(128)S(1)} %copy-done.6, s32[16,16]{1,0:T(8,128)S(1)} %copy-done.5, s32[16]{0:T(128)S(1)} %copy-done.7, bf16[256,3072]{1,0:T(8,128)(2,1)S(1)} %bitcast.10, bf16[256,1024]{1,0:T(8,128)(2,1)S(1)} %bitcast.12), custom_call_target="tpu_custom_call" | custom-call | flops 1207959552 | tf_op jit(solution)/shard_map/attend_own/pallas_call | solution.py:77
  8.5 0.0 collective-permute-done.3.final_across
  8.5 0.5 %collective-permute-done.4.decode_across = bf16[32,432]{1,0:T(8,128)(2,1)S(1)} collective-permute-done((bf16[32,432]{1,0:T(8,128)(2,1)S(1)}, bf16[32,432]{1,0:T(8,128)(2,1)S(1)}, u32[]{:S(2)}, u32[]{:S(2)}) %collective-permute-start.4) | collective-permute-done | bytes 27680 | tf_op jit(solution)/shard_map/ppermute | solution.py:545
  9.0 0.0 collective-permute-done.refs_1_
  9.0 0.0 collective-permute-done.1.refs_2_
  9.0 0.8 %collective-permute-done.2.refs_3_ = bf16[2,16,1024]{2,1,0:T(8,128)(2,1)S(1)} collective-permute-done((bf16[2,16,1024]{2,1,0:T(8,128)(2,1)}, bf16[2,16,1024]{2,1,0:T(8,128)(2,1)S(1)}, u32[]{:S(2)}, u32[]{:S(2)}) %collective-permute-start.2) | collective-permute-done | bytes 65568 | tf_op jit(solution)/shard_map/ppermute | solution.py:545
  9.8 0.0 copy-done
  9.8 1.3 %collective-permute-start.5 = (bf16[8,16,1024]{2,1,0:T(8,128)(2,1)S(1)}, bf16[8,16,1024]{2,1,0:T(8,128)(2,1)S(1)}, u32[]{:S(2)}, u32[]{:S(2)}) collective-permute-start(bf16[8,16,1024]{2,1,0:T(8,128)(2,1)S(1)} %join_near.1.refs_0_), channel_id=1, source_target_pairs={{0,2},{1,3},{2,0},{3,1},{4,6},{5,7},{6,4},{7,5},{8,10},{9,11},{10,... | collective-permute-start | bytes 786440 | tf_op jit(solution)/shard_map/ppermute | solution.py:545
  11.1 0.1 pack.1.refs_0_
  11.2 1.9 %collective-permute-start.6 = (bf16[2,16,1664]{2,1,0:T(8,128)(2,1)S(1)}, bf16[2,16,1664]{2,1,0:T(8,128)(2,1)S(1)}, u32[]{:S(2)}, u32[]{:S(2)}) collective-permute-start(bf16[2,16,1664]{2,1,0:T(8,128)(2,1)S(1)} %pack.1.refs_0_), channel_id=1, source_target_pairs={{0,8},{1,9},{2,10},{3,11},{4,12},{5,13},{6,14},{7,15},{8,0},{9,1},... | collective-permute-start | bytes 319496 | tf_op jit(solution)/shard_map/ppermute | solution.py:545
  13.1 0.5 %collective-permute-start.7 = (bf16[2,16,1664]{2,1,0:T(8,128)(2,1)S(1)}, bf16[2,16,1664]{2,1,0:T(8,128)(2,1)S(1)}, u32[]{:S(2)}, u32[]{:S(2)}) collective-permute-start(bf16[2,16,1664]{2,1,0:T(8,128)(2,1)S(1)} %pack.1.refs_0_), channel_id=1, source_target_pairs={{0,4},{1,5},{2,6},{3,7},{4,0},{5,1},{6,2},{7,3},{8,12},{9,13},{10,... | collective-permute-start | bytes 319496 | tf_op jit(solution)/shard_map/ppermute | solution.py:545
  13.5 2.5 %attend_own.3 = (bf16[2,1536,256]{2,1,0:T(8,128)(2,1)S(1)}, f32[2,1536,128]{2,1,0:T(8,128)S(1)}, s32[16]{0:T(128)S(1)}) custom-call(s32[1]{0:T(128)} %bitcast.tile_ref, s32[32]{0:T(128)S(1)} %copy-done.6, s32[16,16]{1,0:T(8,128)S(1)} %copy-done.5, s32[16]{0:T(128)S(1)} %copy-done.7, bf16[256,3072]{1,0:T(8,128)(2,1)S(1)} %bitcast.11, ...), custom_call_target="tpu_custom_call" | custom-call | flops 1207959552 | tf_op jit(solution)/shard_map/attend_own/pallas_call | solution.py:77
  16.0 0.9 %collective-permute-done.6.refs_1_ = bf16[2,16,1664]{2,1,0:T(8,128)(2,1)S(1)} collective-permute-done((bf16[2,16,1664]{2,1,0:T(8,128)(2,1)S(1)}, bf16[2,16,1664]{2,1,0:T(8,128)(2,1)S(1)}, u32[]{:S(2)}, u32[]{:S(2)}) %collective-permute-start.6) | collective-permute-done | bytes 106528 | tf_op jit(solution)/shard_map/ppermute | solution.py:545
  16.9 0.6 %collective-permute-done.7.refs_2_ = bf16[2,16,1664]{2,1,0:T(8,128)(2,1)S(1)} collective-permute-done((bf16[2,16,1664]{2,1,0:T(8,128)(2,1)S(1)}, bf16[2,16,1664]{2,1,0:T(8,128)(2,1)S(1)}, u32[]{:S(2)}, u32[]{:S(2)}) %collective-permute-start.7) | collective-permute-done | bytes 106528 | tf_op jit(solution)/shard_map/ppermute | solution.py:545
  17.5 0.0 collective-permute-done.5.refs_1_
  17.6 3.7 %collective-permute-start.10 = (bf16[16,16,1024]{2,1,0:T(8,128)(2,1)S(1)}, bf16[16,16,1024]{2,1,0:T(8,128)(2,1)S(1)}, u32[]{:S(2)}, u32[]{:S(2)}) collective-permute-start(bf16[16,16,1024]{2,1,0:T(8,128)(2,1)S(1)} %join_chip.1.refs_4_), channel_id=1, source_target_pairs={{0,1},{1,0},{2,3},{3,2},{4,5},{5,4},{6,7},{7,6},{8,9},{9,8},{10,11... | collective-permute-start | bytes 1572872 | tf_op jit(solution)/shard_map/ppermute | solution.py:545
  21.2 0.0 collective-permute-start.8
  21.3 0.3 collective-permute-start.9
  21.6 1.2 %collective-permute-done.10.refs_5_ = bf16[16,16,1024]{2,1,0:T(8,128)(2,1)S(1)} collective-permute-done((bf16[16,16,1024]{2,1,0:T(8,128)(2,1)S(1)}, bf16[16,16,1024]{2,1,0:T(8,128)(2,1)S(1)}, u32[]{:S(2)}, u32[]{:S(2)}) %collective-permute-start.10) | collective-permute-done | bytes 524320 | tf_op jit(solution)/shard_map/ppermute | solution.py:545
  22.8 2.7 %attend_past.1.attended = bf16[256,3072]{1,0:T(8,128)(2,1)S(1)} custom-call(s32[16]{0:T(128)S(1)} %get-tuple-element.52.slots, bf16[2,1536,256]{2,1,0:T(8,128)(2,1)S(1)} %get-tuple-element.53.refs_0_, bf16[2,1536,256]{2,1,0:T(8,128)(2,1)S(1)} %get-tuple-element.54.refs_1_, f32[2,1536,128]{2,1,0:T(8,128)S(1)} %get-tuple-element.55.refs_2_, ...), custom_call_target="tpu_custom_call" | custom-call | flops 10000000000 | tf_op jit(solution)/shard_map/attend_past/pallas_call | solution.py:193
  25.4 0.3 collective-permute-done.8.ours.refs_1_
  25.8 0.0 collective-permute-done.9.theirs.refs_2_
  25.8 0.9 %collective-permute-start.11 = (bf16[2,16,1664]{2,1,0:T(8,128)(2,1)S(1)}, bf16[2,16,1664]{2,1,0:T(8,128)(2,1)S(1)}, u32[]{:S(2)}, u32[]{:S(2)}) collective-permute-start(bf16[2,16,1664]{2,1,0:T(8,128)(2,1)S(1)} %collective-permute-done.8.ours.refs_1_), channel_id=1, source_target_pairs={{0,1},{1,0},{2,3},{3,2},{4,5},{5,4},{6,7},{7,6},{8,9},{9,8},{10,11... | collective-permute-start | bytes 319496 | tf_op jit(solution)/shard_map/ppermute | solution.py:545
  26.6 0.5 %project.1.part = f32[256,64]{1,0:T(8,128)S(1)} custom-call(s32[1]{0:T(128)} %bitcast.tile_ref, bf16[256,3072]{1,0:T(8,128)(2,1)S(1)} %attend_past.1.attended, bf16[6,16,1664]{2,1,0:T(8,128)(2,1)S(1)} %join_panels.1.ours.refs_0_, bf16[6,16,1664]{2,1,0:T(8,128)(2,1)S(1)} %collective-permute-done.9.theirs.refs_2_), custom_call_target="tpu_custom_call" | custom-call | tf_op jit(solution)/shard_map/project/pallas_call | solution.py:281
  27.2 0.4 %collective-permute-done.11.theirs.refs_3_ = bf16[2,16,1664]{2,1,0:T(8,128)(2,1)S(1)} collective-permute-done((bf16[2,16,1664]{2,1,0:T(8,128)(2,1)S(1)}, bf16[2,16,1664]{2,1,0:T(8,128)(2,1)S(1)}, u32[]{:S(2)}, u32[]{:S(2)}) %collective-permute-start.11) | collective-permute-done | bytes 106528 | tf_op jit(solution)/shard_map/ppermute | solution.py:545
  27.6 0.4 %finish.1 = (bf16[256,64]{1,0:T(8,128)(2,1)S(1)}, bf16[2,16,128]{2,1,0:T(8,128)(2,1)S(1)}, bf16[2,16,128]{2,1,0:T(8,128)(2,1)S(1)}) custom-call(s32[1]{0:T(128)} %bitcast.tile_ref, bf16[256,3072]{1,0:T(8,128)(2,1)S(1)} %attend_past.1.attended, bf16[2,16,1664]{2,1,0:T(8,128)(2,1)S(1)} %collective-permute-done.8.ours.refs_1_, ...), custom_call_target="tpu_custom_call" | custom-call | tf_op jit(solution)/shard_map/finish/pallas_call | solution.py:315
  28.0 0.4 %collective-permute-start.12 = (bf16[2,16,128]{2,1,0:T(8,128)(2,1)S(1)}, bf16[2,16,128]{2,1,0:T(8,128)(2,1)S(1)}, u32[]{:S(2)}, u32[]{:S(2)}) collective-permute-start(bf16[2,16,128]{2,1,0:T(8,128)(2,1)S(1)} %get-tuple-element.62), channel_id=1, source_target_pairs={{0,1},{1,0},{2,3},{3,2},{4,5},{5,4},{6,7},{7,6},{8,9},{9,8},{10,11... | collective-permute-start | bytes 24584 | tf_op jit(solution)/shard_map/ppermute | solution.py:545
  28.4 2.1 %collective-permute-start.13 = (bf16[2,16,128]{2,1,0:T(8,128)(2,1)S(1)}, bf16[2,16,128]{2,1,0:T(8,128)(2,1)S(1)}, u32[]{:S(2)}, u32[]{:S(2)}) collective-permute-start(bf16[2,16,128]{2,1,0:T(8,128)(2,1)S(1)} %get-tuple-element.63), channel_id=1, source_target_pairs={{1,2},{3,4},{5,6},{7,8},{9,10},{11,12},{13,14},{2,1},{4,3},{6,5},{... | collective-permute-start | bytes 24584 | tf_op jit(solution)/shard_map/ppermute | solution.py:624
  30.5 0.3 unpack.1.kernel
  30.9 1.4 %convolve_inner.1 = (bf16[2,4,128,512]{3,2,1,0:T(8,128)(2,1)}, f32[2,256,512]{2,1,0:T(8,128)S(1)}) custom-call(bf16[2,2,64,64]{3,2,1,0:T(8,128)(2,1)S(1)} %bitcast.14, bf16[2,2,64,256]{3,2,1,0:T(8,128)(2,1)S(1)} %get-tuple-element.66.picks, bf16[432,512]{1,0:T(8,128)(2,1)S(1)} %unpack.1.kernel), custom_call_target="tpu_custom_call" | custom-call | flops 452984832 | bytes 1048576 | tf_op jit(solution)/shard_map/convolve_inner/pallas_call | solution.py:449
  32.3 0.0 collective-permute-done.12.from_pair
  32.3 1.1 %collective-permute-done.13.from_next = bf16[2,16,128]{2,1,0:T(8,128)(2,1)S(1)} collective-permute-done((bf16[2,16,128]{2,1,0:T(8,128)(2,1)S(1)}, bf16[2,16,128]{2,1,0:T(8,128)(2,1)S(1)}, u32[]{:S(2)}, u32[]{:S(2)}) %collective-permute-start.13) | collective-permute-done | bytes 8224 | tf_op jit(solution)/shard_map/ppermute | solution.py:624
  33.4 1.4 %convolve_outer.1 = bf16[2,4,128,512]{3,2,1,0:T(8,128)(2,1)} custom-call(s32[1]{0:T(128)} %bitcast.tile_ref, bf16[2,16,128]{2,1,0:T(8,128)(2,1)S(1)} %collective-permute-done.12.from_pair, bf16[2,16,128]{2,1,0:T(8,128)(2,1)S(1)} %collective-permute-done.13.from_next, ...), custom_call_target="tpu_custom_call", output_to_operand_aliasing={{}: (6, {})} | custom-call | tf_op jit(solution)/shard_map/convolve_outer/pallas_call | solution.py:527
  (4 shorter events, 0.1 us)
Async XLA Ops:
  0.0 4.6 %copy-start.1 = (bf16[192,64]{0,1:T(8,128)(2,1)S(1)}, bf16[192,64]{0,1:T(8,128)(2,1)}, u32[]{:S(2)}) copy-start(bf16[192,64]{0,1:T(8,128)(2,1)} %param.14) | copy-start | bytes 73732
  0.0 5.9 %copy-start.2 = (bf16[432,32]{0,1:T(8,128)(2,1)S(1)}, bf16[432,32]{0,1:T(8,128)(2,1)}, u32[]{:S(2)}) copy-start(bf16[432,32]{0,1:T(8,128)(2,1)} %param.15) | copy-start | bytes 82948
  0.0 6.1 %copy-start.4 = (bf16[2,2,64,1024]{3,2,1,0:T(8,128)(2,1)S(1)}, bf16[2,2,64,1024]{3,2,1,0:T(8,128)(2,1)}, u32[]{:S(2)}) copy-start(bf16[2,2,64,1024]{3,2,1,0:T(8,128)(2,1)} %param.9) | copy-start | bytes 1572868
  0.0 6.1 %copy-start.3 = (bf16[2,2,64,3072]{3,2,1,0:T(8,128)(2,1)S(1)}, bf16[2,2,64,3072]{3,2,1,0:T(8,128)(2,1)}, u32[]{:S(2)}) copy-start(bf16[2,2,64,3072]{3,2,1,0:T(8,128)(2,1)} %param.8) | copy-start | bytes 4718596
  0.0 6.1 %copy-start.6 = (s32[32]{0:T(128)S(1)}, s32[32]{0:T(128)}, u32[]{:S(2)}) copy-start(s32[32]{0:T(128)} %home.3) | copy-start | bytes 388
  0.0 6.1 %copy-start.5 = (s32[16,16]{1,0:T(8,128)S(1)}, s32[16,16]{1,0:T(8,128)}, u32[]{:S(2)}) copy-start(s32[16,16]{1,0:T(8,128)} %blocks.3) | copy-start | bytes 3076
  0.0 6.1 %copy-start.7 = (s32[16]{0:T(128)S(1)}, s32[16]{0:T(128)}, u32[]{:S(2)}) copy-start(s32[16]{0:T(128)} %lens.3) | copy-start | bytes 196
  0.0 8.9 %collective-permute-start = (bf16[2,16,1024]{2,1,0:T(8,128)(2,1)}, bf16[2,16,1024]{2,1,0:T(8,128)(2,1)S(1)}, u32[]{:S(2)}, u32[]{:S(2)}) collective-permute-start(bf16[2,16,1024]{2,1,0:T(8,128)(2,1)} %refs_0_.1), channel_id=1, source_target_pairs={{0,4},{1,5},{2,6},{3,7},{4,0},{5,1},{6,2},{7,3},{8,12},{9,13},{10,... | collective-permute-start | bytes 196616 | tf_op jit(solution)/shard_map/ppermute | solution.py:545
  2.2 6.7 %collective-permute-start.1 = (bf16[2,16,1024]{2,1,0:T(8,128)(2,1)}, bf16[2,16,1024]{2,1,0:T(8,128)(2,1)S(1)}, u32[]{:S(2)}, u32[]{:S(2)}) collective-permute-start(bf16[2,16,1024]{2,1,0:T(8,128)(2,1)} %refs_0_.1), channel_id=1, source_target_pairs={{0,8},{1,9},{2,10},{3,11},{4,12},{5,13},{6,14},{7,15},{8,0},{9,1},... | collective-permute-start | bytes 196616 | tf_op jit(solution)/shard_map/ppermute | solution.py:545
  4.6 5.2 %collective-permute-start.2 = (bf16[2,16,1024]{2,1,0:T(8,128)(2,1)}, bf16[2,16,1024]{2,1,0:T(8,128)(2,1)S(1)}, u32[]{:S(2)}, u32[]{:S(2)}) collective-permute-start(bf16[2,16,1024]{2,1,0:T(8,128)(2,1)} %refs_0_.1), channel_id=1, source_target_pairs={{0,12},{1,13},{2,14},{3,15},{4,8},{5,9},{6,10},{7,11},{8,4},{9,5},... | collective-permute-start | bytes 196616 | tf_op jit(solution)/shard_map/ppermute | solution.py:545
  4.6 3.8 %collective-permute-start.3 = (bf16[64,192]{1,0:T(8,128)(2,1)S(1)}, bf16[64,192]{1,0:T(8,128)(2,1)S(1)}, u32[]{:S(2)}, u32[]{:S(2)}) collective-permute-start(bf16[64,192]{1,0:T(8,128)(2,1)S(1)} %bitcast.6), channel_id=1, source_target_pairs={{0,2},{1,3},{2,0},{3,1},{4,6},{5,7},{6,4},{7,5},{8,10},{9,11},{10,... | collective-permute-start | bytes 73736 | tf_op jit(solution)/shard_map/ppermute | solution.py:545
  5.9 3.1 %collective-permute-start.4 = (bf16[32,432]{1,0:T(8,128)(2,1)S(1)}, bf16[32,432]{1,0:T(8,128)(2,1)S(1)}, u32[]{:S(2)}, u32[]{:S(2)}) collective-permute-start(bf16[32,432]{1,0:T(8,128)(2,1)S(1)} %bitcast.8), channel_id=1, source_target_pairs={{0,2},{1,3},{2,0},{3,1},{4,6},{5,7},{6,4},{7,5},{8,10},{9,11},{10,... | collective-permute-start | bytes 82952 | tf_op jit(solution)/shard_map/ppermute | solution.py:545
  6.2 3.6 %copy-start = (bf16[2,16,1024]{2,1,0:T(8,128)(2,1)S(1)}, bf16[2,16,1024]{2,1,0:T(8,128)(2,1)}, u32[]{:S(2)}) copy-start(bf16[2,16,1024]{2,1,0:T(8,128)(2,1)} %refs_0_.1) | copy-start | bytes 196612
  9.8 7.7 %collective-permute-start.5 = (bf16[8,16,1024]{2,1,0:T(8,128)(2,1)S(1)}, bf16[8,16,1024]{2,1,0:T(8,128)(2,1)S(1)}, u32[]{:S(2)}, u32[]{:S(2)}) collective-permute-start(bf16[8,16,1024]{2,1,0:T(8,128)(2,1)S(1)} %join_near.1.refs_0_), channel_id=1, source_target_pairs={{0,2},{1,3},{2,0},{3,1},{4,6},{5,7},{6,4},{7,5},{8,10},{9,11},{10,... | collective-permute-start | bytes 786440 | tf_op jit(solution)/shard_map/ppermute | solution.py:545
  11.2 5.8 %collective-permute-start.6 = (bf16[2,16,1664]{2,1,0:T(8,128)(2,1)S(1)}, bf16[2,16,1664]{2,1,0:T(8,128)(2,1)S(1)}, u32[]{:S(2)}, u32[]{:S(2)}) collective-permute-start(bf16[2,16,1664]{2,1,0:T(8,128)(2,1)S(1)} %pack.1.refs_0_), channel_id=1, source_target_pairs={{0,8},{1,9},{2,10},{3,11},{4,12},{5,13},{6,14},{7,15},{8,0},{9,1},... | collective-permute-start | bytes 319496 | tf_op jit(solution)/shard_map/ppermute | solution.py:545
  13.1 4.5 %collective-permute-start.7 = (bf16[2,16,1664]{2,1,0:T(8,128)(2,1)S(1)}, bf16[2,16,1664]{2,1,0:T(8,128)(2,1)S(1)}, u32[]{:S(2)}, u32[]{:S(2)}) collective-permute-start(bf16[2,16,1664]{2,1,0:T(8,128)(2,1)S(1)} %pack.1.refs_0_), channel_id=1, source_target_pairs={{0,4},{1,5},{2,6},{3,7},{4,0},{5,1},{6,2},{7,3},{8,12},{9,13},{10,... | collective-permute-start | bytes 319496 | tf_op jit(solution)/shard_map/ppermute | solution.py:545
  17.6 5.2 %collective-permute-start.10 = (bf16[16,16,1024]{2,1,0:T(8,128)(2,1)S(1)}, bf16[16,16,1024]{2,1,0:T(8,128)(2,1)S(1)}, u32[]{:S(2)}, u32[]{:S(2)}) collective-permute-start(bf16[16,16,1024]{2,1,0:T(8,128)(2,1)S(1)} %join_chip.1.refs_4_), channel_id=1, source_target_pairs={{0,1},{1,0},{2,3},{3,2},{4,5},{5,4},{6,7},{7,6},{8,9},{9,8},{10,11... | collective-permute-start | bytes 1572872 | tf_op jit(solution)/shard_map/ppermute | solution.py:545
  21.2 4.5 %collective-permute-start.8 = (bf16[2,16,1664]{2,1,0:T(8,128)(2,1)S(1)}, bf16[2,16,1664]{2,1,0:T(8,128)(2,1)S(1)}, u32[]{:S(2)}, u32[]{:S(2)}) collective-permute-start(bf16[2,16,1664]{2,1,0:T(8,128)(2,1)S(1)} %collective-permute-done.6.refs_1_), channel_id=1, source_target_pairs={{0,4},{1,5},{2,6},{3,7},{4,0},{5,1},{6,2},{7,3},{8,12},{9,13},{10,... | collective-permute-start | bytes 319496 | tf_op jit(solution)/shard_map/ppermute | solution.py:545
  21.3 4.5 %collective-permute-start.9 = (bf16[6,16,1664]{2,1,0:T(8,128)(2,1)S(1)}, bf16[6,16,1664]{2,1,0:T(8,128)(2,1)S(1)}, u32[]{:S(2)}, u32[]{:S(2)}) collective-permute-start(bf16[6,16,1664]{2,1,0:T(8,128)(2,1)S(1)} %join_panels.1.ours.refs_0_), channel_id=1, source_target_pairs={{0,1},{1,0},{2,3},{3,2},{4,5},{5,4},{6,7},{7,6},{8,9},{9,8},{10,11... | collective-permute-start | bytes 958472 | tf_op jit(solution)/shard_map/ppermute | solution.py:545
  25.8 1.8 %collective-permute-start.11 = (bf16[2,16,1664]{2,1,0:T(8,128)(2,1)S(1)}, bf16[2,16,1664]{2,1,0:T(8,128)(2,1)S(1)}, u32[]{:S(2)}, u32[]{:S(2)}) collective-permute-start(bf16[2,16,1664]{2,1,0:T(8,128)(2,1)S(1)} %collective-permute-done.8.ours.refs_1_), channel_id=1, source_target_pairs={{0,1},{1,0},{2,3},{3,2},{4,5},{5,4},{6,7},{7,6},{8,9},{9,8},{10,11... | collective-permute-start | bytes 319496 | tf_op jit(solution)/shard_map/ppermute | solution.py:545
  28.0 4.3 %collective-permute-start.12 = (bf16[2,16,128]{2,1,0:T(8,128)(2,1)S(1)}, bf16[2,16,128]{2,1,0:T(8,128)(2,1)S(1)}, u32[]{:S(2)}, u32[]{:S(2)}) collective-permute-start(bf16[2,16,128]{2,1,0:T(8,128)(2,1)S(1)} %get-tuple-element.62), channel_id=1, source_target_pairs={{0,1},{1,0},{2,3},{3,2},{4,5},{5,4},{6,7},{7,6},{8,9},{9,8},{10,11... | collective-permute-start | bytes 24584 | tf_op jit(solution)/shard_map/ppermute | solution.py:545
  28.4 5.0 %collective-permute-start.13 = (bf16[2,16,128]{2,1,0:T(8,128)(2,1)S(1)}, bf16[2,16,128]{2,1,0:T(8,128)(2,1)S(1)}, u32[]{:S(2)}, u32[]{:S(2)}) collective-permute-start(bf16[2,16,128]{2,1,0:T(8,128)(2,1)S(1)} %get-tuple-element.63), channel_id=1, source_target_pairs={{1,2},{3,4},{5,6},{7,8},{9,10},{11,12},{13,14},{2,1},{4,3},{6,5},{... | collective-permute-start | bytes 24584 | tf_op jit(solution)/shard_map/ppermute | solution.py:624

commit v8 on v7

--- a/solution.py
+++ b/solution.py
@@ -402,24 +402,64 @@
     )()
 
 
-def inner_body(lat, predicted, picks, kernel, features, edges, wide, done, sems):
-    frames, patch_rows, patches, values = predicted.shape
+def border_taps(lat, cells, picks, wide):
+    frames, values = cells.shape[0], picks.shape[1]
+    folds = 128 // values
+    patches = cells.shape[1] * folds
+    broad = 2 * patches
+    chunks = wide.shape[1]
+    span = 3 * lat
+    wide[:, :, 0:8] = jnp.zeros((frames, chunks, 8, 128), F32)
+    wide[:, :, 8 + broad :] = jnp.zeros((frames, chunks, 8, 128), F32)
+    for frame in range(frames):
+        folded = cells[frame]
+        row = jnp.concatenate([folded[:, k * values : (k + 1) * values] for k in range(folds)], axis=0)
+        for side in range(2):
+            spread = jnp.dot(row, picks[side], preferred_element_type=F32)
+            for chunk in range(chunks):
+                wide[frame, chunk, pl.ds(8 + side, patches, stride=2), :] = spread[
+                    :, 128 * chunk : 128 * (chunk + 1)
+                ]
+    ready = [shifted(wide, frame, broad, lat) for frame in range(frames)]
+    lane = lax.broadcasted_iota(jnp.int32, ready[0].shape, 1)
+    rows = []
+    for frame in range(frames):
+        taps = jnp.zeros(ready[0].shape, BF16)
+        for shift_t in range(3):
+            if frame + shift_t - 2 >= 0:
+                taps = jnp.where(lane // span == shift_t, ready[frame + shift_t - 2], taps)
+        rows.append(taps[:, : 3 * span])
+    return rows
+
+
+def border_panel(lat, kernel, edge):
+    span = 3 * lat
+    starts = [pl.multiple_of((3 * shift_t + 2 * edge) * span, lat) for shift_t in range(3)]
+    return jnp.concatenate([kernel[pl.ds(start, span)] for start in starts], axis=0)
+
+
+def inner_body(
+    lat, tile_ref, predicted, from_pair, inner_picks, outer_picks, kernel, features, edge_sum,
+    wide, border, done, sems
+):
+    frames, patch_rows, patches, _ = predicted.shape
     tall, broad = 2 * patch_rows, 2 * patches
     span = 3 * lat
     chunks = wide.shape[1]
-    lanes = 128 * chunks
+    even = tile_ref[0] % 2 == 0
+    pair_edge = jnp.where(even, 1, 0)
     wide[:, :, 0:8] = jnp.zeros((frames, chunks, 8, 128), F32)
     wide[:, :, 8 + broad :] = jnp.zeros((frames, chunks, 8, 128), F32)
     for side in range(2):
         for frame in range(frames):
-            cells = jnp.zeros((patches, lanes), F32)
+            cells = jnp.zeros((patches, 128 * chunks), F32)
             for r in range(patch_rows):
-                cells += jnp.dot(predicted[frame, r], picks[side, r], preferred_element_type=F32)
+                cells += jnp.dot(predicted[frame, r], inner_picks[side, r], preferred_element_type=F32)
             for chunk in range(chunks):
                 wide[frame, chunk, pl.ds(8 + side, patches, stride=2), :] = cells[:, 128 * chunk : 128 * (chunk + 1)]
     stacks = tap_rows(frames, [shifted(wide, f, broad, lat) for f in range(frames)], broad)
-    copies = []
-    for row in list(range(1, tall - 1)) + [0, tall - 1]:
+
+    def own_sum(row):
         first, last = max(row - 1, 0), min(row + 1, tall - 1)
         total = jnp.zeros((frames * broad, kernel.shape[1]), F32)
         for shift_t in range(3):
@@ -429,18 +469,34 @@
                 kernel[start : start + (last + 1 - first) * span],
                 preferred_element_type=F32,
             )
-        if 0 < row < tall - 1:
-            done[row - 1] = total.astype(BF16).reshape(done.shape[1:])
-            copy = pltpu.make_async_copy(done.at[row - 1], features.at[:, row], sems.at[row - 1])
-            copy.start()
-            copies.append(copy)
-        else:
-            edges[0 if row == 0 else 1] = total
+        return total
+
+    copies = []
+
+    def send(index, row, total):
+        done[index] = total.astype(BF16).reshape(done.shape[1:])
+        copy = pltpu.make_async_copy(done.at[index], features.at[:, row], sems.at[index])
+        copy.start()
+        copies.append(copy)
+
+    for row in range(1, tall - 1):
+        send(row - 1, row, own_sum(row))
+    first, last = own_sum(0), own_sum(tall - 1)
+    edge_sum[...] = jnp.where(even, first, last)
+    taps = jnp.concatenate(border_taps(lat, from_pair, outer_picks, border), axis=0)
+    total = jnp.where(even, last, first) + jnp.dot(
+        taps, border_panel(lat, kernel, pair_edge), preferred_element_type=F32
+    )
+    send(tall - 2, pair_edge * (tall - 1), total)
     for copy in copies:
         copy.wait()
 
 
-def convolve_inner(predicted, picks, kernel):
+def border_lanes(lat):
+    return -(-9 * lat // 128)
+
+
+def convolve_inner(tile, predicted, from_pair, inner_picks, outer_picks, kernel):
     frames, patch_rows, patches, values = predicted.shape
     lat = values // 4
     tall, broad = 2 * patch_rows, 2 * patches
@@ -448,16 +504,17 @@
     lanes = -(-tall * 3 * lat // 128) * 128
     return pl.pallas_call(
         functools.partial(inner_body, lat),
-        in_specs=[WHOLE] * 3,
+        in_specs=[SCALARS] + [WHOLE] * 5,
         out_specs=[ANYWHERE, WHOLE],
         out_shape=[
             jax.ShapeDtypeStruct((frames, tall, broad, channels), BF16),
-            jax.ShapeDtypeStruct((2, frames * broad, channels), F32),
+            jax.ShapeDtypeStruct((frames * broad, channels), F32),
         ],
         scratch_shapes=[
             pltpu.VMEM((frames, lanes // 128, broad + 16, 128), F32),
-            pltpu.VMEM((tall - 2, frames, broad, channels), BF16),
-            pltpu.SemaphoreType.DMA((tall - 2,)),
+            pltpu.VMEM((frames, border_lanes(lat), broad + 16, 128), F32),
+            pltpu.VMEM((tall - 1, frames, broad, channels), BF16),
+            pltpu.SemaphoreType.DMA((tall - 1,)),
         ],
         compiler_params=params(16),
         cost_estimate=pl.CostEstimate(
@@ -466,78 +523,43 @@
             transcendentals=0,
         ),
         name="convolve_inner",
-    )(predicted, picks, kernel)
-
-
-def outer_body(lat, tile_ref, from_pair, from_next, picks, kernel, edges, given, features, wide, done, sems):
-    frames, values = from_pair.shape[0], picks.shape[1]
-    folds = 128 // values
-    patches = from_pair.shape[1] * folds
-    even = tile_ref[0] % 2 == 0
-    broad = 2 * patches
-    tall = features.shape[1]
-    span = 3 * lat
-    chunks = wide.shape[2]
-    lanes = 128 * chunks
-    lane = lax.broadcasted_iota(jnp.int32, (broad, lanes), 1)
+    )(tile, predicted, from_pair, inner_picks, outer_picks, kernel)
+
+
+def outer_body(lat, tile_ref, from_next, picks, kernel, edge_sum, given, features, wide, done, sems):
+    frames, tall, broad, _ = features.shape
+    edge = jnp.where(tile_ref[0] % 2 == 0, 0, 1)
+    panel = border_panel(lat, kernel, edge)
     copies = []
-    for edge in range(2):
-        cells = []
-        for frame in range(frames):
-            rows = jnp.where(even == (edge == 0), from_next[frame], from_pair[frame])
-            parts = [rows[:, k * values : (k + 1) * values] for k in range(folds)]
-            cells.append(jnp.concatenate(parts, axis=0))
-        wide[edge, :, :, 0:8] = jnp.zeros((frames, chunks, 8, 128), F32)
-        wide[edge, :, :, 8 + broad :] = jnp.zeros((frames, chunks, 8, 128), F32)
-        for side in range(2):
-            for frame in range(frames):
-                spread = jnp.dot(cells[frame], picks[side], preferred_element_type=F32)
-                for chunk in range(chunks):
-                    wide[edge, frame, chunk, pl.ds(8 + side, patches, stride=2), :] = spread[
-                        :, 128 * chunk : 128 * (chunk + 1)
-                    ]
-        ready = [shifted(wide.at[edge], f, broad, lat) for f in range(frames)]
-        rows = []
-        for frame in range(frames):
-            taps = jnp.zeros((broad, lanes), BF16)
-            for shift_t in range(3):
-                if frame + shift_t - 2 >= 0:
-                    taps = jnp.where(lane // span == shift_t, ready[frame + shift_t - 2], taps)
-            rows.append(taps)
-        shift_y = 2 * edge
-        panel = jnp.concatenate(
-            [kernel[(3 * t + shift_y) * span : (3 * t + shift_y + 1) * span] for t in range(3)], axis=0
-        )
-        total = edges[edge] + jnp.dot(
-            jnp.concatenate(rows, axis=0)[:, : 3 * span], panel, preferred_element_type=F32
-        )
-        done[edge] = total.astype(BF16).reshape(done.shape[1:])
-        copy = pltpu.make_async_copy(done.at[edge], features.at[:, edge * (tall - 1)], sems.at[edge])
+    for frame, taps in enumerate(border_taps(lat, from_next, picks, wide)):
+        total = edge_sum[frame * broad : (frame + 1) * broad] + jnp.dot(
+            taps, panel, preferred_element_type=F32
+        )
+        done[frame] = total.astype(BF16)
+        copy = pltpu.make_async_copy(done.at[frame], features.at[frame, edge * (tall - 1)], sems.at[frame])
         copy.start()
         copies.append(copy)
     for copy in copies:
         copy.wait()
 
 
-def convolve_outer(tile, from_pair, from_next, picks, kernel, edges, features):
-    frames, tall, broad, _ = features.shape
+def convolve_outer(tile, from_next, picks, kernel, edge_sum, features):
+    frames, tall, broad, channels = features.shape
     lat = picks.shape[1] // 2
-    channels = kernel.shape[1]
-    lanes = -(-9 * lat // 128) * 128
     return pl.pallas_call(
         functools.partial(outer_body, lat),
-        in_specs=[SCALARS] + [WHOLE] * 5 + [ANYWHERE],
+        in_specs=[SCALARS] + [WHOLE] * 4 + [ANYWHERE],
         out_specs=ANYWHERE,
         out_shape=jax.ShapeDtypeStruct(features.shape, BF16),
-        input_output_aliases={6: 0},
+        input_output_aliases={5: 0},
         scratch_shapes=[
-            pltpu.VMEM((2, frames, lanes // 128, broad + 16, 128), F32),
-            pltpu.VMEM((2, frames, broad, channels), BF16),
-            pltpu.SemaphoreType.DMA((2,)),
+            pltpu.VMEM((frames, border_lanes(lat), broad + 16, 128), F32),
+            pltpu.VMEM((frames, broad, channels), BF16),
+            pltpu.SemaphoreType.DMA((frames,)),
         ],
         compiler_params=params(16),
         name="convolve_outer",
-    )(tile, from_pair, from_next, picks, kernel, edges, features)
+    )(tile, from_next, picks, kernel, edge_sum, features)
 
 
 def exchange(value, offset):
@@ -623,8 +645,8 @@
     swaps = [(i, i + 1) for i in range(1, count - 1, 2)] + [(i + 1, i) for i in range(1, count - 1, 2)]
     from_next = lax.ppermute(to_next, "seq", swaps)
     from_pair = exchange(to_pair, 1)
-    features, edges = convolve_inner(predicted, inner_picks, decode)
-    return convolve_outer(tile, from_pair, from_next, outer_picks, decode, edges, features)
+    features, edge_sum = convolve_inner(tile, predicted, from_pair, inner_picks, outer_picks, decode)
+    return convolve_outer(tile, from_next, outer_picks, decode, edge_sum, features)
 
 
 def solution(mesh):

time: 34.9 us -> 34.6 us (level)
  waiting for transfers between devices: 5.8 us -> 5.38 us
    pallas_call x1, Pallas kernels: 1.44 us -> 2.08 us  [convolve_inner(): pl.pallas_call(functools.partial(inner_body, lat), in_specs=[SCALARS] + [...]
    ppermute x1, waiting for transfers between devices: 1.06 us -> 0.41 us  [local(): from_next = lax.ppermute(to_next, 'seq', swaps)]
  transfers between devices with their start and end apart: 14 -> 14, of which waited for: 8 -> 8; matrix products, arithmetic and copies ran while one was open for 0% -> 0% of each run, Pallas kernels for 29% -> 30%
where the time goes in v8:
time: 34.6 us; the launch traced here: 34.4 us
  starting transfers between devices  17 us (49%)
  Pallas kernels  11.9 us (34%)
  waiting for transfers between devices  5.38 us (16%)
    ppermute x13, starting transfers between devices, exchange(): return lax.ppermute(value, 'seq', [(i, i ^ offset) for i in range(count)])  14.9 us
    ppermute x13, waiting for transfers between devices, exchange(): return lax.ppermute(value, 'seq', [(i, i ^ offset) for i in range(count)])  4.97 us
    pallas_call x2, Pallas kernels, attend_own(): pl.pallas_call(functools.partial(own_body, turns, blocks_here, groups), i...  4.56 us
    pallas_call x1, Pallas kernels, attend_past(): pl.pallas_call(functools.partial(past_body, sizes, len(packed)), in_specs...  2.67 us
    ppermute x1, starting transfers between devices, local(): from_next = lax.ppermute(to_next, 'seq', swaps)  2.1 us
    pallas_call x1, Pallas kernels, convolve_inner(): pl.pallas_call(functools.partial(inner_body, lat), in_specs=[SCALARS] + [...  2.08 us
    pallas_call x1, Pallas kernels, convolve_outer(): pl.pallas_call(functools.partial(outer_body, lat), in_specs=[SCALARS] + [...  1.07 us
  transfers between devices with their start and end apart: 14, of which 8 were waited for; matrix products, arithmetic and copies ran while one was open for 0% of the time, Pallas kernels for 30%

profile of v8, /device:TPU:1, one launch (start us, length us, event | category | flops | bytes accessed | tf_op | source)
XLA Modules:
  0.0 34.4 jit_solution(7322937331039333271)
XLA Ops:
  0.0 0.0 copy-start.1
  0.0 0.0 copy-start.2
  0.0 0.0 copy-start.4
  0.0 0.0 copy-start.3
  0.0 0.0 copy-start.6
  0.0 0.0 copy-start.5
  0.0 0.0 copy-start.7
  0.0 2.2 %collective-permute-start = (bf16[2,16,1024]{2,1,0:T(8,128)(2,1)}, bf16[2,16,1024]{2,1,0:T(8,128)(2,1)S(1)}, u32[]{:S(2)}, u32[]{:S(2)}) collective-permute-start(bf16[2,16,1024]{2,1,0:T(8,128)(2,1)} %refs_0_.1), channel_id=1, source_target_pairs={{0,4},{1,5},{2,6},{3,7},{4,0},{5,1},{6,2},{7,3},{8,12},{9,13},{10,... | collective-permute-start | bytes 196616 | tf_op jit(solution)/shard_map/ppermute | solution.py:567
  2.2 2.3 %collective-permute-start.1 = (bf16[2,16,1024]{2,1,0:T(8,128)(2,1)}, bf16[2,16,1024]{2,1,0:T(8,128)(2,1)S(1)}, u32[]{:S(2)}, u32[]{:S(2)}) collective-permute-start(bf16[2,16,1024]{2,1,0:T(8,128)(2,1)} %refs_0_.1), channel_id=1, source_target_pairs={{0,8},{1,9},{2,10},{3,11},{4,12},{5,13},{6,14},{7,15},{8,0},{9,1},... | collective-permute-start | bytes 196616 | tf_op jit(solution)/shard_map/ppermute | solution.py:567
  4.6 0.0 collective-permute-start.2
  4.6 0.0 copy-done.1
  4.6 1.3 %collective-permute-start.3 = (bf16[64,192]{1,0:T(8,128)(2,1)S(1)}, bf16[64,192]{1,0:T(8,128)(2,1)S(1)}, u32[]{:S(2)}, u32[]{:S(2)}) collective-permute-start(bf16[64,192]{1,0:T(8,128)(2,1)S(1)} %bitcast.6), channel_id=1, source_target_pairs={{0,2},{1,3},{2,0},{3,1},{4,6},{5,7},{6,4},{7,5},{8,10},{9,11},{10,... | collective-permute-start | bytes 73736 | tf_op jit(solution)/shard_map/ppermute | solution.py:567
  5.9 0.0 copy-done.2
  5.9 0.3 collective-permute-start.4
  6.1 0.0 copy-done.4
  6.1 0.0 copy-done.3
  6.2 0.0 copy-done.6
  6.2 0.0 copy-done.5
  6.2 0.0 copy-done.7
  6.2 0.0 copy-start
  6.2 2.3 %attend_own.2 = (bf16[2,1536,256]{2,1,0:T(8,128)(2,1)S(1)}, f32[2,1536,128]{2,1,0:T(8,128)S(1)}, s32[16]{0:T(128)}) custom-call(s32[1]{0:T(128)} %bitcast.tile_ref, s32[32]{0:T(128)S(1)} %copy-done.6, s32[16,16]{1,0:T(8,128)S(1)} %copy-done.5, s32[16]{0:T(128)S(1)} %copy-done.7, bf16[256,3072]{1,0:T(8,128)(2,1)S(1)} %bitcast.10, bf16[256,1024]{1,0:T(8,128)(2,1)S(1)} %bitcast.12), custom_call_target="tpu_custom_call" | custom-call | flops 1207959552 | tf_op jit(solution)/shard_map/attend_own/pallas_call | solution.py:77
  8.5 0.0 collective-permute-done.3.final_across
  8.5 0.5 %collective-permute-done.4.decode_across = bf16[32,432]{1,0:T(8,128)(2,1)S(1)} collective-permute-done((bf16[32,432]{1,0:T(8,128)(2,1)S(1)}, bf16[32,432]{1,0:T(8,128)(2,1)S(1)}, u32[]{:S(2)}, u32[]{:S(2)}) %collective-permute-start.4) | collective-permute-done | bytes 27680 | tf_op jit(solution)/shard_map/ppermute | solution.py:567
  9.0 0.0 collective-permute-done.refs_1_
  9.0 0.0 collective-permute-done.1.refs_2_
  9.0 0.8 %collective-permute-done.2.refs_3_ = bf16[2,16,1024]{2,1,0:T(8,128)(2,1)S(1)} collective-permute-done((bf16[2,16,1024]{2,1,0:T(8,128)(2,1)}, bf16[2,16,1024]{2,1,0:T(8,128)(2,1)S(1)}, u32[]{:S(2)}, u32[]{:S(2)}) %collective-permute-start.2) | collective-permute-done | bytes 65568 | tf_op jit(solution)/shard_map/ppermute | solution.py:567
  9.8 0.0 copy-done
  9.8 1.3 %collective-permute-start.5 = (bf16[8,16,1024]{2,1,0:T(8,128)(2,1)S(1)}, bf16[8,16,1024]{2,1,0:T(8,128)(2,1)S(1)}, u32[]{:S(2)}, u32[]{:S(2)}) collective-permute-start(bf16[8,16,1024]{2,1,0:T(8,128)(2,1)S(1)} %join_near.1.refs_0_), channel_id=1, source_target_pairs={{0,2},{1,3},{2,0},{3,1},{4,6},{5,7},{6,4},{7,5},{8,10},{9,11},{10,... | collective-permute-start | bytes 786440 | tf_op jit(solution)/shard_map/ppermute | solution.py:567
  11.1 0.1 pack.1.refs_0_
  11.2 1.9 %collective-permute-start.6 = (bf16[2,16,1664]{2,1,0:T(8,128)(2,1)S(1)}, bf16[2,16,1664]{2,1,0:T(8,128)(2,1)S(1)}, u32[]{:S(2)}, u32[]{:S(2)}) collective-permute-start(bf16[2,16,1664]{2,1,0:T(8,128)(2,1)S(1)} %pack.1.refs_0_), channel_id=1, source_target_pairs={{0,8},{1,9},{2,10},{3,11},{4,12},{5,13},{6,14},{7,15},{8,0},{9,1},... | collective-permute-start | bytes 319496 | tf_op jit(solution)/shard_map/ppermute | solution.py:567
  13.1 0.5 %collective-permute-start.7 = (bf16[2,16,1664]{2,1,0:T(8,128)(2,1)S(1)}, bf16[2,16,1664]{2,1,0:T(8,128)(2,1)S(1)}, u32[]{:S(2)}, u32[]{:S(2)}) collective-permute-start(bf16[2,16,1664]{2,1,0:T(8,128)(2,1)S(1)} %pack.1.refs_0_), channel_id=1, source_target_pairs={{0,4},{1,5},{2,6},{3,7},{4,0},{5,1},{6,2},{7,3},{8,12},{9,13},{10,... | collective-permute-start | bytes 319496 | tf_op jit(solution)/shard_map/ppermute | solution.py:567
  13.5 2.3 %attend_own.3 = (bf16[2,1536,256]{2,1,0:T(8,128)(2,1)S(1)}, f32[2,1536,128]{2,1,0:T(8,128)S(1)}, s32[16]{0:T(128)S(1)}) custom-call(s32[1]{0:T(128)} %bitcast.tile_ref, s32[32]{0:T(128)S(1)} %copy-done.6, s32[16,16]{1,0:T(8,128)S(1)} %copy-done.5, s32[16]{0:T(128)S(1)} %copy-done.7, bf16[256,3072]{1,0:T(8,128)(2,1)S(1)} %bitcast.11, ...), custom_call_target="tpu_custom_call" | custom-call | flops 1207959552 | tf_op jit(solution)/shard_map/attend_own/pallas_call | solution.py:77
  15.8 1.1 %collective-permute-done.6.refs_1_ = bf16[2,16,1664]{2,1,0:T(8,128)(2,1)S(1)} collective-permute-done((bf16[2,16,1664]{2,1,0:T(8,128)(2,1)S(1)}, bf16[2,16,1664]{2,1,0:T(8,128)(2,1)S(1)}, u32[]{:S(2)}, u32[]{:S(2)}) %collective-permute-start.6) | collective-permute-done | bytes 106528 | tf_op jit(solution)/shard_map/ppermute | solution.py:567
  16.9 0.6 %collective-permute-done.7.refs_2_ = bf16[2,16,1664]{2,1,0:T(8,128)(2,1)S(1)} collective-permute-done((bf16[2,16,1664]{2,1,0:T(8,128)(2,1)S(1)}, bf16[2,16,1664]{2,1,0:T(8,128)(2,1)S(1)}, u32[]{:S(2)}, u32[]{:S(2)}) %collective-permute-start.7) | collective-permute-done | bytes 106528 | tf_op jit(solution)/shard_map/ppermute | solution.py:567
  17.5 0.0 collective-permute-done.5.refs_1_
  17.6 3.7 %collective-permute-start.10 = (bf16[16,16,1024]{2,1,0:T(8,128)(2,1)S(1)}, bf16[16,16,1024]{2,1,0:T(8,128)(2,1)S(1)}, u32[]{:S(2)}, u32[]{:S(2)}) collective-permute-start(bf16[16,16,1024]{2,1,0:T(8,128)(2,1)S(1)} %join_chip.1.refs_4_), channel_id=1, source_target_pairs={{0,1},{1,0},{2,3},{3,2},{4,5},{5,4},{6,7},{7,6},{8,9},{9,8},{10,11... | collective-permute-start | bytes 1572872 | tf_op jit(solution)/shard_map/ppermute | solution.py:567
  21.2 0.0 collective-permute-start.8
  21.3 0.3 collective-permute-start.9
  21.6 1.2 %collective-permute-done.10.refs_5_ = bf16[16,16,1024]{2,1,0:T(8,128)(2,1)S(1)} collective-permute-done((bf16[16,16,1024]{2,1,0:T(8,128)(2,1)S(1)}, bf16[16,16,1024]{2,1,0:T(8,128)(2,1)S(1)}, u32[]{:S(2)}, u32[]{:S(2)}) %collective-permute-start.10) | collective-permute-done | bytes 524320 | tf_op jit(solution)/shard_map/ppermute | solution.py:567
  22.8 2.7 %attend_past.1.attended = bf16[256,3072]{1,0:T(8,128)(2,1)S(1)} custom-call(s32[16]{0:T(128)S(1)} %get-tuple-element.52.slots, bf16[2,1536,256]{2,1,0:T(8,128)(2,1)S(1)} %get-tuple-element.53.refs_0_, bf16[2,1536,256]{2,1,0:T(8,128)(2,1)S(1)} %get-tuple-element.54.refs_1_, f32[2,1536,128]{2,1,0:T(8,128)S(1)} %get-tuple-element.55.refs_2_, ...), custom_call_target="tpu_custom_call" | custom-call | flops 10000000000 | tf_op jit(solution)/shard_map/attend_past/pallas_call | solution.py:193
  25.4 0.3 collective-permute-done.8.ours.refs_1_
  25.8 0.0 collective-permute-done.9.theirs.refs_2_
  25.8 0.9 %collective-permute-start.11 = (bf16[2,16,1664]{2,1,0:T(8,128)(2,1)S(1)}, bf16[2,16,1664]{2,1,0:T(8,128)(2,1)S(1)}, u32[]{:S(2)}, u32[]{:S(2)}) collective-permute-start(bf16[2,16,1664]{2,1,0:T(8,128)(2,1)S(1)} %collective-permute-done.8.ours.refs_1_), channel_id=1, source_target_pairs={{0,1},{1,0},{2,3},{3,2},{4,5},{5,4},{6,7},{7,6},{8,9},{9,8},{10,11... | collective-permute-start | bytes 319496 | tf_op jit(solution)/shard_map/ppermute | solution.py:567
  26.6 0.5 %project.1.part = f32[256,64]{1,0:T(8,128)S(1)} custom-call(s32[1]{0:T(128)} %bitcast.tile_ref, bf16[256,3072]{1,0:T(8,128)(2,1)S(1)} %attend_past.1.attended, bf16[6,16,1664]{2,1,0:T(8,128)(2,1)S(1)} %join_panels.1.ours.refs_0_, bf16[6,16,1664]{2,1,0:T(8,128)(2,1)S(1)} %collective-permute-done.9.theirs.refs_2_), custom_call_target="tpu_custom_call" | custom-call | tf_op jit(solution)/shard_map/project/pallas_call | solution.py:281
  27.2 0.4 %collective-permute-done.11.theirs.refs_3_ = bf16[2,16,1664]{2,1,0:T(8,128)(2,1)S(1)} collective-permute-done((bf16[2,16,1664]{2,1,0:T(8,128)(2,1)S(1)}, bf16[2,16,1664]{2,1,0:T(8,128)(2,1)S(1)}, u32[]{:S(2)}, u32[]{:S(2)}) %collective-permute-start.11) | collective-permute-done | bytes 106528 | tf_op jit(solution)/shard_map/ppermute | solution.py:567
  27.6 0.4 %finish.1 = (bf16[256,64]{1,0:T(8,128)(2,1)S(1)}, bf16[2,16,128]{2,1,0:T(8,128)(2,1)S(1)}, bf16[2,16,128]{2,1,0:T(8,128)(2,1)S(1)}) custom-call(s32[1]{0:T(128)} %bitcast.tile_ref, bf16[256,3072]{1,0:T(8,128)(2,1)S(1)} %attend_past.1.attended, bf16[2,16,1664]{2,1,0:T(8,128)(2,1)S(1)} %collective-permute-done.8.ours.refs_1_, ...), custom_call_target="tpu_custom_call" | custom-call | tf_op jit(solution)/shard_map/finish/pallas_call | solution.py:315
  28.0 0.4 %collective-permute-start.13 = (bf16[2,16,128]{2,1,0:T(8,128)(2,1)S(1)}, bf16[2,16,128]{2,1,0:T(8,128)(2,1)S(1)}, u32[]{:S(2)}, u32[]{:S(2)}) collective-permute-start(bf16[2,16,128]{2,1,0:T(8,128)(2,1)S(1)} %get-tuple-element.65), channel_id=1, source_target_pairs={{0,1},{1,0},{2,3},{3,2},{4,5},{5,4},{6,7},{7,6},{8,9},{9,8},{10,11... | collective-permute-start | bytes 24584 | tf_op jit(solution)/shard_map/ppermute | solution.py:567
  28.4 2.1 %collective-permute-start.12 = (bf16[2,16,128]{2,1,0:T(8,128)(2,1)S(1)}, bf16[2,16,128]{2,1,0:T(8,128)(2,1)S(1)}, u32[]{:S(2)}, u32[]{:S(2)}) collective-permute-start(bf16[2,16,128]{2,1,0:T(8,128)(2,1)S(1)} %get-tuple-element.62), channel_id=1, source_target_pairs={{1,2},{3,4},{5,6},{7,8},{9,10},{11,12},{13,14},{2,1},{4,3},{6,5},{... | collective-permute-start | bytes 24584 | tf_op jit(solution)/shard_map/ppermute | solution.py:646
  30.5 0.3 unpack.1.kernel
  30.9 0.0 collective-permute-done.13.from_pair
  30.9 2.1 %convolve_inner.1 = (bf16[2,4,128,512]{3,2,1,0:T(8,128)(2,1)}, f32[256,512]{1,0:T(8,128)S(1)}) custom-call(s32[1]{0:T(128)} %bitcast.tile_ref, bf16[2,2,64,64]{3,2,1,0:T(8,128)(2,1)S(1)} %bitcast.14, bf16[2,16,128]{2,1,0:T(8,128)(2,1)S(1)} %collective-permute-done.13.from_pair, bf16[2,2,64,256]{3,2,1,0:T(8,128)(2,1)S(1)} %get-tuple-element.66.inner_picks, ...), custom_call_target="tpu_custom_call" | custom-call | flops 452984832 | bytes 1048576 | tf_op jit(solution)/shard_map/convolve_inner/pallas_call | solution.py:505
  33.0 0.4 %collective-permute-done.12.from_next = bf16[2,16,128]{2,1,0:T(8,128)(2,1)S(1)} collective-permute-done((bf16[2,16,128]{2,1,0:T(8,128)(2,1)S(1)}, bf16[2,16,128]{2,1,0:T(8,128)(2,1)S(1)}, u32[]{:S(2)}, u32[]{:S(2)}) %collective-permute-start.12) | collective-permute-done | bytes 8224 | tf_op jit(solution)/shard_map/ppermute | solution.py:646
  33.4 1.1 %convolve_outer.1 = bf16[2,4,128,512]{3,2,1,0:T(8,128)(2,1)} custom-call(s32[1]{0:T(128)} %bitcast.tile_ref, bf16[2,16,128]{2,1,0:T(8,128)(2,1)S(1)} %collective-permute-done.12.from_next, bf16[2,32,256]{2,1,0:T(8,128)(2,1)S(1)} %get-tuple-element.63.outer_picks.picks, bf16[432,512]{1,0:T(8,128)(2,1)S(1)} %unpack.1.kernel, ...), custom_call_target="tpu_custom_call", output_to_operand_aliasing={{}: (5, {})} | custom-call | tf_op jit(solution)/shard_map/convolve_outer/pallas_call | solution.py:549
  (4 shorter events, 0.1 us)
Async XLA Ops:
  0.0 4.6 %copy-start.1 = (bf16[192,64]{0,1:T(8,128)(2,1)S(1)}, bf16[192,64]{0,1:T(8,128)(2,1)}, u32[]{:S(2)}) copy-start(bf16[192,64]{0,1:T(8,128)(2,1)} %param.14) | copy-start | bytes 73732
  0.0 5.9 %copy-start.2 = (bf16[432,32]{0,1:T(8,128)(2,1)S(1)}, bf16[432,32]{0,1:T(8,128)(2,1)}, u32[]{:S(2)}) copy-start(bf16[432,32]{0,1:T(8,128)(2,1)} %param.15) | copy-start | bytes 82948
  0.0 6.1 %copy-start.4 = (bf16[2,2,64,1024]{3,2,1,0:T(8,128)(2,1)S(1)}, bf16[2,2,64,1024]{3,2,1,0:T(8,128)(2,1)}, u32[]{:S(2)}) copy-start(bf16[2,2,64,1024]{3,2,1,0:T(8,128)(2,1)} %param.9) | copy-start | bytes 1572868
  0.0 6.1 %copy-start.3 = (bf16[2,2,64,3072]{3,2,1,0:T(8,128)(2,1)S(1)}, bf16[2,2,64,3072]{3,2,1,0:T(8,128)(2,1)}, u32[]{:S(2)}) copy-start(bf16[2,2,64,3072]{3,2,1,0:T(8,128)(2,1)} %param.8) | copy-start | bytes 4718596
  0.0 6.1 %copy-start.6 = (s32[32]{0:T(128)S(1)}, s32[32]{0:T(128)}, u32[]{:S(2)}) copy-start(s32[32]{0:T(128)} %home.3) | copy-start | bytes 388
  0.0 6.1 %copy-start.5 = (s32[16,16]{1,0:T(8,128)S(1)}, s32[16,16]{1,0:T(8,128)}, u32[]{:S(2)}) copy-start(s32[16,16]{1,0:T(8,128)} %blocks.3) | copy-start | bytes 3076
  0.0 6.1 %copy-start.7 = (s32[16]{0:T(128)S(1)}, s32[16]{0:T(128)}, u32[]{:S(2)}) copy-start(s32[16]{0:T(128)} %lens.3) | copy-start | bytes 196
  0.0 8.9 %collective-permute-start = (bf16[2,16,1024]{2,1,0:T(8,128)(2,1)}, bf16[2,16,1024]{2,1,0:T(8,128)(2,1)S(1)}, u32[]{:S(2)}, u32[]{:S(2)}) collective-permute-start(bf16[2,16,1024]{2,1,0:T(8,128)(2,1)} %refs_0_.1), channel_id=1, source_target_pairs={{0,4},{1,5},{2,6},{3,7},{4,0},{5,1},{6,2},{7,3},{8,12},{9,13},{10,... | collective-permute-start | bytes 196616 | tf_op jit(solution)/shard_map/ppermute | solution.py:567
  2.2 6.7 %collective-permute-start.1 = (bf16[2,16,1024]{2,1,0:T(8,128)(2,1)}, bf16[2,16,1024]{2,1,0:T(8,128)(2,1)S(1)}, u32[]{:S(2)}, u32[]{:S(2)}) collective-permute-start(bf16[2,16,1024]{2,1,0:T(8,128)(2,1)} %refs_0_.1), channel_id=1, source_target_pairs={{0,8},{1,9},{2,10},{3,11},{4,12},{5,13},{6,14},{7,15},{8,0},{9,1},... | collective-permute-start | bytes 196616 | tf_op jit(solution)/shard_map/ppermute | solution.py:567
  4.6 5.2 %collective-permute-start.2 = (bf16[2,16,1024]{2,1,0:T(8,128)(2,1)}, bf16[2,16,1024]{2,1,0:T(8,128)(2,1)S(1)}, u32[]{:S(2)}, u32[]{:S(2)}) collective-permute-start(bf16[2,16,1024]{2,1,0:T(8,128)(2,1)} %refs_0_.1), channel_id=1, source_target_pairs={{0,12},{1,13},{2,14},{3,15},{4,8},{5,9},{6,10},{7,11},{8,4},{9,5},... | collective-permute-start | bytes 196616 | tf_op jit(solution)/shard_map/ppermute | solution.py:567
  4.6 3.8 %collective-permute-start.3 = (bf16[64,192]{1,0:T(8,128)(2,1)S(1)}, bf16[64,192]{1,0:T(8,128)(2,1)S(1)}, u32[]{:S(2)}, u32[]{:S(2)}) collective-permute-start(bf16[64,192]{1,0:T(8,128)(2,1)S(1)} %bitcast.6), channel_id=1, source_target_pairs={{0,2},{1,3},{2,0},{3,1},{4,6},{5,7},{6,4},{7,5},{8,10},{9,11},{10,... | collective-permute-start | bytes 73736 | tf_op jit(solution)/shard_map/ppermute | solution.py:567
  5.9 3.1 %collective-permute-start.4 = (bf16[32,432]{1,0:T(8,128)(2,1)S(1)}, bf16[32,432]{1,0:T(8,128)(2,1)S(1)}, u32[]{:S(2)}, u32[]{:S(2)}) collective-permute-start(bf16[32,432]{1,0:T(8,128)(2,1)S(1)} %bitcast.8), channel_id=1, source_target_pairs={{0,2},{1,3},{2,0},{3,1},{4,6},{5,7},{6,4},{7,5},{8,10},{9,11},{10,... | collective-permute-start | bytes 82952 | tf_op jit(solution)/shard_map/ppermute | solution.py:567
  6.2 3.6 %copy-start = (bf16[2,16,1024]{2,1,0:T(8,128)(2,1)S(1)}, bf16[2,16,1024]{2,1,0:T(8,128)(2,1)}, u32[]{:S(2)}) copy-start(bf16[2,16,1024]{2,1,0:T(8,128)(2,1)} %refs_0_.1) | copy-start | bytes 196612
  9.8 7.7 %collective-permute-start.5 = (bf16[8,16,1024]{2,1,0:T(8,128)(2,1)S(1)}, bf16[8,16,1024]{2,1,0:T(8,128)(2,1)S(1)}, u32[]{:S(2)}, u32[]{:S(2)}) collective-permute-start(bf16[8,16,1024]{2,1,0:T(8,128)(2,1)S(1)} %join_near.1.refs_0_), channel_id=1, source_target_pairs={{0,2},{1,3},{2,0},{3,1},{4,6},{5,7},{6,4},{7,5},{8,10},{9,11},{10,... | collective-permute-start | bytes 786440 | tf_op jit(solution)/shard_map/ppermute | solution.py:567
  11.2 5.8 %collective-permute-start.6 = (bf16[2,16,1664]{2,1,0:T(8,128)(2,1)S(1)}, bf16[2,16,1664]{2,1,0:T(8,128)(2,1)S(1)}, u32[]{:S(2)}, u32[]{:S(2)}) collective-permute-start(bf16[2,16,1664]{2,1,0:T(8,128)(2,1)S(1)} %pack.1.refs_0_), channel_id=1, source_target_pairs={{0,8},{1,9},{2,10},{3,11},{4,12},{5,13},{6,14},{7,15},{8,0},{9,1},... | collective-permute-start | bytes 319496 | tf_op jit(solution)/shard_map/ppermute | solution.py:567
  13.1 4.5 %collective-permute-start.7 = (bf16[2,16,1664]{2,1,0:T(8,128)(2,1)S(1)}, bf16[2,16,1664]{2,1,0:T(8,128)(2,1)S(1)}, u32[]{:S(2)}, u32[]{:S(2)}) collective-permute-start(bf16[2,16,1664]{2,1,0:T(8,128)(2,1)S(1)} %pack.1.refs_0_), channel_id=1, source_target_pairs={{0,4},{1,5},{2,6},{3,7},{4,0},{5,1},{6,2},{7,3},{8,12},{9,13},{10,... | collective-permute-start | bytes 319496 | tf_op jit(solution)/shard_map/ppermute | solution.py:567
  17.6 5.2 %collective-permute-start.10 = (bf16[16,16,1024]{2,1,0:T(8,128)(2,1)S(1)}, bf16[16,16,1024]{2,1,0:T(8,128)(2,1)S(1)}, u32[]{:S(2)}, u32[]{:S(2)}) collective-permute-start(bf16[16,16,1024]{2,1,0:T(8,128)(2,1)S(1)} %join_chip.1.refs_4_), channel_id=1, source_target_pairs={{0,1},{1,0},{2,3},{3,2},{4,5},{5,4},{6,7},{7,6},{8,9},{9,8},{10,11... | collective-permute-start | bytes 1572872 | tf_op jit(solution)/shard_map/ppermute | solution.py:567
  21.2 4.5 %collective-permute-start.8 = (bf16[2,16,1664]{2,1,0:T(8,128)(2,1)S(1)}, bf16[2,16,1664]{2,1,0:T(8,128)(2,1)S(1)}, u32[]{:S(2)}, u32[]{:S(2)}) collective-permute-start(bf16[2,16,1664]{2,1,0:T(8,128)(2,1)S(1)} %collective-permute-done.6.refs_1_), channel_id=1, source_target_pairs={{0,4},{1,5},{2,6},{3,7},{4,0},{5,1},{6,2},{7,3},{8,12},{9,13},{10,... | collective-permute-start | bytes 319496 | tf_op jit(solution)/shard_map/ppermute | solution.py:567
  21.3 4.5 %collective-permute-start.9 = (bf16[6,16,1664]{2,1,0:T(8,128)(2,1)S(1)}, bf16[6,16,1664]{2,1,0:T(8,128)(2,1)S(1)}, u32[]{:S(2)}, u32[]{:S(2)}) collective-permute-start(bf16[6,16,1664]{2,1,0:T(8,128)(2,1)S(1)} %join_panels.1.ours.refs_0_), channel_id=1, source_target_pairs={{0,1},{1,0},{2,3},{3,2},{4,5},{5,4},{6,7},{7,6},{8,9},{9,8},{10,11... | collective-permute-start | bytes 958472 | tf_op jit(solution)/shard_map/ppermute | solution.py:567
  25.8 1.8 %collective-permute-start.11 = (bf16[2,16,1664]{2,1,0:T(8,128)(2,1)S(1)}, bf16[2,16,1664]{2,1,0:T(8,128)(2,1)S(1)}, u32[]{:S(2)}, u32[]{:S(2)}) collective-permute-start(bf16[2,16,1664]{2,1,0:T(8,128)(2,1)S(1)} %collective-permute-done.8.ours.refs_1_), channel_id=1, source_target_pairs={{0,1},{1,0},{2,3},{3,2},{4,5},{5,4},{6,7},{7,6},{8,9},{9,8},{10,11... | collective-permute-start | bytes 319496 | tf_op jit(solution)/shard_map/ppermute | solution.py:567
  28.0 2.9 %collective-permute-start.13 = (bf16[2,16,128]{2,1,0:T(8,128)(2,1)S(1)}, bf16[2,16,128]{2,1,0:T(8,128)(2,1)S(1)}, u32[]{:S(2)}, u32[]{:S(2)}) collective-permute-start(bf16[2,16,128]{2,1,0:T(8,128)(2,1)S(1)} %get-tuple-element.65), channel_id=1, source_target_pairs={{0,1},{1,0},{2,3},{3,2},{4,5},{5,4},{6,7},{7,6},{8,9},{9,8},{10,11... | collective-permute-start | bytes 24584 | tf_op jit(solution)/shard_map/ppermute | solution.py:567
  28.4 5.0 %collective-permute-start.12 = (bf16[2,16,128]{2,1,0:T(8,128)(2,1)S(1)}, bf16[2,16,128]{2,1,0:T(8,128)(2,1)S(1)}, u32[]{:S(2)}, u32[]{:S(2)}) collective-permute-start(bf16[2,16,128]{2,1,0:T(8,128)(2,1)S(1)} %get-tuple-element.62), channel_id=1, source_target_pairs={{1,2},{3,4},{5,6},{7,8},{9,10},{11,12},{13,14},{2,1},{4,3},{6,5},{... | collective-permute-start | bytes 24584 | tf_op jit(solution)/shard_map/ppermute | solution.py:646

commit v9 on v8

--- a/solution.py
+++ b/solution.py
@@ -439,7 +439,7 @@
 
 
 def inner_body(
-    lat, tile_ref, predicted, from_pair, inner_picks, outer_picks, kernel, features, edge_sum,
+    lat, tile_ref, predicted, from_pair, inner_picks, outer_picks, kernel, features, edge_sum, pair_row,
     wide, border, done, sems
 ):
     frames, patch_rows, patches, _ = predicted.shape
@@ -487,7 +487,7 @@
     total = jnp.where(even, last, first) + jnp.dot(
         taps, border_panel(lat, kernel, pair_edge), preferred_element_type=F32
     )
-    send(tall - 2, pair_edge * (tall - 1), total)
+    pair_row[...] = total.astype(BF16).reshape(pair_row.shape)
     for copy in copies:
         copy.wait()
 
@@ -505,16 +505,17 @@
     return pl.pallas_call(
         functools.partial(inner_body, lat),
         in_specs=[SCALARS] + [WHOLE] * 5,
-        out_specs=[ANYWHERE, WHOLE],
+        out_specs=[ANYWHERE, WHOLE, WHOLE],
         out_shape=[
             jax.ShapeDtypeStruct((frames, tall, broad, channels), BF16),
             jax.ShapeDtypeStruct((frames * broad, channels), F32),
+            jax.ShapeDtypeStruct((frames, broad, channels), BF16),
         ],
         scratch_shapes=[
             pltpu.VMEM((frames, lanes // 128, broad + 16, 128), F32),
             pltpu.VMEM((frames, border_lanes(lat), broad + 16, 128), F32),
-            pltpu.VMEM((tall - 1, frames, broad, channels), BF16),
-            pltpu.SemaphoreType.DMA((tall - 1,)),
+            pltpu.VMEM((tall - 2, frames, broad, channels), BF16),
+            pltpu.SemaphoreType.DMA((tall - 2,)),
         ],
         compiler_params=params(16),
         cost_estimate=pl.CostEstimate(
@@ -526,11 +527,12 @@
     )(tile, predicted, from_pair, inner_picks, outer_picks, kernel)
 
 
-def outer_body(lat, tile_ref, from_next, picks, kernel, edge_sum, given, features, wide, done, sems):
+def outer_body(lat, tile_ref, from_next, picks, kernel, edge_sum, pair_row, given, features, wide, done, sems):
     frames, tall, broad, _ = features.shape
     edge = jnp.where(tile_ref[0] % 2 == 0, 0, 1)
     panel = border_panel(lat, kernel, edge)
-    copies = []
+    copies = [pltpu.make_async_copy(pair_row, features.at[:, (1 - edge) * (tall - 1)], sems.at[frames])]
+    copies[0].start()
     for frame, taps in enumerate(border_taps(lat, from_next, picks, wide)):
         total = edge_sum[frame * broad : (frame + 1) * broad] + jnp.dot(
             taps, panel, preferred_element_type=F32
@@ -543,23 +545,23 @@
         copy.wait()
 
 
-def convolve_outer(tile, from_next, picks, kernel, edge_sum, features):
+def convolve_outer(tile, from_next, picks, kernel, edge_sum, pair_row, features):
     frames, tall, broad, channels = features.shape
     lat = picks.shape[1] // 2
     return pl.pallas_call(
         functools.partial(outer_body, lat),
-        in_specs=[SCALARS] + [WHOLE] * 4 + [ANYWHERE],
+        in_specs=[SCALARS] + [WHOLE] * 5 + [ANYWHERE],
         out_specs=ANYWHERE,
         out_shape=jax.ShapeDtypeStruct(features.shape, BF16),
-        input_output_aliases={5: 0},
+        input_output_aliases={6: 0},
         scratch_shapes=[
             pltpu.VMEM((frames, border_lanes(lat), broad + 16, 128), F32),
             pltpu.VMEM((frames, broad, channels), BF16),
-            pltpu.SemaphoreType.DMA((frames,)),
+            pltpu.SemaphoreType.DMA((frames + 1,)),
         ],
         compiler_params=params(16),
         name="convolve_outer",
-    )(tile, from_next, picks, kernel, edge_sum, features)
+    )(tile, from_next, picks, kernel, edge_sum, pair_row, features)
 
 
 def exchange(value, offset):
@@ -645,8 +647,8 @@
     swaps = [(i, i + 1) for i in range(1, count - 1, 2)] + [(i + 1, i) for i in range(1, count - 1, 2)]
     from_next = lax.ppermute(to_next, "seq", swaps)
     from_pair = exchange(to_pair, 1)
-    features, edge_sum = convolve_inner(tile, predicted, from_pair, inner_picks, outer_picks, decode)
-    return convolve_outer(tile, from_next, outer_picks, decode, edge_sum, features)
+    features, edge_sum, pair_row = convolve_inner(tile, predicted, from_pair, inner_picks, outer_picks, decode)
+    return convolve_outer(tile, from_next, outer_picks, decode, edge_sum, pair_row, features)
 
 
 def solution(mesh):

time: 34.6 us -> 34.6 us (level)
  transfers between devices with their start and end apart: 14 -> 14, of which waited for: 8 -> 8; matrix products, arithmetic and copies ran while one was open for 0% -> 0% of each run, Pallas kernels for 30% -> 29%
where the time goes in v9:
time: 34.6 us; the launch traced here: 34.4 us
  starting transfers between devices  17 us (49%)
  Pallas kernels  11.6 us (34%)
  waiting for transfers between devices  5.63 us (16%)
    ppermute x13, starting transfers between devices, exchange(): return lax.ppermute(value, 'seq', [(i, i ^ offset) for i in range(count)])  14.9 us
    ppermute x13, waiting for transfers between devices, exchange(): return lax.ppermute(value, 'seq', [(i, i ^ offset) for i in range(count)])  4.88 us
    pallas_call x2, Pallas kernels, attend_own(): pl.pallas_call(functools.partial(own_body, turns, blocks_here, groups), i...  4.65 us
    pallas_call x1, Pallas kernels, attend_past(): pl.pallas_call(functools.partial(past_body, sizes, len(packed)), in_specs...  2.67 us
    ppermute x1, starting transfers between devices, local(): from_next = lax.ppermute(to_next, 'seq', swaps)  2.1 us
    pallas_call x1, Pallas kernels, convolve_inner(): pl.pallas_call(functools.partial(inner_body, lat), in_specs=[SCALARS] + [...  1.75 us
    pallas_call x1, Pallas kernels, convolve_outer(): pl.pallas_call(functools.partial(outer_body, lat), in_specs=[SCALARS] + [...  1.08 us
    ppermute x1, waiting for transfers between devices, local(): from_next = lax.ppermute(to_next, 'seq', swaps)  0.75 us
  transfers between devices with their start and end apart: 14, of which 8 were waited for; matrix products, arithmetic and copies ran while one was open for 0% of the time, Pallas kernels for 29%

profile of v9, /device:TPU:1, one launch (start us, length us, event | category | flops | bytes accessed | tf_op | source)
XLA Modules:
  0.0 34.4 jit_solution(14861593102703185917)
XLA Ops:
  0.0 0.0 copy-start.1
  0.0 0.0 copy-start.2
  0.0 0.0 copy-start.4
  0.0 0.0 copy-start.3
  0.0 0.0 copy-start.6
  0.0 0.0 copy-start.5
  0.0 0.0 copy-start.7
  0.0 2.2 %collective-permute-start = (bf16[2,16,1024]{2,1,0:T(8,128)(2,1)}, bf16[2,16,1024]{2,1,0:T(8,128)(2,1)S(1)}, u32[]{:S(2)}, u32[]{:S(2)}) collective-permute-start(bf16[2,16,1024]{2,1,0:T(8,128)(2,1)} %refs_0_.1), channel_id=1, source_target_pairs={{0,4},{1,5},{2,6},{3,7},{4,0},{5,1},{6,2},{7,3},{8,12},{9,13},{10,... | collective-permute-start | bytes 196616 | tf_op jit(solution)/shard_map/ppermute | solution.py:569
  2.2 2.3 %collective-permute-start.1 = (bf16[2,16,1024]{2,1,0:T(8,128)(2,1)}, bf16[2,16,1024]{2,1,0:T(8,128)(2,1)S(1)}, u32[]{:S(2)}, u32[]{:S(2)}) collective-permute-start(bf16[2,16,1024]{2,1,0:T(8,128)(2,1)} %refs_0_.1), channel_id=1, source_target_pairs={{0,8},{1,9},{2,10},{3,11},{4,12},{5,13},{6,14},{7,15},{8,0},{9,1},... | collective-permute-start | bytes 196616 | tf_op jit(solution)/shard_map/ppermute | solution.py:569
  4.6 0.0 collective-permute-start.2
  4.6 0.0 copy-done.1
  4.6 1.3 %collective-permute-start.3 = (bf16[64,192]{1,0:T(8,128)(2,1)S(1)}, bf16[64,192]{1,0:T(8,128)(2,1)S(1)}, u32[]{:S(2)}, u32[]{:S(2)}) collective-permute-start(bf16[64,192]{1,0:T(8,128)(2,1)S(1)} %bitcast.6), channel_id=1, source_target_pairs={{0,2},{1,3},{2,0},{3,1},{4,6},{5,7},{6,4},{7,5},{8,10},{9,11},{10,... | collective-permute-start | bytes 73736 | tf_op jit(solution)/shard_map/ppermute | solution.py:569
  5.9 0.0 copy-done.2
  5.9 0.3 collective-permute-start.4
  6.1 0.0 copy-done.4
  6.1 0.0 copy-done.3
  6.2 0.0 copy-done.6
  6.2 0.0 copy-done.5
  6.2 0.0 copy-done.7
  6.2 0.0 copy-start
  6.2 2.3 %attend_own.2 = (bf16[2,1536,256]{2,1,0:T(8,128)(2,1)S(1)}, f32[2,1536,128]{2,1,0:T(8,128)S(1)}, s32[16]{0:T(128)}) custom-call(s32[1]{0:T(128)} %bitcast.tile_ref, s32[32]{0:T(128)S(1)} %copy-done.6, s32[16,16]{1,0:T(8,128)S(1)} %copy-done.5, s32[16]{0:T(128)S(1)} %copy-done.7, bf16[256,3072]{1,0:T(8,128)(2,1)S(1)} %bitcast.10, bf16[256,1024]{1,0:T(8,128)(2,1)S(1)} %bitcast.12), custom_call_target="tpu_custom_call" | custom-call | flops 1207959552 | tf_op jit(solution)/shard_map/attend_own/pallas_call | solution.py:77
  8.5 0.0 collective-permute-done.3.final_across
  8.5 0.5 %collective-permute-done.4.decode_across = bf16[32,432]{1,0:T(8,128)(2,1)S(1)} collective-permute-done((bf16[32,432]{1,0:T(8,128)(2,1)S(1)}, bf16[32,432]{1,0:T(8,128)(2,1)S(1)}, u32[]{:S(2)}, u32[]{:S(2)}) %collective-permute-start.4) | collective-permute-done | bytes 27680 | tf_op jit(solution)/shard_map/ppermute | solution.py:569
  9.0 0.0 collective-permute-done.refs_1_
  9.0 0.0 collective-permute-done.1.refs_2_
  9.0 0.8 %collective-permute-done.2.refs_3_ = bf16[2,16,1024]{2,1,0:T(8,128)(2,1)S(1)} collective-permute-done((bf16[2,16,1024]{2,1,0:T(8,128)(2,1)}, bf16[2,16,1024]{2,1,0:T(8,128)(2,1)S(1)}, u32[]{:S(2)}, u32[]{:S(2)}) %collective-permute-start.2) | collective-permute-done | bytes 65568 | tf_op jit(solution)/shard_map/ppermute | solution.py:569
  9.8 0.0 copy-done
  9.8 1.3 %collective-permute-start.5 = (bf16[8,16,1024]{2,1,0:T(8,128)(2,1)S(1)}, bf16[8,16,1024]{2,1,0:T(8,128)(2,1)S(1)}, u32[]{:S(2)}, u32[]{:S(2)}) collective-permute-start(bf16[8,16,1024]{2,1,0:T(8,128)(2,1)S(1)} %join_near.1.refs_0_), channel_id=1, source_target_pairs={{0,2},{1,3},{2,0},{3,1},{4,6},{5,7},{6,4},{7,5},{8,10},{9,11},{10,... | collective-permute-start | bytes 786440 | tf_op jit(solution)/shard_map/ppermute | solution.py:569
  11.1 0.1 pack.1.refs_0_
  11.2 1.9 %collective-permute-start.6 = (bf16[2,16,1664]{2,1,0:T(8,128)(2,1)S(1)}, bf16[2,16,1664]{2,1,0:T(8,128)(2,1)S(1)}, u32[]{:S(2)}, u32[]{:S(2)}) collective-permute-start(bf16[2,16,1664]{2,1,0:T(8,128)(2,1)S(1)} %pack.1.refs_0_), channel_id=1, source_target_pairs={{0,8},{1,9},{2,10},{3,11},{4,12},{5,13},{6,14},{7,15},{8,0},{9,1},... | collective-permute-start | bytes 319496 | tf_op jit(solution)/shard_map/ppermute | solution.py:569
  13.1 0.5 %collective-permute-start.7 = (bf16[2,16,1664]{2,1,0:T(8,128)(2,1)S(1)}, bf16[2,16,1664]{2,1,0:T(8,128)(2,1)S(1)}, u32[]{:S(2)}, u32[]{:S(2)}) collective-permute-start(bf16[2,16,1664]{2,1,0:T(8,128)(2,1)S(1)} %pack.1.refs_0_), channel_id=1, source_target_pairs={{0,4},{1,5},{2,6},{3,7},{4,0},{5,1},{6,2},{7,3},{8,12},{9,13},{10,... | collective-permute-start | bytes 319496 | tf_op jit(solution)/shard_map/ppermute | solution.py:569
  13.5 2.4 %attend_own.3 = (bf16[2,1536,256]{2,1,0:T(8,128)(2,1)S(1)}, f32[2,1536,128]{2,1,0:T(8,128)S(1)}, s32[16]{0:T(128)S(1)}) custom-call(s32[1]{0:T(128)} %bitcast.tile_ref, s32[32]{0:T(128)S(1)} %copy-done.6, s32[16,16]{1,0:T(8,128)S(1)} %copy-done.5, s32[16]{0:T(128)S(1)} %copy-done.7, bf16[256,3072]{1,0:T(8,128)(2,1)S(1)} %bitcast.11, ...), custom_call_target="tpu_custom_call" | custom-call | flops 1207959552 | tf_op jit(solution)/shard_map/attend_own/pallas_call | solution.py:77
  15.9 1.0 %collective-permute-done.6.refs_1_ = bf16[2,16,1664]{2,1,0:T(8,128)(2,1)S(1)} collective-permute-done((bf16[2,16,1664]{2,1,0:T(8,128)(2,1)S(1)}, bf16[2,16,1664]{2,1,0:T(8,128)(2,1)S(1)}, u32[]{:S(2)}, u32[]{:S(2)}) %collective-permute-start.6) | collective-permute-done | bytes 106528 | tf_op jit(solution)/shard_map/ppermute | solution.py:569
  16.9 0.6 %collective-permute-done.7.refs_2_ = bf16[2,16,1664]{2,1,0:T(8,128)(2,1)S(1)} collective-permute-done((bf16[2,16,1664]{2,1,0:T(8,128)(2,1)S(1)}, bf16[2,16,1664]{2,1,0:T(8,128)(2,1)S(1)}, u32[]{:S(2)}, u32[]{:S(2)}) %collective-permute-start.7) | collective-permute-done | bytes 106528 | tf_op jit(solution)/shard_map/ppermute | solution.py:569
  17.5 0.0 collective-permute-done.5.refs_1_
  17.6 3.7 %collective-permute-start.10 = (bf16[16,16,1024]{2,1,0:T(8,128)(2,1)S(1)}, bf16[16,16,1024]{2,1,0:T(8,128)(2,1)S(1)}, u32[]{:S(2)}, u32[]{:S(2)}) collective-permute-start(bf16[16,16,1024]{2,1,0:T(8,128)(2,1)S(1)} %join_chip.1.refs_4_), channel_id=1, source_target_pairs={{0,1},{1,0},{2,3},{3,2},{4,5},{5,4},{6,7},{7,6},{8,9},{9,8},{10,11... | collective-permute-start | bytes 1572872 | tf_op jit(solution)/shard_map/ppermute | solution.py:569
  21.2 0.0 collective-permute-start.8
  21.3 0.3 collective-permute-start.9
  21.6 1.2 %collective-permute-done.10.refs_5_ = bf16[16,16,1024]{2,1,0:T(8,128)(2,1)S(1)} collective-permute-done((bf16[16,16,1024]{2,1,0:T(8,128)(2,1)S(1)}, bf16[16,16,1024]{2,1,0:T(8,128)(2,1)S(1)}, u32[]{:S(2)}, u32[]{:S(2)}) %collective-permute-start.10) | collective-permute-done | bytes 524320 | tf_op jit(solution)/shard_map/ppermute | solution.py:569
  22.8 2.7 %attend_past.1.attended = bf16[256,3072]{1,0:T(8,128)(2,1)S(1)} custom-call(s32[16]{0:T(128)S(1)} %get-tuple-element.53.slots, bf16[2,1536,256]{2,1,0:T(8,128)(2,1)S(1)} %get-tuple-element.54.refs_0_, bf16[2,1536,256]{2,1,0:T(8,128)(2,1)S(1)} %get-tuple-element.55.refs_1_, f32[2,1536,128]{2,1,0:T(8,128)S(1)} %get-tuple-element.56.refs_2_, ...), custom_call_target="tpu_custom_call" | custom-call | flops 10000000000 | tf_op jit(solution)/shard_map/attend_past/pallas_call | solution.py:193
  25.4 0.3 collective-permute-done.8.ours.refs_1_
  25.8 0.0 collective-permute-done.9.theirs.refs_2_
  25.8 0.9 %collective-permute-start.11 = (bf16[2,16,1664]{2,1,0:T(8,128)(2,1)S(1)}, bf16[2,16,1664]{2,1,0:T(8,128)(2,1)S(1)}, u32[]{:S(2)}, u32[]{:S(2)}) collective-permute-start(bf16[2,16,1664]{2,1,0:T(8,128)(2,1)S(1)} %collective-permute-done.8.ours.refs_1_), channel_id=1, source_target_pairs={{0,1},{1,0},{2,3},{3,2},{4,5},{5,4},{6,7},{7,6},{8,9},{9,8},{10,11... | collective-permute-start | bytes 319496 | tf_op jit(solution)/shard_map/ppermute | solution.py:569
  26.6 0.5 %project.1.part = f32[256,64]{1,0:T(8,128)S(1)} custom-call(s32[1]{0:T(128)} %bitcast.tile_ref, bf16[256,3072]{1,0:T(8,128)(2,1)S(1)} %attend_past.1.attended, bf16[6,16,1664]{2,1,0:T(8,128)(2,1)S(1)} %join_panels.1.ours.refs_0_, bf16[6,16,1664]{2,1,0:T(8,128)(2,1)S(1)} %collective-permute-done.9.theirs.refs_2_), custom_call_target="tpu_custom_call" | custom-call | tf_op jit(solution)/shard_map/project/pallas_call | solution.py:281
  27.2 0.4 %collective-permute-done.11.theirs.refs_3_ = bf16[2,16,1664]{2,1,0:T(8,128)(2,1)S(1)} collective-permute-done((bf16[2,16,1664]{2,1,0:T(8,128)(2,1)S(1)}, bf16[2,16,1664]{2,1,0:T(8,128)(2,1)S(1)}, u32[]{:S(2)}, u32[]{:S(2)}) %collective-permute-start.11) | collective-permute-done | bytes 106528 | tf_op jit(solution)/shard_map/ppermute | solution.py:569
  27.6 0.4 %finish.1 = (bf16[256,64]{1,0:T(8,128)(2,1)S(1)}, bf16[2,16,128]{2,1,0:T(8,128)(2,1)S(1)}, bf16[2,16,128]{2,1,0:T(8,128)(2,1)S(1)}) custom-call(s32[1]{0:T(128)} %bitcast.tile_ref, bf16[256,3072]{1,0:T(8,128)(2,1)S(1)} %attend_past.1.attended, bf16[2,16,1664]{2,1,0:T(8,128)(2,1)S(1)} %collective-permute-done.8.ours.refs_1_, ...), custom_call_target="tpu_custom_call" | custom-call | tf_op jit(solution)/shard_map/finish/pallas_call | solution.py:315
  28.0 0.4 %collective-permute-start.13 = (bf16[2,16,128]{2,1,0:T(8,128)(2,1)S(1)}, bf16[2,16,128]{2,1,0:T(8,128)(2,1)S(1)}, u32[]{:S(2)}, u32[]{:S(2)}) collective-permute-start(bf16[2,16,128]{2,1,0:T(8,128)(2,1)S(1)} %get-tuple-element.66), channel_id=1, source_target_pairs={{0,1},{1,0},{2,3},{3,2},{4,5},{5,4},{6,7},{7,6},{8,9},{9,8},{10,11... | collective-permute-start | bytes 24584 | tf_op jit(solution)/shard_map/ppermute | solution.py:569
  28.4 2.1 %collective-permute-start.12 = (bf16[2,16,128]{2,1,0:T(8,128)(2,1)S(1)}, bf16[2,16,128]{2,1,0:T(8,128)(2,1)S(1)}, u32[]{:S(2)}, u32[]{:S(2)}) collective-permute-start(bf16[2,16,128]{2,1,0:T(8,128)(2,1)S(1)} %get-tuple-element.63), channel_id=1, source_target_pairs={{1,2},{3,4},{5,6},{7,8},{9,10},{11,12},{13,14},{2,1},{4,3},{6,5},{... | collective-permute-start | bytes 24584 | tf_op jit(solution)/shard_map/ppermute | solution.py:648
  30.5 0.3 unpack.1.kernel
  30.9 0.0 collective-permute-done.13.from_pair
  30.9 1.7 %convolve_inner.1 = (bf16[2,4,128,512]{3,2,1,0:T(8,128)(2,1)}, f32[256,512]{1,0:T(8,128)S(1)}, bf16[2,128,512]{2,1,0:T(8,128)(2,1)S(1)}) custom-call(s32[1]{0:T(128)} %bitcast.tile_ref, bf16[2,2,64,64]{3,2,1,0:T(8,128)(2,1)S(1)} %bitcast.14, bf16[2,16,128]{2,1,0:T(8,128)(2,1)S(1)} %collective-permute-done.13.from_pair, ...), custom_call_target="tpu_custom_call" | custom-call | flops 452984832 | bytes 1048576 | tf_op jit(solution)/shard_map/convolve_inner/pallas_call | solution.py:505
  32.6 0.7 %collective-permute-done.12.from_next = bf16[2,16,128]{2,1,0:T(8,128)(2,1)S(1)} collective-permute-done((bf16[2,16,128]{2,1,0:T(8,128)(2,1)S(1)}, bf16[2,16,128]{2,1,0:T(8,128)(2,1)S(1)}, u32[]{:S(2)}, u32[]{:S(2)}) %collective-permute-start.12) | collective-permute-done | bytes 8224 | tf_op jit(solution)/shard_map/ppermute | solution.py:648
  33.4 1.1 %convolve_outer.1 = bf16[2,4,128,512]{3,2,1,0:T(8,128)(2,1)} custom-call(s32[1]{0:T(128)} %bitcast.tile_ref, bf16[2,16,128]{2,1,0:T(8,128)(2,1)S(1)} %collective-permute-done.12.from_next, bf16[2,32,256]{2,1,0:T(8,128)(2,1)S(1)} %get-tuple-element.64.outer_picks.picks, bf16[432,512]{1,0:T(8,128)(2,1)S(1)} %unpack.1.kernel, ...), custom_call_target="tpu_custom_call", output_to_operand_aliasing={{}: (6, {})} | custom-call | tf_op jit(solution)/shard_map/convolve_outer/pallas_call | solution.py:551
  (4 shorter events, 0.1 us)
Async XLA Ops:
  0.0 4.6 %copy-start.1 = (bf16[192,64]{0,1:T(8,128)(2,1)S(1)}, bf16[192,64]{0,1:T(8,128)(2,1)}, u32[]{:S(2)}) copy-start(bf16[192,64]{0,1:T(8,128)(2,1)} %param.14) | copy-start | bytes 73732
  0.0 5.9 %copy-start.2 = (bf16[432,32]{0,1:T(8,128)(2,1)S(1)}, bf16[432,32]{0,1:T(8,128)(2,1)}, u32[]{:S(2)}) copy-start(bf16[432,32]{0,1:T(8,128)(2,1)} %param.15) | copy-start | bytes 82948
  0.0 6.1 %copy-start.4 = (bf16[2,2,64,1024]{3,2,1,0:T(8,128)(2,1)S(1)}, bf16[2,2,64,1024]{3,2,1,0:T(8,128)(2,1)}, u32[]{:S(2)}) copy-start(bf16[2,2,64,1024]{3,2,1,0:T(8,128)(2,1)} %param.9) | copy-start | bytes 1572868
  0.0 6.1 %copy-start.3 = (bf16[2,2,64,3072]{3,2,1,0:T(8,128)(2,1)S(1)}, bf16[2,2,64,3072]{3,2,1,0:T(8,128)(2,1)}, u32[]{:S(2)}) copy-start(bf16[2,2,64,3072]{3,2,1,0:T(8,128)(2,1)} %param.8) | copy-start | bytes 4718596
  0.0 6.1 %copy-start.6 = (s32[32]{0:T(128)S(1)}, s32[32]{0:T(128)}, u32[]{:S(2)}) copy-start(s32[32]{0:T(128)} %home.3) | copy-start | bytes 388
  0.0 6.1 %copy-start.5 = (s32[16,16]{1,0:T(8,128)S(1)}, s32[16,16]{1,0:T(8,128)}, u32[]{:S(2)}) copy-start(s32[16,16]{1,0:T(8,128)} %blocks.3) | copy-start | bytes 3076
  0.0 6.1 %copy-start.7 = (s32[16]{0:T(128)S(1)}, s32[16]{0:T(128)}, u32[]{:S(2)}) copy-start(s32[16]{0:T(128)} %lens.3) | copy-start | bytes 196
  0.0 8.9 %collective-permute-start = (bf16[2,16,1024]{2,1,0:T(8,128)(2,1)}, bf16[2,16,1024]{2,1,0:T(8,128)(2,1)S(1)}, u32[]{:S(2)}, u32[]{:S(2)}) collective-permute-start(bf16[2,16,1024]{2,1,0:T(8,128)(2,1)} %refs_0_.1), channel_id=1, source_target_pairs={{0,4},{1,5},{2,6},{3,7},{4,0},{5,1},{6,2},{7,3},{8,12},{9,13},{10,... | collective-permute-start | bytes 196616 | tf_op jit(solution)/shard_map/ppermute | solution.py:569
  2.2 6.7 %collective-permute-start.1 = (bf16[2,16,1024]{2,1,0:T(8,128)(2,1)}, bf16[2,16,1024]{2,1,0:T(8,128)(2,1)S(1)}, u32[]{:S(2)}, u32[]{:S(2)}) collective-permute-start(bf16[2,16,1024]{2,1,0:T(8,128)(2,1)} %refs_0_.1), channel_id=1, source_target_pairs={{0,8},{1,9},{2,10},{3,11},{4,12},{5,13},{6,14},{7,15},{8,0},{9,1},... | collective-permute-start | bytes 196616 | tf_op jit(solution)/shard_map/ppermute | solution.py:569
  4.6 5.2 %collective-permute-start.2 = (bf16[2,16,1024]{2,1,0:T(8,128)(2,1)}, bf16[2,16,1024]{2,1,0:T(8,128)(2,1)S(1)}, u32[]{:S(2)}, u32[]{:S(2)}) collective-permute-start(bf16[2,16,1024]{2,1,0:T(8,128)(2,1)} %refs_0_.1), channel_id=1, source_target_pairs={{0,12},{1,13},{2,14},{3,15},{4,8},{5,9},{6,10},{7,11},{8,4},{9,5},... | collective-permute-start | bytes 196616 | tf_op jit(solution)/shard_map/ppermute | solution.py:569
  4.6 3.8 %collective-permute-start.3 = (bf16[64,192]{1,0:T(8,128)(2,1)S(1)}, bf16[64,192]{1,0:T(8,128)(2,1)S(1)}, u32[]{:S(2)}, u32[]{:S(2)}) collective-permute-start(bf16[64,192]{1,0:T(8,128)(2,1)S(1)} %bitcast.6), channel_id=1, source_target_pairs={{0,2},{1,3},{2,0},{3,1},{4,6},{5,7},{6,4},{7,5},{8,10},{9,11},{10,... | collective-permute-start | bytes 73736 | tf_op jit(solution)/shard_map/ppermute | solution.py:569
  5.9 3.1 %collective-permute-start.4 = (bf16[32,432]{1,0:T(8,128)(2,1)S(1)}, bf16[32,432]{1,0:T(8,128)(2,1)S(1)}, u32[]{:S(2)}, u32[]{:S(2)}) collective-permute-start(bf16[32,432]{1,0:T(8,128)(2,1)S(1)} %bitcast.8), channel_id=1, source_target_pairs={{0,2},{1,3},{2,0},{3,1},{4,6},{5,7},{6,4},{7,5},{8,10},{9,11},{10,... | collective-permute-start | bytes 82952 | tf_op jit(solution)/shard_map/ppermute | solution.py:569
  6.2 3.6 %copy-start = (bf16[2,16,1024]{2,1,0:T(8,128)(2,1)S(1)}, bf16[2,16,1024]{2,1,0:T(8,128)(2,1)}, u32[]{:S(2)}) copy-start(bf16[2,16,1024]{2,1,0:T(8,128)(2,1)} %refs_0_.1) | copy-start | bytes 196612
  9.8 7.7 %collective-permute-start.5 = (bf16[8,16,1024]{2,1,0:T(8,128)(2,1)S(1)}, bf16[8,16,1024]{2,1,0:T(8,128)(2,1)S(1)}, u32[]{:S(2)}, u32[]{:S(2)}) collective-permute-start(bf16[8,16,1024]{2,1,0:T(8,128)(2,1)S(1)} %join_near.1.refs_0_), channel_id=1, source_target_pairs={{0,2},{1,3},{2,0},{3,1},{4,6},{5,7},{6,4},{7,5},{8,10},{9,11},{10,... | collective-permute-start | bytes 786440 | tf_op jit(solution)/shard_map/ppermute | solution.py:569
  11.2 5.8 %collective-permute-start.6 = (bf16[2,16,1664]{2,1,0:T(8,128)(2,1)S(1)}, bf16[2,16,1664]{2,1,0:T(8,128)(2,1)S(1)}, u32[]{:S(2)}, u32[]{:S(2)}) collective-permute-start(bf16[2,16,1664]{2,1,0:T(8,128)(2,1)S(1)} %pack.1.refs_0_), channel_id=1, source_target_pairs={{0,8},{1,9},{2,10},{3,11},{4,12},{5,13},{6,14},{7,15},{8,0},{9,1},... | collective-permute-start | bytes 319496 | tf_op jit(solution)/shard_map/ppermute | solution.py:569
  13.1 4.5 %collective-permute-start.7 = (bf16[2,16,1664]{2,1,0:T(8,128)(2,1)S(1)}, bf16[2,16,1664]{2,1,0:T(8,128)(2,1)S(1)}, u32[]{:S(2)}, u32[]{:S(2)}) collective-permute-start(bf16[2,16,1664]{2,1,0:T(8,128)(2,1)S(1)} %pack.1.refs_0_), channel_id=1, source_target_pairs={{0,4},{1,5},{2,6},{3,7},{4,0},{5,1},{6,2},{7,3},{8,12},{9,13},{10,... | collective-permute-start | bytes 319496 | tf_op jit(solution)/shard_map/ppermute | solution.py:569
  17.6 5.2 %collective-permute-start.10 = (bf16[16,16,1024]{2,1,0:T(8,128)(2,1)S(1)}, bf16[16,16,1024]{2,1,0:T(8,128)(2,1)S(1)}, u32[]{:S(2)}, u32[]{:S(2)}) collective-permute-start(bf16[16,16,1024]{2,1,0:T(8,128)(2,1)S(1)} %join_chip.1.refs_4_), channel_id=1, source_target_pairs={{0,1},{1,0},{2,3},{3,2},{4,5},{5,4},{6,7},{7,6},{8,9},{9,8},{10,11... | collective-permute-start | bytes 1572872 | tf_op jit(solution)/shard_map/ppermute | solution.py:569
  21.2 4.5 %collective-permute-start.8 = (bf16[2,16,1664]{2,1,0:T(8,128)(2,1)S(1)}, bf16[2,16,1664]{2,1,0:T(8,128)(2,1)S(1)}, u32[]{:S(2)}, u32[]{:S(2)}) collective-permute-start(bf16[2,16,1664]{2,1,0:T(8,128)(2,1)S(1)} %collective-permute-done.6.refs_1_), channel_id=1, source_target_pairs={{0,4},{1,5},{2,6},{3,7},{4,0},{5,1},{6,2},{7,3},{8,12},{9,13},{10,... | collective-permute-start | bytes 319496 | tf_op jit(solution)/shard_map/ppermute | solution.py:569
  21.3 4.5 %collective-permute-start.9 = (bf16[6,16,1664]{2,1,0:T(8,128)(2,1)S(1)}, bf16[6,16,1664]{2,1,0:T(8,128)(2,1)S(1)}, u32[]{:S(2)}, u32[]{:S(2)}) collective-permute-start(bf16[6,16,1664]{2,1,0:T(8,128)(2,1)S(1)} %join_panels.1.ours.refs_0_), channel_id=1, source_target_pairs={{0,1},{1,0},{2,3},{3,2},{4,5},{5,4},{6,7},{7,6},{8,9},{9,8},{10,11... | collective-permute-start | bytes 958472 | tf_op jit(solution)/shard_map/ppermute | solution.py:569
  25.8 1.8 %collective-permute-start.11 = (bf16[2,16,1664]{2,1,0:T(8,128)(2,1)S(1)}, bf16[2,16,1664]{2,1,0:T(8,128)(2,1)S(1)}, u32[]{:S(2)}, u32[]{:S(2)}) collective-permute-start(bf16[2,16,1664]{2,1,0:T(8,128)(2,1)S(1)} %collective-permute-done.8.ours.refs_1_), channel_id=1, source_target_pairs={{0,1},{1,0},{2,3},{3,2},{4,5},{5,4},{6,7},{7,6},{8,9},{9,8},{10,11... | collective-permute-start | bytes 319496 | tf_op jit(solution)/shard_map/ppermute | solution.py:569
  28.0 2.9 %collective-permute-start.13 = (bf16[2,16,128]{2,1,0:T(8,128)(2,1)S(1)}, bf16[2,16,128]{2,1,0:T(8,128)(2,1)S(1)}, u32[]{:S(2)}, u32[]{:S(2)}) collective-permute-start(bf16[2,16,128]{2,1,0:T(8,128)(2,1)S(1)} %get-tuple-element.66), channel_id=1, source_target_pairs={{0,1},{1,0},{2,3},{3,2},{4,5},{5,4},{6,7},{7,6},{8,9},{9,8},{10,11... | collective-permute-start | bytes 24584 | tf_op jit(solution)/shard_map/ppermute | solution.py:569
  28.4 5.0 %collective-permute-start.12 = (bf16[2,16,128]{2,1,0:T(8,128)(2,1)S(1)}, bf16[2,16,128]{2,1,0:T(8,128)(2,1)S(1)}, u32[]{:S(2)}, u32[]{:S(2)}) collective-permute-start(bf16[2,16,128]{2,1,0:T(8,128)(2,1)S(1)} %get-tuple-element.63), channel_id=1, source_target_pairs={{1,2},{3,4},{5,6},{7,8},{9,10},{11,12},{13,14},{2,1},{4,3},{6,5},{... | collective-permute-start | bytes 24584 | tf_op jit(solution)/shard_map/ppermute | solution.py:648

commit v10 on v9

--- a/solution.py
+++ b/solution.py
@@ -102,19 +102,19 @@
     minus = jnp.where(lane < 3, -1.0, 0.0)
     zero = jnp.zeros((block_tokens, HEAD_DIM), BF16)
     homes = [(ref, k) for ref, size in zip(gathered, sizes) for k in range(size)]
+    found = []
     for place, (ref, k) in enumerate(homes):
         slot = slots[place]
-        listed = slot >= 0
-        block = ref[k * blocks_here + jnp.maximum(slot, 0)]
-        live = jnp.where(listed, 1.0, 0.0)
-        level = (minus * live).astype(BF16)
-        counted = jnp.full((block_tokens, HEAD_DIM), live, F32).astype(BF16)
-        rows = slice(place * block_tokens, (place + 1) * block_tokens)
-        for g in range(KV_HEADS):
-            keys[g, rows, :HEAD_DIM] = jnp.where(listed, block[:, head_columns(g)], zero)
-            keys[g, rows, HEAD_DIM:] = level
-            values[g, rows, :HEAD_DIM] = jnp.where(listed, block[:, head_columns(KV_HEADS + g)], zero)
-            values[g, rows, HEAD_DIM:] = counted
+        found.append((ref, k * blocks_here + jnp.maximum(slot, 0), slot >= 0))
+
+    def fill(g):
+        for place, (ref, index, listed) in enumerate(found):
+            live = jnp.where(listed, 1.0, 0.0)
+            rows = slice(place * block_tokens, (place + 1) * block_tokens)
+            keys[g, rows, :HEAD_DIM] = jnp.where(listed, ref[index, :, head_columns(g)], zero)
+            keys[g, rows, HEAD_DIM:] = (minus * live).astype(BF16)
+            values[g, rows, :HEAD_DIM] = jnp.where(listed, ref[index, :, head_columns(KV_HEADS + g)], zero)
+            values[g, rows, HEAD_DIM:] = jnp.full((block_tokens, HEAD_DIM), live, F32).astype(BF16)
 
     heads = GROUP if keys.shape[1] <= 512 else 1
     steps = KV_HEADS * GROUP // heads
@@ -159,12 +159,18 @@
 
     largest = jnp.zeros(worst.shape, F32)
     if heads == GROUP:
+        fill(0)
         score = scores(*place(0))
         for step in range(steps):
-            ahead = scores(*place(step + 1)) if step + 1 < steps else None
+            ahead = None
+            if step + 1 < steps:
+                fill(step + 1)
+                ahead = scores(*place(step + 1))
             largest = quick(step, score, largest)
             score = ahead
     else:
+        for g in range(KV_HEADS):
+            fill(g)
         largest = over_steps(lambda step, seen: quick(step, scores(*place(step)), seen), largest)
     worst[...] = largest
 

time: 34.6 us -> 34.6 us (level)
  no operation moved by 1% of the time
where the time goes in v10:
time: 34.6 us; the launch traced here: 34.4 us
  starting transfers between devices  17 us (49%)
  Pallas kernels  11.7 us (34%)
  waiting for transfers between devices  5.58 us (16%)
    ppermute x13, starting transfers between devices, exchange(): return lax.ppermute(value, 'seq', [(i, i ^ offset) for i in range(count)])  14.9 us
    ppermute x13, waiting for transfers between devices, exchange(): return lax.ppermute(value, 'seq', [(i, i ^ offset) for i in range(count)])  4.84 us
    pallas_call x2, Pallas kernels, attend_own(): pl.pallas_call(functools.partial(own_body, turns, blocks_here, groups), i...  4.7 us
    pallas_call x1, Pallas kernels, attend_past(): pl.pallas_call(functools.partial(past_body, sizes, len(packed)), in_specs...  2.66 us
    ppermute x1, starting transfers between devices, local(): from_next = lax.ppermute(to_next, 'seq', swaps)  2.1 us
    pallas_call x1, Pallas kernels, convolve_inner(): pl.pallas_call(functools.partial(inner_body, lat), in_specs=[SCALARS] + [...  1.75 us
    pallas_call x1, Pallas kernels, convolve_outer(): pl.pallas_call(functools.partial(outer_body, lat), in_specs=[SCALARS] + [...  1.08 us
    ppermute x1, waiting for transfers between devices, local(): from_next = lax.ppermute(to_next, 'seq', swaps)  0.75 us
  transfers between devices with their start and end apart: 14, of which 8 were waited for; matrix products, arithmetic and copies ran while one was open for 0% of the time, Pallas kernels for 29%

profile of v10, /device:TPU:1, one launch (start us, length us, event | category | flops | bytes accessed | tf_op | source)
XLA Modules:
  0.0 34.4 jit_solution(3675432818989881486)
XLA Ops:
  0.0 0.0 copy-start.1
  0.0 0.0 copy-start.2
  0.0 0.0 copy-start.4
  0.0 0.0 copy-start.3
  0.0 0.0 copy-start.6
  0.0 0.0 copy-start.5
  0.0 0.0 copy-start.7
  0.0 2.2 %collective-permute-start = (bf16[2,16,1024]{2,1,0:T(8,128)(2,1)}, bf16[2,16,1024]{2,1,0:T(8,128)(2,1)S(1)}, u32[]{:S(2)}, u32[]{:S(2)}) collective-permute-start(bf16[2,16,1024]{2,1,0:T(8,128)(2,1)} %refs_0_.1), channel_id=1, source_target_pairs={{0,4},{1,5},{2,6},{3,7},{4,0},{5,1},{6,2},{7,3},{8,12},{9,13},{10,... | collective-permute-start | bytes 196616 | tf_op jit(solution)/shard_map/ppermute | solution.py:575
  2.2 2.3 %collective-permute-start.1 = (bf16[2,16,1024]{2,1,0:T(8,128)(2,1)}, bf16[2,16,1024]{2,1,0:T(8,128)(2,1)S(1)}, u32[]{:S(2)}, u32[]{:S(2)}) collective-permute-start(bf16[2,16,1024]{2,1,0:T(8,128)(2,1)} %refs_0_.1), channel_id=1, source_target_pairs={{0,8},{1,9},{2,10},{3,11},{4,12},{5,13},{6,14},{7,15},{8,0},{9,1},... | collective-permute-start | bytes 196616 | tf_op jit(solution)/shard_map/ppermute | solution.py:575
  4.6 0.0 collective-permute-start.2
  4.6 0.0 copy-done.1
  4.6 1.3 %collective-permute-start.3 = (bf16[64,192]{1,0:T(8,128)(2,1)S(1)}, bf16[64,192]{1,0:T(8,128)(2,1)S(1)}, u32[]{:S(2)}, u32[]{:S(2)}) collective-permute-start(bf16[64,192]{1,0:T(8,128)(2,1)S(1)} %bitcast.6), channel_id=1, source_target_pairs={{0,2},{1,3},{2,0},{3,1},{4,6},{5,7},{6,4},{7,5},{8,10},{9,11},{10,... | collective-permute-start | bytes 73736 | tf_op jit(solution)/shard_map/ppermute | solution.py:575
  5.9 0.0 copy-done.2
  5.9 0.3 collective-permute-start.4
  6.1 0.0 copy-done.4
  6.1 0.0 copy-done.3
  6.2 0.0 copy-done.6
  6.2 0.0 copy-done.5
  6.2 0.0 copy-done.7
  6.2 0.0 copy-start
  6.2 2.3 %attend_own.2 = (bf16[2,1536,256]{2,1,0:T(8,128)(2,1)S(1)}, f32[2,1536,128]{2,1,0:T(8,128)S(1)}, s32[16]{0:T(128)}) custom-call(s32[1]{0:T(128)} %bitcast.tile_ref, s32[32]{0:T(128)S(1)} %copy-done.6, s32[16,16]{1,0:T(8,128)S(1)} %copy-done.5, s32[16]{0:T(128)S(1)} %copy-done.7, bf16[256,3072]{1,0:T(8,128)(2,1)S(1)} %bitcast.10, bf16[256,1024]{1,0:T(8,128)(2,1)S(1)} %bitcast.12), custom_call_target="tpu_custom_call" | custom-call | flops 1207959552 | tf_op jit(solution)/shard_map/attend_own/pallas_call | solution.py:77
  8.5 0.0 collective-permute-done.3.final_across
  8.5 0.5 %collective-permute-done.4.decode_across = bf16[32,432]{1,0:T(8,128)(2,1)S(1)} collective-permute-done((bf16[32,432]{1,0:T(8,128)(2,1)S(1)}, bf16[32,432]{1,0:T(8,128)(2,1)S(1)}, u32[]{:S(2)}, u32[]{:S(2)}) %collective-permute-start.4) | collective-permute-done | bytes 27680 | tf_op jit(solution)/shard_map/ppermute | solution.py:575
  9.0 0.0 collective-permute-done.refs_1_
  9.0 0.0 collective-permute-done.1.refs_2_
  9.0 0.8 %collective-permute-done.2.refs_3_ = bf16[2,16,1024]{2,1,0:T(8,128)(2,1)S(1)} collective-permute-done((bf16[2,16,1024]{2,1,0:T(8,128)(2,1)}, bf16[2,16,1024]{2,1,0:T(8,128)(2,1)S(1)}, u32[]{:S(2)}, u32[]{:S(2)}) %collective-permute-start.2) | collective-permute-done | bytes 65568 | tf_op jit(solution)/shard_map/ppermute | solution.py:575
  9.8 0.0 copy-done
  9.8 1.3 %collective-permute-start.5 = (bf16[8,16,1024]{2,1,0:T(8,128)(2,1)S(1)}, bf16[8,16,1024]{2,1,0:T(8,128)(2,1)S(1)}, u32[]{:S(2)}, u32[]{:S(2)}) collective-permute-start(bf16[8,16,1024]{2,1,0:T(8,128)(2,1)S(1)} %join_near.1.refs_0_), channel_id=1, source_target_pairs={{0,2},{1,3},{2,0},{3,1},{4,6},{5,7},{6,4},{7,5},{8,10},{9,11},{10,... | collective-permute-start | bytes 786440 | tf_op jit(solution)/shard_map/ppermute | solution.py:575
  11.1 0.1 pack.1.refs_0_
  11.2 1.9 %collective-permute-start.6 = (bf16[2,16,1664]{2,1,0:T(8,128)(2,1)S(1)}, bf16[2,16,1664]{2,1,0:T(8,128)(2,1)S(1)}, u32[]{:S(2)}, u32[]{:S(2)}) collective-permute-start(bf16[2,16,1664]{2,1,0:T(8,128)(2,1)S(1)} %pack.1.refs_0_), channel_id=1, source_target_pairs={{0,8},{1,9},{2,10},{3,11},{4,12},{5,13},{6,14},{7,15},{8,0},{9,1},... | collective-permute-start | bytes 319496 | tf_op jit(solution)/shard_map/ppermute | solution.py:575
  13.1 0.5 %collective-permute-start.7 = (bf16[2,16,1664]{2,1,0:T(8,128)(2,1)S(1)}, bf16[2,16,1664]{2,1,0:T(8,128)(2,1)S(1)}, u32[]{:S(2)}, u32[]{:S(2)}) collective-permute-start(bf16[2,16,1664]{2,1,0:T(8,128)(2,1)S(1)} %pack.1.refs_0_), channel_id=1, source_target_pairs={{0,4},{1,5},{2,6},{3,7},{4,0},{5,1},{6,2},{7,3},{8,12},{9,13},{10,... | collective-permute-start | bytes 319496 | tf_op jit(solution)/shard_map/ppermute | solution.py:575
  13.5 2.4 %attend_own.3 = (bf16[2,1536,256]{2,1,0:T(8,128)(2,1)S(1)}, f32[2,1536,128]{2,1,0:T(8,128)S(1)}, s32[16]{0:T(128)S(1)}) custom-call(s32[1]{0:T(128)} %bitcast.tile_ref, s32[32]{0:T(128)S(1)} %copy-done.6, s32[16,16]{1,0:T(8,128)S(1)} %copy-done.5, s32[16]{0:T(128)S(1)} %copy-done.7, bf16[256,3072]{1,0:T(8,128)(2,1)S(1)} %bitcast.11, ...), custom_call_target="tpu_custom_call" | custom-call | flops 1207959552 | tf_op jit(solution)/shard_map/attend_own/pallas_call | solution.py:77
  16.0 1.0 %collective-permute-done.6.refs_1_ = bf16[2,16,1664]{2,1,0:T(8,128)(2,1)S(1)} collective-permute-done((bf16[2,16,1664]{2,1,0:T(8,128)(2,1)S(1)}, bf16[2,16,1664]{2,1,0:T(8,128)(2,1)S(1)}, u32[]{:S(2)}, u32[]{:S(2)}) %collective-permute-start.6) | collective-permute-done | bytes 106528 | tf_op jit(solution)/shard_map/ppermute | solution.py:575
  16.9 0.6 %collective-permute-done.7.refs_2_ = bf16[2,16,1664]{2,1,0:T(8,128)(2,1)S(1)} collective-permute-done((bf16[2,16,1664]{2,1,0:T(8,128)(2,1)S(1)}, bf16[2,16,1664]{2,1,0:T(8,128)(2,1)S(1)}, u32[]{:S(2)}, u32[]{:S(2)}) %collective-permute-start.7) | collective-permute-done | bytes 106528 | tf_op jit(solution)/shard_map/ppermute | solution.py:575
  17.5 0.0 collective-permute-done.5.refs_1_
  17.6 3.7 %collective-permute-start.10 = (bf16[16,16,1024]{2,1,0:T(8,128)(2,1)S(1)}, bf16[16,16,1024]{2,1,0:T(8,128)(2,1)S(1)}, u32[]{:S(2)}, u32[]{:S(2)}) collective-permute-start(bf16[16,16,1024]{2,1,0:T(8,128)(2,1)S(1)} %join_chip.1.refs_4_), channel_id=1, source_target_pairs={{0,1},{1,0},{2,3},{3,2},{4,5},{5,4},{6,7},{7,6},{8,9},{9,8},{10,11... | collective-permute-start | bytes 1572872 | tf_op jit(solution)/shard_map/ppermute | solution.py:575
  21.2 0.0 collective-permute-start.8
  21.3 0.3 collective-permute-start.9
  21.6 1.2 %collective-permute-done.10.refs_5_ = bf16[16,16,1024]{2,1,0:T(8,128)(2,1)S(1)} collective-permute-done((bf16[16,16,1024]{2,1,0:T(8,128)(2,1)S(1)}, bf16[16,16,1024]{2,1,0:T(8,128)(2,1)S(1)}, u32[]{:S(2)}, u32[]{:S(2)}) %collective-permute-start.10) | collective-permute-done | bytes 524320 | tf_op jit(solution)/shard_map/ppermute | solution.py:575
  22.8 2.7 %attend_past.1.attended = bf16[256,3072]{1,0:T(8,128)(2,1)S(1)} custom-call(s32[16]{0:T(128)S(1)} %get-tuple-element.53.slots, bf16[2,1536,256]{2,1,0:T(8,128)(2,1)S(1)} %get-tuple-element.54.refs_0_, bf16[2,1536,256]{2,1,0:T(8,128)(2,1)S(1)} %get-tuple-element.55.refs_1_, f32[2,1536,128]{2,1,0:T(8,128)S(1)} %get-tuple-element.56.refs_2_, ...), custom_call_target="tpu_custom_call" | custom-call | flops 10000000000 | tf_op jit(solution)/shard_map/attend_past/pallas_call | solution.py:199
  25.4 0.3 collective-permute-done.8.ours.refs_1_
  25.8 0.0 collective-permute-done.9.theirs.refs_2_
  25.8 0.9 %collective-permute-start.11 = (bf16[2,16,1664]{2,1,0:T(8,128)(2,1)S(1)}, bf16[2,16,1664]{2,1,0:T(8,128)(2,1)S(1)}, u32[]{:S(2)}, u32[]{:S(2)}) collective-permute-start(bf16[2,16,1664]{2,1,0:T(8,128)(2,1)S(1)} %collective-permute-done.8.ours.refs_1_), channel_id=1, source_target_pairs={{0,1},{1,0},{2,3},{3,2},{4,5},{5,4},{6,7},{7,6},{8,9},{9,8},{10,11... | collective-permute-start | bytes 319496 | tf_op jit(solution)/shard_map/ppermute | solution.py:575
  26.6 0.5 %project.1.part = f32[256,64]{1,0:T(8,128)S(1)} custom-call(s32[1]{0:T(128)} %bitcast.tile_ref, bf16[256,3072]{1,0:T(8,128)(2,1)S(1)} %attend_past.1.attended, bf16[6,16,1664]{2,1,0:T(8,128)(2,1)S(1)} %join_panels.1.ours.refs_0_, bf16[6,16,1664]{2,1,0:T(8,128)(2,1)S(1)} %collective-permute-done.9.theirs.refs_2_), custom_call_target="tpu_custom_call" | custom-call | tf_op jit(solution)/shard_map/project/pallas_call | solution.py:287
  27.2 0.4 %collective-permute-done.11.theirs.refs_3_ = bf16[2,16,1664]{2,1,0:T(8,128)(2,1)S(1)} collective-permute-done((bf16[2,16,1664]{2,1,0:T(8,128)(2,1)S(1)}, bf16[2,16,1664]{2,1,0:T(8,128)(2,1)S(1)}, u32[]{:S(2)}, u32[]{:S(2)}) %collective-permute-start.11) | collective-permute-done | bytes 106528 | tf_op jit(solution)/shard_map/ppermute | solution.py:575
  27.6 0.4 %finish.1 = (bf16[256,64]{1,0:T(8,128)(2,1)S(1)}, bf16[2,16,128]{2,1,0:T(8,128)(2,1)S(1)}, bf16[2,16,128]{2,1,0:T(8,128)(2,1)S(1)}) custom-call(s32[1]{0:T(128)} %bitcast.tile_ref, bf16[256,3072]{1,0:T(8,128)(2,1)S(1)} %attend_past.1.attended, bf16[2,16,1664]{2,1,0:T(8,128)(2,1)S(1)} %collective-permute-done.8.ours.refs_1_, ...), custom_call_target="tpu_custom_call" | custom-call | tf_op jit(solution)/shard_map/finish/pallas_call | solution.py:321
  28.0 0.4 %collective-permute-start.13 = (bf16[2,16,128]{2,1,0:T(8,128)(2,1)S(1)}, bf16[2,16,128]{2,1,0:T(8,128)(2,1)S(1)}, u32[]{:S(2)}, u32[]{:S(2)}) collective-permute-start(bf16[2,16,128]{2,1,0:T(8,128)(2,1)S(1)} %get-tuple-element.66), channel_id=1, source_target_pairs={{0,1},{1,0},{2,3},{3,2},{4,5},{5,4},{6,7},{7,6},{8,9},{9,8},{10,11... | collective-permute-start | bytes 24584 | tf_op jit(solution)/shard_map/ppermute | solution.py:575
  28.4 2.1 %collective-permute-start.12 = (bf16[2,16,128]{2,1,0:T(8,128)(2,1)S(1)}, bf16[2,16,128]{2,1,0:T(8,128)(2,1)S(1)}, u32[]{:S(2)}, u32[]{:S(2)}) collective-permute-start(bf16[2,16,128]{2,1,0:T(8,128)(2,1)S(1)} %get-tuple-element.63), channel_id=1, source_target_pairs={{1,2},{3,4},{5,6},{7,8},{9,10},{11,12},{13,14},{2,1},{4,3},{6,5},{... | collective-permute-start | bytes 24584 | tf_op jit(solution)/shard_map/ppermute | solution.py:654
  30.5 0.3 unpack.1.kernel
  30.9 0.0 collective-permute-done.13.from_pair
  30.9 1.7 %convolve_inner.1 = (bf16[2,4,128,512]{3,2,1,0:T(8,128)(2,1)}, f32[256,512]{1,0:T(8,128)S(1)}, bf16[2,128,512]{2,1,0:T(8,128)(2,1)S(1)}) custom-call(s32[1]{0:T(128)} %bitcast.tile_ref, bf16[2,2,64,64]{3,2,1,0:T(8,128)(2,1)S(1)} %bitcast.14, bf16[2,16,128]{2,1,0:T(8,128)(2,1)S(1)} %collective-permute-done.13.from_pair, ...), custom_call_target="tpu_custom_call" | custom-call | flops 452984832 | bytes 1048576 | tf_op jit(solution)/shard_map/convolve_inner/pallas_call | solution.py:511
  32.6 0.7 %collective-permute-done.12.from_next = bf16[2,16,128]{2,1,0:T(8,128)(2,1)S(1)} collective-permute-done((bf16[2,16,128]{2,1,0:T(8,128)(2,1)S(1)}, bf16[2,16,128]{2,1,0:T(8,128)(2,1)S(1)}, u32[]{:S(2)}, u32[]{:S(2)}) %collective-permute-start.12) | collective-permute-done | bytes 8224 | tf_op jit(solution)/shard_map/ppermute | solution.py:654
  33.4 1.1 %convolve_outer.1 = bf16[2,4,128,512]{3,2,1,0:T(8,128)(2,1)} custom-call(s32[1]{0:T(128)} %bitcast.tile_ref, bf16[2,16,128]{2,1,0:T(8,128)(2,1)S(1)} %collective-permute-done.12.from_next, bf16[2,32,256]{2,1,0:T(8,128)(2,1)S(1)} %get-tuple-element.64.outer_picks.picks, bf16[432,512]{1,0:T(8,128)(2,1)S(1)} %unpack.1.kernel, ...), custom_call_target="tpu_custom_call", output_to_operand_aliasing={{}: (6, {})} | custom-call | tf_op jit(solution)/shard_map/convolve_outer/pallas_call | solution.py:557
  (4 shorter events, 0.1 us)
Async XLA Ops:
  0.0 4.6 %copy-start.1 = (bf16[192,64]{0,1:T(8,128)(2,1)S(1)}, bf16[192,64]{0,1:T(8,128)(2,1)}, u32[]{:S(2)}) copy-start(bf16[192,64]{0,1:T(8,128)(2,1)} %param.14) | copy-start | bytes 73732
  0.0 5.9 %copy-start.2 = (bf16[432,32]{0,1:T(8,128)(2,1)S(1)}, bf16[432,32]{0,1:T(8,128)(2,1)}, u32[]{:S(2)}) copy-start(bf16[432,32]{0,1:T(8,128)(2,1)} %param.15) | copy-start | bytes 82948
  0.0 6.1 %copy-start.4 = (bf16[2,2,64,1024]{3,2,1,0:T(8,128)(2,1)S(1)}, bf16[2,2,64,1024]{3,2,1,0:T(8,128)(2,1)}, u32[]{:S(2)}) copy-start(bf16[2,2,64,1024]{3,2,1,0:T(8,128)(2,1)} %param.9) | copy-start | bytes 1572868
  0.0 6.1 %copy-start.3 = (bf16[2,2,64,3072]{3,2,1,0:T(8,128)(2,1)S(1)}, bf16[2,2,64,3072]{3,2,1,0:T(8,128)(2,1)}, u32[]{:S(2)}) copy-start(bf16[2,2,64,3072]{3,2,1,0:T(8,128)(2,1)} %param.8) | copy-start | bytes 4718596
  0.0 6.1 %copy-start.6 = (s32[32]{0:T(128)S(1)}, s32[32]{0:T(128)}, u32[]{:S(2)}) copy-start(s32[32]{0:T(128)} %home.3) | copy-start | bytes 388
  0.0 6.1 %copy-start.5 = (s32[16,16]{1,0:T(8,128)S(1)}, s32[16,16]{1,0:T(8,128)}, u32[]{:S(2)}) copy-start(s32[16,16]{1,0:T(8,128)} %blocks.3) | copy-start | bytes 3076
  0.0 6.1 %copy-start.7 = (s32[16]{0:T(128)S(1)}, s32[16]{0:T(128)}, u32[]{:S(2)}) copy-start(s32[16]{0:T(128)} %lens.3) | copy-start | bytes 196
  0.0 8.9 %collective-permute-start = (bf16[2,16,1024]{2,1,0:T(8,128)(2,1)}, bf16[2,16,1024]{2,1,0:T(8,128)(2,1)S(1)}, u32[]{:S(2)}, u32[]{:S(2)}) collective-permute-start(bf16[2,16,1024]{2,1,0:T(8,128)(2,1)} %refs_0_.1), channel_id=1, source_target_pairs={{0,4},{1,5},{2,6},{3,7},{4,0},{5,1},{6,2},{7,3},{8,12},{9,13},{10,... | collective-permute-start | bytes 196616 | tf_op jit(solution)/shard_map/ppermute | solution.py:575
  2.2 6.7 %collective-permute-start.1 = (bf16[2,16,1024]{2,1,0:T(8,128)(2,1)}, bf16[2,16,1024]{2,1,0:T(8,128)(2,1)S(1)}, u32[]{:S(2)}, u32[]{:S(2)}) collective-permute-start(bf16[2,16,1024]{2,1,0:T(8,128)(2,1)} %refs_0_.1), channel_id=1, source_target_pairs={{0,8},{1,9},{2,10},{3,11},{4,12},{5,13},{6,14},{7,15},{8,0},{9,1},... | collective-permute-start | bytes 196616 | tf_op jit(solution)/shard_map/ppermute | solution.py:575
  4.6 5.2 %collective-permute-start.2 = (bf16[2,16,1024]{2,1,0:T(8,128)(2,1)}, bf16[2,16,1024]{2,1,0:T(8,128)(2,1)S(1)}, u32[]{:S(2)}, u32[]{:S(2)}) collective-permute-start(bf16[2,16,1024]{2,1,0:T(8,128)(2,1)} %refs_0_.1), channel_id=1, source_target_pairs={{0,12},{1,13},{2,14},{3,15},{4,8},{5,9},{6,10},{7,11},{8,4},{9,5},... | collective-permute-start | bytes 196616 | tf_op jit(solution)/shard_map/ppermute | solution.py:575
  4.6 3.8 %collective-permute-start.3 = (bf16[64,192]{1,0:T(8,128)(2,1)S(1)}, bf16[64,192]{1,0:T(8,128)(2,1)S(1)}, u32[]{:S(2)}, u32[]{:S(2)}) collective-permute-start(bf16[64,192]{1,0:T(8,128)(2,1)S(1)} %bitcast.6), channel_id=1, source_target_pairs={{0,2},{1,3},{2,0},{3,1},{4,6},{5,7},{6,4},{7,5},{8,10},{9,11},{10,... | collective-permute-start | bytes 73736 | tf_op jit(solution)/shard_map/ppermute | solution.py:575
  5.9 3.1 %collective-permute-start.4 = (bf16[32,432]{1,0:T(8,128)(2,1)S(1)}, bf16[32,432]{1,0:T(8,128)(2,1)S(1)}, u32[]{:S(2)}, u32[]{:S(2)}) collective-permute-start(bf16[32,432]{1,0:T(8,128)(2,1)S(1)} %bitcast.8), channel_id=1, source_target_pairs={{0,2},{1,3},{2,0},{3,1},{4,6},{5,7},{6,4},{7,5},{8,10},{9,11},{10,... | collective-permute-start | bytes 82952 | tf_op jit(solution)/shard_map/ppermute | solution.py:575
  6.2 3.6 %copy-start = (bf16[2,16,1024]{2,1,0:T(8,128)(2,1)S(1)}, bf16[2,16,1024]{2,1,0:T(8,128)(2,1)}, u32[]{:S(2)}) copy-start(bf16[2,16,1024]{2,1,0:T(8,128)(2,1)} %refs_0_.1) | copy-start | bytes 196612
  9.8 7.7 %collective-permute-start.5 = (bf16[8,16,1024]{2,1,0:T(8,128)(2,1)S(1)}, bf16[8,16,1024]{2,1,0:T(8,128)(2,1)S(1)}, u32[]{:S(2)}, u32[]{:S(2)}) collective-permute-start(bf16[8,16,1024]{2,1,0:T(8,128)(2,1)S(1)} %join_near.1.refs_0_), channel_id=1, source_target_pairs={{0,2},{1,3},{2,0},{3,1},{4,6},{5,7},{6,4},{7,5},{8,10},{9,11},{10,... | collective-permute-start | bytes 786440 | tf_op jit(solution)/shard_map/ppermute | solution.py:575
  11.2 5.8 %collective-permute-start.6 = (bf16[2,16,1664]{2,1,0:T(8,128)(2,1)S(1)}, bf16[2,16,1664]{2,1,0:T(8,128)(2,1)S(1)}, u32[]{:S(2)}, u32[]{:S(2)}) collective-permute-start(bf16[2,16,1664]{2,1,0:T(8,128)(2,1)S(1)} %pack.1.refs_0_), channel_id=1, source_target_pairs={{0,8},{1,9},{2,10},{3,11},{4,12},{5,13},{6,14},{7,15},{8,0},{9,1},... | collective-permute-start | bytes 319496 | tf_op jit(solution)/shard_map/ppermute | solution.py:575
  13.1 4.5 %collective-permute-start.7 = (bf16[2,16,1664]{2,1,0:T(8,128)(2,1)S(1)}, bf16[2,16,1664]{2,1,0:T(8,128)(2,1)S(1)}, u32[]{:S(2)}, u32[]{:S(2)}) collective-permute-start(bf16[2,16,1664]{2,1,0:T(8,128)(2,1)S(1)} %pack.1.refs_0_), channel_id=1, source_target_pairs={{0,4},{1,5},{2,6},{3,7},{4,0},{5,1},{6,2},{7,3},{8,12},{9,13},{10,... | collective-permute-start | bytes 319496 | tf_op jit(solution)/shard_map/ppermute | solution.py:575
  17.6 5.2 %collective-permute-start.10 = (bf16[16,16,1024]{2,1,0:T(8,128)(2,1)S(1)}, bf16[16,16,1024]{2,1,0:T(8,128)(2,1)S(1)}, u32[]{:S(2)}, u32[]{:S(2)}) collective-permute-start(bf16[16,16,1024]{2,1,0:T(8,128)(2,1)S(1)} %join_chip.1.refs_4_), channel_id=1, source_target_pairs={{0,1},{1,0},{2,3},{3,2},{4,5},{5,4},{6,7},{7,6},{8,9},{9,8},{10,11... | collective-permute-start | bytes 1572872 | tf_op jit(solution)/shard_map/ppermute | solution.py:575
  21.2 4.5 %collective-permute-start.8 = (bf16[2,16,1664]{2,1,0:T(8,128)(2,1)S(1)}, bf16[2,16,1664]{2,1,0:T(8,128)(2,1)S(1)}, u32[]{:S(2)}, u32[]{:S(2)}) collective-permute-start(bf16[2,16,1664]{2,1,0:T(8,128)(2,1)S(1)} %collective-permute-done.6.refs_1_), channel_id=1, source_target_pairs={{0,4},{1,5},{2,6},{3,7},{4,0},{5,1},{6,2},{7,3},{8,12},{9,13},{10,... | collective-permute-start | bytes 319496 | tf_op jit(solution)/shard_map/ppermute | solution.py:575
  21.3 4.5 %collective-permute-start.9 = (bf16[6,16,1664]{2,1,0:T(8,128)(2,1)S(1)}, bf16[6,16,1664]{2,1,0:T(8,128)(2,1)S(1)}, u32[]{:S(2)}, u32[]{:S(2)}) collective-permute-start(bf16[6,16,1664]{2,1,0:T(8,128)(2,1)S(1)} %join_panels.1.ours.refs_0_), channel_id=1, source_target_pairs={{0,1},{1,0},{2,3},{3,2},{4,5},{5,4},{6,7},{7,6},{8,9},{9,8},{10,11... | collective-permute-start | bytes 958472 | tf_op jit(solution)/shard_map/ppermute | solution.py:575
  25.8 1.8 %collective-permute-start.11 = (bf16[2,16,1664]{2,1,0:T(8,128)(2,1)S(1)}, bf16[2,16,1664]{2,1,0:T(8,128)(2,1)S(1)}, u32[]{:S(2)}, u32[]{:S(2)}) collective-permute-start(bf16[2,16,1664]{2,1,0:T(8,128)(2,1)S(1)} %collective-permute-done.8.ours.refs_1_), channel_id=1, source_target_pairs={{0,1},{1,0},{2,3},{3,2},{4,5},{5,4},{6,7},{7,6},{8,9},{9,8},{10,11... | collective-permute-start | bytes 319496 | tf_op jit(solution)/shard_map/ppermute | solution.py:575
  28.0 2.9 %collective-permute-start.13 = (bf16[2,16,128]{2,1,0:T(8,128)(2,1)S(1)}, bf16[2,16,128]{2,1,0:T(8,128)(2,1)S(1)}, u32[]{:S(2)}, u32[]{:S(2)}) collective-permute-start(bf16[2,16,128]{2,1,0:T(8,128)(2,1)S(1)} %get-tuple-element.66), channel_id=1, source_target_pairs={{0,1},{1,0},{2,3},{3,2},{4,5},{5,4},{6,7},{7,6},{8,9},{9,8},{10,11... | collective-permute-start | bytes 24584 | tf_op jit(solution)/shard_map/ppermute | solution.py:575
  28.4 5.0 %collective-permute-start.12 = (bf16[2,16,128]{2,1,0:T(8,128)(2,1)S(1)}, bf16[2,16,128]{2,1,0:T(8,128)(2,1)S(1)}, u32[]{:S(2)}, u32[]{:S(2)}) collective-permute-start(bf16[2,16,128]{2,1,0:T(8,128)(2,1)S(1)} %get-tuple-element.63), channel_id=1, source_target_pairs={{1,2},{3,4},{5,6},{7,8},{9,10},{11,12},{13,14},{2,1},{4,3},{6,5},{... | collective-permute-start | bytes 24584 | tf_op jit(solution)/shard_map/ppermute | solution.py:654

commit v11 on v10

--- a/solution.py
+++ b/solution.py
@@ -446,7 +446,7 @@
 
 def inner_body(
     lat, tile_ref, predicted, from_pair, inner_picks, outer_picks, kernel, features, edge_sum, pair_row,
-    wide, border, done, sems
+    next_panel, wide, border, done, sems
 ):
     frames, patch_rows, patches, _ = predicted.shape
     tall, broad = 2 * patch_rows, 2 * patches
@@ -494,6 +494,7 @@
         taps, border_panel(lat, kernel, pair_edge), preferred_element_type=F32
     )
     pair_row[...] = total.astype(BF16).reshape(pair_row.shape)
+    next_panel[...] = border_panel(lat, kernel, 1 - pair_edge)
     for copy in copies:
         copy.wait()
 
@@ -511,11 +512,12 @@
     return pl.pallas_call(
         functools.partial(inner_body, lat),
         in_specs=[SCALARS] + [WHOLE] * 5,
-        out_specs=[ANYWHERE, WHOLE, WHOLE],
+        out_specs=[ANYWHERE, WHOLE, WHOLE, WHOLE],
         out_shape=[
             jax.ShapeDtypeStruct((frames, tall, broad, channels), BF16),
             jax.ShapeDtypeStruct((frames * broad, channels), F32),
             jax.ShapeDtypeStruct((frames, broad, channels), BF16),
+            jax.ShapeDtypeStruct((9 * lat, channels), BF16),
         ],
         scratch_shapes=[
             pltpu.VMEM((frames, lanes // 128, broad + 16, 128), F32),
@@ -533,15 +535,14 @@
     )(tile, predicted, from_pair, inner_picks, outer_picks, kernel)
 
 
-def outer_body(lat, tile_ref, from_next, picks, kernel, edge_sum, pair_row, given, features, wide, done, sems):
+def outer_body(lat, tile_ref, from_next, picks, panel, edge_sum, pair_row, given, features, wide, done, sems):
     frames, tall, broad, _ = features.shape
     edge = jnp.where(tile_ref[0] % 2 == 0, 0, 1)
-    panel = border_panel(lat, kernel, edge)
     copies = [pltpu.make_async_copy(pair_row, features.at[:, (1 - edge) * (tall - 1)], sems.at[frames])]
     copies[0].start()
     for frame, taps in enumerate(border_taps(lat, from_next, picks, wide)):
         total = edge_sum[frame * broad : (frame + 1) * broad] + jnp.dot(
-            taps, panel, preferred_element_type=F32
+            taps, panel[...], preferred_element_type=F32
         )
         done[frame] = total.astype(BF16)
         copy = pltpu.make_async_copy(done.at[frame], features.at[frame, edge * (tall - 1)], sems.at[frame])
@@ -551,7 +552,7 @@
         copy.wait()
 
 
-def convolve_outer(tile, from_next, picks, kernel, edge_sum, pair_row, features):
+def convolve_outer(tile, from_next, picks, panel, edge_sum, pair_row, features):
     frames, tall, broad, channels = features.shape
     lat = picks.shape[1] // 2
     return pl.pallas_call(
@@ -567,7 +568,7 @@
         ],
         compiler_params=params(16),
         name="convolve_outer",
-    )(tile, from_next, picks, kernel, edge_sum, pair_row, features)
+    )(tile, from_next, picks, panel, edge_sum, pair_row, features)
 
 
 def exchange(value, offset):
@@ -653,8 +654,8 @@
     swaps = [(i, i + 1) for i in range(1, count - 1, 2)] + [(i + 1, i) for i in range(1, count - 1, 2)]
     from_next = lax.ppermute(to_next, "seq", swaps)
     from_pair = exchange(to_pair, 1)
-    features, edge_sum, pair_row = convolve_inner(tile, predicted, from_pair, inner_picks, outer_picks, decode)
-    return convolve_outer(tile, from_next, outer_picks, decode, edge_sum, pair_row, features)
+    features, edge_sum, pair_row, next_panel = convolve_inner(tile, predicted, from_pair, inner_picks, outer_picks, decode)
+    return convolve_outer(tile, from_next, outer_picks, next_panel, edge_sum, pair_row, features)
 
 
 def solution(mesh):

time: 34.6 us -> 34.6 us (level)
  transfers between devices with their start and end apart: 14 -> 14, of which waited for: 8 -> 8; matrix products, arithmetic and copies ran while one was open for 0% -> 0% of each run, Pallas kernels for 29% -> 30%
where the time goes in v11:
time: 34.6 us; the launch traced here: 34.4 us
  starting transfers between devices  17 us (49%)
  Pallas kernels  11.7 us (34%)
  waiting for transfers between devices  5.53 us (16%)
    ppermute x13, starting transfers between devices, exchange(): return lax.ppermute(value, 'seq', [(i, i ^ offset) for i in range(count)])  14.9 us
    ppermute x13, waiting for transfers between devices, exchange(): return lax.ppermute(value, 'seq', [(i, i ^ offset) for i in range(count)])  4.84 us
    pallas_call x2, Pallas kernels, attend_own(): pl.pallas_call(functools.partial(own_body, turns, blocks_here, groups), i...  4.7 us
    pallas_call x1, Pallas kernels, attend_past(): pl.pallas_call(functools.partial(past_body, sizes, len(packed)), in_specs...  2.66 us
    ppermute x1, starting transfers between devices, local(): from_next = lax.ppermute(to_next, 'seq', swaps)  2.1 us
    pallas_call x1, Pallas kernels, convolve_inner(): pl.pallas_call(functools.partial(inner_body, lat), in_specs=[SCALARS] + [...  1.8 us
    pallas_call x1, Pallas kernels, convolve_outer(): pl.pallas_call(functools.partial(outer_body, lat), in_specs=[SCALARS] + [...  1.08 us
  transfers between devices with their start and end apart: 14, of which 8 were waited for; matrix products, arithmetic and copies ran while one was open for 0% of the time, Pallas kernels for 30%

profile of v11, /device:TPU:1, one launch (start us, length us, event | category | flops | bytes accessed | tf_op | source)
XLA Modules:
  0.0 34.4 jit_solution(10863987004747810518)
XLA Ops:
  0.0 0.0 copy-start.1
  0.0 0.0 copy-start.2
  0.0 0.0 copy-start.4
  0.0 0.0 copy-start.3
  0.0 0.0 copy-start.6
  0.0 0.0 copy-start.5
  0.0 0.0 copy-start.7
  0.0 2.2 %collective-permute-start = (bf16[2,16,1024]{2,1,0:T(8,128)(2,1)}, bf16[2,16,1024]{2,1,0:T(8,128)(2,1)S(1)}, u32[]{:S(2)}, u32[]{:S(2)}) collective-permute-start(bf16[2,16,1024]{2,1,0:T(8,128)(2,1)} %refs_0_.1), channel_id=1, source_target_pairs={{0,4},{1,5},{2,6},{3,7},{4,0},{5,1},{6,2},{7,3},{8,12},{9,13},{10,... | collective-permute-start | bytes 196616 | tf_op jit(solution)/shard_map/ppermute | solution.py:576
  2.2 2.3 %collective-permute-start.1 = (bf16[2,16,1024]{2,1,0:T(8,128)(2,1)}, bf16[2,16,1024]{2,1,0:T(8,128)(2,1)S(1)}, u32[]{:S(2)}, u32[]{:S(2)}) collective-permute-start(bf16[2,16,1024]{2,1,0:T(8,128)(2,1)} %refs_0_.1), channel_id=1, source_target_pairs={{0,8},{1,9},{2,10},{3,11},{4,12},{5,13},{6,14},{7,15},{8,0},{9,1},... | collective-permute-start | bytes 196616 | tf_op jit(solution)/shard_map/ppermute | solution.py:576
  4.6 0.0 collective-permute-start.2
  4.6 0.0 copy-done.1
  4.6 1.3 %collective-permute-start.3 = (bf16[64,192]{1,0:T(8,128)(2,1)S(1)}, bf16[64,192]{1,0:T(8,128)(2,1)S(1)}, u32[]{:S(2)}, u32[]{:S(2)}) collective-permute-start(bf16[64,192]{1,0:T(8,128)(2,1)S(1)} %bitcast.6), channel_id=1, source_target_pairs={{0,2},{1,3},{2,0},{3,1},{4,6},{5,7},{6,4},{7,5},{8,10},{9,11},{10,... | collective-permute-start | bytes 73736 | tf_op jit(solution)/shard_map/ppermute | solution.py:576
  5.9 0.0 copy-done.2
  5.9 0.3 collective-permute-start.4
  6.1 0.0 copy-done.4
  6.1 0.0 copy-done.3
  6.2 0.0 copy-done.6
  6.2 0.0 copy-done.5
  6.2 0.0 copy-done.7
  6.2 0.0 copy-start
  6.2 2.3 %attend_own.2 = (bf16[2,1536,256]{2,1,0:T(8,128)(2,1)S(1)}, f32[2,1536,128]{2,1,0:T(8,128)S(1)}, s32[16]{0:T(128)}) custom-call(s32[1]{0:T(128)} %bitcast.tile_ref, s32[32]{0:T(128)S(1)} %copy-done.6, s32[16,16]{1,0:T(8,128)S(1)} %copy-done.5, s32[16]{0:T(128)S(1)} %copy-done.7, bf16[256,3072]{1,0:T(8,128)(2,1)S(1)} %bitcast.10, bf16[256,1024]{1,0:T(8,128)(2,1)S(1)} %bitcast.12), custom_call_target="tpu_custom_call" | custom-call | flops 1207959552 | tf_op jit(solution)/shard_map/attend_own/pallas_call | solution.py:77
  8.5 0.0 collective-permute-done.3.final_across
  8.5 0.5 %collective-permute-done.4.decode_across = bf16[32,432]{1,0:T(8,128)(2,1)S(1)} collective-permute-done((bf16[32,432]{1,0:T(8,128)(2,1)S(1)}, bf16[32,432]{1,0:T(8,128)(2,1)S(1)}, u32[]{:S(2)}, u32[]{:S(2)}) %collective-permute-start.4) | collective-permute-done | bytes 27680 | tf_op jit(solution)/shard_map/ppermute | solution.py:576
  9.0 0.0 collective-permute-done.refs_1_
  9.0 0.0 collective-permute-done.1.refs_2_
  9.0 0.8 %collective-permute-done.2.refs_3_ = bf16[2,16,1024]{2,1,0:T(8,128)(2,1)S(1)} collective-permute-done((bf16[2,16,1024]{2,1,0:T(8,128)(2,1)}, bf16[2,16,1024]{2,1,0:T(8,128)(2,1)S(1)}, u32[]{:S(2)}, u32[]{:S(2)}) %collective-permute-start.2) | collective-permute-done | bytes 65568 | tf_op jit(solution)/shard_map/ppermute | solution.py:576
  9.8 0.0 copy-done
  9.8 1.3 %collective-permute-start.5 = (bf16[8,16,1024]{2,1,0:T(8,128)(2,1)S(1)}, bf16[8,16,1024]{2,1,0:T(8,128)(2,1)S(1)}, u32[]{:S(2)}, u32[]{:S(2)}) collective-permute-start(bf16[8,16,1024]{2,1,0:T(8,128)(2,1)S(1)} %join_near.1.refs_0_), channel_id=1, source_target_pairs={{0,2},{1,3},{2,0},{3,1},{4,6},{5,7},{6,4},{7,5},{8,10},{9,11},{10,... | collective-permute-start | bytes 786440 | tf_op jit(solution)/shard_map/ppermute | solution.py:576
  11.1 0.1 pack.1.refs_0_
  11.2 1.9 %collective-permute-start.6 = (bf16[2,16,1664]{2,1,0:T(8,128)(2,1)S(1)}, bf16[2,16,1664]{2,1,0:T(8,128)(2,1)S(1)}, u32[]{:S(2)}, u32[]{:S(2)}) collective-permute-start(bf16[2,16,1664]{2,1,0:T(8,128)(2,1)S(1)} %pack.1.refs_0_), channel_id=1, source_target_pairs={{0,8},{1,9},{2,10},{3,11},{4,12},{5,13},{6,14},{7,15},{8,0},{9,1},... | collective-permute-start | bytes 319496 | tf_op jit(solution)/shard_map/ppermute | solution.py:576
  13.1 0.5 %collective-permute-start.7 = (bf16[2,16,1664]{2,1,0:T(8,128)(2,1)S(1)}, bf16[2,16,1664]{2,1,0:T(8,128)(2,1)S(1)}, u32[]{:S(2)}, u32[]{:S(2)}) collective-permute-start(bf16[2,16,1664]{2,1,0:T(8,128)(2,1)S(1)} %pack.1.refs_0_), channel_id=1, source_target_pairs={{0,4},{1,5},{2,6},{3,7},{4,0},{5,1},{6,2},{7,3},{8,12},{9,13},{10,... | collective-permute-start | bytes 319496 | tf_op jit(solution)/shard_map/ppermute | solution.py:576
  13.5 2.4 %attend_own.3 = (bf16[2,1536,256]{2,1,0:T(8,128)(2,1)S(1)}, f32[2,1536,128]{2,1,0:T(8,128)S(1)}, s32[16]{0:T(128)S(1)}) custom-call(s32[1]{0:T(128)} %bitcast.tile_ref, s32[32]{0:T(128)S(1)} %copy-done.6, s32[16,16]{1,0:T(8,128)S(1)} %copy-done.5, s32[16]{0:T(128)S(1)} %copy-done.7, bf16[256,3072]{1,0:T(8,128)(2,1)S(1)} %bitcast.11, ...), custom_call_target="tpu_custom_call" | custom-call | flops 1207959552 | tf_op jit(solution)/shard_map/attend_own/pallas_call | solution.py:77
  16.0 1.0 %collective-permute-done.6.refs_1_ = bf16[2,16,1664]{2,1,0:T(8,128)(2,1)S(1)} collective-permute-done((bf16[2,16,1664]{2,1,0:T(8,128)(2,1)S(1)}, bf16[2,16,1664]{2,1,0:T(8,128)(2,1)S(1)}, u32[]{:S(2)}, u32[]{:S(2)}) %collective-permute-start.6) | collective-permute-done | bytes 106528 | tf_op jit(solution)/shard_map/ppermute | solution.py:576
  16.9 0.6 %collective-permute-done.7.refs_2_ = bf16[2,16,1664]{2,1,0:T(8,128)(2,1)S(1)} collective-permute-done((bf16[2,16,1664]{2,1,0:T(8,128)(2,1)S(1)}, bf16[2,16,1664]{2,1,0:T(8,128)(2,1)S(1)}, u32[]{:S(2)}, u32[]{:S(2)}) %collective-permute-start.7) | collective-permute-done | bytes 106528 | tf_op jit(solution)/shard_map/ppermute | solution.py:576
  17.5 0.0 collective-permute-done.5.refs_1_
  17.6 3.7 %collective-permute-start.10 = (bf16[16,16,1024]{2,1,0:T(8,128)(2,1)S(1)}, bf16[16,16,1024]{2,1,0:T(8,128)(2,1)S(1)}, u32[]{:S(2)}, u32[]{:S(2)}) collective-permute-start(bf16[16,16,1024]{2,1,0:T(8,128)(2,1)S(1)} %join_chip.1.refs_4_), channel_id=1, source_target_pairs={{0,1},{1,0},{2,3},{3,2},{4,5},{5,4},{6,7},{7,6},{8,9},{9,8},{10,11... | collective-permute-start | bytes 1572872 | tf_op jit(solution)/shard_map/ppermute | solution.py:576
  21.2 0.0 collective-permute-start.8
  21.3 0.3 collective-permute-start.9
  21.6 1.2 %collective-permute-done.10.refs_5_ = bf16[16,16,1024]{2,1,0:T(8,128)(2,1)S(1)} collective-permute-done((bf16[16,16,1024]{2,1,0:T(8,128)(2,1)S(1)}, bf16[16,16,1024]{2,1,0:T(8,128)(2,1)S(1)}, u32[]{:S(2)}, u32[]{:S(2)}) %collective-permute-start.10) | collective-permute-done | bytes 524320 | tf_op jit(solution)/shard_map/ppermute | solution.py:576
  22.8 2.7 %attend_past.1.attended = bf16[256,3072]{1,0:T(8,128)(2,1)S(1)} custom-call(s32[16]{0:T(128)S(1)} %get-tuple-element.54.slots, bf16[2,1536,256]{2,1,0:T(8,128)(2,1)S(1)} %get-tuple-element.55.refs_0_, bf16[2,1536,256]{2,1,0:T(8,128)(2,1)S(1)} %get-tuple-element.56.refs_1_, f32[2,1536,128]{2,1,0:T(8,128)S(1)} %get-tuple-element.57.refs_2_, ...), custom_call_target="tpu_custom_call" | custom-call | flops 10000000000 | tf_op jit(solution)/shard_map/attend_past/pallas_call | solution.py:199
  25.4 0.3 collective-permute-done.8.ours.refs_1_
  25.8 0.0 collective-permute-done.9.theirs.refs_2_
  25.8 0.9 %collective-permute-start.11 = (bf16[2,16,1664]{2,1,0:T(8,128)(2,1)S(1)}, bf16[2,16,1664]{2,1,0:T(8,128)(2,1)S(1)}, u32[]{:S(2)}, u32[]{:S(2)}) collective-permute-start(bf16[2,16,1664]{2,1,0:T(8,128)(2,1)S(1)} %collective-permute-done.8.ours.refs_1_), channel_id=1, source_target_pairs={{0,1},{1,0},{2,3},{3,2},{4,5},{5,4},{6,7},{7,6},{8,9},{9,8},{10,11... | collective-permute-start | bytes 319496 | tf_op jit(solution)/shard_map/ppermute | solution.py:576
  26.6 0.5 %project.1.part = f32[256,64]{1,0:T(8,128)S(1)} custom-call(s32[1]{0:T(128)} %bitcast.tile_ref, bf16[256,3072]{1,0:T(8,128)(2,1)S(1)} %attend_past.1.attended, bf16[6,16,1664]{2,1,0:T(8,128)(2,1)S(1)} %join_panels.1.ours.refs_0_, bf16[6,16,1664]{2,1,0:T(8,128)(2,1)S(1)} %collective-permute-done.9.theirs.refs_2_), custom_call_target="tpu_custom_call" | custom-call | tf_op jit(solution)/shard_map/project/pallas_call | solution.py:287
  27.2 0.4 %collective-permute-done.11.theirs.refs_3_ = bf16[2,16,1664]{2,1,0:T(8,128)(2,1)S(1)} collective-permute-done((bf16[2,16,1664]{2,1,0:T(8,128)(2,1)S(1)}, bf16[2,16,1664]{2,1,0:T(8,128)(2,1)S(1)}, u32[]{:S(2)}, u32[]{:S(2)}) %collective-permute-start.11) | collective-permute-done | bytes 106528 | tf_op jit(solution)/shard_map/ppermute | solution.py:576
  27.6 0.4 %finish.1 = (bf16[256,64]{1,0:T(8,128)(2,1)S(1)}, bf16[2,16,128]{2,1,0:T(8,128)(2,1)S(1)}, bf16[2,16,128]{2,1,0:T(8,128)(2,1)S(1)}) custom-call(s32[1]{0:T(128)} %bitcast.tile_ref, bf16[256,3072]{1,0:T(8,128)(2,1)S(1)} %attend_past.1.attended, bf16[2,16,1664]{2,1,0:T(8,128)(2,1)S(1)} %collective-permute-done.8.ours.refs_1_, ...), custom_call_target="tpu_custom_call" | custom-call | tf_op jit(solution)/shard_map/finish/pallas_call | solution.py:321
  28.0 0.4 %collective-permute-start.13 = (bf16[2,16,128]{2,1,0:T(8,128)(2,1)S(1)}, bf16[2,16,128]{2,1,0:T(8,128)(2,1)S(1)}, u32[]{:S(2)}, u32[]{:S(2)}) collective-permute-start(bf16[2,16,128]{2,1,0:T(8,128)(2,1)S(1)} %get-tuple-element.67), channel_id=1, source_target_pairs={{0,1},{1,0},{2,3},{3,2},{4,5},{5,4},{6,7},{7,6},{8,9},{9,8},{10,11... | collective-permute-start | bytes 24584 | tf_op jit(solution)/shard_map/ppermute | solution.py:576
  28.4 2.1 %collective-permute-start.12 = (bf16[2,16,128]{2,1,0:T(8,128)(2,1)S(1)}, bf16[2,16,128]{2,1,0:T(8,128)(2,1)S(1)}, u32[]{:S(2)}, u32[]{:S(2)}) collective-permute-start(bf16[2,16,128]{2,1,0:T(8,128)(2,1)S(1)} %get-tuple-element.64), channel_id=1, source_target_pairs={{1,2},{3,4},{5,6},{7,8},{9,10},{11,12},{13,14},{2,1},{4,3},{6,5},{... | collective-permute-start | bytes 24584 | tf_op jit(solution)/shard_map/ppermute | solution.py:655
  30.5 0.3 unpack.1.kernel
  30.9 0.0 collective-permute-done.13.from_pair
  30.9 1.8 %convolve_inner.1 = (bf16[2,4,128,512]{3,2,1,0:T(8,128)(2,1)}, f32[256,512]{1,0:T(8,128)S(1)}, bf16[2,128,512]{2,1,0:T(8,128)(2,1)S(1)}, bf16[144,512]{1,0:T(8,128)(2,1)S(1)}) custom-call(s32[1]{0:T(128)} %bitcast.tile_ref, bf16[2,2,64,64]{3,2,1,0:T(8,128)(2,1)S(1)} %bitcast.14, bf16[2,16,128]{2,1,0:T(8,128)(2,1)S(1)} %collective-permute-done.13.from_pair, ...), custom_call_target="tpu_custom_call" | custom-call | flops 452984832 | bytes 1048576 | tf_op jit(solution)/shard_map/convolve_inner/pallas_call | solution.py:512
  32.7 0.7 %collective-permute-done.12.from_next = bf16[2,16,128]{2,1,0:T(8,128)(2,1)S(1)} collective-permute-done((bf16[2,16,128]{2,1,0:T(8,128)(2,1)S(1)}, bf16[2,16,128]{2,1,0:T(8,128)(2,1)S(1)}, u32[]{:S(2)}, u32[]{:S(2)}) %collective-permute-start.12) | collective-permute-done | bytes 8224 | tf_op jit(solution)/shard_map/ppermute | solution.py:655
  33.4 1.1 %convolve_outer.1 = bf16[2,4,128,512]{3,2,1,0:T(8,128)(2,1)} custom-call(s32[1]{0:T(128)} %bitcast.tile_ref, bf16[2,16,128]{2,1,0:T(8,128)(2,1)S(1)} %collective-permute-done.12.from_next, bf16[2,32,256]{2,1,0:T(8,128)(2,1)S(1)} %get-tuple-element.65.outer_picks.picks, bf16[144,512]{1,0:T(8,128)(2,1)S(1)} %get-tuple-element.69.panel, ...), custom_call_target="tpu_custom_call", output_to_operand_aliasing={{}: (6, {})} | custom-call | tf_op jit(solution)/shard_map/convolve_outer/pallas_call | solution.py:558
  (4 shorter events, 0.1 us)
Async XLA Ops:
  0.0 4.6 %copy-start.1 = (bf16[192,64]{0,1:T(8,128)(2,1)S(1)}, bf16[192,64]{0,1:T(8,128)(2,1)}, u32[]{:S(2)}) copy-start(bf16[192,64]{0,1:T(8,128)(2,1)} %param.14) | copy-start | bytes 73732
  0.0 5.9 %copy-start.2 = (bf16[432,32]{0,1:T(8,128)(2,1)S(1)}, bf16[432,32]{0,1:T(8,128)(2,1)}, u32[]{:S(2)}) copy-start(bf16[432,32]{0,1:T(8,128)(2,1)} %param.15) | copy-start | bytes 82948
  0.0 6.1 %copy-start.4 = (bf16[2,2,64,1024]{3,2,1,0:T(8,128)(2,1)S(1)}, bf16[2,2,64,1024]{3,2,1,0:T(8,128)(2,1)}, u32[]{:S(2)}) copy-start(bf16[2,2,64,1024]{3,2,1,0:T(8,128)(2,1)} %param.9) | copy-start | bytes 1572868
  0.0 6.1 %copy-start.3 = (bf16[2,2,64,3072]{3,2,1,0:T(8,128)(2,1)S(1)}, bf16[2,2,64,3072]{3,2,1,0:T(8,128)(2,1)}, u32[]{:S(2)}) copy-start(bf16[2,2,64,3072]{3,2,1,0:T(8,128)(2,1)} %param.8) | copy-start | bytes 4718596
  0.0 6.1 %copy-start.6 = (s32[32]{0:T(128)S(1)}, s32[32]{0:T(128)}, u32[]{:S(2)}) copy-start(s32[32]{0:T(128)} %home.3) | copy-start | bytes 388
  0.0 6.1 %copy-start.5 = (s32[16,16]{1,0:T(8,128)S(1)}, s32[16,16]{1,0:T(8,128)}, u32[]{:S(2)}) copy-start(s32[16,16]{1,0:T(8,128)} %blocks.3) | copy-start | bytes 3076
  0.0 6.1 %copy-start.7 = (s32[16]{0:T(128)S(1)}, s32[16]{0:T(128)}, u32[]{:S(2)}) copy-start(s32[16]{0:T(128)} %lens.3) | copy-start | bytes 196
  0.0 8.9 %collective-permute-start = (bf16[2,16,1024]{2,1,0:T(8,128)(2,1)}, bf16[2,16,1024]{2,1,0:T(8,128)(2,1)S(1)}, u32[]{:S(2)}, u32[]{:S(2)}) collective-permute-start(bf16[2,16,1024]{2,1,0:T(8,128)(2,1)} %refs_0_.1), channel_id=1, source_target_pairs={{0,4},{1,5},{2,6},{3,7},{4,0},{5,1},{6,2},{7,3},{8,12},{9,13},{10,... | collective-permute-start | bytes 196616 | tf_op jit(solution)/shard_map/ppermute | solution.py:576
  2.2 6.7 %collective-permute-start.1 = (bf16[2,16,1024]{2,1,0:T(8,128)(2,1)}, bf16[2,16,1024]{2,1,0:T(8,128)(2,1)S(1)}, u32[]{:S(2)}, u32[]{:S(2)}) collective-permute-start(bf16[2,16,1024]{2,1,0:T(8,128)(2,1)} %refs_0_.1), channel_id=1, source_target_pairs={{0,8},{1,9},{2,10},{3,11},{4,12},{5,13},{6,14},{7,15},{8,0},{9,1},... | collective-permute-start | bytes 196616 | tf_op jit(solution)/shard_map/ppermute | solution.py:576
  4.6 5.2 %collective-permute-start.2 = (bf16[2,16,1024]{2,1,0:T(8,128)(2,1)}, bf16[2,16,1024]{2,1,0:T(8,128)(2,1)S(1)}, u32[]{:S(2)}, u32[]{:S(2)}) collective-permute-start(bf16[2,16,1024]{2,1,0:T(8,128)(2,1)} %refs_0_.1), channel_id=1, source_target_pairs={{0,12},{1,13},{2,14},{3,15},{4,8},{5,9},{6,10},{7,11},{8,4},{9,5},... | collective-permute-start | bytes 196616 | tf_op jit(solution)/shard_map/ppermute | solution.py:576
  4.6 3.8 %collective-permute-start.3 = (bf16[64,192]{1,0:T(8,128)(2,1)S(1)}, bf16[64,192]{1,0:T(8,128)(2,1)S(1)}, u32[]{:S(2)}, u32[]{:S(2)}) collective-permute-start(bf16[64,192]{1,0:T(8,128)(2,1)S(1)} %bitcast.6), channel_id=1, source_target_pairs={{0,2},{1,3},{2,0},{3,1},{4,6},{5,7},{6,4},{7,5},{8,10},{9,11},{10,... | collective-permute-start | bytes 73736 | tf_op jit(solution)/shard_map/ppermute | solution.py:576
  5.9 3.1 %collective-permute-start.4 = (bf16[32,432]{1,0:T(8,128)(2,1)S(1)}, bf16[32,432]{1,0:T(8,128)(2,1)S(1)}, u32[]{:S(2)}, u32[]{:S(2)}) collective-permute-start(bf16[32,432]{1,0:T(8,128)(2,1)S(1)} %bitcast.8), channel_id=1, source_target_pairs={{0,2},{1,3},{2,0},{3,1},{4,6},{5,7},{6,4},{7,5},{8,10},{9,11},{10,... | collective-permute-start | bytes 82952 | tf_op jit(solution)/shard_map/ppermute | solution.py:576
  6.2 3.6 %copy-start = (bf16[2,16,1024]{2,1,0:T(8,128)(2,1)S(1)}, bf16[2,16,1024]{2,1,0:T(8,128)(2,1)}, u32[]{:S(2)}) copy-start(bf16[2,16,1024]{2,1,0:T(8,128)(2,1)} %refs_0_.1) | copy-start | bytes 196612
  9.8 7.7 %collective-permute-start.5 = (bf16[8,16,1024]{2,1,0:T(8,128)(2,1)S(1)}, bf16[8,16,1024]{2,1,0:T(8,128)(2,1)S(1)}, u32[]{:S(2)}, u32[]{:S(2)}) collective-permute-start(bf16[8,16,1024]{2,1,0:T(8,128)(2,1)S(1)} %join_near.1.refs_0_), channel_id=1, source_target_pairs={{0,2},{1,3},{2,0},{3,1},{4,6},{5,7},{6,4},{7,5},{8,10},{9,11},{10,... | collective-permute-start | bytes 786440 | tf_op jit(solution)/shard_map/ppermute | solution.py:576
  11.2 5.8 %collective-permute-start.6 = (bf16[2,16,1664]{2,1,0:T(8,128)(2,1)S(1)}, bf16[2,16,1664]{2,1,0:T(8,128)(2,1)S(1)}, u32[]{:S(2)}, u32[]{:S(2)}) collective-permute-start(bf16[2,16,1664]{2,1,0:T(8,128)(2,1)S(1)} %pack.1.refs_0_), channel_id=1, source_target_pairs={{0,8},{1,9},{2,10},{3,11},{4,12},{5,13},{6,14},{7,15},{8,0},{9,1},... | collective-permute-start | bytes 319496 | tf_op jit(solution)/shard_map/ppermute | solution.py:576
  13.1 4.5 %collective-permute-start.7 = (bf16[2,16,1664]{2,1,0:T(8,128)(2,1)S(1)}, bf16[2,16,1664]{2,1,0:T(8,128)(2,1)S(1)}, u32[]{:S(2)}, u32[]{:S(2)}) collective-permute-start(bf16[2,16,1664]{2,1,0:T(8,128)(2,1)S(1)} %pack.1.refs_0_), channel_id=1, source_target_pairs={{0,4},{1,5},{2,6},{3,7},{4,0},{5,1},{6,2},{7,3},{8,12},{9,13},{10,... | collective-permute-start | bytes 319496 | tf_op jit(solution)/shard_map/ppermute | solution.py:576
  17.6 5.2 %collective-permute-start.10 = (bf16[16,16,1024]{2,1,0:T(8,128)(2,1)S(1)}, bf16[16,16,1024]{2,1,0:T(8,128)(2,1)S(1)}, u32[]{:S(2)}, u32[]{:S(2)}) collective-permute-start(bf16[16,16,1024]{2,1,0:T(8,128)(2,1)S(1)} %join_chip.1.refs_4_), channel_id=1, source_target_pairs={{0,1},{1,0},{2,3},{3,2},{4,5},{5,4},{6,7},{7,6},{8,9},{9,8},{10,11... | collective-permute-start | bytes 1572872 | tf_op jit(solution)/shard_map/ppermute | solution.py:576
  21.2 4.5 %collective-permute-start.8 = (bf16[2,16,1664]{2,1,0:T(8,128)(2,1)S(1)}, bf16[2,16,1664]{2,1,0:T(8,128)(2,1)S(1)}, u32[]{:S(2)}, u32[]{:S(2)}) collective-permute-start(bf16[2,16,1664]{2,1,0:T(8,128)(2,1)S(1)} %collective-permute-done.6.refs_1_), channel_id=1, source_target_pairs={{0,4},{1,5},{2,6},{3,7},{4,0},{5,1},{6,2},{7,3},{8,12},{9,13},{10,... | collective-permute-start | bytes 319496 | tf_op jit(solution)/shard_map/ppermute | solution.py:576
  21.3 4.5 %collective-permute-start.9 = (bf16[6,16,1664]{2,1,0:T(8,128)(2,1)S(1)}, bf16[6,16,1664]{2,1,0:T(8,128)(2,1)S(1)}, u32[]{:S(2)}, u32[]{:S(2)}) collective-permute-start(bf16[6,16,1664]{2,1,0:T(8,128)(2,1)S(1)} %join_panels.1.ours.refs_0_), channel_id=1, source_target_pairs={{0,1},{1,0},{2,3},{3,2},{4,5},{5,4},{6,7},{7,6},{8,9},{9,8},{10,11... | collective-permute-start | bytes 958472 | tf_op jit(solution)/shard_map/ppermute | solution.py:576
  25.8 1.8 %collective-permute-start.11 = (bf16[2,16,1664]{2,1,0:T(8,128)(2,1)S(1)}, bf16[2,16,1664]{2,1,0:T(8,128)(2,1)S(1)}, u32[]{:S(2)}, u32[]{:S(2)}) collective-permute-start(bf16[2,16,1664]{2,1,0:T(8,128)(2,1)S(1)} %collective-permute-done.8.ours.refs_1_), channel_id=1, source_target_pairs={{0,1},{1,0},{2,3},{3,2},{4,5},{5,4},{6,7},{7,6},{8,9},{9,8},{10,11... | collective-permute-start | bytes 319496 | tf_op jit(solution)/shard_map/ppermute | solution.py:576
  28.0 2.9 %collective-permute-start.13 = (bf16[2,16,128]{2,1,0:T(8,128)(2,1)S(1)}, bf16[2,16,128]{2,1,0:T(8,128)(2,1)S(1)}, u32[]{:S(2)}, u32[]{:S(2)}) collective-permute-start(bf16[2,16,128]{2,1,0:T(8,128)(2,1)S(1)} %get-tuple-element.67), channel_id=1, source_target_pairs={{0,1},{1,0},{2,3},{3,2},{4,5},{5,4},{6,7},{7,6},{8,9},{9,8},{10,11... | collective-permute-start | bytes 24584 | tf_op jit(solution)/shard_map/ppermute | solution.py:576
  28.4 5.0 %collective-permute-start.12 = (bf16[2,16,128]{2,1,0:T(8,128)(2,1)S(1)}, bf16[2,16,128]{2,1,0:T(8,128)(2,1)S(1)}, u32[]{:S(2)}, u32[]{:S(2)}) collective-permute-start(bf16[2,16,128]{2,1,0:T(8,128)(2,1)S(1)} %get-tuple-element.64), channel_id=1, source_target_pairs={{1,2},{3,4},{5,6},{7,8},{9,10},{11,12},{13,14},{2,1},{4,3},{6,5},{... | collective-permute-start | bytes 24584 | tf_op jit(solution)/shard_map/ppermute | solution.py:655
